TPU v7x, 32 devices: a whole 2x2x4 slice. The times are simulated.
32 devices in a mesh: experts: 4 (over z), context: 4 (over x, core), dp: 2 (over y).
Axes of the slice: x: 2, y: 2, z: 4, core: 2. Of those that a mesh axis runs over, the one named last changes fastest.
Arguments:
- tokens: bfloat16 [8, 1024, 1024], P(('experts', 'dp'), 'context'), may hold values from -6 to 6
- doc_starts: int32 [8, 8], P(('experts', 'dp')), may hold values from 0 to 1023, as said below
- expert_ids: int32 [8, 1024, 2], P(('experts', 'dp'), 'context'), may hold values from 0 to 3, all different within a row; in each aligned block of 256 rows (0 to 255, 256 to 511, ..., all dimensions but the last counted through in order) at most 160 rows name the same one
- attn_in: bfloat16 [2, 1024, 3072], P(None, ('experts', 'context', 'dp')), may hold values from -0.1875 to 0.1875
- attn_out: bfloat16 [2, 1024, 1024], P(None, ('experts', 'context', 'dp')), may hold values from -1 to 1
- router: bfloat16 [2, 1024, 4], P(None, ('experts', 'context', 'dp')), may hold values from -0.09375 to 0.09375
- gains: bfloat16 [2, 1024, 2], P(None, ('experts', 'context', 'dp')), may hold values from 0.099609375 to 1.8984375
- rel_table: bfloat16 [2, 512], P(None, ('experts', 'context', 'dp')), may hold values from -4 to 4
- expert_in: bfloat16 [2, 4, 1024, 5632], P(None, 'experts'), may hold values from -0.1875 to 0.1875
- expert_out: bfloat16 [2, 4, 1024, 2816], P(None, 'experts'), may hold values from -0.109375 to 0.109375
- out_grad: bfloat16 [8, 1024, 1024], P(('experts', 'dp'), 'context'), may hold values from -6 to 6
Outputs:
- result: bfloat16 [8, 1024, 1024], P(('experts', 'dp'), 'context')
- tokens_grad: float32 [8, 1024, 1024], P(('experts', 'dp'), 'context')
- attn_in_grad: float32 [2, 1024, 3072], P(None, ('experts', 'context', 'dp'))
- attn_out_grad: float32 [2, 1024, 1024], P(None, ('experts', 'context', 'dp'))
- router_grad: float32 [2, 1024, 4], P(None, ('experts', 'context', 'dp'))
- gains_grad: float32 [2, 1024, 2], P(None, ('experts', 'context', 'dp'))
- rel_table_grad: float32 [2, 512], P(None, ('experts', 'context', 'dp'))
- expert_in_grad: float32 [2, 4, 1024, 5632], P(None, 'experts', ('context', 'dp'))
- expert_out_grad: float32 [2, 4, 1024, 2816], P(None, 'experts', ('context', 'dp'))
Inputs may be any that keep to these rules, and one draw needn't show every extreme that they name: `doc_starts`: each row holds the document starts of one sequence, not falling, the first 0; equal values mark empty documents. `expert_ids`: the two experts of a token differ; within each aligned block of 256 tokens no expert is named more than 160 times.
All inputs are finite; a program needn't handle non-finite values.
Results may differ from a plain program's by a relative error of at most 0.023.
Values may be sent and summed in bfloat16 or wider, within the bound.
No kernel may reach another device: no remote copies, remote signals or barrier semaphores. Data moves between devices by JAX's collectives and lax.ppermute only.
A program may use at most 384 MiB of HBM per device.

v0:
```python
import math

import jax
import jax.numpy as jnp
import numpy as np
from jax import lax
from jax.sharding import PartitionSpec as P

D = 1024
HEADS = 16
HEAD_DIM = 64
FF = 2816
BUCKETS = 32
MAX_DISTANCE = 128
LAYERS = 2


EPSILON = 1e-06
NEGATIVE = -1e30
SCORE_SCALE = 0.125


def bucket_bounds(bucket_count, far_reach):
    half_count = bucket_count // 2
    bounds = list(range(1, half_count + 1))
    for section_index in range(1, half_count):
        bounds.append(
            int(math.ceil(half_count * (far_reach / half_count) ** (section_index / half_count)))
        )
    return np.array(bounds, np.int32)


def bucket_of(distance):
    bounds = jnp.asarray(bucket_bounds(BUCKETS, MAX_DISTANCE))
    return jnp.sum((distance[..., None] >= bounds).astype(jnp.int32), -1)


def rms_scale(inputs):
    return lax.rsqrt(jnp.mean(inputs * inputs, -1, keepdims=True) + EPSILON)


def norm_back(inputs, gain_row, upstream):
    inverse = rms_scale(inputs)
    scaled = upstream * gain_row
    inner_mean = jnp.mean(inputs * scaled, -1, keepdims=True)
    grad_inputs = inverse * scaled - inputs * (inverse * inverse * inverse) * inner_mean
    grad_gain = jnp.sum(upstream * inputs * inverse, 0)
    return (grad_inputs, grad_gain)


def glu_value(gate_part, up_part):
    return jax.nn.gelu(gate_part, approximate=True) * up_part


def layout(query_rows, starts):
    key_total = query_rows * lax.axis_size("context")
    key_places = jnp.arange(key_total, dtype=jnp.int32)
    query_places = lax.axis_index("context") * query_rows + jnp.arange(query_rows, dtype=jnp.int32)
    owner_keys = jnp.sum((starts[None, :] <= key_places[:, None]).astype(jnp.int32), 1)
    owner_queries = jnp.sum((starts[None, :] <= query_places[:, None]).astype(jnp.int32), 1)
    allowed = (owner_queries[:, None] == owner_keys[None, :]) & (
        key_places[None, :] <= query_places[:, None]
    )
    return allowed


def masked_bias(bias_table, allowed, query_offset):
    query_rows = allowed.shape[0]
    key_total = allowed.shape[1]
    skew_width = key_total + query_rows - 1
    distance = query_offset + jnp.arange(skew_width, dtype=jnp.int32) - (key_total - 1)
    bucket_hits = (
        bucket_of(jnp.maximum(distance, 0))[:, None]
        == jnp.arange(BUCKETS, dtype=jnp.int32)[None, :]
    ).astype(jnp.float32)
    offset_row = jnp.dot(bucket_hits, bias_table, precision=lax.Precision.HIGHEST).T[:, ::-1]
    padded_row = jnp.pad(offset_row, ((0, 0), (0, 1)))
    tiled = jnp.tile(padded_row, (1, query_rows))[:, : query_rows * skew_width]
    skewed = tiled.reshape(HEADS, query_rows, skew_width)[
        :, :, query_rows - 1 : query_rows - 1 + key_total
    ]
    return jnp.where(allowed[None], skewed, NEGATIVE)


def score_grid(queries, keys_all, bias_grid):
    query_rows = queries.shape[0]
    raw_scores = jnp.einsum(
        "qhd,khd->hqk",
        queries.reshape(query_rows, HEADS, HEAD_DIM),
        keys_all.reshape(keys_all.shape[0], HEADS, HEAD_DIM),
        preferred_element_type=jnp.float32,
    )
    return raw_scores * SCORE_SCALE + bias_grid


def table_grad(grad_scores, query_offset):
    query_rows = grad_scores.shape[1]
    key_total = grad_scores.shape[2]
    skew_width = key_total + query_rows
    padded = jnp.pad(grad_scores[:, :, ::-1], ((0, 0), (0, 0), (0, query_rows)))
    flat_grid = padded.reshape(HEADS, query_rows * skew_width)[:, : query_rows * (skew_width - 1)]
    column = jnp.sum(flat_grid.reshape(HEADS, query_rows, skew_width - 1), 1, dtype=jnp.float32)
    distance = query_offset + jnp.arange(skew_width - 1, dtype=jnp.int32) - (key_total - 1)
    bucket_hits = (
        (
            bucket_of(jnp.maximum(distance, 0))[:, None]
            == jnp.arange(BUCKETS, dtype=jnp.int32)[None, :]
        )
        & (distance[:, None] >= 0)
    ).astype(jnp.float32)
    return jnp.dot(column, bucket_hits, precision=lax.Precision.HIGHEST).T.reshape(BUCKETS * HEADS)


def attention_forward(stream, gain_row, w_attn_in, w_attn_out, bias_grid):
    query_rows = stream.shape[0]
    normed_low = (stream * rms_scale(stream) * gain_row).astype(jnp.bfloat16)
    packed = jnp.dot(normed_low, w_attn_in, preferred_element_type=jnp.float32).astype(jnp.bfloat16)
    keys_all, values_all = (
        lax.all_gather(packed[:, D : 2 * D], "context", axis=0, tiled=True),
        lax.all_gather(packed[:, 2 * D :], "context", axis=0, tiled=True),
    )
    scores = score_grid(packed[:, :D], keys_all, bias_grid)
    row_peak = jnp.max(scores, -1, keepdims=True)
    log_total = row_peak + jnp.log(jnp.sum(jnp.exp(scores - row_peak), -1, keepdims=True))
    weights = jnp.exp(scores - log_total).astype(jnp.bfloat16)
    mixed_rows = (
        jnp.einsum(
            "hqk,khd->qhd",
            weights,
            values_all.reshape(-1, HEADS, HEAD_DIM),
            preferred_element_type=jnp.float32,
        )
        .reshape(query_rows, D)
        .astype(jnp.bfloat16)
    )
    attended = jnp.dot(mixed_rows, w_attn_out, preferred_element_type=jnp.float32)
    return (attended, (normed_low, packed, keys_all, values_all, bias_grid, log_total, mixed_rows))


def attention_backward(
    layer_input, gain_row, w_attn_in, w_attn_out, attn_state, grad_middle, query_offset
):
    normed_low, packed, keys_all, values_all, bias_grid, log_total, mixed_rows = attn_state
    query_rows = layer_input.shape[0]
    key_total = keys_all.shape[0]
    grad_low = grad_middle.astype(jnp.bfloat16)
    grad_w_out = jnp.einsum("qd,qf->df", mixed_rows, grad_low, preferred_element_type=jnp.float32)
    grad_mixed = (
        jnp.einsum("qf,df->qd", grad_low, w_attn_out, preferred_element_type=jnp.float32)
        .astype(jnp.bfloat16)
        .reshape(query_rows, HEADS, HEAD_DIM)
    )
    scores = score_grid(packed[:, :D], keys_all, bias_grid)
    softmax_p = jnp.exp(scores - log_total)
    values_heads = values_all.reshape(key_total, HEADS, HEAD_DIM)
    keys_heads = keys_all.reshape(key_total, HEADS, HEAD_DIM)
    queries = packed[:, :D].reshape(query_rows, HEADS, HEAD_DIM)
    grad_prob = jnp.einsum(
        "qhd,khd->hqk", grad_mixed, values_heads, preferred_element_type=jnp.float32
    )
    row_dot = jnp.sum(softmax_p * grad_prob, -1, keepdims=True)
    grad_scores = (softmax_p * (grad_prob - row_dot)).astype(jnp.bfloat16)
    weights = softmax_p.astype(jnp.bfloat16)
    grad_queries = (
        jnp.einsum("hqk,khd->qhd", grad_scores, keys_heads, preferred_element_type=jnp.float32)
        * SCORE_SCALE
    )
    grad_keys = (
        jnp.einsum("hqk,qhd->khd", grad_scores, queries, preferred_element_type=jnp.float32)
        * SCORE_SCALE
    )
    grad_values = jnp.einsum(
        "hqk,qhd->khd", weights, grad_mixed, preferred_element_type=jnp.float32
    )
    grad_keys_mine, grad_values_mine = (
        lax.psum_scatter(
            grad_keys.reshape(key_total, D).astype(jnp.bfloat16),
            "context",
            scatter_dimension=0,
            tiled=True,
        ).astype(jnp.float32),
        lax.psum_scatter(
            grad_values.reshape(key_total, D).astype(jnp.bfloat16),
            "context",
            scatter_dimension=0,
            tiled=True,
        ).astype(jnp.float32),
    )
    grad_packed = jnp.concatenate(
        [grad_queries.reshape(query_rows, D), grad_keys_mine, grad_values_mine], 1
    ).astype(jnp.bfloat16)
    grad_w_in = jnp.einsum("qd,qf->df", normed_low, grad_packed, preferred_element_type=jnp.float32)
    grad_normed = jnp.einsum(
        "qf,df->qd", grad_packed, w_attn_in, preferred_element_type=jnp.float32
    )
    grad_input, grad_gain = norm_back(layer_input, gain_row, grad_normed)
    grad_table = table_grad(grad_scores, query_offset)
    return (grad_input, grad_w_in, grad_w_out, grad_gain, grad_table)


def experts_forward(middle, gain_row, w_router, routes, w_in_local, w_out_local):
    normed = middle * rms_scale(middle) * gain_row
    router_float = w_router.astype(jnp.float32)
    logits = jnp.dot(normed, router_float, precision=lax.Precision.HIGHEST)
    softmax_p = jax.nn.softmax(logits, -1)
    query_rows = normed.shape[0]
    experts_total = router_float.shape[1]
    capacity = (10 * query_rows + 4 * experts_total - 1) // (4 * experts_total)
    pick_table = (
        routes[:, :, None] == jnp.arange(experts_total, dtype=jnp.int32)[None, None, :]
    ).astype(jnp.float32)
    picked = jnp.sum(softmax_p[:, None, :] * pick_table, -1)
    pick_total = jnp.sum(picked, -1, keepdims=True)
    gate_values = picked / pick_total
    flat_hits = pick_table.reshape(query_rows * 2, experts_total).astype(jnp.int32)
    slot_index = jnp.sum(flat_hits * jnp.cumsum(flat_hits, 0), -1) - 1
    expert_index = routes.reshape(query_rows * 2)
    doubled = jnp.repeat(normed.astype(jnp.bfloat16), 2, axis=0)
    outgoing = (
        jnp.zeros((experts_total, capacity, D), jnp.bfloat16)
        .at[expert_index, slot_index]
        .set(doubled)
    )
    local_count = w_in_local.shape[0]
    arrived = lax.all_to_all(outgoing, "experts", split_axis=0, concat_axis=0, tiled=True)
    sources = arrived.shape[0] // local_count
    grouped = arrived.reshape(sources, local_count, arrived.shape[1], D)
    inner_rows = jnp.einsum(
        "nlcd,ldf->nlcf", grouped, w_in_local, preferred_element_type=jnp.float32
    )
    hidden = glu_value(inner_rows[..., :FF], inner_rows[..., FF:]).astype(jnp.bfloat16)
    produced = jnp.einsum(
        "nlcf,ldf->nlcd", hidden, w_out_local, preferred_element_type=jnp.float32
    ).astype(jnp.bfloat16)
    produced, inner_rows, arrived = (
        produced.reshape(arrived.shape),
        inner_rows.reshape(arrived.shape[0], arrived.shape[1], 2 * FF),
        arrived,
    )
    returned = lax.all_to_all(produced, "experts", split_axis=0, concat_axis=0, tiled=True)
    chosen_out = returned[expert_index, slot_index].astype(jnp.float32).reshape(query_rows, 2, D)
    mixture = jnp.sum(gate_values[:, :, None] * chosen_out, 1)
    kept_state = (
        normed,
        router_float,
        softmax_p,
        pick_table,
        gate_values,
        pick_total,
        expert_index,
        slot_index,
        chosen_out,
        inner_rows,
        arrived,
    )
    return (mixture, kept_state)


def experts_backward(kept_state, middle, gain_row, w_in_local, w_out_local, upstream):
    (
        normed,
        router_float,
        softmax_p,
        pick_table,
        gate_values,
        pick_total,
        expert_index,
        slot_index,
        chosen_out,
        inner_rows,
        arrived,
    ) = kept_state
    query_rows = normed.shape[0]
    local_count = w_in_local.shape[0]
    grad_gates = jnp.sum(upstream[:, None, :] * chosen_out, -1)
    grad_rows = (
        (gate_values[:, :, None] * upstream[:, None, :])
        .astype(jnp.bfloat16)
        .reshape(query_rows * 2, D)
    )
    outgoing = jnp.zeros(arrived.shape, jnp.bfloat16).at[expert_index, slot_index].set(grad_rows)
    arrived_grad = lax.all_to_all(outgoing, "experts", split_axis=0, concat_axis=0, tiled=True)
    sources = arrived.shape[0] // local_count
    grouped = arrived.reshape(sources, local_count, arrived.shape[1], D)
    grouped_grad = arrived_grad.reshape(grouped.shape)
    inner_split = inner_rows.reshape(sources, local_count, arrived.shape[1], 2 * FF)
    hidden, pull_back = jax.vjp(glu_value, inner_split[..., :FF], inner_split[..., FF:])
    grad_hidden = jnp.einsum(
        "nlcd,ldf->nlcf", grouped_grad, w_out_local, preferred_element_type=jnp.float32
    )
    grad_gate, grad_up = pull_back(grad_hidden)
    grad_inner = jnp.concatenate([grad_gate, grad_up], -1).astype(jnp.bfloat16)
    grad_w_in = jnp.einsum(
        "nlcd,nlcf->ldf", grouped, grad_inner, preferred_element_type=jnp.float32
    )
    grad_w_out = jnp.einsum(
        "nlcd,nlcf->ldf",
        grouped_grad,
        hidden.astype(jnp.bfloat16),
        preferred_element_type=jnp.float32,
    )
    sent_back = (
        jnp.einsum("nlcf,ldf->nlcd", grad_inner, w_in_local, preferred_element_type=jnp.float32)
        .astype(jnp.bfloat16)
        .reshape(arrived.shape)
    )
    came_back = lax.all_to_all(sent_back, "experts", split_axis=0, concat_axis=0, tiled=True)
    grad_normed = jnp.sum(
        came_back[expert_index, slot_index].astype(jnp.float32).reshape(query_rows, 2, D), 1
    )
    gate_gap = grad_gates[:, 0] - grad_gates[:, 1]
    grad_picked = (
        jnp.stack([gate_values[:, 1] * gate_gap, -gate_values[:, 0] * gate_gap], -1) / pick_total
    )
    grad_soft = jnp.sum(grad_picked[:, :, None] * pick_table, 1)
    grad_logits = softmax_p * (grad_soft - jnp.sum(softmax_p * grad_soft, -1, keepdims=True))
    grad_router = jnp.dot(normed.T, grad_logits, precision=lax.Precision.HIGHEST)
    grad_normed = grad_normed + jnp.dot(
        grad_logits, router_float.T, precision=lax.Precision.HIGHEST
    )
    grad_middle, grad_gain = norm_back(middle, gain_row, grad_normed)
    return (grad_middle, grad_router, grad_gain, grad_w_in, grad_w_out)


def on_device(
    tokens,
    doc_starts,
    expert_ids,
    attn_in,
    attn_out,
    router,
    gains,
    rel_table,
    expert_in,
    expert_out,
    out_grad,
):
    stream = tokens[0].astype(jnp.float32)
    starts = doc_starts[0]
    routes = expert_ids[0]
    query_rows = stream.shape[0]
    query_offset = lax.axis_index("context") * query_rows
    allowed = layout(query_rows, starts)
    layer_store = []
    for layer_index in range(LAYERS):
        w_attn_in, w_attn_out, w_router, w_gains, w_table = (
            lax.all_gather(attn_in[layer_index], ("experts", "context", "dp"), axis=0, tiled=True),
            lax.all_gather(attn_out[layer_index], ("experts", "context", "dp"), axis=0, tiled=True),
            lax.all_gather(router[layer_index], ("experts", "context", "dp"), axis=0, tiled=True),
            lax.all_gather(gains[layer_index], ("experts", "context", "dp"), axis=0, tiled=True),
            lax.all_gather(
                rel_table[layer_index], ("experts", "context", "dp"), axis=0, tiled=True
            ),
        )
        gain_pair = w_gains.astype(jnp.float32)
        bias_grid = masked_bias(
            w_table.astype(jnp.float32).reshape(BUCKETS, HEADS), allowed, query_offset
        )
        attended, attn_state = attention_forward(
            stream, gain_pair[:, 0], w_attn_in, w_attn_out, bias_grid
        )
        middle = stream + attended
        mixture, moe_state = experts_forward(
            middle,
            gain_pair[:, 1],
            w_router,
            routes,
            expert_in[layer_index],
            expert_out[layer_index],
        )
        layer_store.append(
            (stream, middle, w_attn_in, w_attn_out, gain_pair, attn_state, moe_state)
        )
        stream = middle + mixture
    result = stream.astype(jnp.bfloat16)[None]
    upstream = out_grad[0].astype(jnp.float32)
    dense_store = []
    expert_store = []
    for layer_index in range(LAYERS - 1, -1, -1):
        layer_input, middle, w_attn_in, w_attn_out, gain_pair, attn_state, moe_state = layer_store[
            layer_index
        ]
        grad_branch, grad_router, grad_gain_two, grad_w_in, grad_w_out = experts_backward(
            moe_state,
            middle,
            gain_pair[:, 1],
            expert_in[layer_index],
            expert_out[layer_index],
            upstream,
        )
        grad_middle = upstream + grad_branch
        grad_input, grad_attn_in, grad_attn_out, grad_gain_one, grad_table = attention_backward(
            layer_input,
            gain_pair[:, 0],
            w_attn_in,
            w_attn_out,
            attn_state,
            grad_middle,
            query_offset,
        )
        upstream = grad_middle + grad_input
        grad_gains = jnp.stack([grad_gain_one, grad_gain_two], 1)
        dense_parts = (
            lax.psum_scatter(
                grad_attn_in, ("experts", "context", "dp"), scatter_dimension=0, tiled=True
            ),
            lax.psum_scatter(
                grad_attn_out, ("experts", "context", "dp"), scatter_dimension=0, tiled=True
            ),
            lax.psum_scatter(
                grad_router, ("experts", "context", "dp"), scatter_dimension=0, tiled=True
            ),
            lax.psum_scatter(
                grad_gains, ("experts", "context", "dp"), scatter_dimension=0, tiled=True
            ),
            lax.psum_scatter(
                grad_table, ("experts", "context", "dp"), scatter_dimension=0, tiled=True
            ),
        )
        expert_parts = (
            lax.psum_scatter(
                grad_w_in.astype(jnp.bfloat16), ("context", "dp"), scatter_dimension=1, tiled=True
            ).astype(jnp.float32),
            lax.psum_scatter(
                grad_w_out.astype(jnp.bfloat16), ("context", "dp"), scatter_dimension=1, tiled=True
            ).astype(jnp.float32),
        )
        dense_store.insert(0, dense_parts)
        expert_store.insert(0, expert_parts)
    dense_grads = tuple(
        (jnp.stack([layer_entry[member] for layer_entry in dense_store]) for member in range(5))
    )
    expert_grads = tuple(
        (jnp.stack([layer_entry[member] for layer_entry in expert_store]) for member in range(2))
    )
    return (
        result,
        upstream[None],
        dense_grads[0],
        dense_grads[1],
        dense_grads[2],
        dense_grads[3],
        dense_grads[4],
        expert_grads[0],
        expert_grads[1],
    )


def solution(mesh):
    return jax.shard_map(
        on_device,
        mesh=mesh,
        in_specs=(
            P(("experts", "dp"), "context", None),
            P(("experts", "dp"), None),
            P(("experts", "dp"), "context", None),
            P(None, ("experts", "context", "dp"), None),
            P(None, ("experts", "context", "dp"), None),
            P(None, ("experts", "context", "dp"), None),
            P(None, ("experts", "context", "dp"), None),
            P(None, ("experts", "context", "dp")),
            P(None, "experts", None, None),
            P(None, "experts", None, None),
            P(("experts", "dp"), "context", None),
        ),
        out_specs=(
            P(("experts", "dp"), "context", None),
            P(("experts", "dp"), "context", None),
            P(None, ("experts", "context", "dp"), None),
            P(None, ("experts", "context", "dp"), None),
            P(None, ("experts", "context", "dp"), None),
            P(None, ("experts", "context", "dp"), None),
            P(None, ("experts", "context", "dp")),
            P(None, "experts", ("context", "dp"), None),
            P(None, "experts", ("context", "dp"), None),
        ),
        check_vma=False,
    )
```

profile of v0, /device:TPU:0, one launch (start us, length us, event | category | flops | bytes accessed | tf_op | source)
XLA Modules:
  0.0 2829.8 jit_solution(9662925082692762972)
XLA Ops:
  9.9 74.4 %all-gather = bf16[1,1024,2]{2,0,1:T(2,128)(2,1)S(1)} all-gather(bf16[1,32,2]{2,0,1:T(2,128)(2,1)S(1)} %copy.182), channel_id=2, replica_groups=mesh['experts'=4,'context'=4,'dp'=2] {'experts','context','dp'}, dimensions={1}, use_global_device_ids=true | all-gather | bytes 4224 | tf_op jit(solution)/shard_map/all_gather | solution.py:350
  96.6 38.6 %all-reduce.9 = (bf16[512]{0:T(512)(128)(2,1)S(1)}, bf16[512]{0:T(512)(128)(2,1)}) all-reduce(bf16[512]{0:T(512)(128)(2,1)S(1)} %dynamic-update-slice, bf16[512]{0:T(512)(128)(2,1)S(1)} %dynamic-update-slice.1), channel_id=4, replica_groups=mesh['experts'=4,'context'=4,'dp'=2] {'experts','context','dp'}, use_global_device_ids=true, to_apply=%add.4 | all-reduce | flops 1024 | bytes 4096
  147.0 18.5 copy.190
  172.9 38.0 %reshape.624 = f32[16,256,1279]{2,1,0:T(8,128)} reshape(f32[16,327424]{1,0:T(8,128)} %slice.212) | data formatting | bytes 41910272 | tf_op jit(solution)/shard_map/reshape | solution.py:79
  257.1 33.2 %scatter_fusion = bf16[4,160,1024]{2,1,0:T(8,128)(2,1)S(1)} fusion(bf16[4,160,1024]{2,1,0:T(8,128)(2,1)S(1)} %broadcast.361.clone, s32[512]{0:T(512)S(1)} %bitcast.336, bf16[512,1024]{1,0:T(8,128)(2,1)S(1)} %reshape.681), kind=kCustom, calls=%fused_computation.4 | custom fusion | bytes 3149824 | tf_op jit(solution)/shard_map/scatter | solution.py:222
  290.3 34.5 %all_to_all.40 = bf16[4,160,1024]{2,1,0:T(8,128)(2,1)S(1)} all-to-all(bf16[4,160,1024]{2,1,0:T(8,128)(2,1)S(1)} %scatter_fusion), channel_id=1, replica_groups=mesh['experts'=4,'context'=4,'dp'=2] {'experts'}, dimensions={0} | all-to-all | bytes 2621440 | tf_op jit(solution)/shard_map/all_to_all | solution.py:225
  355.4 84.9 %all-gather.4 = bf16[1,1024,4]{2,0,1:T(2,128)(2,1)S(1)} all-gather(bf16[1,32,4]{2,0,1:T(2,128)(2,1)S(1)} %copy.183), channel_id=6, replica_groups=mesh['experts'=4,'context'=4,'dp'=2] {'experts','context','dp'}, dimensions={1}, use_global_device_ids=true | all-gather | bytes 8448 | tf_op jit(solution)/shard_map/all_gather | solution.py:349
  440.6 66.2 %all-gather.5 = bf16[1,1024,2]{2,0,1:T(2,128)(2,1)S(1)} all-gather(bf16[1,32,2]{2,0,1:T(2,128)(2,1)S(1)} %copy.184), channel_id=7, replica_groups=mesh['experts'=4,'context'=4,'dp'=2] {'experts','context','dp'}, dimensions={1}, use_global_device_ids=true | all-gather | bytes 4224 | tf_op jit(solution)/shard_map/all_gather | solution.py:350
  541.0 18.5 copy.192
  566.9 38.2 %reshape.634 = f32[16,256,1279]{2,1,0:T(8,128)} reshape(f32[16,327424]{1,0:T(8,128)} %slice.222) | data formatting | bytes 41910272 | tf_op jit(solution)/shard_map/reshape | solution.py:79
  652.0 74.9 %scatter_fusion.1 = bf16[4,160,1024]{2,1,0:T(8,128)(2,1)} fusion(bf16[4,160,1024]{2,1,0:T(8,128)(2,1)} %broadcast.361.clone.1, s32[512]{0:T(512)S(1)} %bitcast.337, bf16[512,1024]{1,0:T(8,128)(2,1)S(1)} %reshape.687), kind=kCustom, calls=%fused_computation.5 | custom fusion | bytes 3149824 | tf_op jit(solution)/shard_map/scatter | solution.py:222
  731.5 84.8 %all-gather.9 = bf16[1,1024,4]{2,0,1:T(2,128)(2,1)S(1)} all-gather(bf16[1,32,4]{2,0,1:T(2,128)(2,1)S(1)} %copy.185), channel_id=11, replica_groups=mesh['experts'=4,'context'=4,'dp'=2] {'experts','context','dp'}, dimensions={1}, use_global_device_ids=true | all-gather | bytes 8448 | tf_op jit(solution)/shard_map/all_gather | solution.py:349
  825.0 75.3 %scatter_fusion.2 = bf16[4,160,1024]{2,1,0:T(8,128)(2,1)} fusion(bf16[4,160,1024]{2,1,0:T(8,128)(2,1)} %broadcast.361.clone.2, s32[512]{0:T(512)S(1)} %bitcast.338, bf16[512,1024]{1,0:T(8,128)(2,1)S(1)} %multiply_convert_fusion.7), kind=kCustom, calls=%fused_computation.6 | custom fusion | bytes 3149824 | tf_op jit(solution)/shard_map/scatter | solution.py:281
  932.7 15.7 fusion.72
  974.7 22.1 all-to-all-done.5
  1101.7 26.9 reduce-scatter.25.cloned.1.call-done
  1141.0 50.7 %scatter_fusion.3 = bf16[4,160,1024]{2,1,0:T(8,128)(2,1)S(1)} fusion(bf16[4,160,1024]{2,1,0:T(8,128)(2,1)S(1)} %broadcast.361, s32[512]{0:T(512)S(1)} %bitcast.339, bf16[512,1024]{1,0:T(8,128)(2,1)} %multiply_convert_fusion.6), kind=kCustom, calls=%fused_computation.7 | custom fusion | bytes 3149824 | tf_op jit(solution)/shard_map/scatter | solution.py:281
  1191.6 36.2 %all_to_all.41 = bf16[4,160,1024]{2,1,0:T(8,128)(2,1)S(1)} all-to-all(bf16[4,160,1024]{2,1,0:T(8,128)(2,1)S(1)} %scatter_fusion.3), channel_id=1, replica_groups=mesh['experts'=4,'context'=4,'dp'=2] {'experts'}, dimensions={0} | all-to-all | bytes 2621440 | tf_op jit(solution)/shard_map/all_to_all | solution.py:282
  1263.3 27.6 all-to-all-done.7
  1351.7 27.5 reduce-scatter.29.cloned.1.call-done
  1444.1 125.0 %rev.15 = bf16[16,256,1024]{2,1,0:T(8,128)(2,1)} reverse(bf16[16,256,1024]{2,1,0:T(8,128)(2,1)} %copy-done), dimensions={2} | reverse | bytes 16777216 | tf_op jit(solution)/shard_map/rev | solution.py:100
  1611.5 37.8 %reshape.654 = f32[16,256,1279]{2,1,0:T(8,128)} reshape(f32[16,327424]{1,0:T(8,128)} %slice_convert_fusion) | data formatting | bytes 41910272 | tf_op jit(solution)/shard_map/convert_element_type | solution.py:102
  1659.9 119.5 %reduce-scatter.49.cloned.1.call-done = f32[32,4]{1,0:T(8,128)} async-done(((f32[1024,4]{1,0:T(8,128)}), f32[32,4]{1,0:T(8,128)}) %reduce-scatter.49.cloned.1.call-update) | async-done | bytes 528
  1780.8 125.1 %rev.14 = bf16[16,256,1024]{2,1,0:T(8,128)(2,1)} reverse(bf16[16,256,1024]{2,1,0:T(8,128)(2,1)} %copy-done.1), dimensions={2} | reverse | bytes 16777216 | tf_op jit(solution)/shard_map/rev | solution.py:100
  1947.8 39.5 %reshape.653 = f32[16,256,1279]{2,1,0:T(8,128)} reshape(f32[16,327424]{1,0:T(8,128)} %slice_convert_fusion.1) | data formatting | bytes 41910272 | tf_op jit(solution)/shard_map/convert_element_type | solution.py:102
  1997.1 37.5 %all-reduce.8 = (f32[512]{0:T(512)S(1)}, f32[512]{0:T(512)S(1)}) all-reduce(f32[512]{0:T(512)S(1)} %reshape.646, f32[512]{0:T(512)S(1)} %reshape.644), channel_id=25, replica_groups=mesh['experts'=4,'context'=4,'dp'=2] {'experts','context','dp'}, use_global_device_ids=true, to_apply=%region_64.65.clone | all-reduce | flops 1024 | bytes 8192
  2040.9 138.1 %reduce-scatter.39.cloned.1.call-done = f32[32,1024]{1,0:T(8,128)} async-done(((f32[1024,1024]{1,0:T(8,128)}), f32[32,1024]{1,0:T(8,128)}) %reduce-scatter.39.cloned.1.call-update) | async-done | bytes 131088 | tf_op jit(solution)/shard_map/reduce_scatter | solution.py:407
  2179.0 141.3 %reduce-scatter.37.cloned.1.call-done = f32[32,1024]{1,0:T(8,128)} async-done(((f32[1024,1024]{1,0:T(8,128)}), f32[32,1024]{1,0:T(8,128)}) %reduce-scatter.37.cloned.1.call-update) | async-done | bytes 131088 | tf_op jit(solution)/shard_map/reduce_scatter | solution.py:407
  2322.0 85.5 %reduce-scatter.43.cloned.1.call-done = bf16[1,128,5632]{2,1,0:T(8,128)(2,1)} async-done(((bf16[1,1024,5632]{2,1,0:T(8,128)(2,1)}), bf16[1,128,5632]{2,1,0:T(8,128)(2,1)}) %reduce-scatter.43.cloned.1.call-update) | async-done | bytes 1441808 | tf_op jit(solution)/shard_map/reduce_scatter | solution.py:421
  2407.5 90.3 %reduce-scatter.41.cloned.1.call-done = bf16[1,128,5632]{2,1,0:T(8,128)(2,1)} async-done(((bf16[1,1024,5632]{2,1,0:T(8,128)(2,1)}), bf16[1,128,5632]{2,1,0:T(8,128)(2,1)}) %reduce-scatter.41.cloned.1.call-update) | async-done | bytes 1441808 | tf_op jit(solution)/shard_map/reduce_scatter | solution.py:421
  2502.5 156.7 %reduce-scatter.35.cloned.1.call-done = f32[32,3072]{1,0:T(8,128)} async-done(((f32[1024,3072]{1,0:T(8,128)}), f32[32,3072]{1,0:T(8,128)}) %reduce-scatter.35.cloned.1.call-update) | async-done | bytes 393232 | tf_op jit(solution)/shard_map/reduce_scatter | solution.py:404
  2659.2 161.4 %reduce-scatter.33.cloned.1.call-done = f32[32,3072]{1,0:T(8,128)} async-done(((f32[1024,3072]{1,0:T(8,128)}), f32[32,3072]{1,0:T(8,128)}) %reduce-scatter.33.cloned.1.call-update) | async-done | bytes 393232 | tf_op jit(solution)/shard_map/reduce_scatter | solution.py:404
  (521 shorter events, 669.1 us)
Async XLA Ops:
  7.2 80.0 %all-gather.27.cloned.1.call-start = ((), (), s32[]{:S(2)}) async-start(), calls=%async_computation.40 | async-start | bytes 6488064 | tf_op jit(solution)/shard_map/all_gather | solution.py:347
  9.0 202.5 %all-gather.21.cloned.1.call-start = ((), (), s32[]{:S(2)}) async-start(), calls=%async_computation.25 | async-start | bytes 2621440 | tf_op jit(solution)/shard_map/all_gather | solution.py:119
  85.3 422.5 %copy-start.64 = (f32[1024]{0:T(1024)}, f32[1024]{0:T(1024)S(1)}, u32[]{:S(2)}) copy-start(f32[1024]{0:T(1024)S(1)} %get-tuple-element.21) | copy-start | bytes 12292
  93.3 121.3 %all-gather.19.cloned.1.call-start = ((), (), s32[]{:S(2)}) async-start(), calls=%async_computation.24 | async-start | bytes 2621440 | tf_op jit(solution)/shard_map/all_gather | solution.py:120
  94.0 156.5 %all-gather.29.cloned.1.call-start = ((), (), s32[]{:S(2)}) async-start(), calls=%async_computation.41 | async-start | bytes 2162688 | tf_op jit(solution)/shard_map/all_gather | solution.py:348
  94.8 428.6 %all-gather.31.cloned.1.call-start = ((), (), s32[]{:S(2)}) async-start(), calls=%async_computation.42 | async-start | bytes 6488064 | tf_op jit(solution)/shard_map/all_gather | solution.py:347
  351.0 159.0 %all-to-all-start.1 = ((bf16[4,160,1024]{2,1,0:T(8,128)(2,1)}), bf16[4,160,1024]{2,1,0:T(8,128)(2,1)S(1)}, u32[]{:S(2)}, u32[]{:S(2)}) async-start(bf16[4,160,1024]{2,1,0:T(8,128)(2,1)} %fusion.99), calls=%async_computation.1 | async-start | bytes 2621440 | tf_op jit(solution)/shard_map/all_to_all | solution.py:240
  354.5 251.6 %all-gather.25.cloned.1.call-start = ((), (), s32[]{:S(2)}) async-start(), calls=%async_computation.27 | async-start | bytes 2621440 | tf_op jit(solution)/shard_map/all_gather | solution.py:119
  529.2 79.9 %all-gather.23.cloned.1.call-start = ((), (), s32[]{:S(2)}) async-start(), calls=%async_computation.26 | async-start | bytes 2621440 | tf_op jit(solution)/shard_map/all_gather | solution.py:120
  529.9 115.1 %all-gather.33.cloned.1.call-start = ((), (), s32[]{:S(2)}) async-start(), calls=%async_computation.43 | async-start | bytes 2162688 | tf_op jit(solution)/shard_map/all_gather | solution.py:348
  647.6 404.3 %copy-start.85 = (f32[256]{0:T(256)}, f32[256]{0:T(256)S(1)}, u32[]{:S(2)}) copy-start(f32[256]{0:T(256)S(1)} %get-tuple-element.71) | copy-start | bytes 3076
  726.9 173.4 %all-to-all-start.2 = ((bf16[4,160,1024]{2,1,0:T(8,128)(2,1)}), bf16[4,160,1024]{2,1,0:T(8,128)(2,1)}, u32[]{:S(2)}, u32[]{:S(2)}) async-start(bf16[4,160,1024]{2,1,0:T(8,128)(2,1)} %scatter_fusion.1), calls=%async_computation.2 | async-start | bytes 2621440 | tf_op jit(solution)/shard_map/all_to_all | solution.py:225
  900.4 32.3 %all-to-all-start.4 = ((bf16[4,160,1024]{2,1,0:T(8,128)(2,1)}), bf16[4,160,1024]{2,1,0:T(8,128)(2,1)S(1)}, u32[]{:S(2)}, u32[]{:S(2)}) async-start(bf16[4,160,1024]{2,1,0:T(8,128)(2,1)} %scatter_fusion.2), calls=%async_computation.4 | async-start | bytes 2621440 | tf_op jit(solution)/shard_map/all_to_all | solution.py:282
  962.4 34.4 %all-to-all-start.5 = ((bf16[4,160,1024]{2,1,0:T(8,128)(2,1)}), bf16[4,160,1024]{2,1,0:T(8,128)(2,1)S(1)}, u32[]{:S(2)}, u32[]{:S(2)}) async-start(bf16[4,160,1024]{2,1,0:T(8,128)(2,1)} %fusion.102), calls=%async_computation.5 | async-start | bytes 2621440 | tf_op jit(solution)/shard_map/all_to_all | solution.py:307
  996.8 34.3 %all-to-all-start.3 = ((bf16[4,160,1024]{2,1,0:T(8,128)(2,1)}), bf16[4,160,1024]{2,1,0:T(8,128)(2,1)S(1)}, u32[]{:S(2)}, u32[]{:S(2)}) async-start(bf16[4,160,1024]{2,1,0:T(8,128)(2,1)} %fusion.96), calls=%async_computation.3 | async-start | bytes 2621440 | tf_op jit(solution)/shard_map/all_to_all | solution.py:240
  1000.3 101.3 %reduce-scatter.27.cloned.1.call-start = ((), (), s32[]{:S(2)}) async-start(), calls=%async_computation.29 | async-start | bytes 2621440 | tf_op jit(solution)/shard_map/reduce_scatter | solution.py:182
  1065.7 62.8 %reduce-scatter.25.cloned.1.call-start = ((), (), s32[]{:S(2)}) async-start(), calls=%async_computation.28 | async-start | bytes 2621440 | tf_op jit(solution)/shard_map/reduce_scatter | solution.py:176
  1256.8 34.0 %all-to-all-start.7 = ((bf16[4,160,1024]{2,1,0:T(8,128)(2,1)}), bf16[4,160,1024]{2,1,0:T(8,128)(2,1)S(1)}, u32[]{:S(2)}, u32[]{:S(2)}) async-start(bf16[4,160,1024]{2,1,0:T(8,128)(2,1)} %fusion.105), calls=%async_computation.9 | async-start | bytes 2621440 | tf_op jit(solution)/shard_map/all_to_all | solution.py:307
  1260.4 91.4 %reduce-scatter.31.cloned.1.call-start = ((), (), s32[]{:S(2)}) async-start(), calls=%async_computation.31 | async-start | bytes 2621440 | tf_op jit(solution)/shard_map/reduce_scatter | solution.py:182
  1314.9 64.3 %reduce-scatter.29.cloned.1.call-start = ((), (), s32[]{:S(2)}) async-start(), calls=%async_computation.30 | async-start | bytes 2621440 | tf_op jit(solution)/shard_map/reduce_scatter | solution.py:176
  1337.8 320.5 %reduce-scatter.51.cloned.1.call-start = ((), (), s32[]{:S(2)}) async-start(), calls=%async_computation.45 | async-start | bytes 540672
  1340.6 318.5 %reduce-scatter.55.cloned.1.call-start = ((), (), s32[]{:S(2)}) async-start(), calls=%async_computation.47 | async-start | bytes 540672
  1341.8 437.5 %reduce-scatter.49.cloned.1.call-start = ((), (), s32[]{:S(2)}) async-start(), calls=%async_computation.44 | async-start | bytes 540672
  1344.6 691.9 %reduce-scatter.53.cloned.1.call-start = ((), (), s32[]{:S(2)}) async-start(), calls=%async_computation.46 | async-start | bytes 540672
  1386.9 650.9 %reduce-scatter.47.cloned.1.call-start = ((), (), s32[]{:S(2)}) async-start(), calls=%async_computation.39 | async-start | bytes 6488064 | tf_op jit(solution)/shard_map/reduce_scatter | solution.py:424
  1395.6 642.3 %reduce-scatter.45.cloned.1.call-start = ((), (), s32[]{:S(2)}) async-start(), calls=%async_computation.38 | async-start | bytes 6488064 | tf_op jit(solution)/shard_map/reduce_scatter | solution.py:424
  1405.3 773.7 %reduce-scatter.39.cloned.1.call-start = ((), (), s32[]{:S(2)}) async-start(), calls=%async_computation.35 | async-start | bytes 4325376 | tf_op jit(solution)/shard_map/reduce_scatter | solution.py:407
  1409.3 911.0 %reduce-scatter.37.cloned.1.call-start = ((), (), s32[]{:S(2)}) async-start(), calls=%async_computation.34 | async-start | bytes 4325376 | tf_op jit(solution)/shard_map/reduce_scatter | solution.py:407
  1412.2 995.3 %reduce-scatter.43.cloned.1.call-start = ((), (), s32[]{:S(2)}) async-start(), calls=%async_computation.37 | async-start | bytes 12976128 | tf_op jit(solution)/shard_map/reduce_scatter | solution.py:421
  1427.4 1070.4 %reduce-scatter.41.cloned.1.call-start = ((), (), s32[]{:S(2)}) async-start(), calls=%async_computation.36 | async-start | bytes 12976128 | tf_op jit(solution)/shard_map/reduce_scatter | solution.py:421
  1443.8 1215.4 %reduce-scatter.35.cloned.1.call-start = ((), (), s32[]{:S(2)}) async-start(), calls=%async_computation.33 | async-start | bytes 12976128 | tf_op jit(solution)/shard_map/reduce_scatter | solution.py:404
  1599.3 1221.4 %reduce-scatter.33.cloned.1.call-start = ((), (), s32[]{:S(2)}) async-start(), calls=%async_computation.32 | async-start | bytes 12976128 | tf_op jit(solution)/shard_map/reduce_scatter | solution.py:404
  (118 other events, 2950.1 us)
Sparse Core Ops, SparseCore 0:
  11.5 73.0 all-gather.26
  93.4 20.6 all-gather.20
  116.2 23.0 all-gather.18
  142.8 56.4 all-gather.28
  202.1 68.3 all-gather.30
  529.3 20.5 all-gather.24
  552.0 22.5 all-gather.22
  577.7 56.5 all-gather.32
  1065.9 28.6 reduce-scatter.26
  1097.1 31.4 reduce-scatter.24
  1315.0 29.5 reduce-scatter.30
  1347.7 31.4 reduce-scatter.28
  1381.4 133.9 reduce-scatter.50
  1517.6 129.9 reduce-scatter.54
  1649.7 129.6 reduce-scatter.48
  1782.1 130.0 reduce-scatter.52
  1916.1 55.1 reduce-scatter.46
  1975.0 59.8 reduce-scatter.44
  2037.1 141.8 reduce-scatter.38
  2181.2 139.1 reduce-scatter.36
  2323.8 83.6 reduce-scatter.42
  2411.0 86.7 reduce-scatter.40
  2503.8 155.3 reduce-scatter.34
  2666.1 154.4 reduce-scatter.32
where the time goes:
time: 2880 us; the launch traced here: 2830 us
  waiting for transfers between devices  1030 us (36%)
  local copies, waits for them, and re-layouts  858 us (30%)
  blocking collectives  457 us (16%)
  matrix products  317 us (11%)
  other arithmetic  128 us (4%)
    reduce_scatter x2, waiting for transfers between devices, on_device(): lax.psum_scatter(grad_attn_in, ('experts', 'context', 'dp'), scatter_dime...  318 us
    reduce_scatter x2, waiting for transfers between devices, on_device(): lax.psum_scatter(grad_attn_out, ('experts', 'context', 'dp'), scatter_dim...  279 us
    rev x2, local copies, waits for them, and re-layouts, table_grad(): padded = jnp.pad(grad_scores[:, :, ::-1], ((0, 0), (0, 0), (0, query_rows)))  250 us
    reduce_scatter x2, waiting for transfers between devices, on_device(): lax.psum_scatter(grad_w_in.astype(jnp.bfloat16), ('context', 'dp'), scatt...  176 us
    all_gather x2, blocking collectives, on_device(): lax.all_gather(router[layer_index], ('experts', 'context', 'dp'), axis=0,...  170 us
    all_gather x2, blocking collectives, on_device(): lax.all_gather(gains[layer_index], ('experts', 'context', 'dp'), axis=0,...  141 us
    scatter x2, local copies, waits for them, and re-layouts, experts_backward(): jnp.zeros(arrived.shape, jnp.bfloat16).at[expert_index, slot_index]  126 us
    unnamed x28, waiting for transfers between devices  122 us
  transfers between devices with their start and end apart: 30, of which 13 were waited for; matrix products, arithmetic and copies ran while one was open for 36% of the time, Pallas kernels for 0%

commit v1 on v0

v1 whole, which is shorter than its diff:
```python
import math

import jax
import jax.numpy as jnp
import numpy as np
from jax import lax
from jax.experimental import pallas as pl
from jax.experimental.pallas import tpu as pltpu
from jax.sharding import PartitionSpec as P

D = 1024
HEADS = 16
HEAD_DIM = 64
FF = 2816
BUCKETS = 32
MAX_DISTANCE = 128
LAYERS = 2
EPSILON = 1e-06
NEGATIVE = -1e30
SCORE_SCALE = 0.125
ALL = ("experts", "context", "dp")
GROUP = 4
OWN = HEADS // GROUP
OWN_COLS = OWN * HEAD_DIM
PACKED = 3 * OWN_COLS
LANES = 128
REACH = 512
FF_TILE = 256
FF_STEPS = FF // FF_TILE
MIB = 1 << 20

bf16 = jnp.bfloat16
f32 = jnp.float32


def bucket_bounds(bucket_count, far_reach):
    half_count = bucket_count // 2
    bounds = list(range(1, half_count + 1))
    for section_index in range(1, half_count):
        bounds.append(
            int(math.ceil(half_count * (far_reach / half_count) ** (section_index / half_count)))
        )
    return np.array(bounds, np.int32)


def bucket_hits():
    distance = np.arange(REACH)
    bucket = (distance[:, None] >= bucket_bounds(BUCKETS, MAX_DISTANCE)).sum(-1)
    return (np.arange(BUCKETS)[:, None] == bucket[None, :]).astype(np.float32)


def dot(a, b, ca, cb, precision=None):
    return lax.dot_general(
        a, b, (((ca,), (cb,)), ((), ())), precision=precision, preferred_element_type=f32
    )


def whole_call(body, out_shape, args, *, flops=0, limit=48, scratch=(), smem=0, name=None):
    specs = [pl.BlockSpec(memory_space=pltpu.SMEM)] * smem + [
        pl.BlockSpec(memory_space=pltpu.VMEM)
    ] * (len(args) - smem)
    outs = tuple(out_shape)
    moved = sum(a.size * a.dtype.itemsize for a in list(args) + list(outs))
    return pl.pallas_call(
        body,
        out_shape=outs,
        in_specs=specs,
        out_specs=tuple(pl.BlockSpec(memory_space=pltpu.VMEM) for _ in outs),
        scratch_shapes=list(scratch),
        compiler_params=pltpu.CompilerParams(vmem_limit_bytes=limit * MIB),
        cost_estimate=pl.CostEstimate(
            flops=int(flops), bytes_accessed=int(moved), transcendentals=0
        ),
        name=name,
    )(*args)


def shape(dims, dtype):
    return jax.ShapeDtypeStruct(dims, dtype)


def rms_scale(inputs):
    return lax.rsqrt(jnp.mean(inputs * inputs, -1, keepdims=True) + EPSILON)


def norm_back(inputs, gain_row, upstream):
    inverse = rms_scale(inputs)
    scaled = upstream * gain_row
    inner_mean = jnp.mean(inputs * scaled, -1, keepdims=True)
    grad_inputs = inverse * scaled - inputs * (inverse * inverse * inverse) * inner_mean
    grad_gain = jnp.sum(upstream * inputs * inverse, 0, keepdims=True)
    return grad_inputs, grad_gain


def near_bias(bias_ref, head, rows):
    row = bias_ref[head : head + 1, :]
    return pltpu.roll(jnp.broadcast_to(row, (rows, REACH)), 0, 1, stride=1, stride_axis=0)


def masked_scores(keys, queries, near, low, key_block, query_block, rows):
    scores = dot(keys, queries, 1, 1)
    key_place = lax.broadcasted_iota(jnp.int32, (rows, rows), 0)
    seen = key_place >= low - key_block * rows
    if key_block == query_block:
        scores = scores + near[:, :rows]
        seen = seen & (key_place <= lax.broadcasted_iota(jnp.int32, (rows, rows), 1))
    elif key_block == query_block - 1:
        scores = scores + near[:, rows:]
    return jnp.where(seen, scores, NEGATIVE)


def attention_forward_body(
    place_ref, n0, n1, n2, n3, w_ref, bias_ref, low_ref, wo_ref,
    packed_ref, log_ref, mixed_ref, keep_ref, send_ref,
):
    me = place_ref[0]
    rows = n0.shape[0]
    for r, piece in enumerate((n0, n1, n2, n3)):
        packed_ref[r * rows : (r + 1) * rows, :] = dot(piece[...], w_ref[...], 1, 0).astype(bf16)
    lane = lax.broadcasted_iota(jnp.int32, (rows, LANES), 1)
    starts = [pl.multiple_of((b ^ me) * rows, rows) for b in range(GROUP)]
    for pair in range(OWN // 2):
        at = pair * LANES

        def part(b, which):
            column = which * OWN_COLS + at
            return packed_ref[pl.ds(starts[b], rows), column : column + LANES]

        sides = [(lane // HEAD_DIM) == side for side in range(2)]
        nears = [near_bias(bias_ref, pair * 2 + side, rows) for side in range(2)]
        for qb in range(GROUP):
            low = low_ref[:, qb * rows : (qb + 1) * rows]
            queries = part(qb, 0) * SCORE_SCALE
            total = None
            for side in range(2):
                mine = jnp.where(sides[side], queries, 0).astype(bf16)
                tiles = [
                    masked_scores(part(kb, 1), mine, nears[side], low, kb, qb, rows)
                    for kb in range(qb + 1)
                ]
                peak = jnp.max(tiles[0], 0, keepdims=True)
                for tile in tiles[1:]:
                    peak = jnp.maximum(peak, jnp.max(tile, 0, keepdims=True))
                weight_sum = jnp.zeros((1, rows), f32)
                out = jnp.zeros((LANES, rows), f32)
                for kb, tile in enumerate(tiles):
                    power = jnp.exp(tile - peak)
                    weight_sum = weight_sum + jnp.sum(power, 0, keepdims=True)
                    values = jnp.where(sides[side], part(kb, 2), 0).astype(bf16)
                    out = out + dot(values, power.astype(bf16), 0, 0)
                out = out / weight_sum
                total = out if total is None else total + out
                head = pair * 2 + side
                log_ref[head : head + 1, qb * rows : (qb + 1) * rows] = peak + jnp.log(weight_sum)
            mixed_ref[pl.ds(starts[qb], rows), at : at + LANES] = total.T.astype(bf16)
    width = wo_ref.shape[2]
    for r, (target, offset) in enumerate(
        ((keep_ref, 0), (send_ref, 0), (keep_ref, rows), (send_ref, rows))
    ):
        mixed = mixed_ref[r * rows : (r + 1) * rows, :]
        for q in range(wo_ref.shape[0]):
            target[offset : offset + rows, q * width : (q + 1) * width] = dot(
                mixed, wo_ref[q], 1, 0
            ).astype(target.dtype)


def attention_forward(place, pieces, w_in, bias_rows, low, w_out):
    rows = pieces[0].shape[0]
    total = GROUP * rows
    return whole_call(
        attention_forward_body,
        (
            shape((total, PACKED), bf16),
            shape((8, total), f32),
            shape((total, OWN_COLS), bf16),
            shape((2 * rows, D), f32),
            shape((2 * rows, D), bf16),
        ),
        [place, *pieces, w_in, bias_rows, low, w_out],
        smem=1,
        flops=2 * total * D * (PACKED + OWN_COLS) + 2 * total * total * OWN_COLS * 2,
        name="attention_forward",
    )


def attention_backward_body(
    place_ref, d0, d1, d2, d3, w_ref, bias_ref, low_ref, wo_ref, packed_ref, log_ref,
    grad_packed_ref, keep_ref, send_ref, table_ref, grad_mixed_ref, dk_ref, dv_ref,
):
    me = place_ref[0]
    rows = d0.shape[0]
    width = wo_ref.shape[2]
    for r, piece in enumerate((d0, d1, d2, d3)):
        got = jnp.zeros((rows, OWN_COLS), f32)
        for q in range(wo_ref.shape[0]):
            got = got + dot(piece[:, q * width : (q + 1) * width], wo_ref[q], 1, 1)
        grad_mixed_ref[r * rows : (r + 1) * rows, :] = got.astype(bf16)
    lane = lax.broadcasted_iota(jnp.int32, (rows, LANES), 1)
    starts = [pl.multiple_of((b ^ me) * rows, rows) for b in range(GROUP)]
    table_ref[...] = jnp.zeros(table_ref.shape, f32)
    for pair in range(OWN // 2):
        at = pair * LANES

        def part(b, which):
            column = which * OWN_COLS + at
            return packed_ref[pl.ds(starts[b], rows), column : column + LANES]

        sides = [(lane // HEAD_DIM) == side for side in range(2)]
        nears = [near_bias(bias_ref, pair * 2 + side, rows) for side in range(2)]
        diag = [jnp.zeros((rows, rows), f32) for _ in range(2)]
        before = [jnp.zeros((rows, rows), f32) for _ in range(2)]
        far = [jnp.zeros((1, rows), f32) for _ in range(2)]
        dk_ref[...] = jnp.zeros(dk_ref.shape, f32)
        dv_ref[...] = jnp.zeros(dv_ref.shape, f32)
        for qb in range(GROUP):
            low = low_ref[:, qb * rows : (qb + 1) * rows]
            queries = part(qb, 0) * SCORE_SCALE
            upstream = grad_mixed_ref[pl.ds(starts[qb], rows), at : at + LANES]
            grad_queries = jnp.zeros((LANES, rows), f32)
            for side in range(2):
                head = pair * 2 + side
                mine = jnp.where(sides[side], queries, 0).astype(bf16)
                above = jnp.where(sides[side], upstream, 0).astype(bf16)
                log_total = log_ref[head : head + 1, qb * rows : (qb + 1) * rows]
                probs, grads = [], []
                row_dot = jnp.zeros((1, rows), f32)
                for kb in range(qb + 1):
                    scores = masked_scores(part(kb, 1), mine, nears[side], low, kb, qb, rows)
                    prob = jnp.exp(scores - log_total)
                    grad = dot(part(kb, 2), above, 1, 1)
                    row_dot = row_dot + jnp.sum(prob * grad, 0, keepdims=True)
                    probs.append(prob)
                    grads.append(grad)
                for kb in range(qb + 1):
                    grad_score = probs[kb] * (grads[kb] - row_dot)
                    if kb == qb:
                        diag[side] = diag[side] + grad_score
                    elif kb == qb - 1:
                        before[side] = before[side] + grad_score
                    else:
                        far[side] = far[side] + jnp.sum(grad_score, 0, keepdims=True)
                    grad_low = grad_score.astype(bf16)
                    keys = jnp.where(sides[side], part(kb, 1), 0).astype(bf16)
                    grad_queries = grad_queries + dot(keys, grad_low, 0, 0)
                    span = slice(kb * rows, (kb + 1) * rows)
                    dk_ref[span, :] += dot(grad_low, mine, 1, 0)
                    dv_ref[span, :] += dot(probs[kb].astype(bf16), above, 1, 0)
            grad_packed_ref[pl.ds(starts[qb], rows), at : at + LANES] = (
                grad_queries.T * SCORE_SCALE
            ).astype(bf16)
        for kb in range(GROUP):
            span = slice(kb * rows, (kb + 1) * rows)
            for which, source in ((1, dk_ref), (2, dv_ref)):
                column = which * OWN_COLS + at
                grad_packed_ref[pl.ds(starts[kb], rows), column : column + LANES] = source[
                    span, :
                ].astype(bf16)
        distance = lax.broadcasted_iota(jnp.int32, (1, REACH), 1)
        for side in range(2):
            head = pair * 2 + side
            skewed = jnp.concatenate([diag[side], before[side]], 1)
            row_index = lax.broadcasted_iota(jnp.int32, (rows, REACH), 0)
            step = 1
            while step < rows:
                skewed = jnp.where(
                    (row_index & step) != 0, pltpu.roll(skewed, REACH - step, 1), skewed
                )
                step *= 2
            by_distance = jnp.sum(skewed, 0, keepdims=True)
            far_sum = jnp.sum(far[side], 1, keepdims=True)
            table_ref[head : head + 1, :] = by_distance + jnp.where(
                distance == REACH - 1, far_sum, 0.0
            )
    for r, (target, offset) in enumerate(
        ((keep_ref, 0), (send_ref, 0), (keep_ref, rows), (send_ref, rows))
    ):
        target[offset : offset + rows, :] = dot(
            grad_packed_ref[r * rows : (r + 1) * rows, :], w_ref[...], 1, 1
        ).astype(target.dtype)


def attention_backward(place, pieces, w_in, bias_rows, low, w_out, packed, log_total):
    rows = pieces[0].shape[0]
    total = GROUP * rows
    return whole_call(
        attention_backward_body,
        (
            shape((total, PACKED), bf16),
            shape((2 * rows, D), f32),
            shape((2 * rows, D), bf16),
            shape((8, REACH), f32),
        ),
        [place, *pieces, w_in, bias_rows, low, w_out, packed, log_total],
        smem=1,
        scratch=[
            pltpu.VMEM((total, OWN_COLS), bf16),
            pltpu.VMEM((total, LANES), f32),
            pltpu.VMEM((total, LANES), f32),
        ],
        flops=2 * total * D * (PACKED + OWN_COLS) + 2 * total * total * OWN_COLS * 5,
        name="attention_backward",
    )


def dense_grad_body(n0, n1, n2, n3, d0, d1, d2, d3, grad_packed_ref, mixed_ref, out_in, out_out):
    rows = n0.shape[0]
    total_in = None
    total_out = None
    for r, (normed, upstream) in enumerate(zip((n0, n1, n2, n3), (d0, d1, d2, d3))):
        span = slice(r * rows, (r + 1) * rows)
        one = dot(normed[...], grad_packed_ref[span, :], 0, 0)
        two = dot(mixed_ref[span, :], upstream[...], 0, 0)
        total_in = one if total_in is None else total_in + one
        total_out = two if total_out is None else total_out + two
    out_in[...] = total_in.astype(out_in.dtype)
    out_out[...] = total_out.astype(out_out.dtype)


def dense_grads(normed, upstream, grad_packed, mixed):
    rows = normed[0].shape[0]
    return whole_call(
        dense_grad_body,
        (shape((D, PACKED), bf16), shape((OWN_COLS, D), bf16)),
        [*normed, *upstream, grad_packed, mixed],
        flops=2 * GROUP * rows * D * (PACKED + OWN_COLS),
        name="dense_grads",
    )


def dispatch_grid(dest_rows, slots, tokens):
    place = lax.broadcasted_iota(jnp.int32, (slots, tokens), 0)
    first = place == dest_rows[0:1, :]
    second = place == dest_rows[1:2, :]
    return first, second


def one_hot(flags):
    return jnp.where(flags, 1.0, 0.0).astype(bf16)


def collect_grid(meta, slots):
    tokens = meta.shape[0]
    place = lax.broadcasted_iota(jnp.int32, (tokens, slots), 1)
    first = place == meta[:, 0:1].astype(jnp.int32)
    second = place == meta[:, 1:2].astype(jnp.int32)
    return first, second


def scatter_grads(upstream, meta, dest_rows, slots):
    tokens = upstream.shape[0]
    first, second = dispatch_grid(dest_rows, slots, tokens)
    return (
        dot(one_hot(first), (meta[:, 2:3] * upstream).astype(bf16), 1, 0)
        + dot(one_hot(second), (meta[:, 3:4] * upstream).astype(bf16), 1, 0)
    ).astype(bf16)


def route_body(experts, capacity, last, *refs):
    if last:
        (x_ref, keep_ref, recv_ref, far_ref, gain_ref, router_ref, ids_ref, idst_ref, grad_ref,
         middle_ref, rows_ref, soft_ref, meta_ref, dest_ref, sent_ref) = refs
    else:
        (x_ref, keep_ref, recv_ref, far_ref, gain_ref, router_ref, ids_ref, idst_ref,
         middle_ref, rows_ref, soft_ref, meta_ref, dest_ref) = refs
    tokens = x_ref.shape[0]
    slots = experts * capacity
    middle = (
        x_ref[...].astype(f32)
        + keep_ref[:tokens, :]
        + recv_ref[:tokens, :].astype(f32)
        + far_ref[...].astype(f32)
    )
    middle_ref[...] = middle
    normed = middle * rms_scale(middle) * gain_ref[...]
    lane = lax.broadcasted_iota(jnp.int32, (tokens, LANES), 1)
    logits = dot(normed, router_ref[...], 1, 1, lax.Precision.HIGHEST)
    logits = jnp.where(lane < experts, logits, NEGATIVE)
    power = jnp.exp(logits - jnp.max(logits, -1, keepdims=True))
    soft = power / jnp.sum(power, -1, keepdims=True)
    soft_ref[...] = soft
    ids = ids_ref[...]
    hit0 = lane == ids[:, 0:1]
    hit1 = lane == ids[:, 1:2]
    picked0 = jnp.sum(jnp.where(hit0, soft, 0.0), -1, keepdims=True)
    picked1 = jnp.sum(jnp.where(hit1, soft, 0.0), -1, keepdims=True)
    pick_total = picked0 + picked1
    down = lax.broadcasted_iota(jnp.int32, (tokens, tokens), 0)
    across = lax.broadcasted_iota(jnp.int32, (tokens, tokens), 1)
    counts = dot(one_hot(across < down), one_hot(hit0 | hit1), 1, 0)
    dest0 = ids[:, 0:1].astype(f32) * capacity + jnp.sum(
        jnp.where(hit0, counts, 0.0), -1, keepdims=True
    )
    dest1 = ids[:, 1:2].astype(f32) * capacity + jnp.sum(
        jnp.where(hit1, counts, 0.0), -1, keepdims=True
    )
    fields = (dest0, dest1, picked0 / pick_total, picked1 / pick_total, pick_total)
    meta = jnp.zeros((tokens, LANES), f32)
    for index, field in enumerate(fields):
        meta = jnp.where(lane == index, field, meta)
    meta_ref[...] = meta
    idst = idst_ref[...]
    sub = lax.broadcasted_iota(jnp.int32, (16, tokens), 0)
    row0 = sub == idst[0:1, :]
    row1 = sub == idst[1:2, :]
    row_counts = dot(one_hot(row0 | row1), one_hot(down < across), 1, 0)
    destr0 = idst[0:1, :] * capacity + jnp.sum(
        jnp.where(row0, row_counts, 0.0), 0, keepdims=True
    ).astype(jnp.int32)
    destr1 = idst[1:2, :] * capacity + jnp.sum(
        jnp.where(row1, row_counts, 0.0), 0, keepdims=True
    ).astype(jnp.int32)
    dest_rows = jnp.where(
        lax.broadcasted_iota(jnp.int32, (8, tokens), 0) == 0, destr0, destr1
    )
    dest_ref[...] = dest_rows
    first, second = dispatch_grid(dest_rows, slots, tokens)
    rows_ref[...] = dot(one_hot(first | second), normed.astype(bf16), 1, 0).astype(bf16)
    if last:
        sent_ref[...] = scatter_grads(grad_ref[...].astype(f32), meta, dest_rows, slots)


def route(experts, capacity, x, keep, recv, far, gain, router, ids, idst, grad=None):
    tokens = x.shape[0]
    slots = experts * capacity
    outs = [
        shape((tokens, D), f32),
        shape((slots, D), bf16),
        shape((tokens, LANES), f32),
        shape((tokens, LANES), f32),
        shape((8, tokens), jnp.int32),
    ]
    args = [x, keep, recv, far, gain, router, ids, idst]
    if grad is not None:
        outs.append(shape((slots, D), bf16))
        args.append(grad)

    def body(*refs):
        route_body(experts, capacity, grad is not None, *refs)

    return whole_call(body, outs, args, flops=2 * slots * tokens * D, name="route")


def combine_body(last, *refs):
    if last:
        middle_ref, back_ref, meta_ref, out_ref = refs
    else:
        middle_ref, back_ref, meta_ref, gain_ref, out_ref, normed_ref = refs
    meta = meta_ref[...]
    first, second = collect_grid(meta, back_ref.shape[0])
    x = (
        middle_ref[...]
        + meta[:, 2:3] * dot(one_hot(first), back_ref[...], 1, 0)
        + meta[:, 3:4] * dot(one_hot(second), back_ref[...], 1, 0)
    )
    out_ref[...] = x.astype(out_ref.dtype)
    if not last:
        normed_ref[...] = (x * rms_scale(x) * gain_ref[...]).astype(bf16)


def combine(middle, back, meta, gain=None):
    tokens = middle.shape[0]
    args = [middle, back, meta]
    outs = [shape((tokens, D), bf16 if gain is None else f32)]
    if gain is not None:
        args.append(gain)
        outs.append(shape((tokens, D), bf16))

    def body(*refs):
        combine_body(gain is None, *refs)

    return whole_call(
        body, outs, args, flops=4 * tokens * D * back.shape[0], name="combine"
    )


def expert_token_back_body(
    experts, back_ref, came_ref, g_ref, middle_ref, soft_ref, meta_ref, ids_ref, gain_ref,
    router_ref, dmiddle_ref, dattn_ref, small_ref,
):
    meta = meta_ref[...]
    g = g_ref[...].astype(f32)
    slots = back_ref.shape[0]
    first, second = collect_grid(meta, slots)
    grad_gate0 = jnp.sum(g * dot(one_hot(first), back_ref[...], 1, 0), -1, keepdims=True)
    grad_gate1 = jnp.sum(g * dot(one_hot(second), back_ref[...], 1, 0), -1, keepdims=True)
    grad_normed = dot(one_hot(first | second), came_ref[...], 1, 0)
    gap = (grad_gate0 - grad_gate1) / meta[:, 4:5]
    ids = ids_ref[...]
    lane = lax.broadcasted_iota(jnp.int32, meta.shape, 1)
    grad_soft = jnp.where(lane == ids[:, 0:1], meta[:, 3:4] * gap, 0.0) + jnp.where(
        lane == ids[:, 1:2], -meta[:, 2:3] * gap, 0.0
    )
    soft = soft_ref[...]
    grad_logits = soft * (grad_soft - jnp.sum(soft * grad_soft, -1, keepdims=True))
    middle = middle_ref[...]
    normed = middle * rms_scale(middle) * gain_ref[...]
    grad_router = dot(grad_logits.T, normed, 1, 0, lax.Precision.HIGHEST)
    grad_normed = grad_normed + dot(
        grad_logits, router_ref[...], 1, 0, lax.Precision.HIGHEST
    )
    grad_branch, grad_gain = norm_back(middle, gain_ref[...], grad_normed)
    dmiddle = g + grad_branch
    dmiddle_ref[...] = dmiddle
    dattn_ref[...] = dmiddle.astype(bf16)
    small_ref[:16, :] = grad_router[:16, :]
    small_ref[16:24, :] = jnp.broadcast_to(grad_gain, (8, D))


def expert_token_back(experts, back, came, g, middle, soft, meta, ids, gain, router):
    tokens = middle.shape[0]

    def body(*refs):
        expert_token_back_body(experts, *refs)

    return whole_call(
        body,
        (shape((tokens, D), f32), shape((tokens, D), bf16), shape((24, D), f32)),
        [back, came, g, middle, soft, meta, ids, gain, router],
        flops=6 * tokens * D * back.shape[0],
        name="expert_token_back",
    )


def attention_token_back_body(first_layer, *refs):
    if first_layer:
        x_ref, dmiddle_ref, keep_ref, recv_ref, far_ref, gain_ref, out_ref, small_ref = refs
    else:
        (x_ref, dmiddle_ref, keep_ref, recv_ref, far_ref, gain_ref, meta_ref, dest_ref,
         out_ref, small_ref, sent_ref) = refs
    tokens = x_ref.shape[0]
    grad_normed = (
        keep_ref[:tokens, :] + recv_ref[:tokens, :].astype(f32) + far_ref[...].astype(f32)
    )
    grad_branch, grad_gain = norm_back(x_ref[...].astype(f32), gain_ref[...], grad_normed)
    g = dmiddle_ref[...] + grad_branch
    out_ref[...] = g
    small_ref[...] = jnp.broadcast_to(grad_gain, (8, D))
    if not first_layer:
        sent_ref[...] = scatter_grads(g, meta_ref[...], dest_ref[...], sent_ref.shape[0])


def attention_token_back(x, dmiddle, keep, recv, far, gain, meta=None, dest=None, slots=0):
    tokens = x.shape[0]
    outs = [shape((tokens, D), f32), shape((8, D), f32)]
    args = [x, dmiddle, keep, recv, far, gain]
    if meta is not None:
        outs.append(shape((slots, D), bf16))
        args += [meta, dest]

    def body(*refs):
        attention_token_back_body(meta is None, *refs)

    return whole_call(
        body, outs, args, flops=4 * tokens * D * slots, name="attention_token_back"
    )


def gelu_parts(gate):
    inner = math.sqrt(2.0 / math.pi) * (gate + 0.044715 * gate * gate * gate)
    return jnp.tanh(inner)


def expert_forward_body(rows_ref, wg_ref, wu_ref, wo_ref, produced_ref, acts_ref, total_ref):
    step = pl.program_id(0)
    rows = rows_ref[...]
    gate = dot(rows, wg_ref[0, 0], 1, 0)
    up = dot(rows, wu_ref[0, 0], 1, 0)
    acts_ref[0] = gate.astype(bf16)
    acts_ref[1] = up.astype(bf16)
    hidden = (0.5 * gate * (1.0 + gelu_parts(gate)) * up).astype(bf16)
    out = dot(hidden, wo_ref[0, 0], 1, 1)

    @pl.when(step == 0)
    def _():
        total_ref[...] = out

    @pl.when(step > 0)
    def _():
        total_ref[...] += out

    @pl.when(step == FF_STEPS - 1)
    def _():
        produced_ref[...] = total_ref[...].astype(bf16)


def weight_specs(layer):
    return [
        pl.BlockSpec((1, 1, D, FF_TILE), lambda s: (layer, 0, 0, s)),
        pl.BlockSpec((1, 1, D, FF_TILE), lambda s: (layer, 0, 0, FF_STEPS + s)),
        pl.BlockSpec((1, 1, D, FF_TILE), lambda s: (layer, 0, 0, s)),
    ]


def expert_forward(layer, rows, w_in, w_out):
    count = rows.shape[0]
    return pl.pallas_call(
        expert_forward_body,
        grid=(FF_STEPS,),
        out_shape=(shape((count, D), bf16), shape((2, count, FF), bf16)),
        in_specs=[pl.BlockSpec((count, D), lambda s: (0, 0))] + weight_specs(layer),
        out_specs=(
            pl.BlockSpec((count, D), lambda s: (0, 0)),
            pl.BlockSpec((2, count, FF_TILE), lambda s: (0, 0, s)),
        ),
        scratch_shapes=[pltpu.VMEM((count, D), f32)],
        compiler_params=pltpu.CompilerParams(vmem_limit_bytes=40 * MIB),
        cost_estimate=pl.CostEstimate(
            flops=6 * count * D * FF, bytes_accessed=6 * D * FF, transcendentals=count * FF
        ),
        name="expert_forward",
    )(rows, w_in, w_in, w_out)


def expert_backward_body(
    grad_ref, acts_ref, wg_ref, wu_ref, wo_ref, drows_ref, grads_ref, total_ref
):
    step = pl.program_id(0)
    grad_hidden = dot(grad_ref[...], wo_ref[0, 0], 1, 0)
    gate = acts_ref[0].astype(f32)
    up = acts_ref[1].astype(f32)
    curve = gelu_parts(gate)
    value = 0.5 * gate * (1.0 + curve)
    slope = 0.5 * (1.0 + curve) + 0.5 * gate * (1.0 - curve * curve) * math.sqrt(
        2.0 / math.pi
    ) * (1.0 + 3.0 * 0.044715 * gate * gate)
    grad_gate = (grad_hidden * up * slope).astype(bf16)
    grad_up = (grad_hidden * value).astype(bf16)
    grads_ref[0] = grad_gate
    grads_ref[1] = grad_up
    grads_ref[2] = (value * up).astype(bf16)
    out = dot(grad_gate, wg_ref[0, 0], 1, 1) + dot(grad_up, wu_ref[0, 0], 1, 1)

    @pl.when(step == 0)
    def _():
        total_ref[...] = out

    @pl.when(step > 0)
    def _():
        total_ref[...] += out

    @pl.when(step == FF_STEPS - 1)
    def _():
        drows_ref[...] = total_ref[...].astype(bf16)


def expert_backward(layer, grad, acts, w_in, w_out):
    count = grad.shape[0]
    return pl.pallas_call(
        expert_backward_body,
        grid=(FF_STEPS,),
        out_shape=(shape((count, D), bf16), shape((3, count, FF), bf16)),
        in_specs=[
            pl.BlockSpec((count, D), lambda s: (0, 0)),
            pl.BlockSpec((2, count, FF_TILE), lambda s: (0, 0, s)),
        ]
        + weight_specs(layer),
        out_specs=(
            pl.BlockSpec((count, D), lambda s: (0, 0)),
            pl.BlockSpec((3, count, FF_TILE), lambda s: (0, 0, s)),
        ),
        scratch_shapes=[pltpu.VMEM((count, D), f32)],
        compiler_params=pltpu.CompilerParams(vmem_limit_bytes=48 * MIB),
        cost_estimate=pl.CostEstimate(
            flops=6 * count * D * FF, bytes_accessed=6 * D * FF, transcendentals=count * FF
        ),
        name="expert_backward",
    )(grad, acts, w_in, w_in, w_out)


def expert_grads_body(shares, rows_ref, grad_ref, parts_ref, out_ref, rows_t, grad_t):
    @pl.when(pl.program_id(0) == 0)
    def _():
        rows_t[...] = rows_ref[...].T
        grad_t[...] = grad_ref[...].T

    tall = D // shares
    for which in range(3):
        left = rows_t if which < 2 else grad_t
        got = dot(left[...], parts_ref[which], 1, 0).astype(bf16)
        for share in range(shares):
            out_ref[share, which] = got[share * tall : (share + 1) * tall, :]


def expert_grads(shares, rows, grad, parts):
    count = rows.shape[0]
    tall = D // shares

    def body(*refs):
        expert_grads_body(shares, *refs)

    return pl.pallas_call(
        body,
        grid=(FF_STEPS,),
        out_shape=shape((shares, 3, tall, FF), bf16),
        in_specs=[
            pl.BlockSpec((count, D), lambda s: (0, 0)),
            pl.BlockSpec((count, D), lambda s: (0, 0)),
            pl.BlockSpec((3, count, FF_TILE), lambda s: (0, 0, s)),
        ],
        out_specs=pl.BlockSpec((shares, 3, tall, FF_TILE), lambda s: (0, 0, 0, s)),
        scratch_shapes=[pltpu.VMEM((D, count), bf16), pltpu.VMEM((D, count), bf16)],
        compiler_params=pltpu.CompilerParams(vmem_limit_bytes=40 * MIB),
        cost_estimate=pl.CostEstimate(
            flops=6 * count * D * FF, bytes_accessed=6 * D * FF, transcendentals=0
        ),
        name="expert_grads",
    )(rows, grad, parts)


TWIN = [(i, i ^ 1) for i in range(GROUP)]
ACROSS = [(i, i ^ 2) for i in range(GROUP)]


def share_pieces(piece):
    across = lax.ppermute(piece, "context", ACROSS)
    twin = lax.ppermute(piece, "context", TWIN)
    return [piece, twin, across, lax.ppermute(across, "context", TWIN)]


def sum_pieces(keep, send):
    rows = keep.shape[0] // 2
    recv = lax.ppermute(send, "context", TWIN)
    other = (keep[rows:] + recv[rows:].astype(f32)).astype(bf16)
    return keep, recv, lax.ppermute(other, "context", ACROSS)


def exchange(rows):
    return lax.all_to_all(rows, "experts", split_axis=0, concat_axis=0, tiled=True)


def on_device(
    tokens, doc_starts, expert_ids, attn_in, attn_out, router, gains, rel_table,
    expert_in, expert_out, out_grad,
):
    experts = lax.axis_size("experts")
    pairs = lax.axis_size("dp")
    share = attn_in.shape[1]
    table_share = rel_table.shape[1]
    direct = share * pairs == HEAD_DIM and experts * GROUP == HEADS
    place = lax.axis_index("context").astype(jnp.int32).reshape(1)
    start_tokens = tokens[0]
    ids = expert_ids[0]
    idst = ids.T
    rows = start_tokens.shape[0]
    capacity = (10 * rows + 4 * experts - 1) // (4 * experts)
    slots = experts * capacity
    grad_in = out_grad[0]
    places = jnp.arange(GROUP * rows, dtype=jnp.int32)
    starts = doc_starts[0]
    low = jnp.max(
        jnp.where(starts[:, None] <= places[None, :], starts[:, None], 0), 0, keepdims=True
    )

    small = jnp.zeros((share, LANES), bf16)
    for layer in range(LAYERS):
        small = small.at[:, 32 * layer : 32 * layer + experts].set(router[layer])
        small = small.at[:, 32 * layer + 16 : 32 * layer + 18].set(gains[layer])
        small = small.at[0, 64 + 32 * layer : 64 + 32 * layer + table_share].set(rel_table[layer])
    split_in = attn_in.reshape(LAYERS, share, 3, OWN, GROUP, HEAD_DIM).transpose(4, 0, 1, 2, 3, 5)
    split_in = split_in.reshape(GROUP, LAYERS, share, PACKED)
    packet = jnp.concatenate(
        [split_in[:, 0], split_in[:, 1], jnp.broadcast_to(small, (GROUP, share, LANES))], -1
    )
    packet = lax.all_to_all(packet, "context", split_axis=0, concat_axis=0)
    packet = packet.reshape(GROUP * share, 2 * PACKED + LANES)

    def out_rows(layer):
        width = D // GROUP
        return jnp.concatenate(
            [attn_out[layer][:, q * width : (q + 1) * width] for q in range(GROUP)], 0
        )

    def gather(part):
        got = lax.all_gather(part, ("experts", "dp"), axis=0, tiled=False)
        return got.reshape(experts, pairs, GROUP, share, part.shape[-1])

    w_in, w_out = [], []
    small_all = None
    for layer in range(LAYERS):
        columns = [packet[:, layer * PACKED : (layer + 1) * PACKED]]
        if layer == 0:
            columns.append(packet[:, 2 * PACKED :])
        if direct:
            columns.append(out_rows(layer))
        got = gather(jnp.concatenate(columns, 1))
        w_in.append(got[..., :PACKED].transpose(0, 2, 1, 3, 4).reshape(D, PACKED))
        if layer == 0:
            small_all = got[..., PACKED : PACKED + LANES].transpose(0, 2, 1, 3, 4)
        if direct:
            w_out.append(
                got[..., -D // GROUP :].transpose(2, 0, 1, 3, 4).reshape(GROUP, OWN_COLS, D // GROUP)
            )
        else:
            full = lax.all_gather(attn_out[layer], ALL, axis=0, tiled=True)
            mine = lax.dynamic_index_in_dim(
                full.reshape(OWN, GROUP, HEAD_DIM, D), place[0], 1, keepdims=False
            )
            w_out.append(mine.reshape(OWN_COLS, GROUP, D // GROUP).transpose(1, 0, 2))
    by_feature = small_all.reshape(D, LANES).T
    hits = jnp.asarray(bucket_hits())
    gain_a, gain_b, routers, bias_rows = [], [], [], []
    for layer in range(LAYERS):
        top = 32 * layer
        gain_a.append(by_feature[top + 16 : top + 17].astype(f32))
        gain_b.append(by_feature[top + 17 : top + 18].astype(f32))
        routers.append(
            jnp.pad(by_feature[top : top + experts].astype(f32), ((0, LANES - experts), (0, 0)))
        )
        table = small_all[:, :, :, 0, 64 + top : 64 + top + table_share].reshape(
            BUCKETS, OWN, GROUP
        )
        table = lax.dynamic_index_in_dim(table, place[0], 2, keepdims=False).astype(f32)
        row = jnp.dot((table - table[-1:]).T, hits, precision=lax.Precision.HIGHEST)
        bias_rows.append(jnp.pad(row, ((0, 8 - OWN), (0, 0))))

    def first_norm(piece):
        wide = piece.astype(f32)
        return (wide * rms_scale(wide) * gain_a[0]).astype(bf16)

    pieces = [first_norm(piece) for piece in share_pieces(start_tokens)]
    x = start_tokens
    kept = []
    for layer in range(LAYERS):
        packed, log_total, mixed, keep, send = attention_forward(
            place, pieces, w_in[layer], bias_rows[layer], low, w_out[layer]
        )
        keep, recv, far = sum_pieces(keep, send)
        last = layer == LAYERS - 1
        routed = route(
            experts, capacity, x, keep, recv, far, gain_b[layer], routers[layer], ids, idst,
            grad_in if last else None,
        )
        middle, sent_rows, soft, meta, dest = routed[:5]
        arrived = exchange(sent_rows)
        if last:
            arrived_grad = exchange(routed[5])
        produced, acts = expert_forward(layer, arrived, expert_in, expert_out)
        back = exchange(produced)
        kept.append(
            (x, pieces, packed, log_total, mixed, middle, soft, meta, dest, arrived, acts, back)
        )
        if last:
            (result,) = combine(middle, back, meta)
        else:
            x, normed = combine(middle, back, meta, gain_a[layer + 1])
            pieces = share_pieces(normed)

    g = grad_in
    dense_out, expert_out_grads = [], []
    for layer in range(LAYERS - 1, -1, -1):
        x, pieces, packed, log_total, mixed, middle, soft, meta, dest, arrived, acts, back = kept[
            layer
        ]
        drows, parts = expert_backward(layer, arrived_grad, acts, expert_in, expert_out)
        came = exchange(drows)
        weight_grads = expert_grads(GROUP * pairs, arrived, arrived_grad, parts)
        expert_out_grads.insert(
            0, lax.psum_scatter(weight_grads, ("context", "dp"), scatter_dimension=0, tiled=False)
        )
        dmiddle, dattn, small_b = expert_token_back(
            experts, back, came, g, middle, soft, meta, ids, gain_b[layer], routers[layer]
        )
        grad_pieces = share_pieces(dattn)
        grad_packed, keep, send, by_distance = attention_backward(
            place, grad_pieces, w_in[layer], bias_rows[layer], low, w_out[layer], packed, log_total
        )
        keep, recv, far = sum_pieces(keep, send)
        grad_w_in, grad_w_out = dense_grads(pieces, grad_pieces, grad_packed, mixed)
        if layer > 0:
            below = kept[layer - 1]
            g, small_a, sent = attention_token_back(
                x, dmiddle, keep, recv, far, gain_a[layer], below[7], below[8], slots
            )
            arrived_grad = exchange(sent)
        else:
            g, small_a = attention_token_back(x, dmiddle, keep, recv, far, gain_a[layer])

        by_bucket = jnp.dot(hits, by_distance[:OWN].T, precision=lax.Precision.HIGHEST)
        spread = jnp.where(
            jnp.arange(GROUP)[None, None, :] == place[0], by_bucket[:, :, None], 0.0
        ).reshape(experts, GROUP, pairs, 1, table_share)
        features = jnp.concatenate([small_b[:experts], small_a[:1], small_b[16:17]], 0).T
        features = features.reshape(experts, GROUP, pairs, share, experts + 2)
        small_grad = jnp.zeros((experts, GROUP, pairs, share, LANES), f32)
        small_grad = small_grad.at[..., : experts + 2].set(features)
        small_grad = small_grad.at[..., :1, 64 : 64 + table_share].set(spread)
        pack = jnp.concatenate(
            [
                grad_w_in.reshape(experts, GROUP, pairs, share, PACKED),
                small_grad.astype(bf16),
            ],
            -1,
        ).transpose(0, 2, 1, 3, 4)
        pack = pack.reshape(experts * pairs, GROUP * share, PACKED + LANES)
        if direct:
            width = D // GROUP
            outer = grad_w_out.reshape(experts * pairs, share, GROUP, width).transpose(0, 2, 1, 3)
            pack = jnp.concatenate(
                [pack, outer.reshape(experts * pairs, GROUP * share, width)], -1
            )
        mine = lax.psum_scatter(pack, ("experts", "dp"), scatter_dimension=0, tiled=False)
        inner = mine[:, : PACKED + LANES].reshape(GROUP, share, PACKED + LANES)
        inner = lax.all_to_all(inner, "context", split_axis=0, concat_axis=0)
        g_in = inner[..., :PACKED].astype(f32).reshape(GROUP, share, 3, OWN, HEAD_DIM)
        g_in = g_in.transpose(1, 2, 3, 0, 4).reshape(share, 3 * D)
        g_small = jnp.sum(inner[..., PACKED:].astype(f32), 0)
        if direct:
            width = D // GROUP
            g_out = mine[:, -width:].astype(f32).reshape(GROUP, share, width)
            g_out = g_out.transpose(1, 0, 2).reshape(share, D)
        else:
            placed = jnp.where(
                jnp.arange(GROUP)[None, :, None, None] == place[0],
                grad_w_out.reshape(OWN, 1, HEAD_DIM, D),
                jnp.zeros((), bf16),
            ).reshape(D, D)
            g_out = lax.psum_scatter(placed, ALL, scatter_dimension=0, tiled=True).astype(f32)
        dense_out.insert(
            0,
            (
                g_in,
                g_out,
                g_small[:, :experts],
                g_small[:, experts : experts + 2],
                g_small[0, 64 : 64 + table_share],
            ),
        )
    dense = tuple(jnp.stack([entry[k] for entry in dense_out]) for k in range(5))
    tall = expert_out_grads[0].shape[1]
    wide = [entry.astype(f32) for entry in expert_out_grads]
    grad_expert_in = jnp.stack(
        [entry[:2].transpose(1, 0, 2).reshape(1, tall, 2 * FF) for entry in wide]
    )
    grad_expert_out = jnp.stack([entry[2:3] for entry in wide])
    return (result[None], g[None], *dense, grad_expert_in, grad_expert_out)


def solution(mesh):
    return jax.shard_map(
        on_device,
        mesh=mesh,
        in_specs=(
            P(("experts", "dp"), "context", None),
            P(("experts", "dp"), None),
            P(("experts", "dp"), "context", None),
            P(None, ("experts", "context", "dp"), None),
            P(None, ("experts", "context", "dp"), None),
            P(None, ("experts", "context", "dp"), None),
            P(None, ("experts", "context", "dp"), None),
            P(None, ("experts", "context", "dp")),
            P(None, "experts", None, None),
            P(None, "experts", None, None),
            P(("experts", "dp"), "context", None),
        ),
        out_specs=(
            P(("experts", "dp"), "context", None),
            P(("experts", "dp"), "context", None),
            P(None, ("experts", "context", "dp"), None),
            P(None, ("experts", "context", "dp"), None),
            P(None, ("experts", "context", "dp"), None),
            P(None, ("experts", "context", "dp"), None),
            P(None, ("experts", "context", "dp")),
            P(None, "experts", ("context", "dp"), None),
            P(None, "experts", ("context", "dp"), None),
        ),
        check_vma=False,
    )
```

time: 2880 us -> 1100 us (0.38); the launches traced: 2830 us -> 1100 us
  local copies, waits for them, and re-layouts: 858 us -> 118 us
  waiting for transfers between devices: 1030 us -> 467 us
  matrix products: 317 us -> 1.59 us
  blocking collectives: 457 us -> 171 us
  Pallas kernels: 0 us -> 238 us
  other arithmetic: 128 us -> 51.2 us
    reduce_scatter x12 -> x4, waiting for transfers between devices: 828 us -> 280 us  [the longest x2 220 us: on_device(): lax.psum_scatter(weight_grads, ('context', 'dp'), scatter_dimension=0, ti...]
    dot_general x44 -> x4, matrix products: 312 us -> 1.59 us  [the longest x2 1.17 us: on_device(): jnp.dot(hits, by_distance[:OWN].T, precision=lax.Precision.HIGHEST)]
    all_gather x4 -> x0, blocking collectives: 310 us -> none  [the longest x2 170 us: on_device(): lax.all_gather(router[layer_index], ('experts', 'context', 'dp'), axis=0,...]
    rev x2 -> x0, local copies, waits for them, and re-layouts: 250 us -> none  [table_grad(): padded = jnp.pad(grad_scores[:, :, ::-1], ((0, 0), (0, 0), (0, query_rows)))]
    pallas_call x0 -> x20, Pallas kernels: none -> 238 us  [the longest x14 100 us: whole_call(): pl.pallas_call(body, out_shape=outs, in_specs=specs, out_specs=tuple((pl....]
    scatter x4 -> x8, local copies, waits for them, and re-layouts: 234 us -> 13.4 us  [the longest x2 8.14 us: on_device(): small_grad = small_grad.at[..., :1, 64:64 + table_share].set(spread)]
    unnamed x28 -> x6, waiting for transfers between devices: 122 us -> 0.1 us
    all_to_all x2 -> x5, blocking collectives: 70.7 us -> 171 us  [exchange(): lax.all_to_all(rows, 'experts', split_axis=0, concat_axis=0, tiled=True)]
  transfers between devices with their start and end apart: 30 -> 32, of which waited for: 13 -> 21; matrix products, arithmetic and copies ran while one was open for 36% -> 5% of each run, Pallas kernels for 0% -> 11%
where the time goes in v1:
time: 1100 us
  waiting for transfers between devices  467 us (42%)
  Pallas kernels  238 us (22%)
  blocking collectives  171 us (16%)
  local copies, waits for them, and re-layouts  118 us (11%)
  other arithmetic  51.2 us (5%)
  starting transfers between devices  34.9 us (3%)
  between operations  15.7 us (1%)
    reduce_scatter x2, waiting for transfers between devices, on_device(): lax.psum_scatter(weight_grads, ('context', 'dp'), scatter_dimension=0, ti...  220 us
    all_to_all x5, blocking collectives, exchange(): lax.all_to_all(rows, 'experts', split_axis=0, concat_axis=0, tiled=True)  171 us
    pallas_call x14, Pallas kernels, whole_call(): pl.pallas_call(body, out_shape=outs, in_specs=specs, out_specs=tuple((pl....  100 us
    pallas_call x2, Pallas kernels, expert_backward(): pl.pallas_call(expert_backward_body, grid=(FF_STEPS,), out_shape=(shape((...  61.3 us
    reduce_scatter x2, waiting for transfers between devices, on_device(): lax.psum_scatter(pack, ('experts', 'dp'), scatter_dimension=0, tiled=False)  60.2 us
    unnamed x238, local copies, waits for them, and re-layouts  52.1 us
    all_to_all x3, waiting for transfers between devices, exchange(): lax.all_to_all(rows, 'experts', split_axis=0, concat_axis=0, tiled=True)  46.2 us
    ppermute x4, waiting for transfers between devices, share_pieces(): across = lax.ppermute(piece, 'context', ACROSS)  44 us
  transfers between devices with their start and end apart: 32, of which 21 were waited for; matrix products, arithmetic and copies ran while one was open for 5% of the time, Pallas kernels for 11%

profile of v1, /device:TPU:0, one launch (start us, length us, event | category | flops | bytes accessed | tf_op | source)
XLA Modules:
  0.0 1097.6 jit_solution(14543460884626049375)
XLA Ops:
  33.3 6.9 all-to-all-done
  43.0 12.0 %collective-permute-done.1 = bf16[256,1024]{1,0:T(8,128)(2,1)S(1)} collective-permute-done((bf16[256,1024]{1,0:T(8,128)(2,1)S(1)}, bf16[256,1024]{1,0:T(8,128)(2,1)S(1)}, u32[]{:S(2)}, u32[]{:S(2)}) %collective-permute-start.1) | collective-permute-done | bytes 524320 | tf_op jit(solution)/shard_map/ppermute | solution.py:715
  58.5 36.4 %all-gather.5.cloned.1.call-done = bf16[1024,1152]{1,0:T(8,128)(2,1)} async-done(((bf16[128,1152]{1,0:T(8,128)(2,1)}), bf16[1024,1152]{1,0:T(8,128)(2,1)}) %all-gather.5.cloned.1.call-update) | async-done | bytes 2359312 | tf_op jit(solution)/shard_map/all_gather | solution.py:774
  104.4 12.6 %attention_forward.2 = (bf16[1024,768]{1,0:T(8,128)(2,1)S(1)}, f32[8,1024]{1,0:T(8,128)S(1)}, bf16[1024,256]{1,0:T(8,128)(2,1)S(1)}, f32[512,1024]{1,0:T(8,128)}, bf16[512,1024]{1,0:T(8,128)(2,1)S(1)}) custom-call(s32[1]{0:T(128)} %bitcast.1.place_ref, bf16[256,1024]{1,0:T(8,128)(2,1)S(1)} %get-tuple-element.287.n0, ...), custom_call_target="tpu_custom_call" | custom-call | flops 3221225472 | bytes 9490436 | tf_op jit(solution)/shard_map/attention_forward/pallas_call | solution.py:64
  123.6 12.1 %collective-permute-done.4.refs_3_ = bf16[256,1024]{1,0:T(8,128)(2,1)S(1)} collective-permute-done((bf16[256,1024]{1,0:T(8,128)(2,1)S(1)}, bf16[256,1024]{1,0:T(8,128)(2,1)S(1)}, u32[]{:S(2)}, u32[]{:S(2)}) %collective-permute-start.4) | collective-permute-done | bytes 524320 | tf_op jit(solution)/shard_map/ppermute | solution.py:724
  147.0 38.7 %all-to-all-done.1 = bf16[4,160,1024]{2,1,0:T(8,128)(2,1)S(1)} async-done(((bf16[4,160,1024]{2,1,0:T(8,128)(2,1)}), bf16[4,160,1024]{2,1,0:T(8,128)(2,1)S(1)}, u32[]{:S(2)}, u32[]{:S(2)}) %all-to-all-start.1) | async-done | bytes 1310752 | tf_op jit(solution)/shard_map/all_to_all | solution.py:728
  185.7 19.7 %expert_forward.2 = (bf16[640,1024]{1,0:T(8,128)(2,1)S(1)}, bf16[2,640,2816]{2,1,0:T(8,128)(2,1)S(1)}) custom-call(bf16[640,1024]{1,0:T(8,128)(2,1)S(1)} %bitcast.148, bf16[2,1,1024,5632]{3,2,1,0:T(8,128)(2,1)} %wu_ref.7, bf16[2,1,1024,5632]{3,2,1,0:T(8,128)(2,1)} %wu_ref.7, bf16[2,1,1024,2816]{3,2,1,0:T(8,128)(2,1)} %wo_ref.7), custom_call_target="tpu_custom_call" | custom-call | flops 11072962560 | bytes 17301504 | tf_op jit(solution)/shard_map/expert_forward/pallas_call | solution.py:596
  208.4 33.4 %all_to_all.103 = bf16[4,160,1024]{2,1,0:T(8,128)(2,1)S(1)} all-to-all(bf16[4,160,1024]{2,1,0:T(8,128)(2,1)S(1)} %bitcast.165), channel_id=1, replica_groups=mesh['experts'=4,'context'=4,'dp'=2] {'experts'}, dimensions={0} | all-to-all | bytes 2621440 | tf_op jit(solution)/shard_map/all_to_all | solution.py:728
  246.7 9.8 collective-permute-done.6.n2
  261.5 12.5 %attention_forward.3 = (bf16[1024,768]{1,0:T(8,128)(2,1)S(1)}, f32[8,1024]{1,0:T(8,128)S(1)}, bf16[1024,256]{1,0:T(8,128)(2,1)S(1)}, f32[512,1024]{1,0:T(8,128)}, bf16[512,1024]{1,0:T(8,128)(2,1)S(1)}) custom-call(s32[1]{0:T(128)} %bitcast.1.place_ref, bf16[256,1024]{1,0:T(8,128)(2,1)} %get-tuple-element.189.n0, ...), custom_call_target="tpu_custom_call" | custom-call | flops 3221225472 | bytes 9490436 | tf_op jit(solution)/shard_map/attention_forward/pallas_call | solution.py:64
  281.6 12.0 %collective-permute-done.9.refs_3_ = bf16[256,1024]{1,0:T(8,128)(2,1)S(1)} collective-permute-done((bf16[256,1024]{1,0:T(8,128)(2,1)S(1)}, bf16[256,1024]{1,0:T(8,128)(2,1)S(1)}, u32[]{:S(2)}, u32[]{:S(2)}) %collective-permute-start.9) | collective-permute-done | bytes 524320 | tf_op jit(solution)/shard_map/ppermute | solution.py:724
  293.6 6.8 route.3
  302.0 34.8 %all_to_all.104 = bf16[4,160,1024]{2,1,0:T(8,128)(2,1)S(1)} all-to-all(bf16[4,160,1024]{2,1,0:T(8,128)(2,1)} %bitcast.200), channel_id=1, replica_groups=mesh['experts'=4,'context'=4,'dp'=2] {'experts'}, dimensions={0} | all-to-all | bytes 2621440 | tf_op jit(solution)/shard_map/all_to_all | solution.py:728
  341.2 19.1 %expert_forward.3 = (bf16[640,1024]{1,0:T(8,128)(2,1)S(1)}, bf16[2,640,2816]{2,1,0:T(8,128)(2,1)S(1)}) custom-call(bf16[640,1024]{1,0:T(8,128)(2,1)S(1)} %bitcast.150, bf16[2,1,1024,5632]{3,2,1,0:T(8,128)(2,1)} %wu_ref.7, bf16[2,1,1024,5632]{3,2,1,0:T(8,128)(2,1)} %wu_ref.7, bf16[2,1,1024,2816]{3,2,1,0:T(8,128)(2,1)} %wo_ref.7), custom_call_target="tpu_custom_call" | custom-call | flops 11072962560 | bytes 17301504 | tf_op jit(solution)/shard_map/expert_forward/pallas_call | solution.py:596
  364.2 7.5 all-to-all-done.5
  375.3 30.8 %expert_backward.2 = (bf16[640,1024]{1,0:T(8,128)(2,1)S(1)}, bf16[3,640,2816]{2,1,0:T(8,128)(2,1)}) custom-call(bf16[640,1024]{1,0:T(8,128)(2,1)} %bitcast.48.grad_ref.refs_1_, bf16[2,640,2816]{2,1,0:T(8,128)(2,1)} %copy-done.2, bf16[2,1,1024,5632]{3,2,1,0:T(8,128)(2,1)} %wu_ref.7, bf16[2,1,1024,5632]{3,2,1,0:T(8,128)(2,1)} %wu_ref.7, ...), custom_call_target="tpu_custom_call" | custom-call | flops 11072962560 | bytes 17301504 | tf_op jit(solution)/shard_map/expert_backward/pallas_call | solution.py:648
  407.3 35.5 %all_to_all.105 = bf16[4,160,1024]{2,1,0:T(8,128)(2,1)} all-to-all(bf16[4,160,1024]{2,1,0:T(8,128)(2,1)} %bitcast.163), channel_id=1, replica_groups=mesh['experts'=4,'context'=4,'dp'=2] {'experts'}, dimensions={0} | all-to-all | bytes 2621440 | tf_op jit(solution)/shard_map/all_to_all | solution.py:728
  450.0 11.1 %collective-permute-done.11.d2 = bf16[256,1024]{1,0:T(8,128)(2,1)S(1)} collective-permute-done((bf16[256,1024]{1,0:T(8,128)(2,1)S(1)}, bf16[256,1024]{1,0:T(8,128)(2,1)S(1)}, u32[]{:S(2)}, u32[]{:S(2)}) %collective-permute-start.11) | collective-permute-done | bytes 524320 | tf_op jit(solution)/shard_map/ppermute | solution.py:715
  462.9 17.0 %attention_backward.2 = (bf16[1024,768]{1,0:T(8,128)(2,1)S(1)}, f32[512,1024]{1,0:T(8,128)}, bf16[512,1024]{1,0:T(8,128)(2,1)S(1)}, f32[8,512]{1,0:T(8,128)S(1)}) custom-call(s32[1]{0:T(128)} %bitcast.1.place_ref, bf16[256,1024]{1,0:T(8,128)(2,1)S(1)} %get-tuple-element.201.d0, bf16[256,1024]{1,0:T(8,128)(2,1)S(1)} %collective-permute-done.10.d1, ...), custom_call_target="tpu_custom_call" | custom-call | flops 4831838208 | bytes 10555396 | tf_op jit(solution)/shard_map/attention_backward/pallas_call | solution.py:64
  486.6 12.6 %collective-permute-done.14.refs_4_ = bf16[256,1024]{1,0:T(8,128)(2,1)S(1)} collective-permute-done((bf16[256,1024]{1,0:T(8,128)(2,1)S(1)}, bf16[256,1024]{1,0:T(8,128)(2,1)S(1)}, u32[]{:S(2)}, u32[]{:S(2)}) %collective-permute-start.14) | collective-permute-done | bytes 524320 | tf_op jit(solution)/shard_map/ppermute | solution.py:724
  502.4 33.5 %all_to_all.106 = bf16[4,160,1024]{2,1,0:T(8,128)(2,1)S(1)} all-to-all(bf16[4,160,1024]{2,1,0:T(8,128)(2,1)S(1)} %bitcast.162), channel_id=1, replica_groups=mesh['experts'=4,'context'=4,'dp'=2] {'experts'}, dimensions={0} | all-to-all | bytes 2621440 | tf_op jit(solution)/shard_map/all_to_all | solution.py:728
  535.9 30.5 %expert_backward.3 = (bf16[640,1024]{1,0:T(8,128)(2,1)S(1)}, bf16[3,640,2816]{2,1,0:T(8,128)(2,1)}) custom-call(bf16[640,1024]{1,0:T(8,128)(2,1)S(1)} %bitcast.152, bf16[2,640,2816]{2,1,0:T(8,128)(2,1)} %copy-done.1, bf16[2,1,1024,5632]{3,2,1,0:T(8,128)(2,1)} %wu_ref.7, bf16[2,1,1024,5632]{3,2,1,0:T(8,128)(2,1)} %wu_ref.7, bf16[2,1,1024,2816]{3,2,1,0:T(8,128)(2,1)} %wo_ref.7), custom_call_target="tpu_custom_call" | custom-call | flops 11072962560 | bytes 17301504 | tf_op jit(solution)/shard_map/expert_backward/pallas_call | solution.py:648
  566.5 33.7 %all_to_all.107 = bf16[4,160,1024]{2,1,0:T(8,128)(2,1)} all-to-all(bf16[4,160,1024]{2,1,0:T(8,128)(2,1)S(1)} %bitcast.164), channel_id=1, replica_groups=mesh['experts'=4,'context'=4,'dp'=2] {'experts'}, dimensions={0} | all-to-all | bytes 2621440 | tf_op jit(solution)/shard_map/all_to_all | solution.py:728
  607.6 11.1 %collective-permute-done.16.d2 = bf16[256,1024]{1,0:T(8,128)(2,1)S(1)} collective-permute-done((bf16[256,1024]{1,0:T(8,128)(2,1)S(1)}, bf16[256,1024]{1,0:T(8,128)(2,1)S(1)}, u32[]{:S(2)}, u32[]{:S(2)}) %collective-permute-start.16) | collective-permute-done | bytes 524320 | tf_op jit(solution)/shard_map/ppermute | solution.py:715
  620.7 17.2 %attention_backward.3 = (bf16[1024,768]{1,0:T(8,128)(2,1)S(1)}, f32[512,1024]{1,0:T(8,128)}, bf16[512,1024]{1,0:T(8,128)(2,1)}, f32[8,512]{1,0:T(8,128)S(1)}) custom-call(s32[1]{0:T(128)} %bitcast.1.place_ref, bf16[256,1024]{1,0:T(8,128)(2,1)S(1)} %get-tuple-element.213.d0, bf16[256,1024]{1,0:T(8,128)(2,1)S(1)} %collective-permute-done.15.d1, ...), custom_call_target="tpu_custom_call" | custom-call | flops 4831838208 | bytes 10555396 | tf_op jit(solution)/shard_map/attention_backward/pallas_call | solution.py:64
  648.5 5.6 dense_grads.3
  714.9 19.5 %expert_grads.3 = bf16[8,3,128,2816]{3,2,1,0:T(8,128)(2,1)} custom-call(bf16[640,1024]{1,0:T(8,128)(2,1)S(1)} %bitcast.151, bf16[640,1024]{1,0:T(8,128)(2,1)} %bitcast.48.grad_ref.refs_1_, bf16[3,640,2816]{2,1,0:T(8,128)(2,1)S(1)} %copy-done.59), custom_call_target="tpu_custom_call" | custom-call | flops 11072962560 | bytes 17301504 | tf_op jit(solution)/shard_map/expert_grads/pallas_call | solution.py:691
  741.3 18.2 %expert_grads.2 = bf16[8,3,128,2816]{3,2,1,0:T(8,128)(2,1)} custom-call(bf16[640,1024]{1,0:T(8,128)(2,1)S(1)} %bitcast.149, bf16[640,1024]{1,0:T(8,128)(2,1)S(1)} %bitcast.153, bf16[3,640,2816]{2,1,0:T(8,128)(2,1)S(1)} %copy-done.60), custom_call_target="tpu_custom_call" | custom-call | flops 11072962560 | bytes 17301504 | tf_op jit(solution)/shard_map/expert_grads/pallas_call | solution.py:691
  767.4 60.2 %reduce-scatter.5.cloned.1.call-done = bf16[1,128,1152]{2,1,0:T(8,128)(2,1)} async-done(((bf16[8,128,1152]{2,1,0:T(8,128)(2,1)}), bf16[1,128,1152]{2,1,0:T(8,128)(2,1)}) %reduce-scatter.5.cloned.1.call-update) | async-done | bytes 294928 | tf_op jit(solution)/shard_map/reduce_scatter | solution.py:901
  844.7 104.0 %reduce-scatter.11.cloned.1.call-done = bf16[1,3,128,2816]{3,2,1,0:T(8,128)(2,1)} async-done(((bf16[8,3,128,2816]{3,2,1,0:T(8,128)(2,1)}), bf16[1,3,128,2816]{3,2,1,0:T(8,128)(2,1)}) %reduce-scatter.11.cloned.1.call-update) | async-done | bytes 2162704 | tf_op jit(solution)/shard_map/reduce_scatter | solution.py:858
  955.5 115.8 %reduce-scatter.9.cloned.1.call-done = bf16[1,3,128,2816]{3,2,1,0:T(8,128)(2,1)} async-done(((bf16[8,3,128,2816]{3,2,1,0:T(8,128)(2,1)}), bf16[1,3,128,2816]{3,2,1,0:T(8,128)(2,1)}) %reduce-scatter.9.cloned.1.call-update) | async-done | bytes 2162704 | tf_op jit(solution)/shard_map/reduce_scatter | solution.py:858
  1081.1 6.4 copy.153
  (457 shorter events, 245.0 us)
Async XLA Ops:
  28.2 12.0 %all-to-all-start = ((bf16[4,32,1664]{2,1,0:T(8,128)(2,1)}), bf16[4,32,1664]{2,1,0:T(8,128)(2,1)S(1)}, u32[]{:S(2)}, u32[]{:S(2)}) async-start(bf16[4,32,1664]{2,1,0:T(8,128)(2,1)} %pad_maximum_fusion.6), calls=%async_computation | async-start | bytes 851968 | tf_op jit(solution)/shard_map/all_to_all | solution.py:764
  32.4 62.5 %all-gather.5.cloned.1.call-start = ((), (), s32[]{:S(2)}) async-start(), calls=%async_computation.19 | async-start | bytes 2654208 | tf_op jit(solution)/shard_map/all_gather | solution.py:774
  41.6 13.4 %collective-permute-start.1 = (bf16[256,1024]{1,0:T(8,128)(2,1)S(1)}, bf16[256,1024]{1,0:T(8,128)(2,1)S(1)}, u32[]{:S(2)}, u32[]{:S(2)}) collective-permute-start(bf16[256,1024]{1,0:T(8,128)(2,1)S(1)} %bitcast.144), channel_id=1, source_target_pairs={{0,4},{2,6},{4,0},{6,2},{1,5},{3,7},{5,1},{7,3},{8,12},{10,14},{12... | collective-permute-start | bytes 1572872 | tf_op jit(solution)/shard_map/ppermute | solution.py:715
  42.1 13.1 %collective-permute-start = (bf16[256,1024]{1,0:T(8,128)(2,1)S(1)}, bf16[256,1024]{1,0:T(8,128)(2,1)S(1)}, u32[]{:S(2)}, u32[]{:S(2)}) collective-permute-start(bf16[256,1024]{1,0:T(8,128)(2,1)S(1)} %bitcast.145), channel_id=1, source_target_pairs={{0,2},{2,0},{4,6},{6,4},{1,3},{3,1},{5,7},{7,5},{8,10},{10,8},{12,... | collective-permute-start | bytes 1572872 | tf_op jit(solution)/shard_map/ppermute | solution.py:716
  55.0 1.9 collective-permute-start.2
  117.6 2.7 collective-permute-start.3
  121.7 14.0 %collective-permute-start.4 = (bf16[256,1024]{1,0:T(8,128)(2,1)S(1)}, bf16[256,1024]{1,0:T(8,128)(2,1)S(1)}, u32[]{:S(2)}, u32[]{:S(2)}) collective-permute-start(bf16[256,1024]{1,0:T(8,128)(2,1)S(1)} %add_convert_fusion.3), channel_id=1, source_target_pairs={{0,4},{2,6},{4,0},{6,2},{1,5},{3,7},{5,1},{7,3},{8,12},{10,14},{12... | collective-permute-start | bytes 1572872 | tf_op jit(solution)/shard_map/ppermute | solution.py:724
  142.5 43.2 %all-to-all-start.1 = ((bf16[4,160,1024]{2,1,0:T(8,128)(2,1)}), bf16[4,160,1024]{2,1,0:T(8,128)(2,1)S(1)}, u32[]{:S(2)}, u32[]{:S(2)}) async-start(bf16[4,160,1024]{2,1,0:T(8,128)(2,1)} %bitcast.29), calls=%async_computation.1 | async-start | bytes 2621440 | tf_op jit(solution)/shard_map/all_to_all | solution.py:728
  146.2 98.9 %all-gather.7.cloned.1.call-start = ((), (), s32[]{:S(2)}) async-start(), calls=%async_computation.20 | async-start | bytes 2359296 | tf_op jit(solution)/shard_map/all_gather | solution.py:774
  243.7 12.8 %collective-permute-start.6 = (bf16[256,1024]{1,0:T(8,128)(2,1)}, bf16[256,1024]{1,0:T(8,128)(2,1)}, u32[]{:S(2)}, u32[]{:S(2)}) collective-permute-start(bf16[256,1024]{1,0:T(8,128)(2,1)} %get-tuple-element.189.n0), channel_id=1, source_target_pairs={{0,4},{2,6},{4,0},{6,2},{1,5},{3,7},{5,1},{7,3},{8,12},{10,14},{12... | collective-permute-start | bytes 1572872 | tf_op jit(solution)/shard_map/ppermute | solution.py:715
  246.6 13.8 %collective-permute-start.5 = (bf16[256,1024]{1,0:T(8,128)(2,1)}, bf16[256,1024]{1,0:T(8,128)(2,1)}, u32[]{:S(2)}, u32[]{:S(2)}) collective-permute-start(bf16[256,1024]{1,0:T(8,128)(2,1)} %get-tuple-element.189.n0), channel_id=1, source_target_pairs={{0,2},{2,0},{4,6},{6,4},{1,3},{3,1},{5,7},{7,5},{8,10},{10,8},{12,... | collective-permute-start | bytes 1572872 | tf_op jit(solution)/shard_map/ppermute | solution.py:716
  256.5 3.9 collective-permute-start.7
  275.2 2.8 collective-permute-start.8
  279.3 14.3 %collective-permute-start.9 = (bf16[256,1024]{1,0:T(8,128)(2,1)S(1)}, bf16[256,1024]{1,0:T(8,128)(2,1)S(1)}, u32[]{:S(2)}, u32[]{:S(2)}) collective-permute-start(bf16[256,1024]{1,0:T(8,128)(2,1)S(1)} %add_convert_fusion.2), channel_id=1, source_target_pairs={{0,4},{2,6},{4,0},{6,2},{1,5},{3,7},{5,1},{7,3},{8,12},{10,14},{12... | collective-permute-start | bytes 1572872 | tf_op jit(solution)/shard_map/ppermute | solution.py:724
  336.9 34.8 %all-to-all-start.5 = ((bf16[4,160,1024]{2,1,0:T(8,128)(2,1)}), bf16[4,160,1024]{2,1,0:T(8,128)(2,1)}, u32[]{:S(2)}, u32[]{:S(2)}) async-start(bf16[4,160,1024]{2,1,0:T(8,128)(2,1)} %bitcast.199), calls=%async_computation.5 | async-start | bytes 2621440 | tf_op jit(solution)/shard_map/all_to_all | solution.py:728
  371.7 35.5 %all-to-all-start.4 = ((bf16[4,160,1024]{2,1,0:T(8,128)(2,1)}), bf16[4,160,1024]{2,1,0:T(8,128)(2,1)S(1)}, u32[]{:S(2)}, u32[]{:S(2)}) async-start(bf16[4,160,1024]{2,1,0:T(8,128)(2,1)} %bitcast.161), calls=%async_computation.4 | async-start | bytes 2621440 | tf_op jit(solution)/shard_map/all_to_all | solution.py:728
  375.2 384.3 %reduce-scatter.7.cloned.1.call-start = ((), (), s32[]{:S(2)}) async-start(), calls=%async_computation.16 | async-start | bytes 2654208 | tf_op jit(solution)/shard_map/reduce_scatter | solution.py:901
  448.6 12.5 %collective-permute-start.11 = (bf16[256,1024]{1,0:T(8,128)(2,1)S(1)}, bf16[256,1024]{1,0:T(8,128)(2,1)S(1)}, u32[]{:S(2)}, u32[]{:S(2)}) collective-permute-start(bf16[256,1024]{1,0:T(8,128)(2,1)S(1)} %get-tuple-element.201.d0), channel_id=1, source_target_pairs={{0,4},{2,6},{4,0},{6,2},{1,5},{3,7},{5,1},{7,3},{8,12},{10,14},{12... | collective-permute-start | bytes 1572872 | tf_op jit(solution)/shard_map/ppermute | solution.py:715
  449.9 11.1 %collective-permute-start.10 = (bf16[256,1024]{1,0:T(8,128)(2,1)S(1)}, bf16[256,1024]{1,0:T(8,128)(2,1)S(1)}, u32[]{:S(2)}, u32[]{:S(2)}) collective-permute-start(bf16[256,1024]{1,0:T(8,128)(2,1)S(1)} %get-tuple-element.201.d0), channel_id=1, source_target_pairs={{0,2},{2,0},{4,6},{6,4},{1,3},{3,1},{5,7},{7,5},{8,10},{10,8},{12,... | collective-permute-start | bytes 1572872 | tf_op jit(solution)/shard_map/ppermute | solution.py:716
  461.0 1.9 collective-permute-start.12
  481.2 2.7 collective-permute-start.13
  485.2 14.0 %collective-permute-start.14 = (bf16[256,1024]{1,0:T(8,128)(2,1)S(1)}, bf16[256,1024]{1,0:T(8,128)(2,1)S(1)}, u32[]{:S(2)}, u32[]{:S(2)}) collective-permute-start(bf16[256,1024]{1,0:T(8,128)(2,1)S(1)} %add_convert_fusion.1), channel_id=1, source_target_pairs={{0,4},{2,6},{4,0},{6,2},{1,5},{3,7},{5,1},{7,3},{8,12},{10,14},{12... | collective-permute-start | bytes 1572872 | tf_op jit(solution)/shard_map/ppermute | solution.py:724
  606.3 12.5 %collective-permute-start.16 = (bf16[256,1024]{1,0:T(8,128)(2,1)S(1)}, bf16[256,1024]{1,0:T(8,128)(2,1)S(1)}, u32[]{:S(2)}, u32[]{:S(2)}) collective-permute-start(bf16[256,1024]{1,0:T(8,128)(2,1)S(1)} %get-tuple-element.213.d0), channel_id=1, source_target_pairs={{0,4},{2,6},{4,0},{6,2},{1,5},{3,7},{5,1},{7,3},{8,12},{10,14},{12... | collective-permute-start | bytes 1572872 | tf_op jit(solution)/shard_map/ppermute | solution.py:715
  607.6 11.1 %collective-permute-start.15 = (bf16[256,1024]{1,0:T(8,128)(2,1)S(1)}, bf16[256,1024]{1,0:T(8,128)(2,1)S(1)}, u32[]{:S(2)}, u32[]{:S(2)}) collective-permute-start(bf16[256,1024]{1,0:T(8,128)(2,1)S(1)} %get-tuple-element.213.d0), channel_id=1, source_target_pairs={{0,2},{2,0},{4,6},{6,4},{1,3},{3,1},{5,7},{7,5},{8,10},{10,8},{12,... | collective-permute-start | bytes 1572872 | tf_op jit(solution)/shard_map/ppermute | solution.py:716
  618.8 1.9 collective-permute-start.17
  639.7 4.0 collective-permute-start.18
  646.1 25.8 %collective-permute-start.19 = (bf16[256,1024]{1,0:T(8,128)(2,1)}, bf16[256,1024]{1,0:T(8,128)(2,1)S(1)}, u32[]{:S(2)}, u32[]{:S(2)}) collective-permute-start(bf16[256,1024]{1,0:T(8,128)(2,1)} %add_convert_fusion), channel_id=1, source_target_pairs={{0,4},{2,6},{4,0},{6,2},{1,5},{3,7},{5,1},{7,3},{8,12},{10,14},{12... | collective-permute-start | bytes 1572872 | tf_op jit(solution)/shard_map/ppermute | solution.py:724
  688.5 139.1 %reduce-scatter.5.cloned.1.call-start = ((), (), s32[]{:S(2)}) async-start(), calls=%async_computation.15 | async-start | bytes 2654208 | tf_op jit(solution)/shard_map/reduce_scatter | solution.py:901
  709.5 239.2 %reduce-scatter.11.cloned.1.call-start = ((), (), s32[]{:S(2)}) async-start(), calls=%async_computation.18 | async-start | bytes 19464192 | tf_op jit(solution)/shard_map/reduce_scatter | solution.py:858
  734.5 336.8 %reduce-scatter.9.cloned.1.call-start = ((), (), s32[]{:S(2)}) async-start(), calls=%async_computation.17 | async-start | bytes 19464192 | tf_op jit(solution)/shard_map/reduce_scatter | solution.py:858
  761.3 68.9 %all-to-all-start.10 = ((bf16[4,32,896]{2,1,0:T(8,128)(2,1)}), bf16[4,32,896]{2,1,0:T(8,128)(2,1)S(1)}, u32[]{:S(2)}, u32[]{:S(2)}) async-start(bf16[4,32,896]{2,1,0:T(8,128)(2,1)} %bitcast.72), calls=%async_computation.12 | async-start | bytes 458752 | tf_op jit(solution)/shard_map/all_to_all | solution.py:903
  830.2 9.2 all-to-all-start.9
  (118 other events, 1636.2 us)
Sparse Core Ops, SparseCore 0:
  41.8 53.0 all-gather.4
  149.8 59.5 all-gather.6
  688.6 66.9 reduce-scatter.6
  759.5 68.0 reduce-scatter.4
  831.0 117.6 reduce-scatter.10
  952.6 118.5 reduce-scatter.8

commit v2 on v1

--- a/solution.py
+++ b/solution.py
@@ -27,6 +27,8 @@
 REACH = 512
 FF_TILE = 256
 FF_STEPS = FF // FF_TILE
+BACK_TILE = 1408
+BACK_STEPS = FF // BACK_TILE
 MIB = 1 << 20
 
 bf16 = jnp.bfloat16
@@ -55,14 +57,23 @@
     )
 
 
-def whole_call(body, out_shape, args, *, flops=0, limit=48, scratch=(), smem=0, name=None):
+def whole_call(
+    body, out_shape, args, *, flops=0, limit=16, scratch=(), smem=0, name=None, after=()
+):
     specs = [pl.BlockSpec(memory_space=pltpu.SMEM)] * smem + [
         pl.BlockSpec(memory_space=pltpu.VMEM)
     ] * (len(args) - smem)
     outs = tuple(out_shape)
     moved = sum(a.size * a.dtype.itemsize for a in list(args) + list(outs))
+    specs += [pl.BlockSpec(memory_space=pltpu.HBM)] * len(after)
+    used = len(args)
+    args = list(args) + [far_away(a) for a in after]
+
+    def ordered(*refs):
+        body(*refs[:used], *refs[used + len(after) :])
+
     return pl.pallas_call(
-        body,
+        ordered,
         out_shape=outs,
         in_specs=specs,
         out_specs=tuple(pl.BlockSpec(memory_space=pltpu.VMEM) for _ in outs),
@@ -75,6 +86,26 @@
     )(*args)
 
 
+def far_away(x):
+    return pltpu.with_memory_space_constraint(x, pltpu.HBM)
+
+
+def hold(x, after):
+    def body(*refs):
+        pass
+
+    return pl.pallas_call(
+        body,
+        out_shape=pltpu.HBM(x.shape, x.dtype),
+        in_specs=[pl.BlockSpec(memory_space=pltpu.HBM)] * (1 + len(after)),
+        out_specs=pl.BlockSpec(memory_space=pltpu.HBM),
+        input_output_aliases={0: 0},
+        compiler_params=pltpu.CompilerParams(vmem_limit_bytes=MIB),
+        cost_estimate=pl.CostEstimate(flops=0, bytes_accessed=0, transcendentals=0),
+        name="hold",
+    )(far_away(x), *[far_away(a) for a in after])
+
+
 def shape(dims, dtype):
     return jax.ShapeDtypeStruct(dims, dtype)
 
@@ -92,8 +123,99 @@
     return grad_inputs, grad_gain
 
 
-def near_bias(bias_ref, head, rows):
-    row = bias_ref[head : head + 1, :]
+def placed(count, offset):
+    index = lax.broadcasted_iota(jnp.int32, (count, LANES), 0)
+    lane = lax.broadcasted_iota(jnp.int32, (count, LANES), 1)
+    return one_hot(lane == index + offset)
+
+
+def prepare_body(direct, in_ref, out_ref, router_ref, gains_ref, table_ref, *packets):
+    share = in_ref.shape[1]
+    for layer in range(LAYERS):
+        for which in range(3):
+            for head in range(OWN):
+                for c in range(GROUP):
+                    source = which * D + (head * GROUP + c) * HEAD_DIM
+                    target = which * OWN_COLS + head * HEAD_DIM
+                    packets[layer][c, :, target : target + HEAD_DIM] = in_ref[
+                        layer, :, source : source + HEAD_DIM
+                    ]
+        if direct:
+            width = D // GROUP
+            for q in range(GROUP):
+                packets[LAYERS + layer][q] = out_ref[layer, :, q * width : (q + 1) * width]
+    small = jnp.zeros((share, LANES), f32)
+    row = lax.broadcasted_iota(jnp.int32, (share, LANES), 0)
+    for layer in range(LAYERS):
+        top = 32 * layer
+        small = small + dot(router_ref[layer], placed(router_ref.shape[2], top), 1, 0)
+        small = small + dot(gains_ref[layer], placed(2, top + 16), 1, 0)
+        bucket = dot(table_ref[layer : layer + 1, :], placed(table_ref.shape[1], top + 64), 1, 0)
+        small = small + jnp.where(row == 0, bucket, 0.0)
+    for c in range(GROUP):
+        packets[0][c, :, PACKED:] = small.astype(bf16)
+
+
+def prepare(direct, attn_in, attn_out, router, gains, rel_table):
+    share = attn_in.shape[1]
+    outs = [shape((GROUP, share, PACKED + LANES), bf16), shape((GROUP, share, PACKED), bf16)]
+    if direct:
+        outs += [shape((GROUP, share, D // GROUP), bf16)] * LAYERS
+
+    def body(*refs):
+        prepare_body(direct, *refs)
+
+    return whole_call(
+        body, outs, [attn_in, attn_out, router, gains, rel_table], name="prepare"
+    )
+
+
+def unpack_body(place_ref, got_ref, hits_ref, w_in_ref, w_out_ref, *rest):
+    experts, pairs, _, share, total = got_ref.shape
+    width = D // GROUP
+    for e in range(experts):
+        for d in range(pairs):
+            for c in range(GROUP):
+                row = ((e * GROUP + c) * pairs + d) * share
+                w_in_ref[row : row + share, :] = got_ref[e, d, c, :, :PACKED]
+                row = (e * pairs + d) * share
+                w_out_ref[c, row : row + share, :] = got_ref[e, d, c, :, total - width :]
+    if not rest:
+        return
+    feature_ref, bias_ref, flat_ref, bucket_ref = rest
+    for e in range(experts):
+        for d in range(pairs):
+            for c in range(GROUP):
+                index = (e * GROUP + c) * pairs + d
+                block = got_ref[e, d, c, :, PACKED : PACKED + LANES].astype(f32)
+                flat_ref[index * share : (index + 1) * share, :] = block
+                bucket_ref[index : index + 1, :] = block[:1, :]
+    feature_ref[...] = flat_ref[...].T
+    head = lax.broadcasted_iota(jnp.int32, (8, LANES), 0)
+    lane = lax.broadcasted_iota(jnp.int32, (8, LANES), 1)
+    for layer in range(LAYERS):
+        mine = jnp.where(
+            (lane == 64 + 32 * layer + head * GROUP + place_ref[0]) & (head < OWN), 1.0, 0.0
+        )
+        table = dot(mine, bucket_ref[...], 1, 1, lax.Precision.HIGHEST)
+        bias_ref[layer] = dot(
+            table - table[:, BUCKETS - 1 :], hits_ref[...], 1, 0, lax.Precision.HIGHEST
+        )
+
+
+def unpack(place, got, hits, first):
+    outs = [shape((D, PACKED), bf16), shape((GROUP, OWN_COLS, D // GROUP), bf16)]
+    scratch = []
+    if first:
+        outs += [shape((LANES, D), f32), shape((LAYERS, 8, REACH), f32)]
+        scratch = [pltpu.VMEM((D, LANES), f32), pltpu.VMEM((BUCKETS, LANES), f32)]
+    return whole_call(
+        unpack_body, outs, [place, got, hits], smem=1, scratch=scratch, name="unpack"
+    )
+
+
+def near_bias(bias_ref, layer, head, rows):
+    row = bias_ref[layer, head : head + 1, :]
     return pltpu.roll(jnp.broadcast_to(row, (rows, REACH)), 0, 1, stride=1, stride_axis=0)
 
 
@@ -110,13 +232,18 @@
 
 
 def attention_forward_body(
-    place_ref, n0, n1, n2, n3, w_ref, bias_ref, low_ref, wo_ref,
-    packed_ref, log_ref, mixed_ref, keep_ref, send_ref,
+    layer, place_ref, n0, n1, n2, n3, w_ref, feature_ref, bias_ref, low_ref, wo_ref,
+    packed_ref, log_ref, mixed_ref, keep_ref, send_ref, *normed_ref,
 ):
     me = place_ref[0]
     rows = n0.shape[0]
     for r, piece in enumerate((n0, n1, n2, n3)):
-        packed_ref[r * rows : (r + 1) * rows, :] = dot(piece[...], w_ref[...], 1, 0).astype(bf16)
+        normed = piece[...]
+        if layer == 0:
+            wide = normed.astype(f32)
+            normed = (wide * rms_scale(wide) * feature_ref[16:17, :]).astype(bf16)
+            normed_ref[0][r * rows : (r + 1) * rows, :] = normed
+        packed_ref[r * rows : (r + 1) * rows, :] = dot(normed, w_ref[...], 1, 0).astype(bf16)
     lane = lax.broadcasted_iota(jnp.int32, (rows, LANES), 1)
     starts = [pl.multiple_of((b ^ me) * rows, rows) for b in range(GROUP)]
     for pair in range(OWN // 2):
@@ -127,7 +254,7 @@
             return packed_ref[pl.ds(starts[b], rows), column : column + LANES]
 
         sides = [(lane // HEAD_DIM) == side for side in range(2)]
-        nears = [near_bias(bias_ref, pair * 2 + side, rows) for side in range(2)]
+        nears = [near_bias(bias_ref, layer, pair * 2 + side, rows) for side in range(2)]
         for qb in range(GROUP):
             low = low_ref[:, qb * rows : (qb + 1) * rows]
             queries = part(qb, 0) * SCORE_SCALE
@@ -164,29 +291,40 @@
             ).astype(target.dtype)
 
 
-def attention_forward(place, pieces, w_in, bias_rows, low, w_out):
+def attention_forward(layer, place, pieces, w_in, feature, bias, low, w_out):
     rows = pieces[0].shape[0]
     total = GROUP * rows
+    outs = [
+        shape((total, PACKED), bf16),
+        shape((8, total), f32),
+        shape((total, OWN_COLS), bf16),
+        shape((2 * rows, D), f32),
+        shape((2 * rows, D), bf16),
+    ]
+    if layer == 0:
+        outs.append(shape((total, D), bf16))
+
+    def body(*refs):
+        attention_forward_body(layer, *refs)
+
     return whole_call(
-        attention_forward_body,
-        (
-            shape((total, PACKED), bf16),
-            shape((8, total), f32),
-            shape((total, OWN_COLS), bf16),
-            shape((2 * rows, D), f32),
-            shape((2 * rows, D), bf16),
-        ),
-        [place, *pieces, w_in, bias_rows, low, w_out],
+        body,
+        outs,
+        [place, *pieces, w_in, feature, bias, low, w_out],
         smem=1,
         flops=2 * total * D * (PACKED + OWN_COLS) + 2 * total * total * OWN_COLS * 2,
+        limit=24,
         name="attention_forward",
     )
 
 
 def attention_backward_body(
-    place_ref, d0, d1, d2, d3, w_ref, bias_ref, low_ref, wo_ref, packed_ref, log_ref,
-    grad_packed_ref, keep_ref, send_ref, table_ref, grad_mixed_ref, dk_ref, dv_ref,
+    layer, place_ref, d0, d1, d2, d3, w_ref, feature_ref, bias_ref, low_ref, wo_ref, packed_ref,
+    log_ref, *refs,
 ):
+    normed_refs = refs[:-8]
+    (grad_packed_ref, keep_ref, send_ref, table_ref, gain_ref, grad_mixed_ref, dk_ref,
+     dv_ref) = refs[-8:]
     me = place_ref[0]
     rows = d0.shape[0]
     width = wo_ref.shape[2]
@@ -206,7 +344,7 @@
             return packed_ref[pl.ds(starts[b], rows), column : column + LANES]
 
         sides = [(lane // HEAD_DIM) == side for side in range(2)]
-        nears = [near_bias(bias_ref, pair * 2 + side, rows) for side in range(2)]
+        nears = [near_bias(bias_ref, layer, pair * 2 + side, rows) for side in range(2)]
         diag = [jnp.zeros((rows, rows), f32) for _ in range(2)]
         before = [jnp.zeros((rows, rows), f32) for _ in range(2)]
         far = [jnp.zeros((1, rows), f32) for _ in range(2)]
@@ -274,56 +412,181 @@
     for r, (target, offset) in enumerate(
         ((keep_ref, 0), (send_ref, 0), (keep_ref, rows), (send_ref, rows))
     ):
-        target[offset : offset + rows, :] = dot(
-            grad_packed_ref[r * rows : (r + 1) * rows, :], w_ref[...], 1, 1
-        ).astype(target.dtype)
-
-
-def attention_backward(place, pieces, w_in, bias_rows, low, w_out, packed, log_total):
+        grad_normed = dot(grad_packed_ref[r * rows : (r + 1) * rows, :], w_ref[...], 1, 1)
+        target[offset : offset + rows, :] = grad_normed.astype(target.dtype)
+        part_gain = jnp.sum(grad_normed * block_of(normed_refs, r, rows).astype(f32), 0, keepdims=True)
+        gain_sum = part_gain if r == 0 else gain_sum + part_gain
+    gain_row = feature_ref[32 * layer + 16 : 32 * layer + 17, :]
+    gain_ref[...] = jnp.broadcast_to(gain_sum / gain_row, gain_ref.shape)
+
+
+def block_of(refs, r, rows):
+    return refs[r][...] if len(refs) > 1 else refs[0][r * rows : (r + 1) * rows, :]
+
+
+def attention_backward(
+    layer, place, pieces, w_in, feature, bias, low, w_out, packed, log_total, normed, after=()
+):
     rows = pieces[0].shape[0]
     total = GROUP * rows
+
+    def body(*refs):
+        attention_backward_body(layer, *refs)
+
     return whole_call(
-        attention_backward_body,
+        body,
         (
             shape((total, PACKED), bf16),
             shape((2 * rows, D), f32),
             shape((2 * rows, D), bf16),
             shape((8, REACH), f32),
+            shape((8, D), f32),
         ),
-        [place, *pieces, w_in, bias_rows, low, w_out, packed, log_total],
+        [place, *pieces, w_in, feature, bias, low, w_out, packed, log_total, *normed],
         smem=1,
+        after=after,
         scratch=[
             pltpu.VMEM((total, OWN_COLS), bf16),
             pltpu.VMEM((total, LANES), f32),
             pltpu.VMEM((total, LANES), f32),
         ],
         flops=2 * total * D * (PACKED + OWN_COLS) + 2 * total * total * OWN_COLS * 5,
+        limit=24,
         name="attention_backward",
     )
 
 
-def dense_grad_body(n0, n1, n2, n3, d0, d1, d2, d3, grad_packed_ref, mixed_ref, out_in, out_out):
-    rows = n0.shape[0]
+def dense_products(normed, upstream, grad_packed_ref, mixed_ref):
+    rows = upstream[0].shape[0]
     total_in = None
     total_out = None
-    for r, (normed, upstream) in enumerate(zip((n0, n1, n2, n3), (d0, d1, d2, d3))):
+    for r in range(GROUP):
         span = slice(r * rows, (r + 1) * rows)
-        one = dot(normed[...], grad_packed_ref[span, :], 0, 0)
-        two = dot(mixed_ref[span, :], upstream[...], 0, 0)
+        one = dot(block_of(normed, r, rows), grad_packed_ref[span, :], 0, 0)
+        two = dot(mixed_ref[span, :], upstream[r][...], 0, 0)
         total_in = one if total_in is None else total_in + one
         total_out = two if total_out is None else total_out + two
-    out_in[...] = total_in.astype(out_in.dtype)
-    out_out[...] = total_out.astype(out_out.dtype)
+    return total_in, total_out
 
 
 def dense_grads(normed, upstream, grad_packed, mixed):
-    rows = normed[0].shape[0]
+    rows = upstream[0].shape[0]
+    count = len(normed)
+
+    def body(*refs):
+        total_in, total_out = dense_products(
+            refs[:count], refs[count : count + GROUP], refs[-4], refs[-3]
+        )
+        refs[-2][...] = total_in.astype(bf16)
+        refs[-1][...] = total_out.astype(bf16)
+
     return whole_call(
-        dense_grad_body,
+        body,
         (shape((D, PACKED), bf16), shape((OWN_COLS, D), bf16)),
         [*normed, *upstream, grad_packed, mixed],
         flops=2 * GROUP * rows * D * (PACKED + OWN_COLS),
         name="dense_grads",
+    )
+
+
+def dense_pack(experts, pairs, share, place, normed, upstream, grad_packed, mixed, small, gain_a,
+               by_distance, hits, after=()):
+    rows = upstream[0].shape[0]
+    count = len(normed)
+    width = D // GROUP
+    total = PACKED + LANES + width
+
+    def body(place_ref, *refs):
+        grad_packed_ref, mixed_ref, small_ref, gain_ref, distance_ref, hits_ref = refs[
+            count + GROUP : count + GROUP + 6
+        ]
+        keep_ref, send_ref, in_ref, out_ref, flat_ref = refs[count + GROUP + 6 :]
+        total_in, total_out = dense_products(
+            refs[:count], refs[count : count + GROUP], grad_packed_ref, mixed_ref
+        )
+        in_ref[...] = total_in
+        out_ref[...] = total_out
+        row = lax.broadcasted_iota(jnp.int32, (8, D), 0)
+        gains = jnp.where(
+            row == 0, gain_ref[...], jnp.where(row == 1, small_ref[16:24, :], 0.0)
+        )
+        features = jnp.concatenate(
+            [small_ref[:16, :], gains, jnp.zeros((LANES - 24, D), f32)], 0
+        )
+        flat_ref[...] = features.T
+        by_bucket = dot(hits_ref[...], distance_ref[...], 1, 1, lax.Precision.HIGHEST)
+        head = lax.broadcasted_iota(jnp.int32, (8, LANES), 0)
+        lane = lax.broadcasted_iota(jnp.int32, (8, LANES), 1)
+        mine = jnp.where((lane == 64 + head * GROUP + place_ref[0]) & (head < OWN), 1.0, 0.0)
+        buckets = dot(by_bucket, mine, 1, 0, lax.Precision.HIGHEST)
+        for index in range(BUCKETS):
+            at = index * share
+            flat_ref[at : at + 1, :] = flat_ref[at : at + 1, :] + buckets[index : index + 1, :]
+        for target, d in ((keep_ref, place_ref[1]), (send_ref, 1 - place_ref[1])):
+            for e in range(experts):
+                for c in range(GROUP):
+                    span = pl.ds(pl.multiple_of(((e * GROUP + c) * pairs + d) * share, share), share)
+                    to = slice(c * share, (c + 1) * share)
+                    target[e, to, :PACKED] = in_ref[span, :].astype(target.dtype)
+                    target[e, to, PACKED : PACKED + LANES] = flat_ref[span, :].astype(target.dtype)
+                    span = pl.ds(pl.multiple_of((e * pairs + d) * share, share), share)
+                    target[e, to, PACKED + LANES :] = out_ref[
+                        span, c * width : (c + 1) * width
+                    ].astype(target.dtype)
+
+    return whole_call(
+        body,
+        (
+            shape((experts, GROUP * share, total), f32),
+            shape((experts, GROUP * share, total), bf16),
+        ),
+        [place, *normed, *upstream, grad_packed, mixed, small, gain_a, by_distance, hits],
+        smem=1,
+        scratch=[
+            pltpu.VMEM((D, PACKED), f32),
+            pltpu.VMEM((OWN_COLS, D), f32),
+            pltpu.VMEM((D, LANES), f32),
+        ],
+        flops=2 * GROUP * rows * D * (PACKED + OWN_COLS),
+        after=after,
+        name="dense_pack",
+    )
+
+
+def finish_dense(experts, share, inner, outer):
+    width = D // GROUP
+
+    def body(*refs):
+        in_ref, out_ref, small_ref = refs[2 * LAYERS :]
+        for layer in range(LAYERS):
+            got, zone = refs[layer], refs[LAYERS + layer]
+            for c in range(GROUP):
+                for which in range(3):
+                    for head in range(OWN):
+                        source = which * OWN_COLS + head * HEAD_DIM
+                        target = which * D + (head * GROUP + c) * HEAD_DIM
+                        in_ref[layer, :, target : target + HEAD_DIM] = got[
+                            c, :, source : source + HEAD_DIM
+                        ].astype(f32)
+                rows = slice(c * share, (c + 1) * share)
+                part = zone[0, rows, PACKED + LANES :].astype(f32)
+                for e in range(1, experts):
+                    part = part + zone[e, rows, PACKED + LANES :].astype(f32)
+                out_ref[layer, :, c * width : (c + 1) * width] = part
+            total = got[0, :, PACKED:].astype(f32)
+            for c in range(1, GROUP):
+                total = total + got[c, :, PACKED:].astype(f32)
+            small_ref[layer] = total
+
+    return whole_call(
+        body,
+        (
+            shape((LAYERS, share, 3 * D), f32),
+            shape((LAYERS, share, D), f32),
+            shape((LAYERS, share, LANES), f32),
+        ),
+        [*inner, *outer],
+        name="finish_dense",
     )
 
 
@@ -355,12 +618,13 @@
     ).astype(bf16)
 
 
-def route_body(experts, capacity, last, *refs):
+def route_body(layer, experts, capacity, last, *refs):
+    top = 32 * layer
     if last:
-        (x_ref, keep_ref, recv_ref, far_ref, gain_ref, router_ref, ids_ref, idst_ref, grad_ref,
+        (x_ref, keep_ref, recv_ref, far_ref, feature_ref, ids_ref, idst_ref, grad_ref,
          middle_ref, rows_ref, soft_ref, meta_ref, dest_ref, sent_ref) = refs
     else:
-        (x_ref, keep_ref, recv_ref, far_ref, gain_ref, router_ref, ids_ref, idst_ref,
+        (x_ref, keep_ref, recv_ref, far_ref, feature_ref, ids_ref, idst_ref,
          middle_ref, rows_ref, soft_ref, meta_ref, dest_ref) = refs
     tokens = x_ref.shape[0]
     slots = experts * capacity
@@ -371,16 +635,16 @@
         + far_ref[...].astype(f32)
     )
     middle_ref[...] = middle
-    normed = middle * rms_scale(middle) * gain_ref[...]
+    normed = middle * rms_scale(middle) * feature_ref[top + 17 : top + 18, :]
     lane = lax.broadcasted_iota(jnp.int32, (tokens, LANES), 1)
-    logits = dot(normed, router_ref[...], 1, 1, lax.Precision.HIGHEST)
-    logits = jnp.where(lane < experts, logits, NEGATIVE)
+    logits = dot(normed, feature_ref[...], 1, 1, lax.Precision.HIGHEST)
+    logits = jnp.where((lane >= top) & (lane < top + experts), logits, NEGATIVE)
     power = jnp.exp(logits - jnp.max(logits, -1, keepdims=True))
     soft = power / jnp.sum(power, -1, keepdims=True)
     soft_ref[...] = soft
     ids = ids_ref[...]
-    hit0 = lane == ids[:, 0:1]
-    hit1 = lane == ids[:, 1:2]
+    hit0 = lane == ids[:, 0:1] + top
+    hit1 = lane == ids[:, 1:2] + top
     picked0 = jnp.sum(jnp.where(hit0, soft, 0.0), -1, keepdims=True)
     picked1 = jnp.sum(jnp.where(hit1, soft, 0.0), -1, keepdims=True)
     pick_total = picked0 + picked1
@@ -419,7 +683,7 @@
         sent_ref[...] = scatter_grads(grad_ref[...].astype(f32), meta, dest_rows, slots)
 
 
-def route(experts, capacity, x, keep, recv, far, gain, router, ids, idst, grad=None):
+def route(layer, experts, capacity, x, keep, recv, far, feature, ids, idst, grad=None):
     tokens = x.shape[0]
     slots = experts * capacity
     outs = [
@@ -429,13 +693,13 @@
         shape((tokens, LANES), f32),
         shape((8, tokens), jnp.int32),
     ]
-    args = [x, keep, recv, far, gain, router, ids, idst]
+    args = [x, keep, recv, far, feature, ids, idst]
     if grad is not None:
         outs.append(shape((slots, D), bf16))
         args.append(grad)
 
     def body(*refs):
-        route_body(experts, capacity, grad is not None, *refs)
+        route_body(layer, experts, capacity, grad is not None, *refs)
 
     return whole_call(body, outs, args, flops=2 * slots * tokens * D, name="route")
 
@@ -454,7 +718,7 @@
     )
     out_ref[...] = x.astype(out_ref.dtype)
     if not last:
-        normed_ref[...] = (x * rms_scale(x) * gain_ref[...]).astype(bf16)
+        normed_ref[...] = (x * rms_scale(x) * gain_ref[48:49, :]).astype(bf16)
 
 
 def combine(middle, back, meta, gain=None):
@@ -474,9 +738,11 @@
 
 
 def expert_token_back_body(
-    experts, back_ref, came_ref, g_ref, middle_ref, soft_ref, meta_ref, ids_ref, gain_ref,
-    router_ref, dmiddle_ref, dattn_ref, small_ref,
+    layer, back_ref, came_ref, g_ref, middle_ref, soft_ref, meta_ref, ids_ref, feature_ref,
+    dmiddle_ref, dattn_ref, small_ref,
 ):
+    top = 32 * layer
+    gain_row = feature_ref[top + 17 : top + 18, :]
     meta = meta_ref[...]
     g = g_ref[...].astype(f32)
     slots = back_ref.shape[0]
@@ -487,68 +753,69 @@
     gap = (grad_gate0 - grad_gate1) / meta[:, 4:5]
     ids = ids_ref[...]
     lane = lax.broadcasted_iota(jnp.int32, meta.shape, 1)
-    grad_soft = jnp.where(lane == ids[:, 0:1], meta[:, 3:4] * gap, 0.0) + jnp.where(
-        lane == ids[:, 1:2], -meta[:, 2:3] * gap, 0.0
+    grad_soft = jnp.where(lane == ids[:, 0:1] + top, meta[:, 3:4] * gap, 0.0) + jnp.where(
+        lane == ids[:, 1:2] + top, -meta[:, 2:3] * gap, 0.0
     )
     soft = soft_ref[...]
     grad_logits = soft * (grad_soft - jnp.sum(soft * grad_soft, -1, keepdims=True))
     middle = middle_ref[...]
-    normed = middle * rms_scale(middle) * gain_ref[...]
+    normed = middle * rms_scale(middle) * gain_row
     grad_router = dot(grad_logits.T, normed, 1, 0, lax.Precision.HIGHEST)
     grad_normed = grad_normed + dot(
-        grad_logits, router_ref[...], 1, 0, lax.Precision.HIGHEST
-    )
-    grad_branch, grad_gain = norm_back(middle, gain_ref[...], grad_normed)
+        grad_logits, feature_ref[...], 1, 0, lax.Precision.HIGHEST
+    )
+    grad_branch, grad_gain = norm_back(middle, gain_row, grad_normed)
     dmiddle = g + grad_branch
     dmiddle_ref[...] = dmiddle
     dattn_ref[...] = dmiddle.astype(bf16)
-    small_ref[:16, :] = grad_router[:16, :]
+    small_ref[:16, :] = grad_router[top : top + 16, :]
     small_ref[16:24, :] = jnp.broadcast_to(grad_gain, (8, D))
 
 
-def expert_token_back(experts, back, came, g, middle, soft, meta, ids, gain, router):
+def expert_token_back(layer, back, came, g, middle, soft, meta, ids, feature, after=()):
     tokens = middle.shape[0]
 
     def body(*refs):
-        expert_token_back_body(experts, *refs)
+        expert_token_back_body(layer, *refs)
 
     return whole_call(
         body,
         (shape((tokens, D), f32), shape((tokens, D), bf16), shape((24, D), f32)),
-        [back, came, g, middle, soft, meta, ids, gain, router],
+        [back, came, g, middle, soft, meta, ids, feature],
+        after=after,
         flops=6 * tokens * D * back.shape[0],
         name="expert_token_back",
     )
 
 
-def attention_token_back_body(first_layer, *refs):
-    if first_layer:
-        x_ref, dmiddle_ref, keep_ref, recv_ref, far_ref, gain_ref, out_ref, small_ref = refs
+def attention_token_back_body(layer, *refs):
+    if layer == 0:
+        x_ref, dmiddle_ref, keep_ref, recv_ref, far_ref, feature_ref, out_ref = refs
     else:
-        (x_ref, dmiddle_ref, keep_ref, recv_ref, far_ref, gain_ref, meta_ref, dest_ref,
-         out_ref, small_ref, sent_ref) = refs
+        (x_ref, dmiddle_ref, keep_ref, recv_ref, far_ref, feature_ref, meta_ref, dest_ref,
+         out_ref, sent_ref) = refs
     tokens = x_ref.shape[0]
     grad_normed = (
         keep_ref[:tokens, :] + recv_ref[:tokens, :].astype(f32) + far_ref[...].astype(f32)
     )
-    grad_branch, grad_gain = norm_back(x_ref[...].astype(f32), gain_ref[...], grad_normed)
+    gain_row = feature_ref[32 * layer + 16 : 32 * layer + 17, :]
+    grad_branch, _ = norm_back(x_ref[...].astype(f32), gain_row, grad_normed)
     g = dmiddle_ref[...] + grad_branch
     out_ref[...] = g
-    small_ref[...] = jnp.broadcast_to(grad_gain, (8, D))
-    if not first_layer:
+    if layer > 0:
         sent_ref[...] = scatter_grads(g, meta_ref[...], dest_ref[...], sent_ref.shape[0])
 
 
-def attention_token_back(x, dmiddle, keep, recv, far, gain, meta=None, dest=None, slots=0):
+def attention_token_back(layer, x, dmiddle, keep, recv, far, feature, meta=None, dest=None, slots=0):
     tokens = x.shape[0]
-    outs = [shape((tokens, D), f32), shape((8, D), f32)]
-    args = [x, dmiddle, keep, recv, far, gain]
+    outs = [shape((tokens, D), f32)]
+    args = [x, dmiddle, keep, recv, far, feature]
     if meta is not None:
         outs.append(shape((slots, D), bf16))
         args += [meta, dest]
 
     def body(*refs):
-        attention_token_back_body(meta is None, *refs)
+        attention_token_back_body(layer, *refs)
 
     return whole_call(
         body, outs, args, flops=4 * tokens * D * slots, name="attention_token_back"
@@ -583,11 +850,11 @@
         produced_ref[...] = total_ref[...].astype(bf16)
 
 
-def weight_specs(layer):
+def weight_specs(layer, tile):
     return [
-        pl.BlockSpec((1, 1, D, FF_TILE), lambda s: (layer, 0, 0, s)),
-        pl.BlockSpec((1, 1, D, FF_TILE), lambda s: (layer, 0, 0, FF_STEPS + s)),
-        pl.BlockSpec((1, 1, D, FF_TILE), lambda s: (layer, 0, 0, s)),
+        pl.BlockSpec((1, 1, D, tile), lambda s: (layer, 0, 0, s)),
+        pl.BlockSpec((1, 1, D, tile), lambda s: (layer, 0, 0, FF // tile + s)),
+        pl.BlockSpec((1, 1, D, tile), lambda s: (layer, 0, 0, s)),
     ]
 
 
@@ -596,19 +863,19 @@
     return pl.pallas_call(
         expert_forward_body,
         grid=(FF_STEPS,),
-        out_shape=(shape((count, D), bf16), shape((2, count, FF), bf16)),
-        in_specs=[pl.BlockSpec((count, D), lambda s: (0, 0))] + weight_specs(layer),
+        out_shape=(shape((count, D), bf16), pltpu.HBM((2, count, FF), bf16)),
+        in_specs=[pl.BlockSpec((count, D), lambda s: (0, 0))] + weight_specs(layer, FF_TILE),
         out_specs=(
             pl.BlockSpec((count, D), lambda s: (0, 0)),
             pl.BlockSpec((2, count, FF_TILE), lambda s: (0, 0, s)),
         ),
         scratch_shapes=[pltpu.VMEM((count, D), f32)],
-        compiler_params=pltpu.CompilerParams(vmem_limit_bytes=40 * MIB),
+        compiler_params=pltpu.CompilerParams(vmem_limit_bytes=28 * MIB),
         cost_estimate=pl.CostEstimate(
             flops=6 * count * D * FF, bytes_accessed=6 * D * FF, transcendentals=count * FF
         ),
         name="expert_forward",
-    )(rows, w_in, w_in, w_out)
+    )(rows, far_away(w_in), far_away(w_in), far_away(w_out))
 
 
 def expert_backward_body(
@@ -638,33 +905,45 @@
     def _():
         total_ref[...] += out
 
-    @pl.when(step == FF_STEPS - 1)
+    @pl.when(step == BACK_STEPS - 1)
     def _():
         drows_ref[...] = total_ref[...].astype(bf16)
 
 
-def expert_backward(layer, grad, acts, w_in, w_out):
+def expert_backward(layer, grad, acts, w_in, w_out, after=()):
     count = grad.shape[0]
+
+    def body(*refs):
+        expert_backward_body(*refs[:5], *refs[5 + len(after) :])
+
     return pl.pallas_call(
-        expert_backward_body,
-        grid=(FF_STEPS,),
-        out_shape=(shape((count, D), bf16), shape((3, count, FF), bf16)),
+        body,
+        grid=(BACK_STEPS,),
+        out_shape=(shape((count, D), bf16), pltpu.HBM((3, count, FF), bf16)),
         in_specs=[
             pl.BlockSpec((count, D), lambda s: (0, 0)),
-            pl.BlockSpec((2, count, FF_TILE), lambda s: (0, 0, s)),
+            pl.BlockSpec((2, count, BACK_TILE), lambda s: (0, 0, s)),
         ]
-        + weight_specs(layer),
+        + weight_specs(layer, BACK_TILE)
+        + [pl.BlockSpec(memory_space=pltpu.HBM)] * len(after),
         out_specs=(
             pl.BlockSpec((count, D), lambda s: (0, 0)),
-            pl.BlockSpec((3, count, FF_TILE), lambda s: (0, 0, s)),
+            pl.BlockSpec((3, count, BACK_TILE), lambda s: (0, 0, s)),
         ),
         scratch_shapes=[pltpu.VMEM((count, D), f32)],
-        compiler_params=pltpu.CompilerParams(vmem_limit_bytes=48 * MIB),
+        compiler_params=pltpu.CompilerParams(vmem_limit_bytes=56 * MIB),
         cost_estimate=pl.CostEstimate(
             flops=6 * count * D * FF, bytes_accessed=6 * D * FF, transcendentals=count * FF
         ),
         name="expert_backward",
-    )(grad, acts, w_in, w_in, w_out)
+    )(
+        grad,
+        far_away(acts),
+        far_away(w_in),
+        far_away(w_in),
+        far_away(w_out),
+        *[far_away(a) for a in after],
+    )
 
 
 def expert_grads_body(shares, rows_ref, grad_ref, parts_ref, out_ref, rows_t, grad_t):
@@ -681,30 +960,63 @@
             out_ref[share, which] = got[share * tall : (share + 1) * tall, :]
 
 
-def expert_grads(shares, rows, grad, parts):
+def expert_grads(shares, rows, grad, parts, after=()):
     count = rows.shape[0]
     tall = D // shares
 
     def body(*refs):
-        expert_grads_body(shares, *refs)
+        expert_grads_body(shares, *refs[:3], *refs[3 + len(after) :])
 
     return pl.pallas_call(
         body,
         grid=(FF_STEPS,),
-        out_shape=shape((shares, 3, tall, FF), bf16),
+        out_shape=pltpu.HBM((shares, 3, tall, FF), bf16),
         in_specs=[
             pl.BlockSpec((count, D), lambda s: (0, 0)),
             pl.BlockSpec((count, D), lambda s: (0, 0)),
             pl.BlockSpec((3, count, FF_TILE), lambda s: (0, 0, s)),
-        ],
+        ]
+        + [pl.BlockSpec(memory_space=pltpu.HBM)] * len(after),
         out_specs=pl.BlockSpec((shares, 3, tall, FF_TILE), lambda s: (0, 0, 0, s)),
         scratch_shapes=[pltpu.VMEM((D, count), bf16), pltpu.VMEM((D, count), bf16)],
-        compiler_params=pltpu.CompilerParams(vmem_limit_bytes=40 * MIB),
+        compiler_params=pltpu.CompilerParams(vmem_limit_bytes=28 * MIB),
         cost_estimate=pl.CostEstimate(
             flops=6 * count * D * FF, bytes_accessed=6 * D * FF, transcendentals=0
         ),
         name="expert_grads",
-    )(rows, grad, parts)
+    )(rows, grad, far_away(parts), *[far_away(a) for a in after])
+
+
+def place_expert_grads(layer, summed, before=None, after=()):
+    tall = summed.shape[1]
+    outs = (
+        pltpu.HBM((LAYERS, 1, tall, 2 * FF), f32),
+        pltpu.HBM((LAYERS, 1, tall, FF), f32),
+    )
+    held = [] if before is None else list(before)
+
+    def body(part_ref, out_part_ref, *refs):
+        in_ref, out_ref = refs[-2:]
+        in_ref[0, 0] = part_ref[0].astype(f32)
+        out_ref[0, 0] = out_part_ref[0].astype(f32)
+
+    return pl.pallas_call(
+        body,
+        grid=(2,),
+        out_shape=outs,
+        in_specs=[
+            pl.BlockSpec((1, tall, FF), lambda s: (s, 0, 0)),
+            pl.BlockSpec((1, tall, FF), lambda s: (2, 0, 0)),
+        ]
+        + [pl.BlockSpec(memory_space=pl.ANY)] * (len(held) + len(after)),
+        out_specs=(
+            pl.BlockSpec((1, 1, tall, FF), lambda s: (layer, 0, 0, s)),
+            pl.BlockSpec((1, 1, tall, FF), lambda s: (layer, 0, 0, 0)),
+        ),
+        input_output_aliases={2: 0, 3: 1} if held else {},
+        compiler_params=pltpu.CompilerParams(vmem_limit_bytes=32 * MIB),
+        name="place_expert_grads",
+    )(far_away(summed), far_away(summed), *[far_away(h) for h in [*held, *after]])
 
 
 TWIN = [(i, i ^ 1) for i in range(GROUP)]
@@ -722,6 +1034,41 @@
     recv = lax.ppermute(send, "context", TWIN)
     other = (keep[rows:] + recv[rows:].astype(f32)).astype(bf16)
     return keep, recv, lax.ppermute(other, "context", ACROSS)
+
+
+def sum_zone(zone):
+    return jnp.sum(zone.astype(f32), 0)
+
+
+def dense_sum(
+    experts, pairs, share, table_share, place, grad_w_in, grad_w_out, small, gain_a, by_distance,
+    hits,
+):
+    by_bucket = jnp.dot(hits, by_distance[:OWN].T, precision=lax.Precision.HIGHEST)
+    buckets = jnp.where(
+        jnp.arange(GROUP)[None, None, :] == place[0], by_bucket[:, :, None], 0.0
+    ).reshape(experts, GROUP, pairs, 1, table_share)
+    features = jnp.concatenate([small[:16], gain_a[:1], small[16:17]], 0).T
+    features = features.reshape(experts, GROUP, pairs, share, 18)
+    flat = jnp.zeros((experts, GROUP, pairs, share, LANES), f32)
+    flat = flat.at[..., :18].set(features).at[..., :1, 64 : 64 + table_share].set(buckets)
+    pack = jnp.concatenate(
+        [grad_w_in.reshape(experts, GROUP, pairs, share, PACKED), flat.astype(bf16)], -1
+    ).transpose(0, 2, 1, 3, 4)
+    pack = pack.reshape(experts * pairs, GROUP * share, PACKED + LANES)
+    mine = lax.psum_scatter(pack, ("experts", "dp"), scatter_dimension=0, tiled=False)
+    inner = lax.all_to_all(
+        mine.reshape(GROUP, share, PACKED + LANES), "context", split_axis=0, concat_axis=0
+    ).astype(f32)
+    g_in = inner[..., :PACKED].reshape(GROUP, share, 3, OWN, HEAD_DIM)
+    g_in = g_in.transpose(1, 2, 3, 0, 4).reshape(share, 3 * D)
+    placed_rows = jnp.where(
+        jnp.arange(GROUP)[None, :, None, None] == place[0],
+        grad_w_out.reshape(OWN, 1, HEAD_DIM, D),
+        jnp.zeros((), bf16),
+    ).reshape(D, D)
+    g_out = lax.psum_scatter(placed_rows, ALL, scatter_dimension=0, tiled=True).astype(f32)
+    return g_in, g_out, jnp.sum(inner[..., PACKED:], 0)
 
 
 def exchange(rows):
@@ -736,8 +1083,8 @@
     pairs = lax.axis_size("dp")
     share = attn_in.shape[1]
     table_share = rel_table.shape[1]
-    direct = share * pairs == HEAD_DIM and experts * GROUP == HEADS
-    place = lax.axis_index("context").astype(jnp.int32).reshape(1)
+    direct = share * pairs == HEAD_DIM and experts * GROUP == HEADS and pairs == 2
+    place = jnp.stack([lax.axis_index("context"), lax.axis_index("dp")]).astype(jnp.int32)
     start_tokens = tokens[0]
     ids = expert_ids[0]
     idst = ids.T
@@ -745,89 +1092,63 @@
     capacity = (10 * rows + 4 * experts - 1) // (4 * experts)
     slots = experts * capacity
     grad_in = out_grad[0]
-    places = jnp.arange(GROUP * rows, dtype=jnp.int32)
-    starts = doc_starts[0]
-    low = jnp.max(
-        jnp.where(starts[:, None] <= places[None, :], starts[:, None], 0), 0, keepdims=True
-    )
-
-    small = jnp.zeros((share, LANES), bf16)
-    for layer in range(LAYERS):
-        small = small.at[:, 32 * layer : 32 * layer + experts].set(router[layer])
-        small = small.at[:, 32 * layer + 16 : 32 * layer + 18].set(gains[layer])
-        small = small.at[0, 64 + 32 * layer : 64 + 32 * layer + table_share].set(rel_table[layer])
-    split_in = attn_in.reshape(LAYERS, share, 3, OWN, GROUP, HEAD_DIM).transpose(4, 0, 1, 2, 3, 5)
-    split_in = split_in.reshape(GROUP, LAYERS, share, PACKED)
-    packet = jnp.concatenate(
-        [split_in[:, 0], split_in[:, 1], jnp.broadcast_to(small, (GROUP, share, LANES))], -1
-    )
-    packet = lax.all_to_all(packet, "context", split_axis=0, concat_axis=0)
-    packet = packet.reshape(GROUP * share, 2 * PACKED + LANES)
-
-    def out_rows(layer):
-        width = D // GROUP
-        return jnp.concatenate(
-            [attn_out[layer][:, q * width : (q + 1) * width] for q in range(GROUP)], 0
-        )
+    hits = jnp.asarray(bucket_hits())
+
+    packets = prepare(direct, attn_in, attn_out, router, gains, rel_table)
+
+    def spread(packet):
+        return lax.all_to_all(packet, "context", split_axis=0, concat_axis=0)
 
     def gather(part):
-        got = lax.all_gather(part, ("experts", "dp"), axis=0, tiled=False)
-        return got.reshape(experts, pairs, GROUP, share, part.shape[-1])
-
-    w_in, w_out = [], []
-    small_all = None
-    for layer in range(LAYERS):
-        columns = [packet[:, layer * PACKED : (layer + 1) * PACKED]]
-        if layer == 0:
-            columns.append(packet[:, 2 * PACKED :])
-        if direct:
-            columns.append(out_rows(layer))
-        got = gather(jnp.concatenate(columns, 1))
-        w_in.append(got[..., :PACKED].transpose(0, 2, 1, 3, 4).reshape(D, PACKED))
-        if layer == 0:
-            small_all = got[..., PACKED : PACKED + LANES].transpose(0, 2, 1, 3, 4)
-        if direct:
-            w_out.append(
-                got[..., -D // GROUP :].transpose(2, 0, 1, 3, 4).reshape(GROUP, OWN_COLS, D // GROUP)
-            )
-        else:
+        return lax.all_gather(part, ("experts", "dp"), axis=0, tiled=False).reshape(
+            experts, pairs, *part.shape
+        )
+
+    if direct:
+        first = gather(jnp.concatenate([spread(packets[0]), packets[2]], -1))
+        second = gather(jnp.concatenate([spread(packets[1]), packets[3]], -1))
+        w_in0, w_out0, feature, bias = unpack(place, first, hits, True)
+        w_in1, w_out1 = unpack(place, second, hits, False)
+        w_in, w_out = [w_in0, w_in1], [w_out0, w_out1]
+    else:
+        w_in, w_out = [], []
+        for layer in range(LAYERS):
+            got = gather(spread(packets[layer])).transpose(0, 2, 1, 3, 4)
+            w_in.append(got[..., :PACKED].reshape(D, PACKED))
+            if layer == 0:
+                small_all = got[..., PACKED:]
             full = lax.all_gather(attn_out[layer], ALL, axis=0, tiled=True)
             mine = lax.dynamic_index_in_dim(
                 full.reshape(OWN, GROUP, HEAD_DIM, D), place[0], 1, keepdims=False
             )
             w_out.append(mine.reshape(OWN_COLS, GROUP, D // GROUP).transpose(1, 0, 2))
-    by_feature = small_all.reshape(D, LANES).T
-    hits = jnp.asarray(bucket_hits())
-    gain_a, gain_b, routers, bias_rows = [], [], [], []
-    for layer in range(LAYERS):
-        top = 32 * layer
-        gain_a.append(by_feature[top + 16 : top + 17].astype(f32))
-        gain_b.append(by_feature[top + 17 : top + 18].astype(f32))
-        routers.append(
-            jnp.pad(by_feature[top : top + experts].astype(f32), ((0, LANES - experts), (0, 0)))
-        )
-        table = small_all[:, :, :, 0, 64 + top : 64 + top + table_share].reshape(
-            BUCKETS, OWN, GROUP
-        )
-        table = lax.dynamic_index_in_dim(table, place[0], 2, keepdims=False).astype(f32)
-        row = jnp.dot((table - table[-1:]).T, hits, precision=lax.Precision.HIGHEST)
-        bias_rows.append(jnp.pad(row, ((0, 8 - OWN), (0, 0))))
-
-    def first_norm(piece):
-        wide = piece.astype(f32)
-        return (wide * rms_scale(wide) * gain_a[0]).astype(bf16)
-
-    pieces = [first_norm(piece) for piece in share_pieces(start_tokens)]
+        feature = small_all.reshape(D, LANES).astype(f32).T
+        bias_rows = []
+        for layer in range(LAYERS):
+            at = 64 + 32 * layer
+            table = small_all[:, :, :, 0, at : at + table_share].reshape(BUCKETS, OWN, GROUP)
+            table = lax.dynamic_index_in_dim(table, place[0], 2, keepdims=False).astype(f32)
+            row = jnp.dot((table - table[-1:]).T, hits, precision=lax.Precision.HIGHEST)
+            bias_rows.append(jnp.pad(row, ((0, 8 - OWN), (0, 0))))
+        bias = jnp.stack(bias_rows)
+    places = jnp.arange(GROUP * rows, dtype=jnp.int32)
+    starts = doc_starts[0]
+    low = jnp.max(
+        jnp.where(starts[:, None] <= places[None, :], starts[:, None], 0), 0, keepdims=True
+    )
+
+    pieces = share_pieces(start_tokens)
     x = start_tokens
     kept = []
     for layer in range(LAYERS):
-        packed, log_total, mixed, keep, send = attention_forward(
-            place, pieces, w_in[layer], bias_rows[layer], low, w_out[layer]
-        )
+        packed, log_total, mixed, keep, send, *normed_all = attention_forward(
+            layer, place, pieces, w_in[layer], feature, bias, low, w_out[layer]
+        )
+        normed_rows = normed_all if layer == 0 else pieces
         keep, recv, far = sum_pieces(keep, send)
         last = layer == LAYERS - 1
         routed = route(
-            experts, capacity, x, keep, recv, far, gain_b[layer], routers[layer], ids, idst,
+            layer, experts, capacity, x, keep, recv, far, feature, ids, idst,
             grad_in if last else None,
         )
         middle, sent_rows, soft, meta, dest = routed[:5]
@@ -837,102 +1158,101 @@
         produced, acts = expert_forward(layer, arrived, expert_in, expert_out)
         back = exchange(produced)
         kept.append(
-            (x, pieces, packed, log_total, mixed, middle, soft, meta, dest, arrived, acts, back)
+            (x, normed_rows, packed, log_total, mixed, middle, soft, meta, dest, arrived, acts, back)
         )
         if last:
             (result,) = combine(middle, back, meta)
         else:
-            x, normed = combine(middle, back, meta, gain_a[layer + 1])
+            x, normed = combine(middle, back, meta, feature)
             pieces = share_pieces(normed)
 
     g = grad_in
-    dense_out, expert_out_grads = [], []
+    inner, outer, expert_totals = [], [], []
+    other = None
+    placed_grads = None
     for layer in range(LAYERS - 1, -1, -1):
-        x, pieces, packed, log_total, mixed, middle, soft, meta, dest, arrived, acts, back = kept[
-            layer
-        ]
+        (x, normed_rows, packed, log_total, mixed, middle, soft, meta, dest, arrived, acts,
+         back) = kept[layer]
         drows, parts = expert_backward(layer, arrived_grad, acts, expert_in, expert_out)
         came = exchange(drows)
-        weight_grads = expert_grads(GROUP * pairs, arrived, arrived_grad, parts)
-        expert_out_grads.insert(
-            0, lax.psum_scatter(weight_grads, ("context", "dp"), scatter_dimension=0, tiled=False)
+        early = [] if other is None else [other]
+        weight_grads = expert_grads(
+            GROUP * pairs, arrived, arrived_grad, parts, after=[back] + early
+        )
+        weight_grads = hold(weight_grads, [came])
+        total = lax.psum_scatter(
+            weight_grads, ("context", "dp"), scatter_dimension=0, tiled=False
         )
         dmiddle, dattn, small_b = expert_token_back(
-            experts, back, came, g, middle, soft, meta, ids, gain_b[layer], routers[layer]
-        )
+            layer, back, came, g, middle, soft, meta, ids, feature,
+            after=[weight_grads] + expert_totals,
+        )
+        early = []
+        if expert_totals:
+            early.append(place_expert_grads(layer + 1, expert_totals[0]))
+            placed_grads = early.pop()
+            early.append(placed_grads[0])
+        expert_totals.append(total)
+        if direct and other is not None:
+            zone = exchange((keep_dense + other.astype(f32)).astype(bf16))
+            outer.append(zone)
+            early.append(zone)
         grad_pieces = share_pieces(dattn)
-        grad_packed, keep, send, by_distance = attention_backward(
-            place, grad_pieces, w_in[layer], bias_rows[layer], low, w_out[layer], packed, log_total
-        )
+        grad_packed, keep, send, by_distance, gain_a = attention_backward(
+            layer, place, grad_pieces, w_in[layer], feature, bias, low, w_out[layer], packed,
+            log_total, normed_rows, after=early,
+        )
+        if direct and other is not None:
+            inner.append(
+                spread(sum_zone(zone)[:, : PACKED + LANES].astype(bf16).reshape(GROUP, share, -1))
+            )
         keep, recv, far = sum_pieces(keep, send)
-        grad_w_in, grad_w_out = dense_grads(pieces, grad_pieces, grad_packed, mixed)
         if layer > 0:
             below = kept[layer - 1]
-            g, small_a, sent = attention_token_back(
-                x, dmiddle, keep, recv, far, gain_a[layer], below[7], below[8], slots
+            g, sent = attention_token_back(
+                layer, x, dmiddle, keep, recv, far, feature, below[7], below[8], slots
             )
             arrived_grad = exchange(sent)
         else:
-            g, small_a = attention_token_back(x, dmiddle, keep, recv, far, gain_a[layer])
-
-        by_bucket = jnp.dot(hits, by_distance[:OWN].T, precision=lax.Precision.HIGHEST)
-        spread = jnp.where(
-            jnp.arange(GROUP)[None, None, :] == place[0], by_bucket[:, :, None], 0.0
-        ).reshape(experts, GROUP, pairs, 1, table_share)
-        features = jnp.concatenate([small_b[:experts], small_a[:1], small_b[16:17]], 0).T
-        features = features.reshape(experts, GROUP, pairs, share, experts + 2)
-        small_grad = jnp.zeros((experts, GROUP, pairs, share, LANES), f32)
-        small_grad = small_grad.at[..., : experts + 2].set(features)
-        small_grad = small_grad.at[..., :1, 64 : 64 + table_share].set(spread)
-        pack = jnp.concatenate(
-            [
-                grad_w_in.reshape(experts, GROUP, pairs, share, PACKED),
-                small_grad.astype(bf16),
-            ],
-            -1,
-        ).transpose(0, 2, 1, 3, 4)
-        pack = pack.reshape(experts * pairs, GROUP * share, PACKED + LANES)
+            (g,) = attention_token_back(layer, x, dmiddle, keep, recv, far, feature)
         if direct:
-            width = D // GROUP
-            outer = grad_w_out.reshape(experts * pairs, share, GROUP, width).transpose(0, 2, 1, 3)
-            pack = jnp.concatenate(
-                [pack, outer.reshape(experts * pairs, GROUP * share, width)], -1
+            keep_dense, send_dense = dense_pack(
+                experts, pairs, share, place, normed_rows, grad_pieces, grad_packed, mixed,
+                small_b, gain_a, by_distance, hits, after=inner,
             )
-        mine = lax.psum_scatter(pack, ("experts", "dp"), scatter_dimension=0, tiled=False)
-        inner = mine[:, : PACKED + LANES].reshape(GROUP, share, PACKED + LANES)
-        inner = lax.all_to_all(inner, "context", split_axis=0, concat_axis=0)
-        g_in = inner[..., :PACKED].astype(f32).reshape(GROUP, share, 3, OWN, HEAD_DIM)
-        g_in = g_in.transpose(1, 2, 3, 0, 4).reshape(share, 3 * D)
-        g_small = jnp.sum(inner[..., PACKED:].astype(f32), 0)
-        if direct:
-            width = D // GROUP
-            g_out = mine[:, -width:].astype(f32).reshape(GROUP, share, width)
-            g_out = g_out.transpose(1, 0, 2).reshape(share, D)
+            other = lax.ppermute(send_dense, "dp", [(0, 1), (1, 0)])
         else:
-            placed = jnp.where(
-                jnp.arange(GROUP)[None, :, None, None] == place[0],
-                grad_w_out.reshape(OWN, 1, HEAD_DIM, D),
-                jnp.zeros((), bf16),
-            ).reshape(D, D)
-            g_out = lax.psum_scatter(placed, ALL, scatter_dimension=0, tiled=True).astype(f32)
-        dense_out.insert(
-            0,
-            (
-                g_in,
-                g_out,
-                g_small[:, :experts],
-                g_small[:, experts : experts + 2],
-                g_small[0, 64 : 64 + table_share],
-            ),
-        )
-    dense = tuple(jnp.stack([entry[k] for entry in dense_out]) for k in range(5))
-    tall = expert_out_grads[0].shape[1]
-    wide = [entry.astype(f32) for entry in expert_out_grads]
-    grad_expert_in = jnp.stack(
-        [entry[:2].transpose(1, 0, 2).reshape(1, tall, 2 * FF) for entry in wide]
-    )
-    grad_expert_out = jnp.stack([entry[2:3] for entry in wide])
-    return (result[None], g[None], *dense, grad_expert_in, grad_expert_out)
+            grad_w_in, grad_w_out = dense_grads(normed_rows, grad_pieces, grad_packed, mixed)
+            inner.append(
+                dense_sum(
+                    experts, pairs, share, table_share, place, grad_w_in, grad_w_out, small_b,
+                    gain_a, by_distance, hits,
+                )
+            )
+    expert_grads_all = place_expert_grads(0, expert_totals[1], placed_grads)
+    if direct:
+        zone = exchange((keep_dense + other.astype(f32)).astype(bf16))
+        outer.append(zone)
+        inner.append(
+            spread(sum_zone(zone)[:, : PACKED + LANES].astype(bf16).reshape(GROUP, share, -1))
+        )
+        grad_attn_in, grad_attn_out, small_grad = finish_dense(
+            experts, share, inner[::-1], outer[::-1]
+        )
+    else:
+        grad_attn_in, grad_attn_out, small_grad = (
+            jnp.stack([entry[k] for entry in inner[::-1]]) for k in range(3)
+        )
+    return (
+        result[None],
+        g[None],
+        grad_attn_in,
+        grad_attn_out,
+        small_grad[..., :experts],
+        small_grad[..., 16:18],
+        small_grad[:, 0, 64 : 64 + table_share],
+        *expert_grads_all,
+    )
 
 
 def solution(mesh):

time: 1100 us -> 772 us (0.70)
  waiting for transfers between devices: 467 us -> 303 us
  blocking collectives: 171 us -> 77.3 us
  local copies, waits for them, and re-layouts: 118 us -> 69.6 us
  other arithmetic: 51.2 us -> 14 us
  starting transfers between devices: 34.9 us -> 54.2 us
    reduce_scatter x2, waiting for transfers between devices: 220 us -> 0.02 us  [on_device(): lax.psum_scatter(weight_grads, ('context', 'dp'), scatter_dimension=0, ti...]
    all_to_all x5 -> x2, blocking collectives: 171 us -> 67.6 us  [exchange(): lax.all_to_all(rows, 'experts', split_axis=0, concat_axis=0, tiled=True)]
    all_to_all x3 -> x8, waiting for transfers between devices: 46.2 us -> 115 us  [exchange(): lax.all_to_all(rows, 'experts', split_axis=0, concat_axis=0, tiled=True)]
    reduce_scatter x2 -> x0, waiting for transfers between devices: 60.2 us -> none  [on_device(): lax.psum_scatter(pack, ('experts', 'dp'), scatter_dimension=0, tiled=False)]
    ppermute x0 -> x2, waiting for transfers between devices: none -> 42 us  [on_device(): other = lax.ppermute(send_dense, 'dp', [(0, 1), (1, 0)])]
    another operation x18 -> x1, other arithmetic: 22.7 us -> 0.07 us  [on_device(): jnp.stack([lax.axis_index('context'), lax.axis_index('dp')])]
    all_to_all x3 -> x8, starting transfers between devices: 11.5 us -> 30.4 us  [exchange(): lax.all_to_all(rows, 'experts', split_axis=0, concat_axis=0, tiled=True)]
    transpose x18 -> x0, local copies, waits for them, and re-layouts: 16.3 us -> none  [the longest x4 5.62 us: on_device(): w_in.append(got[..., :PACKED].transpose(0, 2, 1, 3, 4).reshape(D, PACKED))]
  transfers between devices with their start and end apart: 32 -> 37, of which waited for: 21 -> 22; matrix products, arithmetic and copies ran while one was open for 5% -> 2% of each run, Pallas kernels for 11% -> 26%
where the time goes in v2:
time: 772 us; the launch traced here: 760 us
  waiting for transfers between devices  303 us (39%)
  Pallas kernels  228 us (30%)
  blocking collectives  77.3 us (10%)
  local copies, waits for them, and re-layouts  69.6 us (9%)
  starting transfers between devices  54.2 us (7%)
  between operations  14.7 us (2%)
  other arithmetic  14 us (2%)
    all_to_all x8, waiting for transfers between devices, exchange(): lax.all_to_all(rows, 'experts', split_axis=0, concat_axis=0, tiled=True)  115 us
    pallas_call x18, Pallas kernels, whole_call(): pl.pallas_call(ordered, out_shape=outs, in_specs=specs, out_specs=tuple((...  91.3 us
    all_to_all x2, blocking collectives, exchange(): lax.all_to_all(rows, 'experts', split_axis=0, concat_axis=0, tiled=True)  67.6 us
    unnamed x223, local copies, waits for them, and re-layouts  66.4 us
    ppermute x4, waiting for transfers between devices, share_pieces(): across = lax.ppermute(piece, 'context', ACROSS)  47.9 us
    pallas_call x2, Pallas kernels, expert_backward(): pl.pallas_call(body, grid=(BACK_STEPS,), out_shape=(shape((count, D), bf1...  47.6 us
    ppermute x4, waiting for transfers between devices, sum_pieces(): return (keep, recv, lax.ppermute(other, 'context', ACROSS))  46.3 us
    ppermute x2, waiting for transfers between devices, on_device(): other = lax.ppermute(send_dense, 'dp', [(0, 1), (1, 0)])  42 us
  transfers between devices with their start and end apart: 37, of which 22 were waited for; matrix products, arithmetic and copies ran while one was open for 2% of the time, Pallas kernels for 26%

profile of v2, /device:TPU:0, one launch (start us, length us, event | category | flops | bytes accessed | tf_op | source)
XLA Modules:
  0.0 760.4 jit_solution(6240306273881482470)
XLA Ops:
  12.3 9.7 %all_to_all.118 = bf16[4,32,896]{2,1,0:T(8,128)(2,1)S(1)} all-to-all(bf16[4,32,896]{2,1,0:T(8,128)(2,1)S(1)} %get-tuple-element.79), channel_id=1, replica_groups=mesh['experts'=4,'context'=4,'dp'=2] {'context'}, dimensions={0} | all-to-all | bytes 458752 | tf_op jit(solution)/shard_map/all_to_all | solution.py:1100
  23.2 13.2 %collective-permute-done.1.refs_3_ = bf16[256,1024]{1,0:T(8,128)(2,1)S(1)} collective-permute-done((bf16[256,1024]{1,0:T(8,128)(2,1)}, bf16[256,1024]{1,0:T(8,128)(2,1)S(1)}, u32[]{:S(2)}, u32[]{:S(2)}) %collective-permute-start.1) | collective-permute-done | bytes 524320 | tf_op jit(solution)/shard_map/ppermute | solution.py:1027
  37.3 38.0 %all-gather.5.cloned.1.call-done = bf16[32,32,1152]{2,1,0:T(8,128)(2,1)} async-done(((bf16[4,32,1152]{2,1,0:T(8,128)(2,1)}), bf16[32,32,1152]{2,1,0:T(8,128)(2,1)}) %all-gather.5.cloned.1.call-update) | async-done | bytes 2359312 | tf_op jit(solution)/shard_map/all_gather | solution.py:1103
  83.8 9.9 %attention_forward.2 = (bf16[1024,768]{1,0:T(8,128)(2,1)S(1)}, f32[8,1024]{1,0:T(8,128)S(1)}, bf16[1024,256]{1,0:T(8,128)(2,1)S(1)}, f32[512,1024]{1,0:T(8,128)S...) custom-call(s32[2]{0:T(128)S(1)} %pad_add_fusion.refs_0_, bf16[256,1024]{1,0:T(8,128)(2,1)S(1)} %bitcast.64, ...), custom_call_target="tpu_custom_call" | custom-call | flops 3221225472 | bytes 12128264 | tf_op jit(solution)/shard_map/attention_forward/pallas_call | solution.py:75
  107.1 8.9 %collective-permute-done.4.refs_3_ = bf16[256,1024]{1,0:T(8,128)(2,1)} collective-permute-done((bf16[256,1024]{1,0:T(8,128)(2,1)}, bf16[256,1024]{1,0:T(8,128)(2,1)}, u32[]{:S(2)}, u32[]{:S(2)}) %collective-permute-start.4) | collective-permute-done | bytes 524320 | tf_op jit(solution)/shard_map/ppermute | solution.py:1036
  128.2 37.0 %all-to-all-done.1 = bf16[4,160,1024]{2,1,0:T(8,128)(2,1)S(1)} async-done(((bf16[4,160,1024]{2,1,0:T(8,128)(2,1)}), bf16[4,160,1024]{2,1,0:T(8,128)(2,1)S(1)}, u32[]{:S(2)}, u32[]{:S(2)}) %all-to-all-start.1) | async-done | bytes 1310752 | tf_op jit(solution)/shard_map/all_to_all | solution.py:1075
  165.2 20.3 %expert_forward.2 = (bf16[640,1024]{1,0:T(8,128)(2,1)S(1)}, bf16[2,640,2816]{2,1,0:T(8,128)(2,1)}) custom-call(bf16[640,1024]{1,0:T(8,128)(2,1)S(1)} %bitcast.45, bf16[2,1,1024,5632]{3,2,1,0:T(8,128)(2,1)} %refs_3_.4, bf16[2,1,1024,5632]{3,2,1,0:T(8,128)(2,1)} %refs_3_.4, bf16[2,1,1024,2816]{3,2,1,0:T(8,128)(2,1)} %refs_4_.5), custom_call_target="tpu_custom_call" | custom-call | flops 11072962560 | bytes 17301504 | tf_op jit(solution)/shard_map/expert_forward/pallas_call | solution.py:863
  185.5 33.4 %all_to_all.119 = bf16[4,160,1024]{2,1,0:T(8,128)(2,1)S(1)} all-to-all(bf16[4,160,1024]{2,1,0:T(8,128)(2,1)S(1)} %bitcast.71), channel_id=1, replica_groups=mesh['experts'=4,'context'=4,'dp'=2] {'experts'}, dimensions={0} | all-to-all | bytes 2621440 | tf_op jit(solution)/shard_map/all_to_all | solution.py:1075
  222.3 11.4 %collective-permute-done.6.refs_3_.refs_14_ = bf16[256,1024]{1,0:T(8,128)(2,1)} collective-permute-done((bf16[256,1024]{1,0:T(8,128)(2,1)}, bf16[256,1024]{1,0:T(8,128)(2,1)}, u32[]{:S(2)}, u32[]{:S(2)}) %collective-permute-start.6) | collective-permute-done | bytes 524320 | tf_op jit(solution)/shard_map/ppermute | solution.py:1027
  236.0 11.5 %attention_forward.3 = (bf16[1024,768]{1,0:T(8,128)(2,1)S(1)}, f32[8,1024]{1,0:T(8,128)S(1)}, bf16[1024,256]{1,0:T(8,128)(2,1)S(1)}, f32[512,1024]{1,0:T(8,128)S(1)}, bf16[512,1024]{1,0:T(8,128)(2,1)S(1)}) custom-call(s32[2]{0:T(128)S(1)} %pad_add_fusion.refs_0_, bf16[256,1024]{1,0:T(8,128)(2,1)} %get-tuple-element.92.refs_1_.refs_12_, ...), custom_call_target="tpu_custom_call" | custom-call | flops 3221225472 | bytes 10031112 | tf_op jit(solution)/shard_map/attention_forward/pallas_call | solution.py:75
  253.2 12.8 %collective-permute-done.9.refs_3_ = bf16[256,1024]{1,0:T(8,128)(2,1)S(1)} collective-permute-done((bf16[256,1024]{1,0:T(8,128)(2,1)S(1)}, bf16[256,1024]{1,0:T(8,128)(2,1)S(1)}, u32[]{:S(2)}, u32[]{:S(2)}) %collective-permute-start.9) | collective-permute-done | bytes 524320 | tf_op jit(solution)/shard_map/ppermute | solution.py:1036
  271.2 34.2 %all_to_all.120 = bf16[4,160,1024]{2,1,0:T(8,128)(2,1)S(1)} all-to-all(bf16[4,160,1024]{2,1,0:T(8,128)(2,1)S(1)} %bitcast.70), channel_id=1, replica_groups=mesh['experts'=4,'context'=4,'dp'=2] {'experts'}, dimensions={0} | all-to-all | bytes 2621440 | tf_op jit(solution)/shard_map/all_to_all | solution.py:1075
  309.0 19.7 %expert_forward.3 = (bf16[640,1024]{1,0:T(8,128)(2,1)S(1)}, bf16[2,640,2816]{2,1,0:T(8,128)(2,1)}) custom-call(bf16[640,1024]{1,0:T(8,128)(2,1)S(1)} %bitcast.49, bf16[2,1,1024,5632]{3,2,1,0:T(8,128)(2,1)} %refs_3_.4, bf16[2,1,1024,5632]{3,2,1,0:T(8,128)(2,1)} %refs_3_.4, bf16[2,1,1024,2816]{3,2,1,0:T(8,128)(2,1)} %refs_4_.5), custom_call_target="tpu_custom_call" | custom-call | flops 11072962560 | bytes 17301504 | tf_op jit(solution)/shard_map/expert_forward/pallas_call | solution.py:863
  329.7 9.7 %all-to-all-done.6 = bf16[4,160,1024]{2,1,0:T(8,128)(2,1)S(1)} async-done(((bf16[4,160,1024]{2,1,0:T(8,128)(2,1)}), bf16[4,160,1024]{2,1,0:T(8,128)(2,1)S(1)}, u32[]{:S(2)}, u32[]{:S(2)}) %all-to-all-start.6) | async-done | bytes 1310752 | tf_op jit(solution)/shard_map/all_to_all | solution.py:1075
  344.0 24.1 %expert_backward.2 = (bf16[640,1024]{1,0:T(8,128)(2,1)}, bf16[3,640,2816]{2,1,0:T(8,128)(2,1)}) custom-call(bf16[640,1024]{1,0:T(8,128)(2,1)} %bitcast.51, bf16[2,640,2816]{2,1,0:T(8,128)(2,1)} %get-tuple-element.104.refs_1_, bf16[2,1,1024,5632]{3,2,1,0:T(8,128)(2,1)} %refs_3_.4, bf16[2,1,1024,5632]{3,2,1,0:T(8,128)(2,1)} %refs_3_.4, ...), custom_call_target="tpu_custom_call" | custom-call | flops 11072962560 | bytes 17301504 | tf_op jit(solution)/shard_map/expert_backward/pallas_call | solution.py:919
  368.1 6.7 all-to-all-done.5
  381.0 20.9 %expert_grads.2.refs_0_ = bf16[8,3,128,2816]{3,2,1,0:T(8,128)(2,1)} custom-call(bf16[640,1024]{1,0:T(8,128)(2,1)S(1)} %bitcast.50, bf16[640,1024]{1,0:T(8,128)(2,1)S(1)} %bitcast.52, bf16[3,640,2816]{2,1,0:T(8,128)(2,1)} %get-tuple-element.107.refs_2_, bf16[640,1024]{1,0:T(8,128)(2,1)} %bitcast.42), custom_call_target="tpu_custom_call" | custom-call | flops 11072962560 | bytes 17301504 | tf_op jit(solution)/shard_map/expert_grads/pallas_call | solution.py:970
  401.9 7.2 all-to-all-done.7
  421.0 11.5 %collective-permute-done.11.refs_3_.refs_7_ = bf16[256,1024]{1,0:T(8,128)(2,1)S(1)} collective-permute-done((bf16[256,1024]{1,0:T(8,128)(2,1)S(1)}, bf16[256,1024]{1,0:T(8,128)(2,1)S(1)}, u32[]{:S(2)}, u32[]{:S(2)}) %collective-permute-start.11) | collective-permute-done | bytes 524320 | tf_op jit(solution)/shard_map/ppermute | solution.py:1027
  435.1 15.4 %attention_backward.2 = (bf16[1024,768]{1,0:T(8,128)(2,1)S(1)}, f32[512,1024]{1,0:T(8,128)S(1)}, bf16[512,1024]{1,0:T(8,128)(2,1)S(1)}, f32[8,512]{1,0:T(8,128)S(1)}, f32[8,1024]{1,0:T(8,128)S(1)}) custom-call(s32[2]{0:T(128)S(1)} %copy-done.58, bf16[256,1024]{1,0:T(8,128)(2,1)S(1)} %get-tuple-element.109.refs_1_.refs_5_, ...), custom_call_target="tpu_custom_call" | custom-call | flops 4831838208 | bytes 13225992 | tf_op jit(solution)/shard_map/attention_backward/pallas_call | solution.py:75
  454.7 24.5 %collective-permute-done.14.refs_4_ = bf16[256,1024]{1,0:T(8,128)(2,1)S(1)} collective-permute-done((bf16[256,1024]{1,0:T(8,128)(2,1)S(1)}, bf16[256,1024]{1,0:T(8,128)(2,1)S(1)}, u32[]{:S(2)}, u32[]{:S(2)}) %collective-permute-start.14) | collective-permute-done | bytes 524320 | tf_op jit(solution)/shard_map/ppermute | solution.py:1036
  491.2 5.5 dense_pack.2
  498.1 19.5 %all-to-all-done.8 = bf16[4,160,1024]{2,1,0:T(8,128)(2,1)S(1)} async-done(((bf16[4,160,1024]{2,1,0:T(8,128)(2,1)}), bf16[4,160,1024]{2,1,0:T(8,128)(2,1)S(1)}, u32[]{:S(2)}, u32[]{:S(2)}) %all-to-all-start.8) | async-done | bytes 1310752 | tf_op jit(solution)/shard_map/all_to_all | solution.py:1075
  518.7 23.5 %expert_backward.3 = (bf16[640,1024]{1,0:T(8,128)(2,1)}, bf16[3,640,2816]{2,1,0:T(8,128)(2,1)}) custom-call(bf16[640,1024]{1,0:T(8,128)(2,1)} %bitcast.47, bf16[2,640,2816]{2,1,0:T(8,128)(2,1)} %get-tuple-element.116.refs_1_, bf16[2,1,1024,5632]{3,2,1,0:T(8,128)(2,1)} %refs_3_.4, bf16[2,1,1024,5632]{3,2,1,0:T(8,128)(2,1)} %refs_3_.4, ...), custom_call_target="tpu_custom_call" | custom-call | flops 11072962560 | bytes 17301504 | tf_op jit(solution)/shard_map/expert_backward/pallas_call | solution.py:919
  547.2 20.6 %expert_grads.3.refs_0_ = bf16[8,3,128,2816]{3,2,1,0:T(8,128)(2,1)} custom-call(bf16[640,1024]{1,0:T(8,128)(2,1)S(1)} %bitcast.46, bf16[640,1024]{1,0:T(8,128)(2,1)S(1)} %bitcast.48, bf16[3,640,2816]{2,1,0:T(8,128)(2,1)} %get-tuple-element.120.refs_2_, bf16[640,1024]{1,0:T(8,128)(2,1)} %bitcast.38, bf16[4,128,1152]{2,1,0:T(8,128)(2,1)} %collective-permute-done.15.refs_4_), custom_call_target="tpu_custom_call" | custom-call | flops 11072962560 | bytes 17301504 | tf_op jit(solution)/shard_map/expert_grads/pallas_call | solution.py:970
  567.8 8.8 %all-to-all-done.9 = bf16[4,160,1024]{2,1,0:T(8,128)(2,1)S(1)} async-done(((bf16[4,160,1024]{2,1,0:T(8,128)(2,1)}), bf16[4,160,1024]{2,1,0:T(8,128)(2,1)S(1)}, u32[]{:S(2)}, u32[]{:S(2)}) %all-to-all-start.9) | async-done | bytes 1310752 | tf_op jit(solution)/shard_map/all_to_all | solution.py:1075
  596.8 11.8 %collective-permute-done.17.refs_3_.refs_4_ = bf16[256,1024]{1,0:T(8,128)(2,1)S(1)} collective-permute-done((bf16[256,1024]{1,0:T(8,128)(2,1)}, bf16[256,1024]{1,0:T(8,128)(2,1)S(1)}, u32[]{:S(2)}, u32[]{:S(2)}) %collective-permute-start.17) | collective-permute-done | bytes 524320 | tf_op jit(solution)/shard_map/ppermute | solution.py:1027
  608.6 4.9 all-to-all-done.10.refs_14_.refs_3_
  624.7 15.2 %attention_backward.3 = (bf16[1024,768]{1,0:T(8,128)(2,1)S(1)}, f32[512,1024]{1,0:T(8,128)S(1)}, bf16[512,1024]{1,0:T(8,128)(2,1)S(1)}, f32[8,512]{1,0:T(8,128)S(1)}, f32[8,1024]{1,0:T(8,128)S(1)}) custom-call(s32[2]{0:T(128)S(1)} %copy-done.58, bf16[256,1024]{1,0:T(8,128)(2,1)} %get-tuple-element.128.refs_1_.refs_2_, ...), custom_call_target="tpu_custom_call" | custom-call | flops 4831838208 | bytes 13225992 | tf_op jit(solution)/shard_map/attention_backward/pallas_call | solution.py:75
  653.8 42.0 %collective-permute-done.21 = bf16[4,128,1152]{2,1,0:T(8,128)(2,1)S(1)} collective-permute-done((bf16[4,128,1152]{2,1,0:T(8,128)(2,1)S(1)}, bf16[4,128,1152]{2,1,0:T(8,128)(2,1)S(1)}, u32[]{:S(2)}, u32[]{:S(2)}) %collective-permute-start.21) | collective-permute-done | bytes 1179680 | tf_op jit(solution)/shard_map/ppermute | solution.py:1223
  697.1 4.5 all-to-all-start.12
  708.6 21.9 %all-to-all-done.12.refs_2_ = bf16[4,128,1152]{2,1,0:T(8,128)(2,1)S(1)} async-done(((bf16[4,128,1152]{2,1,0:T(8,128)(2,1)}), bf16[4,128,1152]{2,1,0:T(8,128)(2,1)S(1)}, u32[]{:S(2)}, u32[]{:S(2)}) %all-to-all-start.12) | async-done | bytes 1179680 | tf_op jit(solution)/shard_map/all_to_all | solution.py:1075
  (317 shorter events, 187.4 us)
Async XLA Ops:
  7.2 68.1 %all-gather.5.cloned.1.call-start = ((), (), s32[]{:S(2)}) async-start(), calls=%async_computation.18 | async-start | bytes 2654208 | tf_op jit(solution)/shard_map/all_gather | solution.py:1103
  22.7 13.7 %collective-permute-start.1 = (bf16[256,1024]{1,0:T(8,128)(2,1)}, bf16[256,1024]{1,0:T(8,128)(2,1)S(1)}, u32[]{:S(2)}, u32[]{:S(2)}) collective-permute-start(bf16[256,1024]{1,0:T(8,128)(2,1)} %bitcast.62), channel_id=1, source_target_pairs={{0,4},{2,6},{4,0},{6,2},{1,5},{3,7},{5,1},{7,3},{8,12},{10,14},{12... | collective-permute-start | bytes 1572872 | tf_op jit(solution)/shard_map/ppermute | solution.py:1027
  23.2 55.8 %collective-permute-start = (bf16[256,1024]{1,0:T(8,128)(2,1)}, bf16[256,1024]{1,0:T(8,128)(2,1)S(1)}, u32[]{:S(2)}, u32[]{:S(2)}) collective-permute-start(bf16[256,1024]{1,0:T(8,128)(2,1)} %bitcast.63), channel_id=1, source_target_pairs={{0,2},{2,0},{4,6},{6,4},{1,3},{3,1},{5,7},{7,5},{8,10},{10,8},{12,... | collective-permute-start | bytes 1572872 | tf_op jit(solution)/shard_map/ppermute | solution.py:1028
  36.4 43.4 %collective-permute-start.2 = (bf16[256,1024]{1,0:T(8,128)(2,1)S(1)}, bf16[256,1024]{1,0:T(8,128)(2,1)S(1)}, u32[]{:S(2)}, u32[]{:S(2)}) collective-permute-start(bf16[256,1024]{1,0:T(8,128)(2,1)S(1)} %collective-permute-done.1.refs_3_), channel_id=1, source_target_pairs={{0,2},{2,0},{4,6},{6,4},{1,3},{3,1},{5,7},{7,5},{8,10},{10,8},{12,... | collective-permute-start | bytes 1572872 | tf_op jit(solution)/shard_map/ppermute | solution.py:1029
  100.9 15.1 %collective-permute-start.4 = (bf16[256,1024]{1,0:T(8,128)(2,1)}, bf16[256,1024]{1,0:T(8,128)(2,1)}, u32[]{:S(2)}, u32[]{:S(2)}) collective-permute-start(bf16[256,1024]{1,0:T(8,128)(2,1)} %add_convert_fusion.5), channel_id=1, source_target_pairs={{0,4},{2,6},{4,0},{6,2},{1,5},{3,7},{5,1},{7,3},{8,12},{10,14},{12... | collective-permute-start | bytes 1572872 | tf_op jit(solution)/shard_map/ppermute | solution.py:1036
  102.4 20.6 %all-to-all-start.3 = ((bf16[4,32,768]{2,1,0:T(8,128)(2,1)}), bf16[4,32,768]{2,1,0:T(8,128)(2,1)}, u32[]{:S(2)}, u32[]{:S(2)}) async-start(bf16[4,32,768]{2,1,0:T(8,128)(2,1)} %get-tuple-element.93), calls=%async_computation.3 | async-start | bytes 393216 | tf_op jit(solution)/shard_map/all_to_all | solution.py:1100
  123.0 42.2 %all-to-all-start.1 = ((bf16[4,160,1024]{2,1,0:T(8,128)(2,1)}), bf16[4,160,1024]{2,1,0:T(8,128)(2,1)S(1)}, u32[]{:S(2)}, u32[]{:S(2)}) async-start(bf16[4,160,1024]{2,1,0:T(8,128)(2,1)} %bitcast.67), calls=%async_computation.1 | async-start | bytes 2621440 | tf_op jit(solution)/shard_map/all_to_all | solution.py:1075
  126.5 107.2 %all-gather.7.cloned.1.call-start = ((), (), s32[]{:S(2)}) async-start(), calls=%async_computation.19 | async-start | bytes 2359296 | tf_op jit(solution)/shard_map/all_gather | solution.py:1103
  220.9 12.8 %collective-permute-start.6 = (bf16[256,1024]{1,0:T(8,128)(2,1)}, bf16[256,1024]{1,0:T(8,128)(2,1)}, u32[]{:S(2)}, u32[]{:S(2)}) collective-permute-start(bf16[256,1024]{1,0:T(8,128)(2,1)} %get-tuple-element.92.refs_1_.refs_12_), channel_id=1, source_target_pairs={{0,4},{2,6},{4,0},{6,2},{1,5},{3,7},{5,1},{7,3},{8,12},{10,14},{12... | collective-permute-start | bytes 1572872 | tf_op jit(solution)/shard_map/ppermute | solution.py:1027
  222.3 13.7 %collective-permute-start.5 = (bf16[256,1024]{1,0:T(8,128)(2,1)}, bf16[256,1024]{1,0:T(8,128)(2,1)}, u32[]{:S(2)}, u32[]{:S(2)}) collective-permute-start(bf16[256,1024]{1,0:T(8,128)(2,1)} %get-tuple-element.92.refs_1_.refs_12_), channel_id=1, source_target_pairs={{0,2},{2,0},{4,6},{6,4},{1,3},{3,1},{5,7},{7,5},{8,10},{10,8},{12,... | collective-permute-start | bytes 1572872 | tf_op jit(solution)/shard_map/ppermute | solution.py:1028
  248.8 2.8 collective-permute-start.8
  251.7 14.3 %collective-permute-start.9 = (bf16[256,1024]{1,0:T(8,128)(2,1)S(1)}, bf16[256,1024]{1,0:T(8,128)(2,1)S(1)}, u32[]{:S(2)}, u32[]{:S(2)}) collective-permute-start(bf16[256,1024]{1,0:T(8,128)(2,1)S(1)} %add_convert_fusion.4), channel_id=1, source_target_pairs={{0,4},{2,6},{4,0},{6,2},{1,5},{3,7},{5,1},{7,3},{8,12},{10,14},{12... | collective-permute-start | bytes 1572872 | tf_op jit(solution)/shard_map/ppermute | solution.py:1036
  305.4 33.9 %all-to-all-start.6 = ((bf16[4,160,1024]{2,1,0:T(8,128)(2,1)}), bf16[4,160,1024]{2,1,0:T(8,128)(2,1)S(1)}, u32[]{:S(2)}, u32[]{:S(2)}) async-start(bf16[4,160,1024]{2,1,0:T(8,128)(2,1)} %bitcast.68), calls=%async_computation.6 | async-start | bytes 2621440 | tf_op jit(solution)/shard_map/all_to_all | solution.py:1075
  340.4 34.3 %all-to-all-start.5 = ((bf16[4,160,1024]{2,1,0:T(8,128)(2,1)}), bf16[4,160,1024]{2,1,0:T(8,128)(2,1)S(1)}, u32[]{:S(2)}, u32[]{:S(2)}) async-start(bf16[4,160,1024]{2,1,0:T(8,128)(2,1)} %bitcast.69), calls=%async_computation.5 | async-start | bytes 2621440 | tf_op jit(solution)/shard_map/all_to_all | solution.py:1075
  374.8 34.3 %all-to-all-start.7 = ((bf16[4,160,1024]{2,1,0:T(8,128)(2,1)}), bf16[4,160,1024]{2,1,0:T(8,128)(2,1)S(1)}, u32[]{:S(2)}, u32[]{:S(2)}) async-start(bf16[4,160,1024]{2,1,0:T(8,128)(2,1)} %bitcast.82), calls=%async_computation.7 | async-start | bytes 2621440 | tf_op jit(solution)/shard_map/all_to_all | solution.py:1075
  378.3 207.2 %reduce-scatter.3.cloned.1.call-start = ((), (), s32[]{:S(2)}) async-start(), calls=%async_computation.16 | async-start | bytes 19464192 | tf_op jit(solution)/shard_map/reduce_scatter | solution.py:1183
  419.7 12.7 %collective-permute-start.11 = (bf16[256,1024]{1,0:T(8,128)(2,1)S(1)}, bf16[256,1024]{1,0:T(8,128)(2,1)S(1)}, u32[]{:S(2)}, u32[]{:S(2)}) collective-permute-start(bf16[256,1024]{1,0:T(8,128)(2,1)S(1)} %get-tuple-element.109.refs_1_.refs_5_), channel_id=1, source_target_pairs={{0,4},{2,6},{4,0},{6,2},{1,5},{3,7},{5,1},{7,3},{8,12},{10,14},{12... | collective-permute-start | bytes 1572872 | tf_op jit(solution)/shard_map/ppermute | solution.py:1027
  421.0 11.5 %collective-permute-start.10 = (bf16[256,1024]{1,0:T(8,128)(2,1)S(1)}, bf16[256,1024]{1,0:T(8,128)(2,1)S(1)}, u32[]{:S(2)}, u32[]{:S(2)}) collective-permute-start(bf16[256,1024]{1,0:T(8,128)(2,1)S(1)} %get-tuple-element.109.refs_1_.refs_5_), channel_id=1, source_target_pairs={{0,2},{2,0},{4,6},{6,4},{1,3},{3,1},{5,7},{7,5},{8,10},{10,8},{12,... | collective-permute-start | bytes 1572872 | tf_op jit(solution)/shard_map/ppermute | solution.py:1028
  453.5 25.8 %collective-permute-start.14 = (bf16[256,1024]{1,0:T(8,128)(2,1)S(1)}, bf16[256,1024]{1,0:T(8,128)(2,1)S(1)}, u32[]{:S(2)}, u32[]{:S(2)}) collective-permute-start(bf16[256,1024]{1,0:T(8,128)(2,1)S(1)} %add_convert_fusion.3), channel_id=1, source_target_pairs={{0,4},{2,6},{4,0},{6,2},{1,5},{3,7},{5,1},{7,3},{8,12},{10,14},{12... | collective-permute-start | bytes 1572872 | tf_op jit(solution)/shard_map/ppermute | solution.py:1036
  482.7 34.9 %all-to-all-start.8 = ((bf16[4,160,1024]{2,1,0:T(8,128)(2,1)}), bf16[4,160,1024]{2,1,0:T(8,128)(2,1)S(1)}, u32[]{:S(2)}, u32[]{:S(2)}) async-start(bf16[4,160,1024]{2,1,0:T(8,128)(2,1)} %bitcast.23), calls=%async_computation.8 | async-start | bytes 2621440 | tf_op jit(solution)/shard_map/all_to_all | solution.py:1075
  498.1 47.8 %collective-permute-start.15 = (bf16[4,128,1152]{2,1,0:T(8,128)(2,1)}, bf16[4,128,1152]{2,1,0:T(8,128)(2,1)}, u32[]{:S(2)}, u32[]{:S(2)}) collective-permute-start(bf16[4,128,1152]{2,1,0:T(8,128)(2,1)} %get-tuple-element.126), channel_id=1, source_target_pairs={{0,1},{1,0},{2,3},{3,2},{4,5},{5,4},{6,7},{7,6},{8,9},{9,8},{10,11... | collective-permute-start | bytes 3538952 | tf_op jit(solution)/shard_map/ppermute | solution.py:1223
  542.2 34.4 %all-to-all-start.9 = ((bf16[4,160,1024]{2,1,0:T(8,128)(2,1)}), bf16[4,160,1024]{2,1,0:T(8,128)(2,1)S(1)}, u32[]{:S(2)}, u32[]{:S(2)}) async-start(bf16[4,160,1024]{2,1,0:T(8,128)(2,1)} %bitcast.83), calls=%async_computation.9 | async-start | bytes 2621440 | tf_op jit(solution)/shard_map/all_to_all | solution.py:1075
  545.9 204.3 %reduce-scatter.5.cloned.1.call-start = ((), (), s32[]{:S(2)}) async-start(), calls=%async_computation.17 | async-start | bytes 19464192 | tf_op jit(solution)/shard_map/reduce_scatter | solution.py:1183
  581.0 32.5 %all-to-all-start.10 = ((bf16[4,128,1152]{2,1,0:T(8,128)(2,1)}), bf16[4,128,1152]{2,1,0:T(8,128)(2,1)}, u32[]{:S(2)}, u32[]{:S(2)}) async-start(bf16[4,128,1152]{2,1,0:T(8,128)(2,1)} %add_convert_fusion.1), calls=%async_computation.11 | async-start | bytes 2359296 | tf_op jit(solution)/shard_map/all_to_all | solution.py:1075
  595.3 13.3 %collective-permute-start.17 = (bf16[256,1024]{1,0:T(8,128)(2,1)}, bf16[256,1024]{1,0:T(8,128)(2,1)S(1)}, u32[]{:S(2)}, u32[]{:S(2)}) collective-permute-start(bf16[256,1024]{1,0:T(8,128)(2,1)} %get-tuple-element.128.refs_1_.refs_2_), channel_id=1, source_target_pairs={{0,4},{2,6},{4,0},{6,2},{1,5},{3,7},{5,1},{7,3},{8,12},{10,14},{12... | collective-permute-start | bytes 1572872 | tf_op jit(solution)/shard_map/ppermute | solution.py:1027
  596.8 26.4 %collective-permute-start.16 = (bf16[256,1024]{1,0:T(8,128)(2,1)}, bf16[256,1024]{1,0:T(8,128)(2,1)}, u32[]{:S(2)}, u32[]{:S(2)}) collective-permute-start(bf16[256,1024]{1,0:T(8,128)(2,1)} %get-tuple-element.128.refs_1_.refs_2_), channel_id=1, source_target_pairs={{0,2},{2,0},{4,6},{6,4},{1,3},{3,1},{5,7},{7,5},{8,10},{10,8},{12,... | collective-permute-start | bytes 1572872 | tf_op jit(solution)/shard_map/ppermute | solution.py:1028
  608.6 14.6 %collective-permute-start.18 = (bf16[256,1024]{1,0:T(8,128)(2,1)S(1)}, bf16[256,1024]{1,0:T(8,128)(2,1)}, u32[]{:S(2)}, u32[]{:S(2)}) collective-permute-start(bf16[256,1024]{1,0:T(8,128)(2,1)S(1)} %collective-permute-done.17.refs_3_.refs_4_), channel_id=1, source_target_pairs={{0,2},{2,0},{4,6},{6,4},{1,3},{3,1},{5,7},{7,5},{8,10},{10,8},{12,... | collective-permute-start | bytes 1572872 | tf_op jit(solution)/shard_map/ppermute | solution.py:1029
  615.7 27.7 %all-to-all-start.11 = ((bf16[4,32,896]{2,1,0:T(8,128)(2,1)}), bf16[4,32,896]{2,1,0:T(8,128)(2,1)S(1)}, u32[]{:S(2)}, u32[]{:S(2)}) async-start(bf16[4,32,896]{2,1,0:T(8,128)(2,1)} %bitcast.29), calls=%async_computation.12 | async-start | bytes 458752 | tf_op jit(solution)/shard_map/all_to_all | solution.py:1100
  652.7 43.1 %collective-permute-start.21 = (bf16[4,128,1152]{2,1,0:T(8,128)(2,1)S(1)}, bf16[4,128,1152]{2,1,0:T(8,128)(2,1)S(1)}, u32[]{:S(2)}, u32[]{:S(2)}) collective-permute-start(bf16[4,128,1152]{2,1,0:T(8,128)(2,1)S(1)} %get-tuple-element.142), channel_id=1, source_target_pairs={{0,1},{1,0},{2,3},{3,2},{4,5},{5,4},{6,7},{7,6},{8,9},{9,8},{10,11... | collective-permute-start | bytes 3538952 | tf_op jit(solution)/shard_map/ppermute | solution.py:1223
  697.1 33.4 %all-to-all-start.12 = ((bf16[4,128,1152]{2,1,0:T(8,128)(2,1)}), bf16[4,128,1152]{2,1,0:T(8,128)(2,1)S(1)}, u32[]{:S(2)}, u32[]{:S(2)}) async-start(bf16[4,128,1152]{2,1,0:T(8,128)(2,1)} %add_convert_fusion), calls=%async_computation.13 | async-start | bytes 2359296 | tf_op jit(solution)/shard_map/all_to_all | solution.py:1075
  706.8 32.7 %collective-permute-start.20 = (bf16[256,1024]{1,0:T(8,128)(2,1)}, bf16[256,1024]{1,0:T(8,128)(2,1)}, u32[]{:S(2)}, u32[]{:S(2)}) collective-permute-start(bf16[256,1024]{1,0:T(8,128)(2,1)} %add_convert_fusion.2), channel_id=1, source_target_pairs={{0,4},{2,6},{4,0},{6,2},{1,5},{3,7},{5,1},{7,3},{8,12},{10,14},{12... | collective-permute-start | bytes 1572872 | tf_op jit(solution)/shard_map/ppermute | solution.py:1036
  733.1 12.6 %all-to-all-start.13 = ((bf16[4,32,896]{2,1,0:T(8,128)(2,1)}), bf16[4,32,896]{2,1,0:T(8,128)(2,1)S(1)}, u32[]{:S(2)}, u32[]{:S(2)}) async-start(bf16[4,32,896]{2,1,0:T(8,128)(2,1)} %bitcast.85), calls=%async_computation.14 | async-start | bytes 458752 | tf_op jit(solution)/shard_map/all_to_all | solution.py:1100
  (114 other events, 1117.0 us)
Sparse Core Ops, SparseCore 0:
  22.9 52.3 all-gather.4
  130.0 58.7 all-gather.6
  410.4 139.7 reduce-scatter.2
  577.8 133.2 reduce-scatter.4

commit v3 on v2

--- a/solution.py
+++ b/solution.py
@@ -58,7 +58,8 @@
 
 
 def whole_call(
-    body, out_shape, args, *, flops=0, limit=16, scratch=(), smem=0, name=None, after=()
+    body, out_shape, args, *, flops=0, limit=16, scratch=(), smem=0, name=None, after=(),
+    streamed=False,
 ):
     specs = [pl.BlockSpec(memory_space=pltpu.SMEM)] * smem + [
         pl.BlockSpec(memory_space=pltpu.VMEM)
@@ -72,6 +73,25 @@
     def ordered(*refs):
         body(*refs[:used], *refs[used + len(after) :])
 
+    if streamed:
+        args = args[:smem] + [far_away(a) for a in args[smem:]]
+
+        def full(a):
+            return pl.BlockSpec(a.shape, lambda i: (0,) * len(a.shape))
+
+        return pl.pallas_call(
+            ordered,
+            grid=(1,),
+            out_shape=outs,
+            in_specs=specs[:smem] + [full(a) for a in args[smem:used]] + specs[used:],
+            out_specs=tuple(full(o) for o in outs),
+            scratch_shapes=list(scratch),
+            compiler_params=pltpu.CompilerParams(vmem_limit_bytes=limit * MIB),
+            cost_estimate=pl.CostEstimate(
+                flops=int(flops), bytes_accessed=int(moved), transcendentals=0
+            ),
+            name=name,
+        )(*args)
     return pl.pallas_call(
         ordered,
         out_shape=outs,
@@ -137,13 +157,14 @@
                 for c in range(GROUP):
                     source = which * D + (head * GROUP + c) * HEAD_DIM
                     target = which * OWN_COLS + head * HEAD_DIM
-                    packets[layer][c, :, target : target + HEAD_DIM] = in_ref[
+                    target += layer * (PACKED + LANES)
+                    packets[0][c, :, target : target + HEAD_DIM] = in_ref[
                         layer, :, source : source + HEAD_DIM
                     ]
         if direct:
             width = D // GROUP
             for q in range(GROUP):
-                packets[LAYERS + layer][q] = out_ref[layer, :, q * width : (q + 1) * width]
+                packets[1 + layer][q] = out_ref[layer, :, q * width : (q + 1) * width]
     small = jnp.zeros((share, LANES), f32)
     row = lax.broadcasted_iota(jnp.int32, (share, LANES), 0)
     for layer in range(LAYERS):
@@ -153,12 +174,12 @@
         bucket = dot(table_ref[layer : layer + 1, :], placed(table_ref.shape[1], top + 64), 1, 0)
         small = small + jnp.where(row == 0, bucket, 0.0)
     for c in range(GROUP):
-        packets[0][c, :, PACKED:] = small.astype(bf16)
+        packets[0][c, :, PACKED : PACKED + LANES] = small.astype(bf16)
 
 
 def prepare(direct, attn_in, attn_out, router, gains, rel_table):
     share = attn_in.shape[1]
-    outs = [shape((GROUP, share, PACKED + LANES), bf16), shape((GROUP, share, PACKED), bf16)]
+    outs = [shape((GROUP, share, 2 * PACKED + LANES), bf16)]
     if direct:
         outs += [shape((GROUP, share, D // GROUP), bf16)] * LAYERS
 
@@ -166,51 +187,51 @@
         prepare_body(direct, *refs)
 
     return whole_call(
-        body, outs, [attn_in, attn_out, router, gains, rel_table], name="prepare"
-    )
-
-
-def unpack_body(place_ref, got_ref, hits_ref, w_in_ref, w_out_ref, *rest):
-    experts, pairs, _, share, total = got_ref.shape
+        body, outs, [attn_in, attn_out, router, gains, rel_table], streamed=True, name="prepare"
+    )
+
+
+def unpack(place, hits, experts, pairs, layer, got):
+    share = got.shape[-2]
     width = D // GROUP
-    for e in range(experts):
-        for d in range(pairs):
+    first = layer == 0
+
+    def body(place_ref, hits_ref, got_ref, w_in_ref, w_out_ref, *rest):
+        for index in range(experts * pairs):
+            e, d = index // pairs, index % pairs
             for c in range(GROUP):
-                row = ((e * GROUP + c) * pairs + d) * share
-                w_in_ref[row : row + share, :] = got_ref[e, d, c, :, :PACKED]
-                row = (e * pairs + d) * share
-                w_out_ref[c, row : row + share, :] = got_ref[e, d, c, :, total - width :]
-    if not rest:
-        return
-    feature_ref, bias_ref, flat_ref, bucket_ref = rest
-    for e in range(experts):
-        for d in range(pairs):
-            for c in range(GROUP):
-                index = (e * GROUP + c) * pairs + d
-                block = got_ref[e, d, c, :, PACKED : PACKED + LANES].astype(f32)
-                flat_ref[index * share : (index + 1) * share, :] = block
-                bucket_ref[index : index + 1, :] = block[:1, :]
-    feature_ref[...] = flat_ref[...].T
-    head = lax.broadcasted_iota(jnp.int32, (8, LANES), 0)
-    lane = lax.broadcasted_iota(jnp.int32, (8, LANES), 1)
-    for layer in range(LAYERS):
-        mine = jnp.where(
-            (lane == 64 + 32 * layer + head * GROUP + place_ref[0]) & (head < OWN), 1.0, 0.0
-        )
-        table = dot(mine, bucket_ref[...], 1, 1, lax.Precision.HIGHEST)
-        bias_ref[layer] = dot(
-            table - table[:, BUCKETS - 1 :], hits_ref[...], 1, 0, lax.Precision.HIGHEST
-        )
-
-
-def unpack(place, got, hits, first):
+                owner = (e * GROUP + c) * pairs + d
+                at = owner * share
+                w_in_ref[at : at + share, :] = got_ref[index, c, :, :PACKED]
+                w_out_ref[c, index * share : (index + 1) * share, :] = got_ref[
+                    index, c, :, got_ref.shape[-1] - width :
+                ]
+                if first:
+                    flags = got_ref[index, c, :, PACKED : PACKED + LANES].astype(f32)
+                    rest[2][at : at + share, :] = flags
+                    rest[3][owner : owner + 1, :] = flags[:1, :]
+        if not first:
+            return
+        feature_ref, bias_ref, flat_ref, bucket_ref = rest
+        feature_ref[...] = flat_ref[...].T
+        head = lax.broadcasted_iota(jnp.int32, (8, LANES), 0)
+        lane = lax.broadcasted_iota(jnp.int32, (8, LANES), 1)
+        for other in range(LAYERS):
+            mine = jnp.where(
+                (lane == 64 + 32 * other + head * GROUP + place_ref[0]) & (head < OWN), 1.0, 0.0
+            )
+            table = dot(mine, bucket_ref[...], 1, 1, lax.Precision.HIGHEST)
+            bias_ref[other] = dot(
+                table - table[:, BUCKETS - 1 :], hits_ref[...], 1, 0, lax.Precision.HIGHEST
+            )
+
     outs = [shape((D, PACKED), bf16), shape((GROUP, OWN_COLS, D // GROUP), bf16)]
     scratch = []
     if first:
         outs += [shape((LANES, D), f32), shape((LAYERS, 8, REACH), f32)]
         scratch = [pltpu.VMEM((D, LANES), f32), pltpu.VMEM((BUCKETS, LANES), f32)]
     return whole_call(
-        unpack_body, outs, [place, got, hits], smem=1, scratch=scratch, name="unpack"
+        body, outs, [place, hits, got], smem=1, scratch=scratch, name="unpack"
     )
 
 
@@ -490,17 +511,19 @@
 
 
 def dense_pack(experts, pairs, share, place, normed, upstream, grad_packed, mixed, small, gain_a,
-               by_distance, hits, after=()):
+               by_distance, hits, split, after=()):
     rows = upstream[0].shape[0]
     count = len(normed)
     width = D // GROUP
-    total = PACKED + LANES + width
+    rest = LANES + width
+    total = PACKED if split else PACKED + rest
 
     def body(place_ref, *refs):
         grad_packed_ref, mixed_ref, small_ref, gain_ref, distance_ref, hits_ref = refs[
             count + GROUP : count + GROUP + 6
         ]
-        keep_ref, send_ref, in_ref, out_ref, flat_ref = refs[count + GROUP + 6 :]
+        outs = refs[count + GROUP + 6 : -3]
+        in_ref, out_ref, flat_ref = refs[-3:]
         total_in, total_out = dense_products(
             refs[:count], refs[count : count + GROUP], grad_packed_ref, mixed_ref
         )
@@ -522,24 +545,34 @@
         for index in range(BUCKETS):
             at = index * share
             flat_ref[at : at + 1, :] = flat_ref[at : at + 1, :] + buckets[index : index + 1, :]
-        for target, d in ((keep_ref, place_ref[1]), (send_ref, 1 - place_ref[1])):
+        for side, d in enumerate((place_ref[1], 1 - place_ref[1])):
             for e in range(experts):
                 for c in range(GROUP):
-                    span = pl.ds(pl.multiple_of(((e * GROUP + c) * pairs + d) * share, share), share)
+                    at = ((e * GROUP + c) * pairs + d) * share
+                    span = pl.ds(pl.multiple_of(at, share), share)
                     to = slice(c * share, (c + 1) * share)
+                    target = outs[side]
                     target[e, to, :PACKED] = in_ref[span, :].astype(target.dtype)
-                    target[e, to, PACKED : PACKED + LANES] = flat_ref[span, :].astype(target.dtype)
-                    span = pl.ds(pl.multiple_of((e * pairs + d) * share, share), share)
-                    target[e, to, PACKED + LANES :] = out_ref[
-                        span, c * width : (c + 1) * width
-                    ].astype(target.dtype)
-
+                    out_span = pl.ds(pl.multiple_of((e * pairs + d) * share, share), share)
+                    outer = out_ref[out_span, c * width : (c + 1) * width]
+                    if split:
+                        outs[2][e, side, to, :LANES] = flat_ref[span, :].astype(bf16)
+                        outs[2][e, side, to, LANES:] = outer.astype(bf16)
+                    else:
+                        target[e, to, PACKED : PACKED + LANES] = flat_ref[span, :].astype(
+                            target.dtype
+                        )
+                        target[e, to, PACKED + LANES :] = outer.astype(target.dtype)
+
+    outs = [
+        shape((experts, GROUP * share, total), f32),
+        shape((experts, GROUP * share, total), bf16),
+    ]
+    if split:
+        outs.append(shape((experts, pairs, GROUP * share, rest), bf16))
     return whole_call(
         body,
-        (
-            shape((experts, GROUP * share, total), f32),
-            shape((experts, GROUP * share, total), bf16),
-        ),
+        outs,
         [place, *normed, *upstream, grad_packed, mixed, small, gain_a, by_distance, hits],
         smem=1,
         scratch=[
@@ -549,33 +582,33 @@
         ],
         flops=2 * GROUP * rows * D * (PACKED + OWN_COLS),
         after=after,
+        streamed=True,
+        limit=32,
         name="dense_pack",
     )
 
 
-def finish_dense(experts, share, inner, outer):
+def finish_dense(share, inner, outer):
     width = D // GROUP
 
     def body(*refs):
-        in_ref, out_ref, small_ref = refs[2 * LAYERS :]
+        in_ref, out_ref, small_ref = refs[1 + LAYERS :]
         for layer in range(LAYERS):
-            got, zone = refs[layer], refs[LAYERS + layer]
+            got, rows_out = refs[0], refs[1 + layer]
             for c in range(GROUP):
                 for which in range(3):
                     for head in range(OWN):
                         source = which * OWN_COLS + head * HEAD_DIM
                         target = which * D + (head * GROUP + c) * HEAD_DIM
                         in_ref[layer, :, target : target + HEAD_DIM] = got[
-                            c, :, source : source + HEAD_DIM
+                            c, layer, :, source : source + HEAD_DIM
                         ].astype(f32)
-                rows = slice(c * share, (c + 1) * share)
-                part = zone[0, rows, PACKED + LANES :].astype(f32)
-                for e in range(1, experts):
-                    part = part + zone[e, rows, PACKED + LANES :].astype(f32)
-                out_ref[layer, :, c * width : (c + 1) * width] = part
-            total = got[0, :, PACKED:].astype(f32)
+                out_ref[layer, :, c * width : (c + 1) * width] = rows_out[
+                    c * share : (c + 1) * share, :
+                ]
+            total = got[0, layer, :, PACKED:].astype(f32)
             for c in range(1, GROUP):
-                total = total + got[c, :, PACKED:].astype(f32)
+                total = total + got[c, layer, :, PACKED:].astype(f32)
             small_ref[layer] = total
 
     return whole_call(
@@ -585,7 +618,7 @@
             shape((LAYERS, share, D), f32),
             shape((LAYERS, share, LANES), f32),
         ),
-        [*inner, *outer],
+        [inner, *outer],
         name="finish_dense",
     )
 
@@ -618,10 +651,50 @@
     ).astype(bf16)
 
 
+def slot_rows(idst, capacity):
+    tokens = idst.shape[1]
+    down = lax.broadcasted_iota(jnp.int32, (tokens, tokens), 0)
+    across = lax.broadcasted_iota(jnp.int32, (tokens, tokens), 1)
+    sub = lax.broadcasted_iota(jnp.int32, (16, tokens), 0)
+    row0 = sub == idst[0:1, :]
+    row1 = sub == idst[1:2, :]
+    counts = dot(one_hot(row0 | row1), one_hot(down < across), 1, 0)
+    found = []
+    for index, row in enumerate((row0, row1)):
+        slot = jnp.sum(jnp.where(row, counts, 0.0), 0, keepdims=True).astype(jnp.int32)
+        found.append(idst[index : index + 1, :] * capacity + slot)
+    return jnp.where(lax.broadcasted_iota(jnp.int32, (8, tokens), 0) == 0, found[0], found[1])
+
+
+def send_grads(experts, capacity, idst, grad, after):
+    tokens = grad.shape[0]
+    slots = experts * capacity
+
+    def body(idst_ref, grad_ref, out_ref):
+        first, second = dispatch_grid(slot_rows(idst_ref[...], capacity), slots, tokens)
+        out_ref[...] = dot(one_hot(first | second), grad_ref[...], 1, 0).astype(bf16)
+
+    (out,) = whole_call(
+        body, [shape((slots, D), bf16)], [idst, grad], after=after, name="send_grads"
+    )
+    return out
+
+
+def apply_gates(rows, gates):
+    def body(rows_ref, gates_ref, out_ref):
+        gate = jnp.sum(gates_ref[...].astype(f32), -1, keepdims=True)
+        out_ref[...] = (gate * rows_ref[...].astype(f32)).astype(bf16)
+
+    (out,) = whole_call(
+        body, [shape(rows.shape, bf16)], [rows, gates], streamed=True, name="apply_gates"
+    )
+    return out
+
+
 def route_body(layer, experts, capacity, last, *refs):
     top = 32 * layer
     if last:
-        (x_ref, keep_ref, recv_ref, far_ref, feature_ref, ids_ref, idst_ref, grad_ref,
+        (x_ref, keep_ref, recv_ref, far_ref, feature_ref, ids_ref, idst_ref,
          middle_ref, rows_ref, soft_ref, meta_ref, dest_ref, sent_ref) = refs
     else:
         (x_ref, keep_ref, recv_ref, far_ref, feature_ref, ids_ref, idst_ref,
@@ -662,28 +735,25 @@
     for index, field in enumerate(fields):
         meta = jnp.where(lane == index, field, meta)
     meta_ref[...] = meta
-    idst = idst_ref[...]
-    sub = lax.broadcasted_iota(jnp.int32, (16, tokens), 0)
-    row0 = sub == idst[0:1, :]
-    row1 = sub == idst[1:2, :]
-    row_counts = dot(one_hot(row0 | row1), one_hot(down < across), 1, 0)
-    destr0 = idst[0:1, :] * capacity + jnp.sum(
-        jnp.where(row0, row_counts, 0.0), 0, keepdims=True
-    ).astype(jnp.int32)
-    destr1 = idst[1:2, :] * capacity + jnp.sum(
-        jnp.where(row1, row_counts, 0.0), 0, keepdims=True
-    ).astype(jnp.int32)
-    dest_rows = jnp.where(
-        lax.broadcasted_iota(jnp.int32, (8, tokens), 0) == 0, destr0, destr1
-    )
+    dest_rows = slot_rows(idst_ref[...], capacity)
     dest_ref[...] = dest_rows
     first, second = dispatch_grid(dest_rows, slots, tokens)
     rows_ref[...] = dot(one_hot(first | second), normed.astype(bf16), 1, 0).astype(bf16)
     if last:
-        sent_ref[...] = scatter_grads(grad_ref[...].astype(f32), meta, dest_rows, slots)
-
-
-def route(layer, experts, capacity, x, keep, recv, far, feature, ids, idst, grad=None):
+        total = None
+        for index, flags in enumerate((first, second)):
+            gate = meta[:, 2 + index : 3 + index]
+            spread = jnp.zeros((tokens, LANES), f32)
+            for term in range(3):
+                piece = gate.astype(bf16).astype(f32)
+                spread = jnp.where(lane == term, piece, spread)
+                gate = gate - piece
+            got = dot(one_hot(flags), spread.astype(bf16), 1, 0)
+            total = got if total is None else total + got
+        sent_ref[...] = total.astype(bf16)
+
+
+def route(layer, experts, capacity, x, keep, recv, far, feature, ids, idst, last, after=()):
     tokens = x.shape[0]
     slots = experts * capacity
     outs = [
@@ -694,14 +764,15 @@
         shape((8, tokens), jnp.int32),
     ]
     args = [x, keep, recv, far, feature, ids, idst]
-    if grad is not None:
-        outs.append(shape((slots, D), bf16))
-        args.append(grad)
+    if last:
+        outs.append(shape((slots, LANES), bf16))
 
     def body(*refs):
-        route_body(layer, experts, capacity, grad is not None, *refs)
-
-    return whole_call(body, outs, args, flops=2 * slots * tokens * D, name="route")
+        route_body(layer, experts, capacity, last, *refs)
+
+    return whole_call(
+        body, outs, args, flops=2 * slots * tokens * D, after=after, name="route"
+    )
 
 
 def combine_body(last, *refs):
@@ -784,6 +855,8 @@
         [back, came, g, middle, soft, meta, ids, feature],
         after=after,
         flops=6 * tokens * D * back.shape[0],
+        streamed=True,
+        limit=32,
         name="expert_token_back",
     )
 
@@ -806,7 +879,9 @@
         sent_ref[...] = scatter_grads(g, meta_ref[...], dest_ref[...], sent_ref.shape[0])
 
 
-def attention_token_back(layer, x, dmiddle, keep, recv, far, feature, meta=None, dest=None, slots=0):
+def attention_token_back(
+    layer, x, dmiddle, keep, recv, far, feature, meta=None, dest=None, slots=0, after=()
+):
     tokens = x.shape[0]
     outs = [shape((tokens, D), f32)]
     args = [x, dmiddle, keep, recv, far, feature]
@@ -818,7 +893,7 @@
         attention_token_back_body(layer, *refs)
 
     return whole_call(
-        body, outs, args, flops=4 * tokens * D * slots, name="attention_token_back"
+        body, outs, args, flops=4 * tokens * D * slots, after=after, name="attention_token_back"
     )
 
 
@@ -858,13 +933,19 @@
     ]
 
 
-def expert_forward(layer, rows, w_in, w_out):
+def expert_forward(layer, rows, w_in, w_out, after=()):
     count = rows.shape[0]
+
+    def body(*refs):
+        expert_forward_body(*refs[:4], *refs[4 + len(after) :])
+
     return pl.pallas_call(
-        expert_forward_body,
+        body,
         grid=(FF_STEPS,),
         out_shape=(shape((count, D), bf16), pltpu.HBM((2, count, FF), bf16)),
-        in_specs=[pl.BlockSpec((count, D), lambda s: (0, 0))] + weight_specs(layer, FF_TILE),
+        in_specs=[pl.BlockSpec((count, D), lambda s: (0, 0))]
+        + weight_specs(layer, FF_TILE)
+        + [pl.BlockSpec(memory_space=pltpu.HBM)] * len(after),
         out_specs=(
             pl.BlockSpec((count, D), lambda s: (0, 0)),
             pl.BlockSpec((2, count, FF_TILE), lambda s: (0, 0, s)),
@@ -875,7 +956,13 @@
             flops=6 * count * D * FF, bytes_accessed=6 * D * FF, transcendentals=count * FF
         ),
         name="expert_forward",
-    )(rows, far_away(w_in), far_away(w_in), far_away(w_out))
+    )(
+        rows,
+        far_away(w_in),
+        far_away(w_in),
+        far_away(w_out),
+        *[far_away(a) for a in after],
+    )
 
 
 def expert_backward_body(
@@ -1021,6 +1108,7 @@
 
 TWIN = [(i, i ^ 1) for i in range(GROUP)]
 ACROSS = [(i, i ^ 2) for i in range(GROUP)]
+FLIP = [(0, 1), (1, 0)]
 
 
 def share_pieces(piece):
@@ -1084,7 +1172,9 @@
     share = attn_in.shape[1]
     table_share = rel_table.shape[1]
     direct = share * pairs == HEAD_DIM and experts * GROUP == HEADS and pairs == 2
-    place = jnp.stack([lax.axis_index("context"), lax.axis_index("dp")]).astype(jnp.int32)
+    place = jnp.stack(
+        [lax.axis_index("context"), lax.axis_index("dp"), lax.axis_index("experts")]
+    ).astype(jnp.int32)
     start_tokens = tokens[0]
     ids = expert_ids[0]
     idst = ids.T
@@ -1105,18 +1195,27 @@
         )
 
     if direct:
-        first = gather(jnp.concatenate([spread(packets[0]), packets[2]], -1))
-        second = gather(jnp.concatenate([spread(packets[1]), packets[3]], -1))
-        w_in0, w_out0, feature, bias = unpack(place, first, hits, True)
-        w_in1, w_out1 = unpack(place, second, hits, False)
+        packet = spread(packets[0])
+        top = PACKED + LANES
+
+        def together(columns, rows_out):
+            part = jnp.concatenate([columns, rows_out], -1)
+            return lax.all_gather(part, ("experts", "dp"), axis=0, tiled=False)
+
+        first = together(packet[..., :top], packets[1])
+        w_in0, w_out0, feature, bias = unpack(place, hits, experts, pairs, 0, first)
+        second = together(packet[..., top:], packets[2])
+        w_in1, w_out1 = unpack(place, hits, experts, pairs, 1, second)
         w_in, w_out = [w_in0, w_in1], [w_out0, w_out1]
     else:
         w_in, w_out = [], []
         for layer in range(LAYERS):
-            got = gather(spread(packets[layer])).transpose(0, 2, 1, 3, 4)
+            at = layer * (PACKED + LANES)
+            part = spread(packets[0])[..., at : at + PACKED + LANES]
+            got = gather(part).transpose(0, 2, 1, 3, 4)
             w_in.append(got[..., :PACKED].reshape(D, PACKED))
             if layer == 0:
-                small_all = got[..., PACKED:]
+                small_all = got[..., PACKED : PACKED + LANES]
             full = lax.all_gather(attn_out[layer], ALL, axis=0, tiled=True)
             mine = lax.dynamic_index_in_dim(
                 full.reshape(OWN, GROUP, HEAD_DIM, D), place[0], 1, keepdims=False
@@ -1140,6 +1239,7 @@
     pieces = share_pieces(start_tokens)
     x = start_tokens
     kept = []
+    arrived_grad = exchange(send_grads(experts, capacity, idst, grad_in, [feature]))
     for layer in range(LAYERS):
         packed, log_total, mixed, keep, send, *normed_all = attention_forward(
             layer, place, pieces, w_in[layer], feature, bias, low, w_out[layer]
@@ -1148,15 +1248,19 @@
         keep, recv, far = sum_pieces(keep, send)
         last = layer == LAYERS - 1
         routed = route(
-            layer, experts, capacity, x, keep, recv, far, feature, ids, idst,
-            grad_in if last else None,
+            layer, experts, capacity, x, keep, recv, far, feature, ids, idst, last,
+            after=[arrived_grad] if layer == 0 else [],
         )
         middle, sent_rows, soft, meta, dest = routed[:5]
         arrived = exchange(sent_rows)
         if last:
-            arrived_grad = exchange(routed[5])
-        produced, acts = expert_forward(layer, arrived, expert_in, expert_out)
+            gates = exchange(routed[5])
+        produced, acts = expert_forward(
+            layer, arrived, expert_in, expert_out
+        )
         back = exchange(produced)
+        if last:
+            arrived_grad = apply_gates(arrived_grad, gates)
         kept.append(
             (x, normed_rows, packed, log_total, mixed, middle, soft, meta, dest, arrived, acts, back)
         )
@@ -1184,28 +1288,18 @@
             weight_grads, ("context", "dp"), scatter_dimension=0, tiled=False
         )
         dmiddle, dattn, small_b = expert_token_back(
-            layer, back, came, g, middle, soft, meta, ids, feature,
-            after=[weight_grads] + expert_totals,
-        )
-        early = []
-        if expert_totals:
-            early.append(place_expert_grads(layer + 1, expert_totals[0]))
-            placed_grads = early.pop()
-            early.append(placed_grads[0])
+            layer, back, came, g, middle, soft, meta, ids, feature, after=[weight_grads]
+        )
+        zones = []
+        if direct and other is not None:
+            ours = hold(keep_dense, [dattn]) + other.astype(f32)
+            zones = [exchange(ours.astype(bf16))]
         expert_totals.append(total)
-        if direct and other is not None:
-            zone = exchange((keep_dense + other.astype(f32)).astype(bf16))
-            outer.append(zone)
-            early.append(zone)
         grad_pieces = share_pieces(dattn)
         grad_packed, keep, send, by_distance, gain_a = attention_backward(
             layer, place, grad_pieces, w_in[layer], feature, bias, low, w_out[layer], packed,
-            log_total, normed_rows, after=early,
-        )
-        if direct and other is not None:
-            inner.append(
-                spread(sum_zone(zone)[:, : PACKED + LANES].astype(bf16).reshape(GROUP, share, -1))
-            )
+            log_total, normed_rows,
+        )
         keep, recv, far = sum_pieces(keep, send)
         if layer > 0:
             below = kept[layer - 1]
@@ -1214,13 +1308,30 @@
             )
             arrived_grad = exchange(sent)
         else:
-            (g,) = attention_token_back(layer, x, dmiddle, keep, recv, far, feature)
+            placed_grads = place_expert_grads(layer + 1, expert_totals[0])
+            (g,) = attention_token_back(
+                layer, x, dmiddle, keep, recv, far, feature, after=[placed_grads[0]]
+            )
         if direct:
-            keep_dense, send_dense = dense_pack(
+            keep_dense, send_dense, *rest = dense_pack(
                 experts, pairs, share, place, normed_rows, grad_pieces, grad_packed, mixed,
-                small_b, gain_a, by_distance, hits, after=inner,
+                small_b, gain_a, by_distance, hits, split=layer == 0, after=zones,
             )
-            other = lax.ppermute(send_dense, "dp", [(0, 1), (1, 0)])
+            other = lax.ppermute(send_dense, "dp", FLIP)
+            if layer == 0:
+                (zone,) = zones
+                total = sum_zone(zone)
+                flats = [total[:, : PACKED + LANES].astype(bf16)]
+                outer.append(total[:, PACKED + LANES :])
+                rest = sum_zone(exchange(rest[0]))
+                theirs = lax.ppermute(rest[1].astype(bf16), "dp", FLIP)
+                rest = rest[0] + theirs.astype(f32)
+                ours = hold(keep_dense, [g, result, placed_grads[0]]) + other.astype(f32)
+                total = sum_zone(exchange(ours.astype(bf16)))
+                flats.insert(0, jnp.concatenate([total, rest[:, :LANES]], -1).astype(bf16))
+                outer.append(rest[:, LANES:])
+                flat = jnp.stack([flat.reshape(GROUP, share, -1) for flat in flats], 1)
+                inner = spread(flat)
         else:
             grad_w_in, grad_w_out = dense_grads(normed_rows, grad_pieces, grad_packed, mixed)
             inner.append(
@@ -1231,13 +1342,8 @@
             )
     expert_grads_all = place_expert_grads(0, expert_totals[1], placed_grads)
     if direct:
-        zone = exchange((keep_dense + other.astype(f32)).astype(bf16))
-        outer.append(zone)
-        inner.append(
-            spread(sum_zone(zone)[:, : PACKED + LANES].astype(bf16).reshape(GROUP, share, -1))
-        )
         grad_attn_in, grad_attn_out, small_grad = finish_dense(
-            experts, share, inner[::-1], outer[::-1]
+            share, inner, outer[::-1]
         )
     else:
         grad_attn_in, grad_attn_out, small_grad = (

time: 772 us -> 740 us (0.959)
  waiting for transfers between devices: 303 us -> 272 us
  local copies, waits for them, and re-layouts: 69.6 us -> 48.4 us
  Pallas kernels: 228 us -> 236 us
    ppermute x2 -> x3, waiting for transfers between devices: 42 us -> 7.82 us  [the longest x2 5.11 us: on_device(): other = lax.ppermute(send_dense, 'dp', FLIP)]
    pallas_call x2 -> x8, Pallas kernels: 40 us -> 68.5 us  [the longest x2 39.5 us: expert_forward(): pl.pallas_call(body, grid=(FF_STEPS,), out_shape=(shape((count, D), bf16)...]
    ppermute x4, waiting for transfers between devices: 46.3 us -> 69.9 us  [sum_pieces(): return (keep, recv, lax.ppermute(other, 'context', ACROSS))]
    all_to_all x8 -> x10, waiting for transfers between devices: 115 us -> 94.3 us  [exchange(): lax.all_to_all(rows, 'experts', split_axis=0, concat_axis=0, tiled=True)]
    pallas_call x18 -> x14, Pallas kernels: 91.3 us -> 71.9 us  [whole_call(): pl.pallas_call(ordered, out_shape=outs, in_specs=specs, out_specs=tuple((...]
    unnamed x223 -> x199, local copies, waits for them, and re-layouts: 66.4 us -> 47.5 us
    all_to_all x8 -> x10, starting transfers between devices: 30.4 us -> 44.2 us  [exchange(): lax.all_to_all(rows, 'experts', split_axis=0, concat_axis=0, tiled=True)]
    all_to_all x3 -> x1, waiting for transfers between devices: 0.01 us -> 9.59 us  [spread(): return lax.all_to_all(packet, 'context', split_axis=0, concat_axis=0)]
  transfers between devices with their start and end apart: 37 -> 38, of which waited for: 22 -> 23; matrix products, arithmetic and copies ran while one was open for 2% -> 2% of each run, Pallas kernels for 26% -> 30%
where the time goes in v3:
time: 740 us; the launch traced here: 726 us
  waiting for transfers between devices  272 us (37%)
  Pallas kernels  236 us (32%)
  blocking collectives  79.4 us (11%)
  starting transfers between devices  60.2 us (8%)
  local copies, waits for them, and re-layouts  48.4 us (7%)
  other arithmetic  15.1 us (2%)
  between operations  15 us (2%)
    all_to_all x10, waiting for transfers between devices, exchange(): lax.all_to_all(rows, 'experts', split_axis=0, concat_axis=0, tiled=True)  94.3 us
    pallas_call x14, Pallas kernels, whole_call(): pl.pallas_call(ordered, out_shape=outs, in_specs=specs, out_specs=tuple((...  71.9 us
    ppermute x4, waiting for transfers between devices, sum_pieces(): return (keep, recv, lax.ppermute(other, 'context', ACROSS))  69.9 us
    all_to_all x2, blocking collectives, exchange(): lax.all_to_all(rows, 'experts', split_axis=0, concat_axis=0, tiled=True)  67.5 us
    unnamed x199, local copies, waits for them, and re-layouts  47.5 us
    pallas_call x2, Pallas kernels, expert_backward(): pl.pallas_call(body, grid=(BACK_STEPS,), out_shape=(shape((count, D), bf1...  47.4 us
    all_to_all x10, starting transfers between devices, exchange(): lax.all_to_all(rows, 'experts', split_axis=0, concat_axis=0, tiled=True)  44.2 us
    pallas_call x2, Pallas kernels, expert_grads(): pl.pallas_call(body, grid=(FF_STEPS,), out_shape=pltpu.HBM((shares, 3, ta...  41.4 us
  transfers between devices with their start and end apart: 38, of which 23 were waited for; matrix products, arithmetic and copies ran while one was open for 2% of the time, Pallas kernels for 30%

profile of v3, /device:TPU:0, one launch (start us, length us, event | category | flops | bytes accessed | tf_op | source)
XLA Modules:
  0.0 726.1 jit_solution(1400206169138774128)
XLA Ops:
  11.5 11.8 %all_to_all.124 = bf16[4,32,1664]{2,1,0:T(8,128)(2,1)S(1)} all-to-all(bf16[4,32,1664]{2,1,0:T(8,128)(2,1)S(1)} %get-tuple-element.79), channel_id=1, replica_groups=mesh['experts'=4,'context'=4,'dp'=2] {'context'}, dimensions={0} | all-to-all | bytes 851968 | tf_op jit(solution)/shard_map/all_to_all | solution.py:1190
  25.3 13.4 %collective-permute-done.1.refs_3_ = bf16[256,1024]{1,0:T(8,128)(2,1)S(1)} collective-permute-done((bf16[256,1024]{1,0:T(8,128)(2,1)S(1)}, bf16[256,1024]{1,0:T(8,128)(2,1)S(1)}, u32[]{:S(2)}, u32[]{:S(2)}) %collective-permute-start.1) | collective-permute-done | bytes 524320 | tf_op jit(solution)/shard_map/ppermute | solution.py:1115
  39.1 38.3 %all-gather.5.cloned.1.call-done = bf16[32,32,1152]{2,1,0:T(8,128)(2,1)} async-done(((bf16[4,32,1152]{2,1,0:T(8,128)(2,1)}), bf16[32,32,1152]{2,1,0:T(8,128)(2,1)}) %all-gather.5.cloned.1.call-update) | async-done | bytes 2359312 | tf_op jit(solution)/shard_map/all_gather | solution.py:1203
  94.5 9.9 %attention_forward.2 = (bf16[1024,768]{1,0:T(8,128)(2,1)S(1)}, f32[8,1024]{1,0:T(8,128)S(1)}, bf16[1024,256]{1,0:T(8,128)(2,1)S(1)}, f32[512,1024]{1,0:T(8,128)S...) custom-call(s32[3]{0:T(128)S(1)} %pad_add_fusion.refs_0_, bf16[256,1024]{1,0:T(8,128)(2,1)S(1)} %bitcast.72, ...), custom_call_target="tpu_custom_call" | custom-call | flops 3221225472 | bytes 12128268 | tf_op jit(solution)/shard_map/attention_forward/pallas_call | solution.py:95
  112.2 12.5 %collective-permute-done.4.refs_3_ = bf16[256,1024]{1,0:T(8,128)(2,1)S(1)} collective-permute-done((bf16[256,1024]{1,0:T(8,128)(2,1)S(1)}, bf16[256,1024]{1,0:T(8,128)(2,1)S(1)}, u32[]{:S(2)}, u32[]{:S(2)}) %collective-permute-start.4) | collective-permute-done | bytes 524320 | tf_op jit(solution)/shard_map/ppermute | solution.py:1124
  138.3 38.5 %all-to-all-done.2 = bf16[4,160,1024]{2,1,0:T(8,128)(2,1)S(1)} async-done(((bf16[4,160,1024]{2,1,0:T(8,128)(2,1)}), bf16[4,160,1024]{2,1,0:T(8,128)(2,1)S(1)}, u32[]{:S(2)}, u32[]{:S(2)}) %all-to-all-start.2) | async-done | bytes 1310752 | tf_op jit(solution)/shard_map/all_to_all | solution.py:1163
  176.8 19.8 %expert_forward.2 = (bf16[640,1024]{1,0:T(8,128)(2,1)S(1)}, bf16[2,640,2816]{2,1,0:T(8,128)(2,1)}) custom-call(bf16[640,1024]{1,0:T(8,128)(2,1)S(1)} %bitcast.55, bf16[2,1,1024,5632]{3,2,1,0:T(8,128)(2,1)} %refs_3_.8, bf16[2,1,1024,5632]{3,2,1,0:T(8,128)(2,1)} %refs_3_.8, bf16[2,1,1024,2816]{3,2,1,0:T(8,128)(2,1)} %refs_4_.5), custom_call_target="tpu_custom_call" | custom-call | flops 11072962560 | bytes 17301504 | tf_op jit(solution)/shard_map/expert_forward/pallas_call | solution.py:942
  196.6 33.3 %all_to_all.125 = bf16[4,160,1024]{2,1,0:T(8,128)(2,1)S(1)} all-to-all(bf16[4,160,1024]{2,1,0:T(8,128)(2,1)S(1)} %bitcast.79), channel_id=1, replica_groups=mesh['experts'=4,'context'=4,'dp'=2] {'experts'}, dimensions={0} | all-to-all | bytes 2621440 | tf_op jit(solution)/shard_map/all_to_all | solution.py:1163
  234.3 11.3 %collective-permute-done.6.refs_3_.refs_14_ = bf16[256,1024]{1,0:T(8,128)(2,1)} collective-permute-done((bf16[256,1024]{1,0:T(8,128)(2,1)}, bf16[256,1024]{1,0:T(8,128)(2,1)}, u32[]{:S(2)}, u32[]{:S(2)}) %collective-permute-start.6) | collective-permute-done | bytes 524320 | tf_op jit(solution)/shard_map/ppermute | solution.py:1115
  248.0 11.5 %attention_forward.3 = (bf16[1024,768]{1,0:T(8,128)(2,1)S(1)}, f32[8,1024]{1,0:T(8,128)S(1)}, bf16[1024,256]{1,0:T(8,128)(2,1)S(1)}, f32[512,1024]{1,0:T(8,128)S(1)}, bf16[512,1024]{1,0:T(8,128)(2,1)S(1)}) custom-call(s32[3]{0:T(128)S(1)} %pad_add_fusion.refs_0_, bf16[256,1024]{1,0:T(8,128)(2,1)} %get-tuple-element.92.refs_1_.refs_12_, ...), custom_call_target="tpu_custom_call" | custom-call | flops 3221225472 | bytes 10031116 | tf_op jit(solution)/shard_map/attention_forward/pallas_call | solution.py:95
  264.0 12.8 %collective-permute-done.9.refs_3_ = bf16[256,1024]{1,0:T(8,128)(2,1)S(1)} collective-permute-done((bf16[256,1024]{1,0:T(8,128)(2,1)S(1)}, bf16[256,1024]{1,0:T(8,128)(2,1)S(1)}, u32[]{:S(2)}, u32[]{:S(2)}) %collective-permute-start.9) | collective-permute-done | bytes 524320 | tf_op jit(solution)/shard_map/ppermute | solution.py:1124
  281.4 34.3 %all_to_all.126 = bf16[4,160,1024]{2,1,0:T(8,128)(2,1)S(1)} all-to-all(bf16[4,160,1024]{2,1,0:T(8,128)(2,1)S(1)} %bitcast.78), channel_id=1, replica_groups=mesh['experts'=4,'context'=4,'dp'=2] {'experts'}, dimensions={0} | all-to-all | bytes 2621440 | tf_op jit(solution)/shard_map/all_to_all | solution.py:1163
  319.0 19.7 %expert_forward.3 = (bf16[640,1024]{1,0:T(8,128)(2,1)S(1)}, bf16[2,640,2816]{2,1,0:T(8,128)(2,1)}) custom-call(bf16[640,1024]{1,0:T(8,128)(2,1)S(1)} %bitcast.59, bf16[2,1,1024,5632]{3,2,1,0:T(8,128)(2,1)} %refs_3_.8, bf16[2,1,1024,5632]{3,2,1,0:T(8,128)(2,1)} %refs_3_.8, bf16[2,1,1024,2816]{3,2,1,0:T(8,128)(2,1)} %refs_4_.5), custom_call_target="tpu_custom_call" | custom-call | flops 11072962560 | bytes 17301504 | tf_op jit(solution)/shard_map/expert_forward/pallas_call | solution.py:942
  347.5 24.0 %expert_backward.2 = (bf16[640,1024]{1,0:T(8,128)(2,1)}, bf16[3,640,2816]{2,1,0:T(8,128)(2,1)}) custom-call(bf16[640,1024]{1,0:T(8,128)(2,1)} %copy-done.13, bf16[2,640,2816]{2,1,0:T(8,128)(2,1)} %get-tuple-element.103.refs_1_, bf16[2,1,1024,5632]{3,2,1,0:T(8,128)(2,1)} %refs_3_.8, bf16[2,1,1024,5632]{3,2,1,0:T(8,128)(2,1)} %refs_3_.8, ...), custom_call_target="tpu_custom_call" | custom-call | flops 11072962560 | bytes 17301504 | tf_op jit(solution)/shard_map/expert_backward/pallas_call | solution.py:1006
  381.7 20.7 %expert_grads.2.refs_0_ = bf16[8,3,128,2816]{3,2,1,0:T(8,128)(2,1)} custom-call(bf16[640,1024]{1,0:T(8,128)(2,1)S(1)} %bitcast.60, bf16[640,1024]{1,0:T(8,128)(2,1)S(1)} %copy-done.14, bf16[3,640,2816]{2,1,0:T(8,128)(2,1)} %get-tuple-element.106.refs_2_, bf16[640,1024]{1,0:T(8,128)(2,1)} %bitcast.52), custom_call_target="tpu_custom_call" | custom-call | flops 11072962560 | bytes 17301504 | tf_op jit(solution)/shard_map/expert_grads/pallas_call | solution.py:1057
  402.4 7.5 %all-to-all-done.7 = bf16[4,160,1024]{2,1,0:T(8,128)(2,1)} async-done(((bf16[4,160,1024]{2,1,0:T(8,128)(2,1)}), bf16[4,160,1024]{2,1,0:T(8,128)(2,1)}, u32[]{:S(2)}, u32[]{:S(2)}) %all-to-all-start.7) | async-done | bytes 1310752 | tf_op jit(solution)/shard_map/all_to_all | solution.py:1163
  410.0 6.2 expert_token_back.2
  417.8 11.4 %collective-permute-done.11.refs_3_.refs_7_ = bf16[256,1024]{1,0:T(8,128)(2,1)S(1)} collective-permute-done((bf16[256,1024]{1,0:T(8,128)(2,1)S(1)}, bf16[256,1024]{1,0:T(8,128)(2,1)S(1)}, u32[]{:S(2)}, u32[]{:S(2)}) %collective-permute-start.11) | collective-permute-done | bytes 524320 | tf_op jit(solution)/shard_map/ppermute | solution.py:1115
  431.8 16.5 %attention_backward.2 = (bf16[1024,768]{1,0:T(8,128)(2,1)S(1)}, f32[512,1024]{1,0:T(8,128)S(1)}, bf16[512,1024]{1,0:T(8,128)(2,1)S(1)}, f32[8,512]{1,0:T(8,128)S(1)}, f32[8,1024]{1,0:T(8,128)S(1)}) custom-call(s32[3]{0:T(128)S(1)} %pad_add_fusion.refs_0_, bf16[256,1024]{1,0:T(8,128)(2,1)S(1)} %get-tuple-element.108.refs_1_.refs_5_, ...), custom_call_target="tpu_custom_call" | custom-call | flops 4831838208 | bytes 13225996 | tf_op jit(solution)/shard_map/attention_backward/pallas_call | solution.py:95
  452.1 24.9 %collective-permute-done.14.refs_4_ = bf16[256,1024]{1,0:T(8,128)(2,1)S(1)} collective-permute-done((bf16[256,1024]{1,0:T(8,128)(2,1)S(1)}, bf16[256,1024]{1,0:T(8,128)(2,1)S(1)}, u32[]{:S(2)}, u32[]{:S(2)}) %collective-permute-start.14) | collective-permute-done | bytes 524320 | tf_op jit(solution)/shard_map/ppermute | solution.py:1124
  484.4 6.9 dense_pack.2
  492.7 22.9 %all-to-all-done.8 = bf16[4,160,1024]{2,1,0:T(8,128)(2,1)S(1)} async-done(((bf16[4,160,1024]{2,1,0:T(8,128)(2,1)}), bf16[4,160,1024]{2,1,0:T(8,128)(2,1)S(1)}, u32[]{:S(2)}, u32[]{:S(2)}) %all-to-all-start.8) | async-done | bytes 1310752 | tf_op jit(solution)/shard_map/all_to_all | solution.py:1163
  516.6 23.3 %expert_backward.3 = (bf16[640,1024]{1,0:T(8,128)(2,1)}, bf16[3,640,2816]{2,1,0:T(8,128)(2,1)}) custom-call(bf16[640,1024]{1,0:T(8,128)(2,1)} %bitcast.57, bf16[2,640,2816]{2,1,0:T(8,128)(2,1)} %get-tuple-element.115.refs_1_, bf16[2,1,1024,5632]{3,2,1,0:T(8,128)(2,1)} %refs_3_.8, bf16[2,1,1024,5632]{3,2,1,0:T(8,128)(2,1)} %refs_3_.8, ...), custom_call_target="tpu_custom_call" | custom-call | flops 11072962560 | bytes 17301504 | tf_op jit(solution)/shard_map/expert_backward/pallas_call | solution.py:1006
  544.5 20.7 %expert_grads.3.refs_0_ = bf16[8,3,128,2816]{3,2,1,0:T(8,128)(2,1)} custom-call(bf16[640,1024]{1,0:T(8,128)(2,1)S(1)} %bitcast.56, bf16[640,1024]{1,0:T(8,128)(2,1)S(1)} %bitcast.58, bf16[3,640,2816]{2,1,0:T(8,128)(2,1)} %get-tuple-element.119.refs_2_, bf16[640,1024]{1,0:T(8,128)(2,1)} %bitcast.50, bf16[4,128,1152]{2,1,0:T(8,128)(2,1)} %collective-permute-done.15.refs_4_), custom_call_target="tpu_custom_call" | custom-call | flops 11072962560 | bytes 17301504 | tf_op jit(solution)/shard_map/expert_grads/pallas_call | solution.py:1057
  565.2 10.0 %all-to-all-done.9 = bf16[4,160,1024]{2,1,0:T(8,128)(2,1)} async-done(((bf16[4,160,1024]{2,1,0:T(8,128)(2,1)}), bf16[4,160,1024]{2,1,0:T(8,128)(2,1)}, u32[]{:S(2)}, u32[]{:S(2)}) %all-to-all-start.9) | async-done | bytes 1310752 | tf_op jit(solution)/shard_map/all_to_all | solution.py:1163
  575.2 7.0 expert_token_back.3
  601.0 15.8 %attention_backward.3 = (bf16[1024,768]{1,0:T(8,128)(2,1)S(1)}, f32[512,1024]{1,0:T(8,128)S(1)}, bf16[512,1024]{1,0:T(8,128)(2,1)}, f32[8,512]{1,0:T(8,128)S(1)}, f32[8,1024]{1,0:T(8,128)S(1)}) custom-call(s32[3]{0:T(128)S(1)} %pad_add_fusion.refs_0_, bf16[256,1024]{1,0:T(8,128)(2,1)} %get-tuple-element.127.refs_1_.refs_2_, ...), custom_call_target="tpu_custom_call" | custom-call | flops 4831838208 | bytes 13225996 | tf_op jit(solution)/shard_map/attention_backward/pallas_call | solution.py:95
  620.8 5.9 dense_pack.3
  643.8 19.7 %collective-permute-done.20.refs_4_ = bf16[256,1024]{1,0:T(8,128)(2,1)S(1)} collective-permute-done((bf16[256,1024]{1,0:T(8,128)(2,1)}, bf16[256,1024]{1,0:T(8,128)(2,1)S(1)}, u32[]{:S(2)}, u32[]{:S(2)}) %collective-permute-start.20) | collective-permute-done | bytes 524320 | tf_op jit(solution)/shard_map/ppermute | solution.py:1124
  666.3 5.1 collective-permute-done.21
  686.2 12.3 %all-to-all-done.11 = bf16[4,128,768]{2,1,0:T(8,128)(2,1)S(1)} async-done(((bf16[4,128,768]{2,1,0:T(8,128)(2,1)}), bf16[4,128,768]{2,1,0:T(8,128)(2,1)S(1)}, u32[]{:S(2)}, u32[]{:S(2)}) %all-to-all-start.11) | async-done | bytes 786464 | tf_op jit(solution)/shard_map/all_to_all | solution.py:1163
  702.9 9.6 %all-to-all-done.13.refs_0_ = bf16[4,2,32,896]{3,2,1,0:T(8,128)(2,1)S(1)} async-done(((bf16[4,2,32,896]{3,2,1,0:T(8,128)(2,1)}), bf16[4,2,32,896]{3,2,1,0:T(8,128)(2,1)S(1)}, u32[]{:S(2)}, u32[]{:S(2)}) %all-to-all-start.13) | async-done | bytes 458784 | tf_op jit(solution)/shard_map/all_to_all | solution.py:1190
  (308 shorter events, 173.5 us)
Async XLA Ops:
  7.2 70.2 %all-gather.5.cloned.1.call-start = ((), (), s32[]{:S(2)}) async-start(), calls=%async_computation.18 | async-start | bytes 2654208 | tf_op jit(solution)/shard_map/all_gather | solution.py:1203
  24.8 13.8 %collective-permute-start.1 = (bf16[256,1024]{1,0:T(8,128)(2,1)S(1)}, bf16[256,1024]{1,0:T(8,128)(2,1)S(1)}, u32[]{:S(2)}, u32[]{:S(2)}) collective-permute-start(bf16[256,1024]{1,0:T(8,128)(2,1)S(1)} %bitcast.70), channel_id=1, source_target_pairs={{0,4},{2,6},{4,0},{6,2},{1,5},{3,7},{5,1},{7,3},{8,12},{10,14},{12... | collective-permute-start | bytes 1572872 | tf_op jit(solution)/shard_map/ppermute | solution.py:1115
  25.3 62.0 %collective-permute-start = (bf16[256,1024]{1,0:T(8,128)(2,1)S(1)}, bf16[256,1024]{1,0:T(8,128)(2,1)S(1)}, u32[]{:S(2)}, u32[]{:S(2)}) collective-permute-start(bf16[256,1024]{1,0:T(8,128)(2,1)S(1)} %bitcast.71), channel_id=1, source_target_pairs={{0,2},{2,0},{4,6},{6,4},{1,3},{3,1},{5,7},{7,5},{8,10},{10,8},{12,... | collective-permute-start | bytes 1572872 | tf_op jit(solution)/shard_map/ppermute | solution.py:1116
  38.7 49.4 %collective-permute-start.2 = (bf16[256,1024]{1,0:T(8,128)(2,1)S(1)}, bf16[256,1024]{1,0:T(8,128)(2,1)S(1)}, u32[]{:S(2)}, u32[]{:S(2)}) collective-permute-start(bf16[256,1024]{1,0:T(8,128)(2,1)S(1)} %collective-permute-done.1.refs_3_), channel_id=1, source_target_pairs={{0,2},{2,0},{4,6},{6,4},{1,3},{3,1},{5,7},{7,5},{8,10},{10,8},{12,... | collective-permute-start | bytes 1572872 | tf_op jit(solution)/shard_map/ppermute | solution.py:1117
  82.8 42.7 %all-to-all-start.1 = ((bf16[4,160,1024]{2,1,0:T(8,128)(2,1)}), bf16[4,160,1024]{2,1,0:T(8,128)(2,1)}, u32[]{:S(2)}, u32[]{:S(2)}) async-start(bf16[4,160,1024]{2,1,0:T(8,128)(2,1)} %bitcast.10), calls=%async_computation.1 | async-start | bytes 2621440 | tf_op jit(solution)/shard_map/all_to_all | solution.py:1163
  110.8 14.0 %collective-permute-start.4 = (bf16[256,1024]{1,0:T(8,128)(2,1)S(1)}, bf16[256,1024]{1,0:T(8,128)(2,1)S(1)}, u32[]{:S(2)}, u32[]{:S(2)}) collective-permute-start(bf16[256,1024]{1,0:T(8,128)(2,1)S(1)} %add_convert_fusion.5), channel_id=1, source_target_pairs={{0,4},{2,6},{4,0},{6,2},{1,5},{3,7},{5,1},{7,3},{8,12},{10,14},{12... | collective-permute-start | bytes 1572872 | tf_op jit(solution)/shard_map/ppermute | solution.py:1124
  132.5 44.3 %all-to-all-start.2 = ((bf16[4,160,1024]{2,1,0:T(8,128)(2,1)}), bf16[4,160,1024]{2,1,0:T(8,128)(2,1)S(1)}, u32[]{:S(2)}, u32[]{:S(2)}) async-start(bf16[4,160,1024]{2,1,0:T(8,128)(2,1)} %bitcast.76), calls=%async_computation.2 | async-start | bytes 2621440 | tf_op jit(solution)/shard_map/all_to_all | solution.py:1163
  137.5 108.1 %all-gather.7.cloned.1.call-start = ((), (), s32[]{:S(2)}) async-start(), calls=%async_computation.19 | async-start | bytes 2359296 | tf_op jit(solution)/shard_map/all_gather | solution.py:1203
  232.8 12.8 %collective-permute-start.6 = (bf16[256,1024]{1,0:T(8,128)(2,1)}, bf16[256,1024]{1,0:T(8,128)(2,1)}, u32[]{:S(2)}, u32[]{:S(2)}) collective-permute-start(bf16[256,1024]{1,0:T(8,128)(2,1)} %get-tuple-element.92.refs_1_.refs_12_), channel_id=1, source_target_pairs={{0,4},{2,6},{4,0},{6,2},{1,5},{3,7},{5,1},{7,3},{8,12},{10,14},{12... | collective-permute-start | bytes 1572872 | tf_op jit(solution)/shard_map/ppermute | solution.py:1115
  234.3 13.7 %collective-permute-start.5 = (bf16[256,1024]{1,0:T(8,128)(2,1)}, bf16[256,1024]{1,0:T(8,128)(2,1)}, u32[]{:S(2)}, u32[]{:S(2)}) collective-permute-start(bf16[256,1024]{1,0:T(8,128)(2,1)} %get-tuple-element.92.refs_1_.refs_12_), channel_id=1, source_target_pairs={{0,2},{2,0},{4,6},{6,4},{1,3},{3,1},{5,7},{7,5},{8,10},{10,8},{12,... | collective-permute-start | bytes 1572872 | tf_op jit(solution)/shard_map/ppermute | solution.py:1116
  262.5 14.3 %collective-permute-start.9 = (bf16[256,1024]{1,0:T(8,128)(2,1)S(1)}, bf16[256,1024]{1,0:T(8,128)(2,1)S(1)}, u32[]{:S(2)}, u32[]{:S(2)}) collective-permute-start(bf16[256,1024]{1,0:T(8,128)(2,1)S(1)} %add_convert_fusion.4), channel_id=1, source_target_pairs={{0,4},{2,6},{4,0},{6,2},{1,5},{3,7},{5,1},{7,3},{8,12},{10,14},{12... | collective-permute-start | bytes 1572872 | tf_op jit(solution)/shard_map/ppermute | solution.py:1124
  315.7 24.2 %all-to-all-start.6 = ((bf16[4,160,128]{2,1,0:T(8,128)(2,1)}), bf16[4,160,128]{2,1,0:T(8,128)(2,1)S(1)}, u32[]{:S(2)}, u32[]{:S(2)}) async-start(bf16[4,160,128]{2,1,0:T(8,128)(2,1)} %bitcast.22), calls=%async_computation.6 | async-start | bytes 327680 | tf_op jit(solution)/shard_map/all_to_all | solution.py:1163
  339.8 34.9 %all-to-all-start.5 = ((bf16[4,160,1024]{2,1,0:T(8,128)(2,1)}), bf16[4,160,1024]{2,1,0:T(8,128)(2,1)S(1)}, u32[]{:S(2)}, u32[]{:S(2)}) async-start(bf16[4,160,1024]{2,1,0:T(8,128)(2,1)} %bitcast.77), calls=%async_computation.5 | async-start | bytes 2621440 | tf_op jit(solution)/shard_map/all_to_all | solution.py:1163
  374.7 35.2 %all-to-all-start.7 = ((bf16[4,160,1024]{2,1,0:T(8,128)(2,1)}), bf16[4,160,1024]{2,1,0:T(8,128)(2,1)}, u32[]{:S(2)}, u32[]{:S(2)}) async-start(bf16[4,160,1024]{2,1,0:T(8,128)(2,1)} %bitcast.91), calls=%async_computation.7 | async-start | bytes 2621440 | tf_op jit(solution)/shard_map/all_to_all | solution.py:1163
  379.0 261.0 %reduce-scatter.3.cloned.1.call-start = ((), (), s32[]{:S(2)}) async-start(), calls=%async_computation.16 | async-start | bytes 19464192 | tf_op jit(solution)/shard_map/reduce_scatter | solution.py:1287
  416.3 12.9 %collective-permute-start.11 = (bf16[256,1024]{1,0:T(8,128)(2,1)S(1)}, bf16[256,1024]{1,0:T(8,128)(2,1)S(1)}, u32[]{:S(2)}, u32[]{:S(2)}) collective-permute-start(bf16[256,1024]{1,0:T(8,128)(2,1)S(1)} %get-tuple-element.108.refs_1_.refs_5_), channel_id=1, source_target_pairs={{0,4},{2,6},{4,0},{6,2},{1,5},{3,7},{5,1},{7,3},{8,12},{10,14},{12... | collective-permute-start | bytes 1572872 | tf_op jit(solution)/shard_map/ppermute | solution.py:1115
  417.8 11.4 %collective-permute-start.10 = (bf16[256,1024]{1,0:T(8,128)(2,1)S(1)}, bf16[256,1024]{1,0:T(8,128)(2,1)S(1)}, u32[]{:S(2)}, u32[]{:S(2)}) collective-permute-start(bf16[256,1024]{1,0:T(8,128)(2,1)S(1)} %get-tuple-element.108.refs_1_.refs_5_), channel_id=1, source_target_pairs={{0,2},{2,0},{4,6},{6,4},{1,3},{3,1},{5,7},{7,5},{8,10},{10,8},{12,... | collective-permute-start | bytes 1572872 | tf_op jit(solution)/shard_map/ppermute | solution.py:1116
  451.2 25.8 %collective-permute-start.14 = (bf16[256,1024]{1,0:T(8,128)(2,1)S(1)}, bf16[256,1024]{1,0:T(8,128)(2,1)S(1)}, u32[]{:S(2)}, u32[]{:S(2)}) collective-permute-start(bf16[256,1024]{1,0:T(8,128)(2,1)S(1)} %add_convert_fusion.3), channel_id=1, source_target_pairs={{0,4},{2,6},{4,0},{6,2},{1,5},{3,7},{5,1},{7,3},{8,12},{10,14},{12... | collective-permute-start | bytes 1572872 | tf_op jit(solution)/shard_map/ppermute | solution.py:1124
  480.6 34.9 %all-to-all-start.8 = ((bf16[4,160,1024]{2,1,0:T(8,128)(2,1)}), bf16[4,160,1024]{2,1,0:T(8,128)(2,1)S(1)}, u32[]{:S(2)}, u32[]{:S(2)}) async-start(bf16[4,160,1024]{2,1,0:T(8,128)(2,1)} %bitcast.75), calls=%async_computation.8 | async-start | bytes 2621440 | tf_op jit(solution)/shard_map/all_to_all | solution.py:1163
  492.7 51.8 %collective-permute-start.15 = (bf16[4,128,1152]{2,1,0:T(8,128)(2,1)}, bf16[4,128,1152]{2,1,0:T(8,128)(2,1)}, u32[]{:S(2)}, u32[]{:S(2)}) collective-permute-start(bf16[4,128,1152]{2,1,0:T(8,128)(2,1)} %get-tuple-element.125), channel_id=1, source_target_pairs={{0,1},{1,0},{2,3},{3,2},{4,5},{5,4},{6,7},{7,6},{8,9},{9,8},{10,11... | collective-permute-start | bytes 3538952 | tf_op jit(solution)/shard_map/ppermute | solution.py:1320
  539.9 35.3 %all-to-all-start.9 = ((bf16[4,160,1024]{2,1,0:T(8,128)(2,1)}), bf16[4,160,1024]{2,1,0:T(8,128)(2,1)}, u32[]{:S(2)}, u32[]{:S(2)}) async-start(bf16[4,160,1024]{2,1,0:T(8,128)(2,1)} %bitcast.92), calls=%async_computation.9 | async-start | bytes 2621440 | tf_op jit(solution)/shard_map/all_to_all | solution.py:1163
  544.4 171.3 %reduce-scatter.5.cloned.1.call-start = ((), (), s32[]{:S(2)}) async-start(), calls=%async_computation.17 | async-start | bytes 19464192 | tf_op jit(solution)/shard_map/reduce_scatter | solution.py:1287
  582.3 13.1 %collective-permute-start.17 = (bf16[256,1024]{1,0:T(8,128)(2,1)}, bf16[256,1024]{1,0:T(8,128)(2,1)S(1)}, u32[]{:S(2)}, u32[]{:S(2)}) collective-permute-start(bf16[256,1024]{1,0:T(8,128)(2,1)} %get-tuple-element.127.refs_1_.refs_2_), channel_id=1, source_target_pairs={{0,4},{2,6},{4,0},{6,2},{1,5},{3,7},{5,1},{7,3},{8,12},{10,14},{12... | collective-permute-start | bytes 1572872 | tf_op jit(solution)/shard_map/ppermute | solution.py:1115
  587.3 33.5 %all-to-all-start.10 = ((bf16[4,128,1152]{2,1,0:T(8,128)(2,1)}), bf16[4,128,1152]{2,1,0:T(8,128)(2,1)}, u32[]{:S(2)}, u32[]{:S(2)}) async-start(bf16[4,128,1152]{2,1,0:T(8,128)(2,1)} %add_convert_fusion), calls=%async_computation.11 | async-start | bytes 2359296 | tf_op jit(solution)/shard_map/all_to_all | solution.py:1163
  591.8 3.5 collective-permute-start.16
  620.5 14.7 %collective-permute-start.19 = (bf16[512,1024]{1,0:T(8,128)(2,1)}, bf16[512,1024]{1,0:T(8,128)(2,1)}, u32[]{:S(2)}, u32[]{:S(2)}) collective-permute-start(bf16[512,1024]{1,0:T(8,128)(2,1)} %get-tuple-element.132), channel_id=1, source_target_pairs={{0,2},{2,0},{4,6},{6,4},{1,3},{3,1},{5,7},{7,5},{8,10},{10,8},{12,... | collective-permute-start | bytes 3145736 | tf_op jit(solution)/shard_map/ppermute | solution.py:1122
  629.7 44.4 %all-to-all-start.12 = ((bf16[4,2,128,384]{3,2,1,0:T(8,128)(2,1)}), bf16[4,2,128,384]{3,2,1,0:T(8,128)(2,1)}, u32[]{:S(2)}, u32[]{:S(2)}) async-start(bf16[4,2,128,384]{3,2,1,0:T(8,128)(2,1)} %copy-done.39), calls=%async_computation.13 | async-start | bytes 1572864 | tf_op jit(solution)/shard_map/all_to_all | solution.py:1163
  634.0 37.4 %collective-permute-start.21 = (bf16[4,128,768]{2,1,0:T(8,128)(2,1)}, bf16[4,128,768]{2,1,0:T(8,128)(2,1)}, u32[]{:S(2)}, u32[]{:S(2)}) collective-permute-start(bf16[4,128,768]{2,1,0:T(8,128)(2,1)} %copy-done.54), channel_id=1, source_target_pairs={{0,1},{1,0},{2,3},{3,2},{4,5},{5,4},{6,7},{7,6},{8,9},{9,8},{10,11... | collective-permute-start | bytes 2359304 | tf_op jit(solution)/shard_map/ppermute | solution.py:1320
  637.5 26.0 %collective-permute-start.20 = (bf16[256,1024]{1,0:T(8,128)(2,1)}, bf16[256,1024]{1,0:T(8,128)(2,1)S(1)}, u32[]{:S(2)}, u32[]{:S(2)}) collective-permute-start(bf16[256,1024]{1,0:T(8,128)(2,1)} %add_convert_fusion.2), channel_id=1, source_target_pairs={{0,4},{2,6},{4,0},{6,2},{1,5},{3,7},{5,1},{7,3},{8,12},{10,14},{12... | collective-permute-start | bytes 1572872 | tf_op jit(solution)/shard_map/ppermute | solution.py:1124
  674.1 24.4 %all-to-all-start.11 = ((bf16[4,128,768]{2,1,0:T(8,128)(2,1)}), bf16[4,128,768]{2,1,0:T(8,128)(2,1)S(1)}, u32[]{:S(2)}, u32[]{:S(2)}) async-start(bf16[4,128,768]{2,1,0:T(8,128)(2,1)} %add_convert_fusion.1), calls=%async_computation.12 | async-start | bytes 1572864 | tf_op jit(solution)/shard_map/all_to_all | solution.py:1163
  680.3 5.9 collective-permute-start.22
  699.4 13.1 %all-to-all-start.13 = ((bf16[4,2,32,896]{3,2,1,0:T(8,128)(2,1)}), bf16[4,2,32,896]{3,2,1,0:T(8,128)(2,1)S(1)}, u32[]{:S(2)}, u32[]{:S(2)}) async-start(bf16[4,2,32,896]{3,2,1,0:T(8,128)(2,1)} %pad_maximum_fusion), calls=%async_computation.14 | async-start | bytes 917504 | tf_op jit(solution)/shard_map/all_to_all | solution.py:1190
  (104 other events, 1774.1 us)
Sparse Core Ops, SparseCore 0:
  25.0 52.3 all-gather.4
  141.1 59.3 all-gather.6
  410.1 138.7 reduce-scatter.2
  575.4 135.2 reduce-scatter.4

commit v4 on v3

--- a/solution.py
+++ b/solution.py
@@ -27,8 +27,9 @@
 REACH = 512
 FF_TILE = 256
 FF_STEPS = FF // FF_TILE
-BACK_TILE = 1408
-BACK_STEPS = FF // BACK_TILE
+WIDE_TILE = FF // 2
+EARLY_COLS = 512
+ROWS_HINT = 320
 MIB = 1 << 20
 
 bf16 = jnp.bfloat16
@@ -515,8 +516,9 @@
     rows = upstream[0].shape[0]
     count = len(normed)
     width = D // GROUP
-    rest = LANES + width
-    total = PACKED if split else PACKED + rest
+    cut = EARLY_COLS if split else PACKED
+    rest = PACKED - cut + LANES + width
+    total = cut if split else PACKED + rest
 
     def body(place_ref, *refs):
         grad_packed_ref, mixed_ref, small_ref, gain_ref, distance_ref, hits_ref = refs[
@@ -552,12 +554,14 @@
                     span = pl.ds(pl.multiple_of(at, share), share)
                     to = slice(c * share, (c + 1) * share)
                     target = outs[side]
-                    target[e, to, :PACKED] = in_ref[span, :].astype(target.dtype)
+                    target[e, to, :cut] = in_ref[span, :cut].astype(target.dtype)
                     out_span = pl.ds(pl.multiple_of((e * pairs + d) * share, share), share)
                     outer = out_ref[out_span, c * width : (c + 1) * width]
                     if split:
-                        outs[2][e, side, to, :LANES] = flat_ref[span, :].astype(bf16)
-                        outs[2][e, side, to, LANES:] = outer.astype(bf16)
+                        more = PACKED - cut
+                        outs[2][e, side, to, :more] = in_ref[span, cut:].astype(bf16)
+                        outs[2][e, side, to, more : more + LANES] = flat_ref[span, :].astype(bf16)
+                        outs[2][e, side, to, more + LANES :] = outer.astype(bf16)
                     else:
                         target[e, to, PACKED : PACKED + LANES] = flat_ref[span, :].astype(
                             target.dtype
@@ -623,6 +627,20 @@
     )
 
 
+def stacked(refs):
+    return refs[0][...] if len(refs) == 1 else jnp.concatenate([ref[...] for ref in refs], 0)
+
+
+def store_blocks(refs, rows):
+    count = rows.shape[0] // len(refs)
+    for index, ref in enumerate(refs):
+        ref[...] = rows[index * count : (index + 1) * count, :].astype(ref.dtype)
+
+
+def block_shapes(blocks, slots, width=D):
+    return [shape((slots // blocks, width), bf16)] * blocks
+
+
 def dispatch_grid(dest_rows, slots, tokens):
     place = lax.broadcasted_iota(jnp.int32, (slots, tokens), 0)
     first = place == dest_rows[0:1, :]
@@ -651,7 +669,7 @@
     ).astype(bf16)
 
 
-def slot_rows(idst, capacity):
+def slot_rows(idst, capacity, own):
     tokens = idst.shape[1]
     down = lax.broadcasted_iota(jnp.int32, (tokens, tokens), 0)
     across = lax.broadcasted_iota(jnp.int32, (tokens, tokens), 1)
@@ -662,7 +680,7 @@
     found = []
     for index, row in enumerate((row0, row1)):
         slot = jnp.sum(jnp.where(row, counts, 0.0), 0, keepdims=True).astype(jnp.int32)
-        found.append(idst[index : index + 1, :] * capacity + slot)
+        found.append((idst[index : index + 1, :] ^ own) * capacity + slot)
     return jnp.where(lax.broadcasted_iota(jnp.int32, (8, tokens), 0) == 0, found[0], found[1])
 
 
@@ -671,7 +689,7 @@
     slots = experts * capacity
 
     def body(idst_ref, grad_ref, out_ref):
-        first, second = dispatch_grid(slot_rows(idst_ref[...], capacity), slots, tokens)
+        first, second = dispatch_grid(slot_rows(idst_ref[...], capacity, 0), slots, tokens)
         out_ref[...] = dot(one_hot(first | second), grad_ref[...], 1, 0).astype(bf16)
 
     (out,) = whole_call(
@@ -680,25 +698,34 @@
     return out
 
 
-def apply_gates(rows, gates):
-    def body(rows_ref, gates_ref, out_ref):
-        gate = jnp.sum(gates_ref[...].astype(f32), -1, keepdims=True)
-        out_ref[...] = (gate * rows_ref[...].astype(f32)).astype(bf16)
-
-    (out,) = whole_call(
-        body, [shape(rows.shape, bf16)], [rows, gates], streamed=True, name="apply_gates"
-    )
-    return out
-
-
-def route_body(layer, experts, capacity, last, *refs):
+def apply_gates(experts, blocks, place, rows, gates):
+    slots = gates.shape[0]
+    capacity = slots // experts
+    if blocks == 1:
+        order = jnp.arange(experts) ^ place[2]
+        rows = rows.reshape(experts, capacity, D)[order].reshape(slots, D)
+        gates = gates.reshape(experts, capacity, LANES)[order].reshape(slots, LANES)
+
+    def body(place_ref, rows_ref, gates_ref, *outs):
+        for index, out_ref in enumerate(outs):
+            span = pl.ds(0, slots)
+            if blocks > 1:
+                source = pl.multiple_of((index ^ place_ref[2]) * capacity, capacity)
+                span = pl.ds(source, capacity)
+            out_ref[...] = (gates_ref[span, 0:1] * rows_ref[span, :].astype(f32)).astype(bf16)
+
+    return whole_call(
+        body, block_shapes(blocks, slots), [place, rows, gates], smem=1, streamed=True,
+        name="apply_gates",
+    )
+
+
+def route_body(layer, experts, capacity, last, blocks, place_ref, *refs):
     top = 32 * layer
-    if last:
-        (x_ref, keep_ref, recv_ref, far_ref, feature_ref, ids_ref, idst_ref,
-         middle_ref, rows_ref, soft_ref, meta_ref, dest_ref, sent_ref) = refs
-    else:
-        (x_ref, keep_ref, recv_ref, far_ref, feature_ref, ids_ref, idst_ref,
-         middle_ref, rows_ref, soft_ref, meta_ref, dest_ref) = refs
+    own = place_ref[2]
+    x_ref, keep_ref, recv_ref, far_ref, feature_ref, ids_ref, idst_ref = refs[:7]
+    middle_ref, soft_ref, meta_ref, dest_ref = refs[7:11]
+    rows_refs = refs[11 : 11 + blocks]
     tokens = x_ref.shape[0]
     slots = experts * capacity
     middle = (
@@ -724,10 +751,10 @@
     down = lax.broadcasted_iota(jnp.int32, (tokens, tokens), 0)
     across = lax.broadcasted_iota(jnp.int32, (tokens, tokens), 1)
     counts = dot(one_hot(across < down), one_hot(hit0 | hit1), 1, 0)
-    dest0 = ids[:, 0:1].astype(f32) * capacity + jnp.sum(
+    dest0 = (ids[:, 0:1] ^ own).astype(f32) * capacity + jnp.sum(
         jnp.where(hit0, counts, 0.0), -1, keepdims=True
     )
-    dest1 = ids[:, 1:2].astype(f32) * capacity + jnp.sum(
+    dest1 = (ids[:, 1:2] ^ own).astype(f32) * capacity + jnp.sum(
         jnp.where(hit1, counts, 0.0), -1, keepdims=True
     )
     fields = (dest0, dest1, picked0 / pick_total, picked1 / pick_total, pick_total)
@@ -735,13 +762,16 @@
     for index, field in enumerate(fields):
         meta = jnp.where(lane == index, field, meta)
     meta_ref[...] = meta
-    dest_rows = slot_rows(idst_ref[...], capacity)
+    dest_rows = slot_rows(idst_ref[...], capacity, own)
     dest_ref[...] = dest_rows
     first, second = dispatch_grid(dest_rows, slots, tokens)
-    rows_ref[...] = dot(one_hot(first | second), normed.astype(bf16), 1, 0).astype(bf16)
+    store_blocks(rows_refs, dot(one_hot(first | second), normed.astype(bf16), 1, 0))
     if last:
         total = None
-        for index, flags in enumerate((first, second)):
+        place = lax.broadcasted_iota(jnp.int32, (slots, tokens), 0)
+        for index in range(2):
+            slot = dest_rows[index : index + 1, :] - (idst_ref[index : index + 1, :] ^ own) * capacity
+            flags = place == slot + idst_ref[index : index + 1, :] * capacity
             gate = meta[:, 2 + index : 3 + index]
             spread = jnp.zeros((tokens, LANES), f32)
             for term in range(3):
@@ -750,77 +780,76 @@
                 gate = gate - piece
             got = dot(one_hot(flags), spread.astype(bf16), 1, 0)
             total = got if total is None else total + got
-        sent_ref[...] = total.astype(bf16)
-
-
-def route(layer, experts, capacity, x, keep, recv, far, feature, ids, idst, last, after=()):
+        refs[-1][...] = jnp.broadcast_to(jnp.sum(total, -1, keepdims=True), total.shape)
+
+
+def route(
+    layer, experts, capacity, blocks, place, x, keep, recv, far, feature, ids, idst, last, after=()
+):
     tokens = x.shape[0]
     slots = experts * capacity
     outs = [
         shape((tokens, D), f32),
-        shape((slots, D), bf16),
         shape((tokens, LANES), f32),
         shape((tokens, LANES), f32),
         shape((8, tokens), jnp.int32),
-    ]
-    args = [x, keep, recv, far, feature, ids, idst]
+    ] + block_shapes(blocks, slots)
     if last:
-        outs.append(shape((slots, LANES), bf16))
+        outs.append(shape((slots, LANES), f32))
 
     def body(*refs):
-        route_body(layer, experts, capacity, last, *refs)
+        route_body(layer, experts, capacity, last, blocks, *refs)
 
     return whole_call(
-        body, outs, args, flops=2 * slots * tokens * D, after=after, name="route"
-    )
-
-
-def combine_body(last, *refs):
-    if last:
-        middle_ref, back_ref, meta_ref, out_ref = refs
-    else:
-        middle_ref, back_ref, meta_ref, gain_ref, out_ref, normed_ref = refs
-    meta = meta_ref[...]
-    first, second = collect_grid(meta, back_ref.shape[0])
-    x = (
-        middle_ref[...]
-        + meta[:, 2:3] * dot(one_hot(first), back_ref[...], 1, 0)
-        + meta[:, 3:4] * dot(one_hot(second), back_ref[...], 1, 0)
-    )
-    out_ref[...] = x.astype(out_ref.dtype)
+        body, outs, [place, x, keep, recv, far, feature, ids, idst], smem=1,
+        flops=2 * slots * tokens * D, after=after, name="route",
+    )
+
+
+def combine(middle, back, meta, feature=None):
+    tokens = middle.shape[0]
+    count = len(back)
+    last = feature is None
+    args = [middle, meta, *back]
+    outs = [shape((tokens, D), bf16 if last else f32)]
     if not last:
-        normed_ref[...] = (x * rms_scale(x) * gain_ref[48:49, :]).astype(bf16)
-
-
-def combine(middle, back, meta, gain=None):
-    tokens = middle.shape[0]
-    args = [middle, back, meta]
-    outs = [shape((tokens, D), bf16 if gain is None else f32)]
-    if gain is not None:
-        args.append(gain)
+        args.append(feature)
         outs.append(shape((tokens, D), bf16))
 
-    def body(*refs):
-        combine_body(gain is None, *refs)
+    def body(middle_ref, meta_ref, *refs):
+        meta = meta_ref[...]
+        rows = stacked(refs[:count])
+        first, second = collect_grid(meta, rows.shape[0])
+        x = (
+            middle_ref[...]
+            + meta[:, 2:3] * dot(one_hot(first), rows, 1, 0)
+            + meta[:, 3:4] * dot(one_hot(second), rows, 1, 0)
+        )
+        if last:
+            refs[-1][...] = x.astype(bf16)
+        else:
+            refs[-2][...] = x
+            refs[-1][...] = (x * rms_scale(x) * refs[count][48:49, :]).astype(bf16)
 
     return whole_call(
-        body, outs, args, flops=4 * tokens * D * back.shape[0], name="combine"
+        body, outs, args, flops=4 * tokens * D * count * back[0].shape[0], name="combine"
     )
 
 
 def expert_token_back_body(
-    layer, back_ref, came_ref, g_ref, middle_ref, soft_ref, meta_ref, ids_ref, feature_ref,
+    layer, back_refs, came_refs, g_ref, middle_ref, soft_ref, meta_ref, ids_ref, feature_ref,
     dmiddle_ref, dattn_ref, small_ref,
 ):
+    back, came = stacked(back_refs), stacked(came_refs)
     top = 32 * layer
     gain_row = feature_ref[top + 17 : top + 18, :]
     meta = meta_ref[...]
     g = g_ref[...].astype(f32)
-    slots = back_ref.shape[0]
+    slots = back.shape[0]
     first, second = collect_grid(meta, slots)
-    grad_gate0 = jnp.sum(g * dot(one_hot(first), back_ref[...], 1, 0), -1, keepdims=True)
-    grad_gate1 = jnp.sum(g * dot(one_hot(second), back_ref[...], 1, 0), -1, keepdims=True)
-    grad_normed = dot(one_hot(first | second), came_ref[...], 1, 0)
+    grad_gate0 = jnp.sum(g * dot(one_hot(first), back, 1, 0), -1, keepdims=True)
+    grad_gate1 = jnp.sum(g * dot(one_hot(second), back, 1, 0), -1, keepdims=True)
+    grad_normed = dot(one_hot(first | second), came, 1, 0)
     gap = (grad_gate0 - grad_gate1) / meta[:, 4:5]
     ids = ids_ref[...]
     lane = lax.broadcasted_iota(jnp.int32, meta.shape, 1)
@@ -847,14 +876,15 @@
     tokens = middle.shape[0]
 
     def body(*refs):
-        expert_token_back_body(layer, *refs)
+        count = len(back)
+        expert_token_back_body(layer, refs[:count], refs[count : 2 * count], *refs[2 * count :])
 
     return whole_call(
         body,
         (shape((tokens, D), f32), shape((tokens, D), bf16), shape((24, D), f32)),
-        [back, came, g, middle, soft, meta, ids, feature],
+        [*back, *came, g, middle, soft, meta, ids, feature],
         after=after,
-        flops=6 * tokens * D * back.shape[0],
+        flops=6 * tokens * D * len(back) * back[0].shape[0],
         streamed=True,
         limit=32,
         name="expert_token_back",
@@ -866,7 +896,7 @@
         x_ref, dmiddle_ref, keep_ref, recv_ref, far_ref, feature_ref, out_ref = refs
     else:
         (x_ref, dmiddle_ref, keep_ref, recv_ref, far_ref, feature_ref, meta_ref, dest_ref,
-         out_ref, sent_ref) = refs
+         out_ref, *sent_refs) = refs
     tokens = x_ref.shape[0]
     grad_normed = (
         keep_ref[:tokens, :] + recv_ref[:tokens, :].astype(f32) + far_ref[...].astype(f32)
@@ -876,17 +906,18 @@
     g = dmiddle_ref[...] + grad_branch
     out_ref[...] = g
     if layer > 0:
-        sent_ref[...] = scatter_grads(g, meta_ref[...], dest_ref[...], sent_ref.shape[0])
+        slots = len(sent_refs) * sent_refs[0].shape[0]
+        store_blocks(sent_refs, scatter_grads(g, meta_ref[...], dest_ref[...], slots))
 
 
 def attention_token_back(
-    layer, x, dmiddle, keep, recv, far, feature, meta=None, dest=None, slots=0, after=()
+    layer, x, dmiddle, keep, recv, far, feature, meta=None, dest=None, blocks=1, slots=0, after=()
 ):
     tokens = x.shape[0]
     outs = [shape((tokens, D), f32)]
     args = [x, dmiddle, keep, recv, far, feature]
     if meta is not None:
-        outs.append(shape((slots, D), bf16))
+        outs += block_shapes(blocks, slots)
         args += [meta, dest]
 
     def body(*refs):
@@ -900,29 +931,6 @@
 def gelu_parts(gate):
     inner = math.sqrt(2.0 / math.pi) * (gate + 0.044715 * gate * gate * gate)
     return jnp.tanh(inner)
-
-
-def expert_forward_body(rows_ref, wg_ref, wu_ref, wo_ref, produced_ref, acts_ref, total_ref):
-    step = pl.program_id(0)
-    rows = rows_ref[...]
-    gate = dot(rows, wg_ref[0, 0], 1, 0)
-    up = dot(rows, wu_ref[0, 0], 1, 0)
-    acts_ref[0] = gate.astype(bf16)
-    acts_ref[1] = up.astype(bf16)
-    hidden = (0.5 * gate * (1.0 + gelu_parts(gate)) * up).astype(bf16)
-    out = dot(hidden, wo_ref[0, 0], 1, 1)
-
-    @pl.when(step == 0)
-    def _():
-        total_ref[...] = out
-
-    @pl.when(step > 0)
-    def _():
-        total_ref[...] += out
-
-    @pl.when(step == FF_STEPS - 1)
-    def _():
-        produced_ref[...] = total_ref[...].astype(bf16)
 
 
 def weight_specs(layer, tile):
@@ -933,145 +941,173 @@
     ]
 
 
-def expert_forward(layer, rows, w_in, w_out, after=()):
-    count = rows.shape[0]
-
-    def body(*refs):
-        expert_forward_body(*refs[:4], *refs[4 + len(after) :])
-
+def block_specs(blocks):
+    return [pl.BlockSpec(b.shape, lambda s: (0, 0)) for b in blocks]
+
+
+def expert_call(body, steps, outs, out_specs, args, in_specs, scratch, limit, after, name):
+    used = len(args)
+
+    def ordered(*refs):
+        body(*refs[:used], *refs[used + len(after) :])
+
+    count = ROWS_HINT
     return pl.pallas_call(
-        body,
-        grid=(FF_STEPS,),
-        out_shape=(shape((count, D), bf16), pltpu.HBM((2, count, FF), bf16)),
-        in_specs=[pl.BlockSpec((count, D), lambda s: (0, 0))]
-        + weight_specs(layer, FF_TILE)
-        + [pl.BlockSpec(memory_space=pltpu.HBM)] * len(after),
-        out_specs=(
-            pl.BlockSpec((count, D), lambda s: (0, 0)),
-            pl.BlockSpec((2, count, FF_TILE), lambda s: (0, 0, s)),
-        ),
-        scratch_shapes=[pltpu.VMEM((count, D), f32)],
-        compiler_params=pltpu.CompilerParams(vmem_limit_bytes=28 * MIB),
+        ordered,
+        grid=(steps,),
+        out_shape=tuple(outs),
+        in_specs=list(in_specs) + [pl.BlockSpec(memory_space=pltpu.HBM)] * len(after),
+        out_specs=tuple(out_specs),
+        scratch_shapes=list(scratch),
+        compiler_params=pltpu.CompilerParams(vmem_limit_bytes=limit * MIB),
         cost_estimate=pl.CostEstimate(
             flops=6 * count * D * FF, bytes_accessed=6 * D * FF, transcendentals=count * FF
         ),
-        name="expert_forward",
-    )(
-        rows,
-        far_away(w_in),
-        far_away(w_in),
-        far_away(w_out),
-        *[far_away(a) for a in after],
-    )
-
-
-def expert_backward_body(
-    grad_ref, acts_ref, wg_ref, wu_ref, wo_ref, drows_ref, grads_ref, total_ref
-):
-    step = pl.program_id(0)
-    grad_hidden = dot(grad_ref[...], wo_ref[0, 0], 1, 0)
-    gate = acts_ref[0].astype(f32)
-    up = acts_ref[1].astype(f32)
-    curve = gelu_parts(gate)
-    value = 0.5 * gate * (1.0 + curve)
-    slope = 0.5 * (1.0 + curve) + 0.5 * gate * (1.0 - curve * curve) * math.sqrt(
-        2.0 / math.pi
-    ) * (1.0 + 3.0 * 0.044715 * gate * gate)
-    grad_gate = (grad_hidden * up * slope).astype(bf16)
-    grad_up = (grad_hidden * value).astype(bf16)
-    grads_ref[0] = grad_gate
-    grads_ref[1] = grad_up
-    grads_ref[2] = (value * up).astype(bf16)
-    out = dot(grad_gate, wg_ref[0, 0], 1, 1) + dot(grad_up, wu_ref[0, 0], 1, 1)
-
-    @pl.when(step == 0)
-    def _():
-        total_ref[...] = out
-
-    @pl.when(step > 0)
-    def _():
-        total_ref[...] += out
-
-    @pl.when(step == BACK_STEPS - 1)
-    def _():
-        drows_ref[...] = total_ref[...].astype(bf16)
-
-
-def expert_backward(layer, grad, acts, w_in, w_out, after=()):
-    count = grad.shape[0]
+        name=name,
+    )(*args, *[far_away(a) for a in after])
+
+
+def expert_forward(layer, blocks, w_in, w_out, after=()):
+    number = len(blocks)
+    count = number * blocks[0].shape[0]
+    steps = FF // WIDE_TILE
 
     def body(*refs):
-        expert_backward_body(*refs[:5], *refs[5 + len(after) :])
-
-    return pl.pallas_call(
+        wg_ref, wu_ref, wo_ref = refs[number : number + 3]
+        produced_refs = refs[number + 3 : 2 * number + 3]
+        acts_ref, rows_ref, total_ref = refs[2 * number + 3 :]
+        step = pl.program_id(0)
+
+        @pl.when(step == 0)
+        def _():
+            rows_ref[...] = stacked(refs[:number])
+
+        rows = rows_ref[...]
+        gate = dot(rows, wg_ref[0, 0], 1, 0)
+        up = dot(rows, wu_ref[0, 0], 1, 0)
+        acts_ref[0] = gate.astype(bf16)
+        acts_ref[1] = up.astype(bf16)
+        hidden = (0.5 * gate * (1.0 + gelu_parts(gate)) * up).astype(bf16)
+        out = dot(hidden, wo_ref[0, 0], 1, 1)
+
+        @pl.when(step == 0)
+        def _():
+            total_ref[...] = out
+
+        @pl.when(step == steps - 1)
+        def _():
+            store_blocks(produced_refs, total_ref[...] + out)
+
+    *produced, acts = expert_call(
         body,
-        grid=(BACK_STEPS,),
-        out_shape=(shape((count, D), bf16), pltpu.HBM((3, count, FF), bf16)),
-        in_specs=[
-            pl.BlockSpec((count, D), lambda s: (0, 0)),
-            pl.BlockSpec((2, count, BACK_TILE), lambda s: (0, 0, s)),
-        ]
-        + weight_specs(layer, BACK_TILE)
-        + [pl.BlockSpec(memory_space=pltpu.HBM)] * len(after),
-        out_specs=(
-            pl.BlockSpec((count, D), lambda s: (0, 0)),
-            pl.BlockSpec((3, count, BACK_TILE), lambda s: (0, 0, s)),
-        ),
-        scratch_shapes=[pltpu.VMEM((count, D), f32)],
-        compiler_params=pltpu.CompilerParams(vmem_limit_bytes=56 * MIB),
-        cost_estimate=pl.CostEstimate(
-            flops=6 * count * D * FF, bytes_accessed=6 * D * FF, transcendentals=count * FF
-        ),
-        name="expert_backward",
-    )(
-        grad,
-        far_away(acts),
-        far_away(w_in),
-        far_away(w_in),
-        far_away(w_out),
-        *[far_away(a) for a in after],
-    )
-
-
-def expert_grads_body(shares, rows_ref, grad_ref, parts_ref, out_ref, rows_t, grad_t):
-    @pl.when(pl.program_id(0) == 0)
-    def _():
-        rows_t[...] = rows_ref[...].T
-        grad_t[...] = grad_ref[...].T
-
+        steps,
+        [shape(b.shape, bf16) for b in blocks] + [pltpu.HBM((2, count, FF), bf16)],
+        block_specs(blocks) + [pl.BlockSpec((2, count, WIDE_TILE), lambda s: (0, 0, s))],
+        [*blocks, far_away(w_in), far_away(w_in), far_away(w_out)],
+        block_specs(blocks) + weight_specs(layer, WIDE_TILE),
+        [pltpu.VMEM((count, D), bf16), pltpu.VMEM((count, D), f32)],
+        56,
+        after,
+        "expert_forward",
+    )
+    return produced, acts
+
+
+def expert_backward(layer, blocks, out_blocks, acts, w_in, w_out, after=()):
+    number = len(blocks)
+    count = number * blocks[0].shape[0]
+    steps = FF // WIDE_TILE
+    outs = block_shapes(out_blocks, count)
+
+    def body(*refs):
+        acts_refs = refs[number : number + len(acts)]
+        wg_ref, wu_ref, wo_ref, *rest = refs[number + len(acts) :]
+        drows_refs = rest[:out_blocks]
+        parts_ref, grad_ref, total_ref = rest[out_blocks:]
+        step = pl.program_id(0)
+
+        @pl.when(step == 0)
+        def _():
+            grad_ref[...] = stacked(refs[:number])
+
+        grad_hidden = dot(grad_ref[...], wo_ref[0, 0], 1, 0)
+        gate = jnp.concatenate([ref[0] for ref in acts_refs], 0).astype(f32)
+        up = jnp.concatenate([ref[1] for ref in acts_refs], 0).astype(f32)
+        curve = gelu_parts(gate)
+        value = 0.5 * gate * (1.0 + curve)
+        slope = 0.5 * (1.0 + curve) + 0.5 * gate * (1.0 - curve * curve) * math.sqrt(
+            2.0 / math.pi
+        ) * (1.0 + 3.0 * 0.044715 * gate * gate)
+        grad_gate = (grad_hidden * up * slope).astype(bf16)
+        grad_up = (grad_hidden * value).astype(bf16)
+        parts_ref[0] = grad_gate
+        parts_ref[1] = grad_up
+        parts_ref[2] = (value * up).astype(bf16)
+        out = dot(grad_gate, wg_ref[0, 0], 1, 1) + dot(grad_up, wu_ref[0, 0], 1, 1)
+
+        @pl.when(step == 0)
+        def _():
+            total_ref[...] = out
+
+        @pl.when(step == steps - 1)
+        def _():
+            store_blocks(drows_refs, total_ref[...] + out)
+
+    *drows, parts = expert_call(
+        body,
+        steps,
+        outs + [pltpu.HBM((3, count, FF), bf16)],
+        block_specs(outs) + [pl.BlockSpec((3, count, WIDE_TILE), lambda s: (0, 0, s))],
+        [*blocks, *[far_away(a) for a in acts], far_away(w_in), far_away(w_in), far_away(w_out)],
+        block_specs(blocks)
+        + [pl.BlockSpec((2, a.shape[1], WIDE_TILE), lambda s: (0, 0, s)) for a in acts]
+        + weight_specs(layer, WIDE_TILE),
+        [pltpu.VMEM((count, D), bf16), pltpu.VMEM((count, D), f32)],
+        58,
+        after,
+        "expert_backward",
+    )
+    return drows, parts
+
+
+def expert_grads(shares, rows, grads, parts, after=()):
+    count = len(rows) * rows[0].shape[0]
     tall = D // shares
-    for which in range(3):
-        left = rows_t if which < 2 else grad_t
-        got = dot(left[...], parts_ref[which], 1, 0).astype(bf16)
-        for share in range(shares):
-            out_ref[share, which] = got[share * tall : (share + 1) * tall, :]
-
-
-def expert_grads(shares, rows, grad, parts, after=()):
-    count = rows.shape[0]
-    tall = D // shares
+    first = len(rows)
+    second = first + len(grads)
+    third = second + len(parts)
 
     def body(*refs):
-        expert_grads_body(shares, *refs[:3], *refs[3 + len(after) :])
-
-    return pl.pallas_call(
+        out_ref, rows_t, grad_t = refs[third:]
+
+        @pl.when(pl.program_id(0) == 0)
+        def _():
+            rows_t[...] = stacked(refs[:first]).T
+            grad_t[...] = stacked(refs[first:second]).T
+
+        for which in range(3):
+            left = rows_t if which < 2 else grad_t
+            right = [ref[which] for ref in refs[second:third]]
+            right = right[0] if len(right) == 1 else jnp.concatenate(right, 0)
+            got = dot(left[...], right, 1, 0).astype(bf16)
+            for share in range(shares):
+                out_ref[share, which] = got[share * tall : (share + 1) * tall, :]
+
+    (out,) = expert_call(
         body,
-        grid=(FF_STEPS,),
-        out_shape=pltpu.HBM((shares, 3, tall, FF), bf16),
-        in_specs=[
-            pl.BlockSpec((count, D), lambda s: (0, 0)),
-            pl.BlockSpec((count, D), lambda s: (0, 0)),
-            pl.BlockSpec((3, count, FF_TILE), lambda s: (0, 0, s)),
-        ]
-        + [pl.BlockSpec(memory_space=pltpu.HBM)] * len(after),
-        out_specs=pl.BlockSpec((shares, 3, tall, FF_TILE), lambda s: (0, 0, 0, s)),
-        scratch_shapes=[pltpu.VMEM((D, count), bf16), pltpu.VMEM((D, count), bf16)],
-        compiler_params=pltpu.CompilerParams(vmem_limit_bytes=28 * MIB),
-        cost_estimate=pl.CostEstimate(
-            flops=6 * count * D * FF, bytes_accessed=6 * D * FF, transcendentals=0
-        ),
-        name="expert_grads",
-    )(rows, grad, far_away(parts), *[far_away(a) for a in after])
+        FF_STEPS,
+        [pltpu.HBM((shares, 3, tall, FF), bf16)],
+        [pl.BlockSpec((shares, 3, tall, FF_TILE), lambda s: (0, 0, 0, s))],
+        [*rows, *grads, *[far_away(p) for p in parts]],
+        block_specs(rows)
+        + block_specs(grads)
+        + [pl.BlockSpec((3, p.shape[1], FF_TILE), lambda s: (0, 0, s)) for p in parts],
+        [pltpu.VMEM((D, count), bf16), pltpu.VMEM((D, count), bf16)],
+        32,
+        after,
+        "expert_grads",
+    )
+    return out
 
 
 def place_expert_grads(layer, summed, before=None, after=()):
@@ -1163,6 +1199,15 @@
     return lax.all_to_all(rows, "experts", split_axis=0, concat_axis=0, tiled=True)
 
 
+def swap(blocks, experts):
+    split = blocks if len(blocks) > 1 else jnp.split(blocks[0], experts)
+    moved = [
+        part if k == 0 else lax.ppermute(part, "experts", [(i, i ^ k) for i in range(experts)])
+        for k, part in enumerate(split)
+    ]
+    return moved if len(blocks) > 1 else [jnp.concatenate(moved)]
+
+
 def on_device(
     tokens, doc_starts, expert_ids, attn_in, attn_out, router, gains, rel_table,
     expert_in, expert_out, out_grad,
@@ -1181,6 +1226,8 @@
     rows = start_tokens.shape[0]
     capacity = (10 * rows + 4 * experts - 1) // (4 * experts)
     slots = experts * capacity
+    blocks = experts if experts == 4 and capacity % 16 == 0 else 1
+    chunks = [(0, 1), (2,), (3,)] if blocks == 4 else [(0,)]
     grad_in = out_grad[0]
     hits = jnp.asarray(bucket_hits())
 
@@ -1204,10 +1251,11 @@
 
         first = together(packet[..., :top], packets[1])
         w_in0, w_out0, feature, bias = unpack(place, hits, experts, pairs, 0, first)
-        second = together(packet[..., top:], packets[2])
-        w_in1, w_out1 = unpack(place, hits, experts, pairs, 1, second)
+        second = [together(packet[..., top:], packets[2])]
+        w_in1, w_out1 = unpack(place, hits, experts, pairs, 1, second[0])
         w_in, w_out = [w_in0, w_in1], [w_out0, w_out1]
     else:
+        second = []
         w_in, w_out = [], []
         for layer in range(LAYERS):
             at = layer * (PACKED + LANES)
@@ -1239,7 +1287,6 @@
     pieces = share_pieces(start_tokens)
     x = start_tokens
     kept = []
-    arrived_grad = exchange(send_grads(experts, capacity, idst, grad_in, [feature]))
     for layer in range(LAYERS):
         packed, log_total, mixed, keep, send, *normed_all = attention_forward(
             layer, place, pieces, w_in[layer], feature, bias, low, w_out[layer]
@@ -1247,20 +1294,33 @@
         normed_rows = normed_all if layer == 0 else pieces
         keep, recv, far = sum_pieces(keep, send)
         last = layer == LAYERS - 1
-        routed = route(
-            layer, experts, capacity, x, keep, recv, far, feature, ids, idst, last,
-            after=[arrived_grad] if layer == 0 else [],
-        )
-        middle, sent_rows, soft, meta, dest = routed[:5]
-        arrived = exchange(sent_rows)
+        middle, soft, meta, dest, *sent = route(
+            layer, experts, capacity, blocks, place, x, keep, recv, far, feature, ids, idst, last,
+            after=[arrived_grad] if last else [],
+        )
+        arrived = swap(sent[:blocks], experts)
         if last:
-            gates = exchange(routed[5])
-        produced, acts = expert_forward(
-            layer, arrived, expert_in, expert_out
-        )
-        back = exchange(produced)
-        if last:
-            arrived_grad = apply_gates(arrived_grad, gates)
+            gates = exchange(sent[blocks])
+        produced, acts, drows, parts = [], [], [], []
+        order = second if layer == 0 else []
+        for chunk in chunks:
+            done, kept_acts = expert_forward(
+                layer, [arrived[k] for k in chunk], expert_in, expert_out, after=order
+            )
+            produced += done
+            acts.append(kept_acts)
+            order = done[:1]
+            if last:
+                if not drows:
+                    arrived_grad = apply_gates(experts, blocks, place, arrived_grad, gates)
+                done, some = expert_backward(
+                    layer, [arrived_grad[k] for k in chunk], len(chunk), acts[-1:], expert_in,
+                    expert_out,
+                )
+                drows += done
+                parts.append(some)
+                order = done[:1]
+        back = swap(produced, experts)
         kept.append(
             (x, normed_rows, packed, log_total, mixed, middle, soft, meta, dest, arrived, acts, back)
         )
@@ -1268,7 +1328,9 @@
             (result,) = combine(middle, back, meta)
         else:
             x, normed = combine(middle, back, meta, feature)
-            pieces = share_pieces(normed)
+            ungated = send_grads(experts, capacity, idst, grad_in, [x])
+            arrived_grad = exchange(ungated)
+            pieces = share_pieces(hold(normed, [ungated]))
 
     g = grad_in
     inner, outer, expert_totals = [], [], []
@@ -1277,13 +1339,21 @@
     for layer in range(LAYERS - 1, -1, -1):
         (x, normed_rows, packed, log_total, mixed, middle, soft, meta, dest, arrived, acts,
          back) = kept[layer]
-        drows, parts = expert_backward(layer, arrived_grad, acts, expert_in, expert_out)
-        came = exchange(drows)
+        if layer < LAYERS - 1:
+            drows, parts = [], []
+            for index, chunk in enumerate(chunks):
+                done, some = expert_backward(
+                    layer, [arrived_grad[k] for k in chunk], len(chunk), acts[index : index + 1],
+                    expert_in, expert_out, after=drows[-1:],
+                )
+                drows += done
+                parts.append(some)
+        came = swap(drows, experts)
         early = [] if other is None else [other]
         weight_grads = expert_grads(
-            GROUP * pairs, arrived, arrived_grad, parts, after=[back] + early
-        )
-        weight_grads = hold(weight_grads, [came])
+            GROUP * pairs, arrived, arrived_grad, parts, after=(back if layer else []) + early
+        )
+        weight_grads = hold(weight_grads, came)
         total = lax.psum_scatter(
             weight_grads, ("context", "dp"), scatter_dimension=0, tiled=False
         )
@@ -1303,10 +1373,10 @@
         keep, recv, far = sum_pieces(keep, send)
         if layer > 0:
             below = kept[layer - 1]
-            g, sent = attention_token_back(
-                layer, x, dmiddle, keep, recv, far, feature, below[7], below[8], slots
+            g, *sent = attention_token_back(
+                layer, x, dmiddle, keep, recv, far, feature, below[7], below[8], blocks, slots
             )
-            arrived_grad = exchange(sent)
+            arrived_grad = swap(sent, experts)
         else:
             placed_grads = place_expert_grads(layer + 1, expert_totals[0])
             (g,) = attention_token_back(
@@ -1328,8 +1398,9 @@
                 rest = rest[0] + theirs.astype(f32)
                 ours = hold(keep_dense, [g, result, placed_grads[0]]) + other.astype(f32)
                 total = sum_zone(exchange(ours.astype(bf16)))
-                flats.insert(0, jnp.concatenate([total, rest[:, :LANES]], -1).astype(bf16))
-                outer.append(rest[:, LANES:])
+                more = PACKED + LANES - EARLY_COLS
+                flats.insert(0, jnp.concatenate([total, rest[:, :more]], -1).astype(bf16))
+                outer.append(rest[:, more:])
                 flat = jnp.stack([flat.reshape(GROUP, share, -1) for flat in flats], 1)
                 inner = spread(flat)
         else:

time: 740 us -> 698 us (0.943)
  blocking collectives: 79.4 us -> 11.8 us
  waiting for transfers between devices: 272 us -> 210 us
  Pallas kernels: 236 us -> 288 us
  starting transfers between devices: 60.2 us -> 89.2 us
  local copies, waits for them, and re-layouts: 48.4 us -> 58.9 us
    all_to_all x10 -> x5, waiting for transfers between devices: 94.3 us -> 18.7 us  [exchange(): lax.all_to_all(rows, 'experts', split_axis=0, concat_axis=0, tiled=True)]
    all_to_all x2 -> x0, blocking collectives: 67.5 us -> none  [exchange(): lax.all_to_all(rows, 'experts', split_axis=0, concat_axis=0, tiled=True)]
    pallas_call x6 -> x14, Pallas kernels: 128 us -> 184 us  [expert_call(): pl.pallas_call(ordered, grid=(steps,), out_shape=tuple(outs), in_specs=li...]
    ppermute x0 -> x21, starting transfers between devices: none -> 40 us  [swap(): lax.ppermute(part, 'experts', [(i, i ^ k) for i in range(experts)])]
    ppermute x0 -> x21, waiting for transfers between devices: none -> 24.2 us  [swap(): lax.ppermute(part, 'experts', [(i, i ^ k) for i in range(experts)])]
    ppermute x4, waiting for transfers between devices: 69.9 us -> 47.6 us  [sum_pieces(): return (keep, recv, lax.ppermute(other, 'context', ACROSS))]
    all_to_all x10 -> x5, starting transfers between devices: 44.2 us -> 28.8 us  [exchange(): lax.all_to_all(rows, 'experts', split_axis=0, concat_axis=0, tiled=True)]
    all_gather x2, waiting for transfers between devices: 38.3 us -> 51.2 us  [together(): return lax.all_gather(part, ('experts', 'dp'), axis=0, tiled=False)]
  transfers between devices with their start and end apart: 38 -> 54, of which waited for: 23 -> 23; matrix products, arithmetic and copies ran while one was open for 2% -> 2% of each run, Pallas kernels for 30% -> 40%
where the time goes in v4:
time: 698 us; the launch traced here: 688 us
  Pallas kernels  288 us (41%)
  waiting for transfers between devices  210 us (30%)
  starting transfers between devices  89.2 us (13%)
  local copies, waits for them, and re-layouts  58.9 us (8%)
  between operations  15.2 us (2%)
  other arithmetic  14.8 us (2%)
  blocking collectives  11.8 us (2%)
    pallas_call x14, Pallas kernels, expert_call(): pl.pallas_call(ordered, grid=(steps,), out_shape=tuple(outs), in_specs=li...  184 us
    pallas_call x14, Pallas kernels, whole_call(): pl.pallas_call(ordered, out_shape=outs, in_specs=specs, out_specs=tuple((...  69.4 us
    unnamed x265, local copies, waits for them, and re-layouts  58 us
    all_gather x2, waiting for transfers between devices, together(): return lax.all_gather(part, ('experts', 'dp'), axis=0, tiled=False)  51.2 us
    ppermute x4, waiting for transfers between devices, sum_pieces(): return (keep, recv, lax.ppermute(other, 'context', ACROSS))  47.6 us
    ppermute x4, waiting for transfers between devices, share_pieces(): across = lax.ppermute(piece, 'context', ACROSS)  41.6 us
    ppermute x21, starting transfers between devices, swap(): lax.ppermute(part, 'experts', [(i, i ^ k) for i in range(experts)])  40 us
    all_to_all x5, starting transfers between devices, exchange(): lax.all_to_all(rows, 'experts', split_axis=0, concat_axis=0, tiled=True)  28.8 us
  transfers between devices with their start and end apart: 54, of which 23 were waited for; matrix products, arithmetic and copies ran while one was open for 2% of the time, Pallas kernels for 40%

profile of v4, /device:TPU:0, one launch (start us, length us, event | category | flops | bytes accessed | tf_op | source)
XLA Modules:
  0.0 687.9 jit_solution(17205444647428851648)
XLA Ops:
  11.5 11.8 %all_to_all.47 = bf16[4,32,1664]{2,1,0:T(8,128)(2,1)S(1)} all-to-all(bf16[4,32,1664]{2,1,0:T(8,128)(2,1)S(1)} %get-tuple-element.112), channel_id=1, replica_groups=mesh['experts'=4,'context'=4,'dp'=2] {'context'}, dimensions={0} | all-to-all | bytes 851968 | tf_op jit(solution)/shard_map/all_to_all | solution.py:1237
  25.3 13.4 %collective-permute-done.1.refs_3_ = bf16[256,1024]{1,0:T(8,128)(2,1)S(1)} collective-permute-done((bf16[256,1024]{1,0:T(8,128)(2,1)S(1)}, bf16[256,1024]{1,0:T(8,128)(2,1)S(1)}, u32[]{:S(2)}, u32[]{:S(2)}) %collective-permute-start.1) | collective-permute-done | bytes 524320 | tf_op jit(solution)/shard_map/ppermute | solution.py:1151
  38.9 37.5 %all-gather.5.cloned.1.call-done = bf16[32,32,1152]{2,1,0:T(8,128)(2,1)} async-done(((bf16[4,32,1152]{2,1,0:T(8,128)(2,1)}), bf16[32,32,1152]{2,1,0:T(8,128)(2,1)}) %all-gather.5.cloned.1.call-update) | async-done | bytes 2359312 | tf_op jit(solution)/shard_map/all_gather | solution.py:1250
  79.3 9.9 %attention_forward.2 = (bf16[1024,768]{1,0:T(8,128)(2,1)S(1)}, f32[8,1024]{1,0:T(8,128)S(1)}, bf16[1024,256]{1,0:T(8,128)(2,1)S(1)}, f32[512,1024]{1,0:T(8,128)S...) custom-call(s32[3]{0:T(128)S(1)} %pad_add_fusion.refs_0_, bf16[256,1024]{1,0:T(8,128)(2,1)S(1)} %bitcast.47, ...), custom_call_target="tpu_custom_call" | custom-call | flops 3221225472 | bytes 12128268 | tf_op jit(solution)/shard_map/attention_forward/pallas_call | solution.py:96
  97.8 12.3 %collective-permute-done.4.refs_4_ = bf16[256,1024]{1,0:T(8,128)(2,1)S(1)} collective-permute-done((bf16[256,1024]{1,0:T(8,128)(2,1)S(1)}, bf16[256,1024]{1,0:T(8,128)(2,1)S(1)}, u32[]{:S(2)}, u32[]{:S(2)}) %collective-permute-start.4) | collective-permute-done | bytes 524320 | tf_op jit(solution)/shard_map/ppermute | solution.py:1160
  122.7 13.7 %all-gather.7.cloned.1.call-done = bf16[32,32,1024]{2,1,0:T(8,128)(2,1)} async-done(((bf16[4,32,1024]{2,1,0:T(8,128)(2,1)}), bf16[32,32,1024]{2,1,0:T(8,128)(2,1)}) %all-gather.7.cloned.1.call-update) | async-done | bytes 2097168 | tf_op jit(solution)/shard_map/all_gather | solution.py:1250
  140.6 12.7 %expert_forward.6 = (bf16[160,1024]{1,0:T(8,128)(2,1)}, bf16[160,1024]{1,0:T(8,128)(2,1)}, bf16[2,320,2816]{2,1,0:T(8,128)(2,1)}) custom-call(bf16[160,1024]{1,0:T(8,128)(2,1)} %copy-done.28, bf16[160,1024]{1,0:T(8,128)(2,1)} %copy-done.30, bf16[2,1,1024,5632]{3,2,1,0:T(8,128)(2,1)} %refs_3_.24, bf16[2,1,1024,5632]{3,2,1,0:T(8,128)(2,1)} %refs_3_.24, ...), custom_call_target="tpu_custom_call" | custom-call | flops 5536481280 | bytes 17301504 | tf_op jit(solution)/shard_map/expert_forward/pallas_call | solution.py:955
  154.1 10.0 %expert_forward.7 = (bf16[160,1024]{1,0:T(8,128)(2,1)}, bf16[2,160,2816]{2,1,0:T(8,128)(2,1)}) custom-call(bf16[160,1024]{1,0:T(8,128)(2,1)} %copy-done.32, bf16[2,1,1024,5632]{3,2,1,0:T(8,128)(2,1)} %refs_3_.24, bf16[2,1,1024,5632]{3,2,1,0:T(8,128)(2,1)} %refs_3_.24, bf16[2,1,1024,2816]{3,2,1,0:T(8,128)(2,1)} %refs_4_.17, ...), custom_call_target="tpu_custom_call" | custom-call | flops 5536481280 | bytes 17301504 | tf_op jit(solution)/shard_map/expert_forward/pallas_call | solution.py:955
  167.4 9.9 %expert_forward.8 = (bf16[160,1024]{1,0:T(8,128)(2,1)}, bf16[2,160,2816]{2,1,0:T(8,128)(2,1)}) custom-call(bf16[160,1024]{1,0:T(8,128)(2,1)} %copy-done.34, bf16[2,1,1024,5632]{3,2,1,0:T(8,128)(2,1)} %refs_3_.24, bf16[2,1,1024,5632]{3,2,1,0:T(8,128)(2,1)} %refs_3_.24, bf16[2,1,1024,2816]{3,2,1,0:T(8,128)(2,1)} %refs_4_.17, ...), custom_call_target="tpu_custom_call" | custom-call | flops 5536481280 | bytes 17301504 | tf_op jit(solution)/shard_map/expert_forward/pallas_call | solution.py:955
  179.2 10.7 %collective-permute-done.8.refs_4_.refs_2_ = bf16[160,1024]{1,0:T(8,128)(2,1)S(1)} collective-permute-done((bf16[160,1024]{1,0:T(8,128)(2,1)}, bf16[160,1024]{1,0:T(8,128)(2,1)S(1)}, u32[]{:S(2)}, u32[]{:S(2)}) %collective-permute-start.8) | collective-permute-done | bytes 327712 | tf_op jit(solution)/shard_map/ppermute | solution.py:1205
  195.4 8.9 %collective-permute-done.12.refs_3_.refs_14_ = bf16[256,1024]{1,0:T(8,128)(2,1)S(1)} collective-permute-done((bf16[256,1024]{1,0:T(8,128)(2,1)}, bf16[256,1024]{1,0:T(8,128)(2,1)S(1)}, u32[]{:S(2)}, u32[]{:S(2)}) %collective-permute-start.12) | collective-permute-done | bytes 524320 | tf_op jit(solution)/shard_map/ppermute | solution.py:1151
  205.8 10.9 %all-to-all-start.1 = ((bf16[4,160,1024]{2,1,0:T(8,128)(2,1)}), bf16[4,160,1024]{2,1,0:T(8,128)(2,1)}, u32[]{:S(2)}, u32[]{:S(2)}) async-start(bf16[4,160,1024]{2,1,0:T(8,128)(2,1)} %bitcast.11), calls=%async_computation.1 | async-start | bytes 2621440 | tf_op jit(solution)/shard_map/all_to_all | solution.py:1199
  217.7 10.5 %attention_forward.3 = (bf16[1024,768]{1,0:T(8,128)(2,1)S(1)}, f32[8,1024]{1,0:T(8,128)S(1)}, bf16[1024,256]{1,0:T(8,128)(2,1)S(1)}, f32[512,1024]{1,0:T(8,128)S(1)}, bf16[512,1024]{1,0:T(8,128)(2,1)S(1)}) custom-call(s32[3]{0:T(128)S(1)} %pad_add_fusion.refs_0_, bf16[256,1024]{1,0:T(8,128)(2,1)S(1)} %copy-done.75, ...), custom_call_target="tpu_custom_call" | custom-call | flops 3221225472 | bytes 10031116 | tf_op jit(solution)/shard_map/attention_forward/pallas_call | solution.py:96
  234.7 14.7 %all-to-all-done.1 = bf16[4,160,1024]{2,1,0:T(8,128)(2,1)} async-done(((bf16[4,160,1024]{2,1,0:T(8,128)(2,1)}), bf16[4,160,1024]{2,1,0:T(8,128)(2,1)}, u32[]{:S(2)}, u32[]{:S(2)}) %all-to-all-start.1) | async-done | bytes 1310752 | tf_op jit(solution)/shard_map/all_to_all | solution.py:1199
  273.9 12.7 %expert_forward.9 = (bf16[160,1024]{1,0:T(8,128)(2,1)}, bf16[160,1024]{1,0:T(8,128)(2,1)}, bf16[2,320,2816]{2,1,0:T(8,128)(2,1)}) custom-call(bf16[160,1024]{1,0:T(8,128)(2,1)} %copy-done.36, bf16[160,1024]{1,0:T(8,128)(2,1)} %copy-done.38, bf16[2,1,1024,5632]{3,2,1,0:T(8,128)(2,1)} %refs_3_.24, bf16[2,1,1024,5632]{3,2,1,0:T(8,128)(2,1)} %refs_3_.24, ...), custom_call_target="tpu_custom_call" | custom-call | flops 5536481280 | bytes 17301504 | tf_op jit(solution)/shard_map/expert_forward/pallas_call | solution.py:955
  293.4 14.8 %expert_backward.6 = (bf16[160,1024]{1,0:T(8,128)(2,1)}, bf16[160,1024]{1,0:T(8,128)(2,1)}, bf16[3,320,2816]{2,1,0:T(8,128)(2,1)}) custom-call(bf16[160,1024]{1,0:T(8,128)(2,1)} %copy-done.48, bf16[160,1024]{1,0:T(8,128)(2,1)} %copy-done.50, bf16[2,320,2816]{2,1,0:T(8,128)(2,1)} %get-tuple-element.147.refs_2_, bf16[2,1,1024,5632]{3,2,1,0:T(8,128)(2,1)} %refs_3_.24, ...), custom_call_target="tpu_custom_call" | custom-call | flops 5536481280 | bytes 17301504 | tf_op jit(solution)/shard_map/expert_backward/pallas_call | solution.py:955
  309.5 10.0 %expert_forward.10 = (bf16[160,1024]{1,0:T(8,128)(2,1)}, bf16[2,160,2816]{2,1,0:T(8,128)(2,1)}) custom-call(bf16[160,1024]{1,0:T(8,128)(2,1)} %copy-done.40, bf16[2,1,1024,5632]{3,2,1,0:T(8,128)(2,1)} %refs_3_.24, bf16[2,1,1024,5632]{3,2,1,0:T(8,128)(2,1)} %refs_3_.24, bf16[2,1,1024,2816]{3,2,1,0:T(8,128)(2,1)} %refs_4_.17, ...), custom_call_target="tpu_custom_call" | custom-call | flops 5536481280 | bytes 17301504 | tf_op jit(solution)/shard_map/expert_forward/pallas_call | solution.py:955
  321.3 11.9 %expert_backward.7 = (bf16[160,1024]{1,0:T(8,128)(2,1)}, bf16[3,160,2816]{2,1,0:T(8,128)(2,1)}) custom-call(bf16[160,1024]{1,0:T(8,128)(2,1)} %copy-done.52, bf16[2,160,2816]{2,1,0:T(8,128)(2,1)} %get-tuple-element.152.refs_1_, bf16[2,1,1024,5632]{3,2,1,0:T(8,128)(2,1)} %refs_3_.24, bf16[2,1,1024,5632]{3,2,1,0:T(8,128)(2,1)} %refs_3_.24, ...), custom_call_target="tpu_custom_call" | custom-call | flops 5536481280 | bytes 17301504 | tf_op jit(solution)/shard_map/expert_backward/pallas_call | solution.py:955
  335.1 9.9 %expert_forward.11 = (bf16[160,1024]{1,0:T(8,128)(2,1)}, bf16[2,160,2816]{2,1,0:T(8,128)(2,1)}) custom-call(bf16[160,1024]{1,0:T(8,128)(2,1)} %copy-done.42, bf16[2,1,1024,5632]{3,2,1,0:T(8,128)(2,1)} %refs_3_.24, bf16[2,1,1024,5632]{3,2,1,0:T(8,128)(2,1)} %refs_3_.24, bf16[2,1,1024,2816]{3,2,1,0:T(8,128)(2,1)} %refs_4_.17, ...), custom_call_target="tpu_custom_call" | custom-call | flops 5536481280 | bytes 17301504 | tf_op jit(solution)/shard_map/expert_forward/pallas_call | solution.py:955
  348.2 12.2 %expert_backward.8 = (bf16[160,1024]{1,0:T(8,128)(2,1)}, bf16[3,160,2816]{2,1,0:T(8,128)(2,1)}) custom-call(bf16[160,1024]{1,0:T(8,128)(2,1)} %copy-done.54, bf16[2,160,2816]{2,1,0:T(8,128)(2,1)} %get-tuple-element.157.refs_1_, bf16[2,1,1024,5632]{3,2,1,0:T(8,128)(2,1)} %refs_3_.24, bf16[2,1,1024,5632]{3,2,1,0:T(8,128)(2,1)} %refs_3_.24, ...), custom_call_target="tpu_custom_call" | custom-call | flops 5536481280 | bytes 17301504 | tf_op jit(solution)/shard_map/expert_backward/pallas_call | solution.py:955
  362.0 20.6 %expert_grads.2.refs_0_ = bf16[8,3,128,2816]{3,2,1,0:T(8,128)(2,1)} custom-call(bf16[160,1024]{1,0:T(8,128)(2,1)S(1)} %copy-done.37, bf16[160,1024]{1,0:T(8,128)(2,1)S(1)} %copy-done.39, bf16[160,1024]{1,0:T(8,128)(2,1)S(1)} %copy-done.41, bf16[160,1024]{1,0:T(8,128)(2,1)S(1)} %copy-done.43, bf16[160,1024]{1,0:T(8,128)(2,1)S(1)} %copy-done.49, ...), custom_call_target="tpu_custom_call" | custom-call | flops 5536481280 | bytes 17301504 | tf_op jit(solution)/shard_map/expert_grads/pallas_call | solution.py:955
  402.5 15.2 %attention_backward.2 = (bf16[1024,768]{1,0:T(8,128)(2,1)S(1)}, f32[512,1024]{1,0:T(8,128)S(1)}, bf16[512,1024]{1,0:T(8,128)(2,1)S(1)}, f32[8,512]{1,0:T(8,128)S(1)}, f32[8,1024]{1,0:T(8,128)S(1)}) custom-call(s32[3]{0:T(128)S(1)} %pad_add_fusion.refs_0_, bf16[256,1024]{1,0:T(8,128)(2,1)S(1)} %get-tuple-element.164.refs_1_.refs_5_, ...), custom_call_target="tpu_custom_call" | custom-call | flops 4831838208 | bytes 13225996 | tf_op jit(solution)/shard_map/attention_backward/pallas_call | solution.py:96
  422.7 19.2 %collective-permute-done.29.refs_4_ = bf16[256,1024]{1,0:T(8,128)(2,1)S(1)} collective-permute-done((bf16[256,1024]{1,0:T(8,128)(2,1)S(1)}, bf16[256,1024]{1,0:T(8,128)(2,1)S(1)}, u32[]{:S(2)}, u32[]{:S(2)}) %collective-permute-start.29) | collective-permute-done | bytes 524320 | tf_op jit(solution)/shard_map/ppermute | solution.py:1160
  445.7 11.7 %collective-permute-start.30 = (bf16[160,1024]{1,0:T(8,128)(2,1)S(1)}, bf16[160,1024]{1,0:T(8,128)(2,1)S(1)}, u32[]{:S(2)}, u32[]{:S(2)}) collective-permute-start(bf16[160,1024]{1,0:T(8,128)(2,1)S(1)} %get-tuple-element.171), channel_id=1, source_target_pairs={{0,8},{8,0},{16,24},{24,16},{1,9},{9,1},{17,25},{25,17},{2,10},{10... | collective-permute-start | bytes 983048 | tf_op jit(solution)/shard_map/ppermute | solution.py:1205
  469.3 15.3 %expert_backward.9 = (bf16[160,1024]{1,0:T(8,128)(2,1)}, bf16[160,1024]{1,0:T(8,128)(2,1)}, bf16[3,320,2816]{2,1,0:T(8,128)(2,1)}) custom-call(bf16[160,1024]{1,0:T(8,128)(2,1)} %copy-done.44, bf16[160,1024]{1,0:T(8,128)(2,1)} %copy-done.46, bf16[2,320,2816]{2,1,0:T(8,128)(2,1)} %get-tuple-element.172.refs_2_, bf16[2,1,1024,5632]{3,2,1,0:T(8,128)(2,1)} %refs_3_.24, ...), custom_call_target="tpu_custom_call" | custom-call | flops 5536481280 | bytes 17301504 | tf_op jit(solution)/shard_map/expert_backward/pallas_call | solution.py:955
  490.5 11.8 %expert_backward.10 = (bf16[160,1024]{1,0:T(8,128)(2,1)}, bf16[3,160,2816]{2,1,0:T(8,128)(2,1)}) custom-call(bf16[160,1024]{1,0:T(8,128)(2,1)} %copy-done.60, bf16[2,160,2816]{2,1,0:T(8,128)(2,1)} %get-tuple-element.176.refs_1_, bf16[2,1,1024,5632]{3,2,1,0:T(8,128)(2,1)} %refs_3_.24, bf16[2,1,1024,5632]{3,2,1,0:T(8,128)(2,1)} %refs_3_.24, ...), custom_call_target="tpu_custom_call" | custom-call | flops 5536481280 | bytes 17301504 | tf_op jit(solution)/shard_map/expert_backward/pallas_call | solution.py:955
  503.0 11.8 %expert_backward.11 = (bf16[160,1024]{1,0:T(8,128)(2,1)}, bf16[3,160,2816]{2,1,0:T(8,128)(2,1)}) custom-call(bf16[160,1024]{1,0:T(8,128)(2,1)} %copy-done.62, bf16[2,160,2816]{2,1,0:T(8,128)(2,1)} %get-tuple-element.179.refs_1_, bf16[2,1,1024,5632]{3,2,1,0:T(8,128)(2,1)} %refs_3_.24, bf16[2,1,1024,5632]{3,2,1,0:T(8,128)(2,1)} %refs_3_.24, ...), custom_call_target="tpu_custom_call" | custom-call | flops 5536481280 | bytes 17301504 | tf_op jit(solution)/shard_map/expert_backward/pallas_call | solution.py:955
  519.4 20.6 %expert_grads.3.refs_0_ = bf16[8,3,128,2816]{3,2,1,0:T(8,128)(2,1)} custom-call(bf16[160,1024]{1,0:T(8,128)(2,1)S(1)} %copy-done.29, bf16[160,1024]{1,0:T(8,128)(2,1)S(1)} %copy-done.31, bf16[160,1024]{1,0:T(8,128)(2,1)S(1)} %copy-done.33, bf16[160,1024]{1,0:T(8,128)(2,1)S(1)} %copy-done.35, bf16[160,1024]{1,0:T(8,128)(2,1)S(1)} %copy-done.45, ...), custom_call_target="tpu_custom_call" | custom-call | flops 5536481280 | bytes 17301504 | tf_op jit(solution)/shard_map/expert_grads/pallas_call | solution.py:955
  560.1 11.6 %collective-permute-done.38.refs_3_.refs_4_ = bf16[256,1024]{1,0:T(8,128)(2,1)S(1)} collective-permute-done((bf16[256,1024]{1,0:T(8,128)(2,1)S(1)}, bf16[256,1024]{1,0:T(8,128)(2,1)S(1)}, u32[]{:S(2)}, u32[]{:S(2)}) %collective-permute-start.38) | collective-permute-done | bytes 524320 | tf_op jit(solution)/shard_map/ppermute | solution.py:1151
  579.6 15.1 %attention_backward.3 = (bf16[1024,768]{1,0:T(8,128)(2,1)S(1)}, f32[512,1024]{1,0:T(8,128)S(1)}, bf16[512,1024]{1,0:T(8,128)(2,1)}, f32[8,512]{1,0:T(8,128)S(1)}, f32[8,1024]{1,0:T(8,128)S(1)}) custom-call(s32[3]{0:T(128)S(1)} %pad_add_fusion.refs_0_, bf16[256,1024]{1,0:T(8,128)(2,1)S(1)} %copy-done.71, ...), custom_call_target="tpu_custom_call" | custom-call | flops 4831838208 | bytes 13225996 | tf_op jit(solution)/shard_map/attention_backward/pallas_call | solution.py:96
  621.8 16.1 %collective-permute-done.41.refs_4_ = bf16[256,1024]{1,0:T(8,128)(2,1)} collective-permute-done((bf16[256,1024]{1,0:T(8,128)(2,1)}, bf16[256,1024]{1,0:T(8,128)(2,1)}, u32[]{:S(2)}, u32[]{:S(2)}) %collective-permute-start.41) | collective-permute-done | bytes 524320 | tf_op jit(solution)/shard_map/ppermute | solution.py:1160
  666.5 8.1 %all-to-all-done.6.refs_0_ = bf16[4,2,32,896]{3,2,1,0:T(8,128)(2,1)S(1)} async-done(((bf16[4,2,32,896]{3,2,1,0:T(8,128)(2,1)}), bf16[4,2,32,896]{3,2,1,0:T(8,128)(2,1)S(1)}, u32[]{:S(2)}, u32[]{:S(2)}) %all-to-all-start.6) | async-done | bytes 458784 | tf_op jit(solution)/shard_map/all_to_all | solution.py:1237
  (412 shorter events, 237.2 us)
Async XLA Ops:
  7.2 69.2 %all-gather.5.cloned.1.call-start = ((), (), s32[]{:S(2)}) async-start(), calls=%async_computation.11 | async-start | bytes 2654208 | tf_op jit(solution)/shard_map/all_gather | solution.py:1250
  24.0 112.3 %all-gather.7.cloned.1.call-start = ((), (), s32[]{:S(2)}) async-start(), calls=%async_computation.12 | async-start | bytes 2359296 | tf_op jit(solution)/shard_map/all_gather | solution.py:1250
  25.3 53.9 %collective-permute-start = (bf16[256,1024]{1,0:T(8,128)(2,1)S(1)}, bf16[256,1024]{1,0:T(8,128)(2,1)S(1)}, u32[]{:S(2)}, u32[]{:S(2)}) collective-permute-start(bf16[256,1024]{1,0:T(8,128)(2,1)S(1)} %bitcast.46), channel_id=1, source_target_pairs={{0,2},{2,0},{4,6},{6,4},{1,3},{3,1},{5,7},{7,5},{8,10},{10,8},{12,... | collective-permute-start | bytes 1572872 | tf_op jit(solution)/shard_map/ppermute | solution.py:1152
  38.7 40.5 %collective-permute-start.2 = (bf16[256,1024]{1,0:T(8,128)(2,1)S(1)}, bf16[256,1024]{1,0:T(8,128)(2,1)S(1)}, u32[]{:S(2)}, u32[]{:S(2)}) collective-permute-start(bf16[256,1024]{1,0:T(8,128)(2,1)S(1)} %collective-permute-done.1.refs_3_), channel_id=1, source_target_pairs={{0,2},{2,0},{4,6},{6,4},{1,3},{3,1},{5,7},{7,5},{8,10},{10,8},{12,... | collective-permute-start | bytes 1572872 | tf_op jit(solution)/shard_map/ppermute | solution.py:1153
  118.3 21.6 %collective-permute-start.5 = (bf16[160,1024]{1,0:T(8,128)(2,1)}, bf16[160,1024]{1,0:T(8,128)(2,1)S(1)}, u32[]{:S(2)}, u32[]{:S(2)}) collective-permute-start(bf16[160,1024]{1,0:T(8,128)(2,1)} %get-tuple-element.123), channel_id=1, source_target_pairs={{0,8},{8,0},{16,24},{24,16},{1,9},{9,1},{17,25},{25,17},{2,10},{10... | collective-permute-start | bytes 983048 | tf_op jit(solution)/shard_map/ppermute | solution.py:1205
  119.7 33.6 %collective-permute-start.7 = (bf16[160,1024]{1,0:T(8,128)(2,1)}, bf16[160,1024]{1,0:T(8,128)(2,1)S(1)}, u32[]{:S(2)}, u32[]{:S(2)}) collective-permute-start(bf16[160,1024]{1,0:T(8,128)(2,1)} %get-tuple-element.127), channel_id=1, source_target_pairs={{0,16},{8,24},{16,0},{24,8},{1,17},{9,25},{17,1},{25,9},{2,18},{10... | collective-permute-start | bytes 983048 | tf_op jit(solution)/shard_map/ppermute | solution.py:1205
  120.7 46.0 %collective-permute-start.9 = (bf16[160,1024]{1,0:T(8,128)(2,1)}, bf16[160,1024]{1,0:T(8,128)(2,1)S(1)}, u32[]{:S(2)}, u32[]{:S(2)}) collective-permute-start(bf16[160,1024]{1,0:T(8,128)(2,1)} %get-tuple-element.129), channel_id=1, source_target_pairs={{0,24},{8,16},{16,8},{24,0},{1,25},{9,17},{17,9},{25,1},{2,26},{10... | collective-permute-start | bytes 983048 | tf_op jit(solution)/shard_map/ppermute | solution.py:1205
  153.4 25.8 %collective-permute-start.6 = (bf16[160,1024]{1,0:T(8,128)(2,1)}, bf16[160,1024]{1,0:T(8,128)(2,1)S(1)}, u32[]{:S(2)}, u32[]{:S(2)}) collective-permute-start(bf16[160,1024]{1,0:T(8,128)(2,1)} %get-tuple-element.126), channel_id=1, source_target_pairs={{0,8},{8,0},{16,24},{24,16},{1,9},{9,1},{17,25},{25,17},{2,10},{10... | collective-permute-start | bytes 983048 | tf_op jit(solution)/shard_map/ppermute | solution.py:1205
  164.1 25.8 %collective-permute-start.8 = (bf16[160,1024]{1,0:T(8,128)(2,1)}, bf16[160,1024]{1,0:T(8,128)(2,1)S(1)}, u32[]{:S(2)}, u32[]{:S(2)}) collective-permute-start(bf16[160,1024]{1,0:T(8,128)(2,1)} %get-tuple-element.128.refs_4_), channel_id=1, source_target_pairs={{0,16},{8,24},{16,0},{24,8},{1,17},{9,25},{17,1},{25,9},{2,18},{10... | collective-permute-start | bytes 983048 | tf_op jit(solution)/shard_map/ppermute | solution.py:1205
  195.4 21.3 %collective-permute-start.11 = (bf16[256,1024]{1,0:T(8,128)(2,1)}, bf16[256,1024]{1,0:T(8,128)(2,1)}, u32[]{:S(2)}, u32[]{:S(2)}) collective-permute-start(bf16[256,1024]{1,0:T(8,128)(2,1)} %hold.5.refs_1_.refs_12_), channel_id=1, source_target_pairs={{0,2},{2,0},{4,6},{6,4},{1,3},{3,1},{5,7},{7,5},{8,10},{10,8},{12,... | collective-permute-start | bytes 1572872 | tf_op jit(solution)/shard_map/ppermute | solution.py:1152
  205.8 43.6 %all-to-all-start.1 = ((bf16[4,160,1024]{2,1,0:T(8,128)(2,1)}), bf16[4,160,1024]{2,1,0:T(8,128)(2,1)}, u32[]{:S(2)}, u32[]{:S(2)}) async-start(bf16[4,160,1024]{2,1,0:T(8,128)(2,1)} %bitcast.11), calls=%async_computation.1 | async-start | bytes 2621440 | tf_op jit(solution)/shard_map/all_to_all | solution.py:1199
  259.9 28.2 %all-to-all-start.2 = ((f32[4,160,128]{2,1,0:T(8,128)}), f32[4,160,128]{2,1,0:T(8,128)S(1)}, u32[]{:S(2)}, u32[]{:S(2)}) async-start(f32[4,160,128]{2,1,0:T(8,128)} %bitcast.50), calls=%async_computation.2 | async-start | bytes 655360 | tf_op jit(solution)/shard_map/all_to_all | solution.py:1199
  263.3 354.9 %reduce-scatter.3.cloned.1.call-start = ((), (), s32[]{:S(2)}) async-start(), calls=%async_computation.9 | async-start | bytes 19464192 | tf_op jit(solution)/shard_map/reduce_scatter | solution.py:1357
  263.6 45.2 %collective-permute-start.18 = (bf16[160,1024]{1,0:T(8,128)(2,1)}, bf16[160,1024]{1,0:T(8,128)(2,1)S(1)}, u32[]{:S(2)}, u32[]{:S(2)}) collective-permute-start(bf16[160,1024]{1,0:T(8,128)(2,1)} %copy-done.101), channel_id=1, source_target_pairs={{0,16},{8,24},{16,0},{24,8},{1,17},{9,25},{17,1},{25,9},{2,18},{10... | collective-permute-start | bytes 983048 | tf_op jit(solution)/shard_map/ppermute | solution.py:1205
  266.5 67.9 %collective-permute-start.20 = (bf16[160,1024]{1,0:T(8,128)(2,1)}, bf16[160,1024]{1,0:T(8,128)(2,1)S(1)}, u32[]{:S(2)}, u32[]{:S(2)}) collective-permute-start(bf16[160,1024]{1,0:T(8,128)(2,1)} %copy-done.100), channel_id=1, source_target_pairs={{0,24},{8,16},{16,8},{24,0},{1,25},{9,17},{17,9},{25,1},{2,26},{10... | collective-permute-start | bytes 983048 | tf_op jit(solution)/shard_map/ppermute | solution.py:1205
  286.7 73.7 %collective-permute-start.17 = (bf16[160,1024]{1,0:T(8,128)(2,1)}, bf16[160,1024]{1,0:T(8,128)(2,1)S(1)}, u32[]{:S(2)}, u32[]{:S(2)}) collective-permute-start(bf16[160,1024]{1,0:T(8,128)(2,1)} %get-tuple-element.142), channel_id=1, source_target_pairs={{0,8},{8,0},{16,24},{24,16},{1,9},{9,1},{17,25},{25,17},{2,10},{10... | collective-permute-start | bytes 983048 | tf_op jit(solution)/shard_map/ppermute | solution.py:1205
  308.2 74.4 %collective-permute-start.22 = (bf16[160,1024]{1,0:T(8,128)(2,1)}, bf16[160,1024]{1,0:T(8,128)(2,1)S(1)}, u32[]{:S(2)}, u32[]{:S(2)}) collective-permute-start(bf16[160,1024]{1,0:T(8,128)(2,1)} %get-tuple-element.155), channel_id=1, source_target_pairs={{0,8},{8,0},{16,24},{24,16},{1,9},{9,1},{17,25},{25,17},{2,10},{10... | collective-permute-start | bytes 983048 | tf_op jit(solution)/shard_map/ppermute | solution.py:1205
  319.5 41.6 %collective-permute-start.19 = (bf16[160,1024]{1,0:T(8,128)(2,1)}, bf16[160,1024]{1,0:T(8,128)(2,1)S(1)}, u32[]{:S(2)}, u32[]{:S(2)}) collective-permute-start(bf16[160,1024]{1,0:T(8,128)(2,1)} %get-tuple-element.149), channel_id=1, source_target_pairs={{0,16},{8,24},{16,0},{24,8},{1,17},{9,25},{17,1},{25,9},{2,18},{10... | collective-permute-start | bytes 983048 | tf_op jit(solution)/shard_map/ppermute | solution.py:1205
  333.2 49.5 %collective-permute-start.23 = (bf16[160,1024]{1,0:T(8,128)(2,1)}, bf16[160,1024]{1,0:T(8,128)(2,1)S(1)}, u32[]{:S(2)}, u32[]{:S(2)}) collective-permute-start(bf16[160,1024]{1,0:T(8,128)(2,1)} %get-tuple-element.153.refs_4_), channel_id=1, source_target_pairs={{0,16},{8,24},{16,0},{24,8},{1,17},{9,25},{17,1},{25,9},{2,18},{10... | collective-permute-start | bytes 983048 | tf_op jit(solution)/shard_map/ppermute | solution.py:1205
  360.4 22.2 %collective-permute-start.24 = (bf16[160,1024]{1,0:T(8,128)(2,1)}, bf16[160,1024]{1,0:T(8,128)(2,1)S(1)}, u32[]{:S(2)}, u32[]{:S(2)}) collective-permute-start(bf16[160,1024]{1,0:T(8,128)(2,1)} %get-tuple-element.158), channel_id=1, source_target_pairs={{0,24},{8,16},{16,8},{24,0},{1,25},{9,17},{17,9},{25,1},{2,26},{10... | collective-permute-start | bytes 983048 | tf_op jit(solution)/shard_map/ppermute | solution.py:1205
  384.2 293.5 %reduce-scatter.5.cloned.1.call-start = ((), (), s32[]{:S(2)}) async-start(), calls=%async_computation.10 | async-start | bytes 19464192 | tf_op jit(solution)/shard_map/reduce_scatter | solution.py:1357
  445.7 22.9 %collective-permute-start.30 = (bf16[160,1024]{1,0:T(8,128)(2,1)S(1)}, bf16[160,1024]{1,0:T(8,128)(2,1)S(1)}, u32[]{:S(2)}, u32[]{:S(2)}) collective-permute-start(bf16[160,1024]{1,0:T(8,128)(2,1)S(1)} %get-tuple-element.171), channel_id=1, source_target_pairs={{0,8},{8,0},{16,24},{24,16},{1,9},{9,1},{17,25},{25,17},{2,10},{10... | collective-permute-start | bytes 983048 | tf_op jit(solution)/shard_map/ppermute | solution.py:1205
  464.7 52.6 %collective-permute-start.36 = (bf16[4,128,1152]{2,1,0:T(8,128)(2,1)S(1)}, bf16[4,128,1152]{2,1,0:T(8,128)(2,1)S(1)}, u32[]{:S(2)}, u32[]{:S(2)}) collective-permute-start(bf16[4,128,1152]{2,1,0:T(8,128)(2,1)S(1)} %get-tuple-element.191), channel_id=1, source_target_pairs={{0,1},{1,0},{2,3},{3,2},{4,5},{5,4},{6,7},{7,6},{8,9},{9,8},{10,11... | collective-permute-start | bytes 3538952 | tf_op jit(solution)/shard_map/ppermute | solution.py:1390
  465.0 24.7 %collective-permute-start.32 = (bf16[160,1024]{1,0:T(8,128)(2,1)S(1)}, bf16[160,1024]{1,0:T(8,128)(2,1)S(1)}, u32[]{:S(2)}, u32[]{:S(2)}) collective-permute-start(bf16[160,1024]{1,0:T(8,128)(2,1)S(1)} %get-tuple-element.175), channel_id=1, source_target_pairs={{0,16},{8,24},{16,0},{24,8},{1,17},{9,25},{17,1},{25,9},{2,18},{10... | collective-permute-start | bytes 983048 | tf_op jit(solution)/shard_map/ppermute | solution.py:1205
  467.1 35.2 %collective-permute-start.34 = (bf16[160,1024]{1,0:T(8,128)(2,1)S(1)}, bf16[160,1024]{1,0:T(8,128)(2,1)S(1)}, u32[]{:S(2)}, u32[]{:S(2)}) collective-permute-start(bf16[160,1024]{1,0:T(8,128)(2,1)S(1)} %get-tuple-element.178), channel_id=1, source_target_pairs={{0,24},{8,16},{16,8},{24,0},{1,25},{9,17},{17,9},{25,1},{2,26},{10... | collective-permute-start | bytes 983048 | tf_op jit(solution)/shard_map/ppermute | solution.py:1205
  484.7 55.3 %collective-permute-start.31 = (bf16[160,1024]{1,0:T(8,128)(2,1)}, bf16[160,1024]{1,0:T(8,128)(2,1)}, u32[]{:S(2)}, u32[]{:S(2)}) collective-permute-start(bf16[160,1024]{1,0:T(8,128)(2,1)} %get-tuple-element.174.refs_5_), channel_id=1, source_target_pairs={{0,8},{8,0},{16,24},{24,16},{1,9},{9,1},{17,25},{25,17},{2,10},{10... | collective-permute-start | bytes 983048 | tf_op jit(solution)/shard_map/ppermute | solution.py:1205
  502.2 37.8 %collective-permute-start.33 = (bf16[160,1024]{1,0:T(8,128)(2,1)}, bf16[160,1024]{1,0:T(8,128)(2,1)S(1)}, u32[]{:S(2)}, u32[]{:S(2)}) collective-permute-start(bf16[160,1024]{1,0:T(8,128)(2,1)} %get-tuple-element.177.refs_5_), channel_id=1, source_target_pairs={{0,16},{8,24},{16,0},{24,8},{1,17},{9,25},{17,1},{25,9},{2,18},{10... | collective-permute-start | bytes 983048 | tf_op jit(solution)/shard_map/ppermute | solution.py:1205
  514.9 25.2 %collective-permute-start.35 = (bf16[160,1024]{1,0:T(8,128)(2,1)}, bf16[160,1024]{1,0:T(8,128)(2,1)S(1)}, u32[]{:S(2)}, u32[]{:S(2)}) collective-permute-start(bf16[160,1024]{1,0:T(8,128)(2,1)} %get-tuple-element.180), channel_id=1, source_target_pairs={{0,24},{8,16},{16,8},{24,0},{1,25},{9,17},{17,9},{25,1},{2,26},{10... | collective-permute-start | bytes 983048 | tf_op jit(solution)/shard_map/ppermute | solution.py:1205
  553.4 43.9 %all-to-all-start.3 = ((bf16[4,128,1152]{2,1,0:T(8,128)(2,1)}), bf16[4,128,1152]{2,1,0:T(8,128)(2,1)}, u32[]{:S(2)}, u32[]{:S(2)}) async-start(bf16[4,128,1152]{2,1,0:T(8,128)(2,1)} %add_convert_fusion), calls=%async_computation.4 | async-start | bytes 2359296 | tf_op jit(solution)/shard_map/all_to_all | solution.py:1199
  606.1 37.1 %all-to-all-start.5 = ((bf16[4,2,128,640]{3,2,1,0:T(8,128)(2,1)}), bf16[4,2,128,640]{3,2,1,0:T(8,128)(2,1)}, u32[]{:S(2)}, u32[]{:S(2)}) async-start(bf16[4,2,128,640]{3,2,1,0:T(8,128)(2,1)} %copy-done.56), calls=%async_computation.6 | async-start | bytes 2621440 | tf_op jit(solution)/shard_map/all_to_all | solution.py:1199
  613.2 24.7 %collective-permute-start.41 = (bf16[256,1024]{1,0:T(8,128)(2,1)}, bf16[256,1024]{1,0:T(8,128)(2,1)}, u32[]{:S(2)}, u32[]{:S(2)}) collective-permute-start(bf16[256,1024]{1,0:T(8,128)(2,1)} %add_convert_fusion.2), channel_id=1, source_target_pairs={{0,4},{2,6},{4,0},{6,2},{1,5},{3,7},{5,1},{7,3},{8,12},{10,14},{12... | collective-permute-start | bytes 1572872 | tf_op jit(solution)/shard_map/ppermute | solution.py:1160
  614.7 26.2 %collective-permute-start.42 = (bf16[4,128,512]{2,1,0:T(8,128)(2,1)}, bf16[4,128,512]{2,1,0:T(8,128)(2,1)}, u32[]{:S(2)}, u32[]{:S(2)}) collective-permute-start(bf16[4,128,512]{2,1,0:T(8,128)(2,1)} %copy-done.96), channel_id=1, source_target_pairs={{0,1},{1,0},{2,3},{3,2},{4,5},{5,4},{6,7},{7,6},{8,9},{9,8},{10,11... | collective-permute-start | bytes 1572872 | tf_op jit(solution)/shard_map/ppermute | solution.py:1390
  (152 other events, 1706.6 us)
Sparse Core Ops, SparseCore 0:
  24.2 52.2 all-gather.4
  79.1 57.2 all-gather.6
  384.3 143.9 reduce-scatter.2
  541.0 132.5 reduce-scatter.4

commit v5 on v4

--- a/solution.py
+++ b/solution.py
@@ -1227,7 +1227,8 @@
     capacity = (10 * rows + 4 * experts - 1) // (4 * experts)
     slots = experts * capacity
     blocks = experts if experts == 4 and capacity % 16 == 0 else 1
-    chunks = [(0, 1), (2,), (3,)] if blocks == 4 else [(0,)]
+    fine = [(0, 1), (2,), (3,)] if blocks == 4 else [(0,)]
+    coarse = [(0, 1), (2, 3)] if blocks == 4 else [(0,)]
     grad_in = out_grad[0]
     hits = jnp.asarray(bucket_hits())
 
@@ -1292,18 +1293,19 @@
             layer, place, pieces, w_in[layer], feature, bias, low, w_out[layer]
         )
         normed_rows = normed_all if layer == 0 else pieces
+        last = layer == LAYERS - 1
+        if last:
+            send = hold(send, [arrived_grad])
         keep, recv, far = sum_pieces(keep, send)
-        last = layer == LAYERS - 1
         middle, soft, meta, dest, *sent = route(
             layer, experts, capacity, blocks, place, x, keep, recv, far, feature, ids, idst, last,
-            after=[arrived_grad] if last else [],
         )
         arrived = swap(sent[:blocks], experts)
         if last:
             gates = exchange(sent[blocks])
         produced, acts, drows, parts = [], [], [], []
         order = second if layer == 0 else []
-        for chunk in chunks:
+        for chunk in coarse if last else fine:
             done, kept_acts = expert_forward(
                 layer, [arrived[k] for k in chunk], expert_in, expert_out, after=order
             )
@@ -1341,10 +1343,11 @@
          back) = kept[layer]
         if layer < LAYERS - 1:
             drows, parts = [], []
-            for index, chunk in enumerate(chunks):
+            for index, chunk in enumerate(coarse):
+                some_acts = acts[:1] if index == 0 else acts[1:]
                 done, some = expert_backward(
-                    layer, [arrived_grad[k] for k in chunk], len(chunk), acts[index : index + 1],
-                    expert_in, expert_out, after=drows[-1:],
+                    layer, [arrived_grad[k] for k in chunk], len(chunk), some_acts, expert_in,
+                    expert_out, after=drows[-1:],
                 )
                 drows += done
                 parts.append(some)

time: 698 us -> 696 us (level)
  Pallas kernels: 288 us -> 263 us
  waiting for transfers between devices: 210 us -> 232 us
    pallas_call x14 -> x11, Pallas kernels: 184 us -> 160 us  [expert_call(): pl.pallas_call(ordered, grid=(steps,), out_shape=tuple(outs), in_specs=li...]
    ppermute x4, waiting for transfers between devices: 47.6 us -> 65.7 us  [sum_pieces(): return (keep, recv, lax.ppermute(other, 'context', ACROSS))]
    all_to_all x5, waiting for transfers between devices: 18.7 us -> 6.51 us  [exchange(): lax.all_to_all(rows, 'experts', split_axis=0, concat_axis=0, tiled=True)]
    ppermute x21, waiting for transfers between devices: 24.2 us -> 32.6 us  [swap(): lax.ppermute(part, 'experts', [(i, i ^ k) for i in range(experts)])]
    unnamed x265 -> x267, local copies, waits for them, and re-layouts: 58 us -> 58.5 us
  transfers between devices with their start and end apart: 54 -> 54, of which waited for: 23 -> 25; matrix products, arithmetic and copies ran while one was open for 2% -> 2% of each run, Pallas kernels for 40% -> 37%
where the time goes in v5:
time: 696 us; the launch traced here: 685 us
  Pallas kernels  263 us (38%)
  waiting for transfers between devices  232 us (33%)
  starting transfers between devices  89.2 us (13%)
  local copies, waits for them, and re-layouts  59.4 us (9%)
  between operations  15.3 us (2%)
  other arithmetic  13.9 us (2%)
  blocking collectives  11.8 us (2%)
    pallas_call x11, Pallas kernels, expert_call(): pl.pallas_call(ordered, grid=(steps,), out_shape=tuple(outs), in_specs=li...  160 us
    pallas_call x14, Pallas kernels, whole_call(): pl.pallas_call(ordered, out_shape=outs, in_specs=specs, out_specs=tuple((...  68.5 us
    ppermute x4, waiting for transfers between devices, sum_pieces(): return (keep, recv, lax.ppermute(other, 'context', ACROSS))  65.7 us
    unnamed x267, local copies, waits for them, and re-layouts  58.5 us
    all_gather x2, waiting for transfers between devices, together(): return lax.all_gather(part, ('experts', 'dp'), axis=0, tiled=False)  51.2 us
    ppermute x4, waiting for transfers between devices, share_pieces(): across = lax.ppermute(piece, 'context', ACROSS)  47.2 us
    ppermute x21, starting transfers between devices, swap(): lax.ppermute(part, 'experts', [(i, i ^ k) for i in range(experts)])  43.4 us
    ppermute x21, waiting for transfers between devices, swap(): lax.ppermute(part, 'experts', [(i, i ^ k) for i in range(experts)])  32.6 us
  transfers between devices with their start and end apart: 54, of which 25 were waited for; matrix products, arithmetic and copies ran while one was open for 2% of the time, Pallas kernels for 37%

profile of v5, /device:TPU:0, one launch (start us, length us, event | category | flops | bytes accessed | tf_op | source)
XLA Modules:
  0.0 684.8 jit_solution(13997375720835135385)
XLA Ops:
  11.5 11.8 %all_to_all.47 = bf16[4,32,1664]{2,1,0:T(8,128)(2,1)S(1)} all-to-all(bf16[4,32,1664]{2,1,0:T(8,128)(2,1)S(1)} %get-tuple-element.109), channel_id=1, replica_groups=mesh['experts'=4,'context'=4,'dp'=2] {'context'}, dimensions={0} | all-to-all | bytes 851968 | tf_op jit(solution)/shard_map/all_to_all | solution.py:1238
  25.3 13.4 %collective-permute-done.1.refs_3_ = bf16[256,1024]{1,0:T(8,128)(2,1)S(1)} collective-permute-done((bf16[256,1024]{1,0:T(8,128)(2,1)S(1)}, bf16[256,1024]{1,0:T(8,128)(2,1)S(1)}, u32[]{:S(2)}, u32[]{:S(2)}) %collective-permute-start.1) | collective-permute-done | bytes 524320 | tf_op jit(solution)/shard_map/ppermute | solution.py:1151
  38.9 37.5 %all-gather.5.cloned.1.call-done = bf16[32,32,1152]{2,1,0:T(8,128)(2,1)} async-done(((bf16[4,32,1152]{2,1,0:T(8,128)(2,1)}), bf16[32,32,1152]{2,1,0:T(8,128)(2,1)}) %all-gather.5.cloned.1.call-update) | async-done | bytes 2359312 | tf_op jit(solution)/shard_map/all_gather | solution.py:1251
  79.3 9.9 %attention_forward.2 = (bf16[1024,768]{1,0:T(8,128)(2,1)S(1)}, f32[8,1024]{1,0:T(8,128)S(1)}, bf16[1024,256]{1,0:T(8,128)(2,1)S(1)}, f32[512,1024]{1,0:T(8,128)S...) custom-call(s32[3]{0:T(128)S(1)} %pad_add_fusion.refs_0_, bf16[256,1024]{1,0:T(8,128)(2,1)S(1)} %bitcast.47, ...), custom_call_target="tpu_custom_call" | custom-call | flops 3221225472 | bytes 12128268 | tf_op jit(solution)/shard_map/attention_forward/pallas_call | solution.py:96
  97.8 12.3 %collective-permute-done.4.refs_4_ = bf16[256,1024]{1,0:T(8,128)(2,1)S(1)} collective-permute-done((bf16[256,1024]{1,0:T(8,128)(2,1)S(1)}, bf16[256,1024]{1,0:T(8,128)(2,1)S(1)}, u32[]{:S(2)}, u32[]{:S(2)}) %collective-permute-start.4) | collective-permute-done | bytes 524320 | tf_op jit(solution)/shard_map/ppermute | solution.py:1160
  122.7 13.7 %all-gather.7.cloned.1.call-done = bf16[32,32,1024]{2,1,0:T(8,128)(2,1)} async-done(((bf16[4,32,1024]{2,1,0:T(8,128)(2,1)}), bf16[32,32,1024]{2,1,0:T(8,128)(2,1)}) %all-gather.7.cloned.1.call-update) | async-done | bytes 2097168 | tf_op jit(solution)/shard_map/all_gather | solution.py:1251
  140.6 12.8 %expert_forward.5 = (bf16[160,1024]{1,0:T(8,128)(2,1)}, bf16[160,1024]{1,0:T(8,128)(2,1)}, bf16[2,320,2816]{2,1,0:T(8,128)(2,1)}) custom-call(bf16[160,1024]{1,0:T(8,128)(2,1)} %copy-done.28, bf16[160,1024]{1,0:T(8,128)(2,1)} %copy-done.30, bf16[2,1,1024,5632]{3,2,1,0:T(8,128)(2,1)} %refs_5_.7, bf16[2,1,1024,5632]{3,2,1,0:T(8,128)(2,1)} %refs_5_.7, ...), custom_call_target="tpu_custom_call" | custom-call | flops 5536481280 | bytes 17301504 | tf_op jit(solution)/shard_map/expert_forward/pallas_call | solution.py:955
  154.2 10.0 %expert_forward.6 = (bf16[160,1024]{1,0:T(8,128)(2,1)}, bf16[2,160,2816]{2,1,0:T(8,128)(2,1)}) custom-call(bf16[160,1024]{1,0:T(8,128)(2,1)} %copy-done.32, bf16[2,1,1024,5632]{3,2,1,0:T(8,128)(2,1)} %refs_5_.7, bf16[2,1,1024,5632]{3,2,1,0:T(8,128)(2,1)} %refs_5_.7, bf16[2,1,1024,2816]{3,2,1,0:T(8,128)(2,1)} %refs_6_.1, ...), custom_call_target="tpu_custom_call" | custom-call | flops 5536481280 | bytes 17301504 | tf_op jit(solution)/shard_map/expert_forward/pallas_call | solution.py:955
  167.5 9.9 %expert_forward.7 = (bf16[160,1024]{1,0:T(8,128)(2,1)}, bf16[2,160,2816]{2,1,0:T(8,128)(2,1)}) custom-call(bf16[160,1024]{1,0:T(8,128)(2,1)} %copy-done.34, bf16[2,1,1024,5632]{3,2,1,0:T(8,128)(2,1)} %refs_5_.7, bf16[2,1,1024,5632]{3,2,1,0:T(8,128)(2,1)} %refs_5_.7, bf16[2,1,1024,2816]{3,2,1,0:T(8,128)(2,1)} %refs_6_.1, ...), custom_call_target="tpu_custom_call" | custom-call | flops 5536481280 | bytes 17301504 | tf_op jit(solution)/shard_map/expert_forward/pallas_call | solution.py:955
  179.3 10.7 %collective-permute-done.8.refs_4_.refs_2_ = bf16[160,1024]{1,0:T(8,128)(2,1)S(1)} collective-permute-done((bf16[160,1024]{1,0:T(8,128)(2,1)}, bf16[160,1024]{1,0:T(8,128)(2,1)S(1)}, u32[]{:S(2)}, u32[]{:S(2)}) %collective-permute-start.8) | collective-permute-done | bytes 327712 | tf_op jit(solution)/shard_map/ppermute | solution.py:1205
  193.9 8.2 %all-to-all-start.1 = ((bf16[4,160,1024]{2,1,0:T(8,128)(2,1)}), bf16[4,160,1024]{2,1,0:T(8,128)(2,1)}, u32[]{:S(2)}, u32[]{:S(2)}) async-start(bf16[4,160,1024]{2,1,0:T(8,128)(2,1)} %bitcast.11), calls=%async_computation.1 | async-start | bytes 2621440 | tf_op jit(solution)/shard_map/all_to_all | solution.py:1199
  203.7 11.1 %collective-permute-done.12.refs_3_.refs_14_ = bf16[256,1024]{1,0:T(8,128)(2,1)S(1)} collective-permute-done((bf16[256,1024]{1,0:T(8,128)(2,1)}, bf16[256,1024]{1,0:T(8,128)(2,1)S(1)}, u32[]{:S(2)}, u32[]{:S(2)}) %collective-permute-start.12) | collective-permute-done | bytes 524320 | tf_op jit(solution)/shard_map/ppermute | solution.py:1151
  216.7 9.8 %attention_forward.3 = (bf16[1024,768]{1,0:T(8,128)(2,1)S(1)}, f32[8,1024]{1,0:T(8,128)S(1)}, bf16[1024,256]{1,0:T(8,128)(2,1)S(1)}, f32[512,1024]{1,0:T(8,128)S(1)}, bf16[512,1024]{1,0:T(8,128)(2,1)S(1)}) custom-call(s32[3]{0:T(128)S(1)} %pad_add_fusion.refs_0_, bf16[256,1024]{1,0:T(8,128)(2,1)S(1)} %copy-done.76, ...), custom_call_target="tpu_custom_call" | custom-call | flops 3221225472 | bytes 10031116 | tf_op jit(solution)/shard_map/attention_forward/pallas_call | solution.py:96
  238.2 12.5 %collective-permute-done.15.refs_4_ = bf16[256,1024]{1,0:T(8,128)(2,1)S(1)} collective-permute-done((bf16[256,1024]{1,0:T(8,128)(2,1)S(1)}, bf16[256,1024]{1,0:T(8,128)(2,1)S(1)}, u32[]{:S(2)}, u32[]{:S(2)}) %collective-permute-start.15) | collective-permute-done | bytes 524320 | tf_op jit(solution)/shard_map/ppermute | solution.py:1160
  272.4 12.8 %expert_forward.8 = (bf16[160,1024]{1,0:T(8,128)(2,1)}, bf16[160,1024]{1,0:T(8,128)(2,1)}, bf16[2,320,2816]{2,1,0:T(8,128)(2,1)}) custom-call(bf16[160,1024]{1,0:T(8,128)(2,1)} %copy-done.36, bf16[160,1024]{1,0:T(8,128)(2,1)} %copy-done.38, bf16[2,1,1024,5632]{3,2,1,0:T(8,128)(2,1)} %refs_5_.7, bf16[2,1,1024,5632]{3,2,1,0:T(8,128)(2,1)} %refs_5_.7, ...), custom_call_target="tpu_custom_call" | custom-call | flops 5536481280 | bytes 17301504 | tf_op jit(solution)/shard_map/expert_forward/pallas_call | solution.py:955
  294.4 14.8 %expert_backward.4 = (bf16[160,1024]{1,0:T(8,128)(2,1)}, bf16[160,1024]{1,0:T(8,128)(2,1)}, bf16[3,320,2816]{2,1,0:T(8,128)(2,1)}) custom-call(bf16[160,1024]{1,0:T(8,128)(2,1)} %copy-done.44, bf16[160,1024]{1,0:T(8,128)(2,1)} %copy-done.46, bf16[2,320,2816]{2,1,0:T(8,128)(2,1)} %get-tuple-element.145.refs_2_, bf16[2,1,1024,5632]{3,2,1,0:T(8,128)(2,1)} %refs_5_.7, ...), custom_call_target="tpu_custom_call" | custom-call | flops 5536481280 | bytes 17301504 | tf_op jit(solution)/shard_map/expert_backward/pallas_call | solution.py:955
  310.0 12.8 %expert_forward.9 = (bf16[160,1024]{1,0:T(8,128)(2,1)}, bf16[160,1024]{1,0:T(8,128)(2,1)}, bf16[2,320,2816]{2,1,0:T(8,128)(2,1)}) custom-call(bf16[160,1024]{1,0:T(8,128)(2,1)} %copy-done.56, bf16[160,1024]{1,0:T(8,128)(2,1)} %copy-done.58, bf16[2,1,1024,5632]{3,2,1,0:T(8,128)(2,1)} %refs_5_.7, bf16[2,1,1024,5632]{3,2,1,0:T(8,128)(2,1)} %refs_5_.7, ...), custom_call_target="tpu_custom_call" | custom-call | flops 5536481280 | bytes 17301504 | tf_op jit(solution)/shard_map/expert_forward/pallas_call | solution.py:955
  327.2 15.0 %expert_backward.5 = (bf16[160,1024]{1,0:T(8,128)(2,1)}, bf16[160,1024]{1,0:T(8,128)(2,1)}, bf16[3,320,2816]{2,1,0:T(8,128)(2,1)}) custom-call(bf16[160,1024]{1,0:T(8,128)(2,1)} %copy-done.48, bf16[160,1024]{1,0:T(8,128)(2,1)} %copy-done.50, bf16[2,320,2816]{2,1,0:T(8,128)(2,1)} %get-tuple-element.152.refs_2_, bf16[2,1,1024,5632]{3,2,1,0:T(8,128)(2,1)} %refs_5_.7, ...), custom_call_target="tpu_custom_call" | custom-call | flops 5536481280 | bytes 17301504 | tf_op jit(solution)/shard_map/expert_backward/pallas_call | solution.py:955
  343.7 11.9 %collective-permute-done.20.refs_4_.refs_12_.refs_2_ = bf16[160,1024]{1,0:T(8,128)(2,1)S(1)} collective-permute-done((bf16[160,1024]{1,0:T(8,128)(2,1)}, bf16[160,1024]{1,0:T(8,128)(2,1)S(1)}, u32[]{:S(2)}, u32[]{:S(2)}) %collective-permute-start.20) | collective-permute-done | bytes 327712 | tf_op jit(solution)/shard_map/ppermute | solution.py:1205
  356.5 20.5 %expert_grads.2.refs_0_ = bf16[8,3,128,2816]{3,2,1,0:T(8,128)(2,1)} custom-call(bf16[160,1024]{1,0:T(8,128)(2,1)S(1)} %copy-done.37, bf16[160,1024]{1,0:T(8,128)(2,1)S(1)} %copy-done.39, bf16[160,1024]{1,0:T(8,128)(2,1)S(1)} %copy-done.57, bf16[160,1024]{1,0:T(8,128)(2,1)S(1)} %copy-done.59, bf16[160,1024]{1,0:T(8,128)(2,1)S(1)} %copy-done.45, ...), custom_call_target="tpu_custom_call" | custom-call | flops 5536481280 | bytes 17301504 | tf_op jit(solution)/shard_map/expert_grads/pallas_call | solution.py:955
  386.7 10.8 %collective-permute-done.26.refs_3_.refs_7_ = bf16[256,1024]{1,0:T(8,128)(2,1)S(1)} collective-permute-done((bf16[256,1024]{1,0:T(8,128)(2,1)S(1)}, bf16[256,1024]{1,0:T(8,128)(2,1)S(1)}, u32[]{:S(2)}, u32[]{:S(2)}) %collective-permute-start.26) | collective-permute-done | bytes 524320 | tf_op jit(solution)/shard_map/ppermute | solution.py:1151
  400.1 14.2 %attention_backward.2 = (bf16[1024,768]{1,0:T(8,128)(2,1)S(1)}, f32[512,1024]{1,0:T(8,128)S(1)}, bf16[512,1024]{1,0:T(8,128)(2,1)S(1)}, f32[8,512]{1,0:T(8,128)S(1)}, f32[8,1024]{1,0:T(8,128)S(1)}) custom-call(s32[3]{0:T(128)S(1)} %pad_add_fusion.refs_0_, bf16[256,1024]{1,0:T(8,128)(2,1)S(1)} %get-tuple-element.159.refs_1_.refs_5_, ...), custom_call_target="tpu_custom_call" | custom-call | flops 4831838208 | bytes 13225996 | tf_op jit(solution)/shard_map/attention_backward/pallas_call | solution.py:96
  418.2 23.6 %collective-permute-done.29.refs_4_ = bf16[256,1024]{1,0:T(8,128)(2,1)S(1)} collective-permute-done((bf16[256,1024]{1,0:T(8,128)(2,1)S(1)}, bf16[256,1024]{1,0:T(8,128)(2,1)S(1)}, u32[]{:S(2)}, u32[]{:S(2)}) %collective-permute-start.29) | collective-permute-done | bytes 524320 | tf_op jit(solution)/shard_map/ppermute | solution.py:1160
  445.6 8.8 %collective-permute-start.30 = (bf16[160,1024]{1,0:T(8,128)(2,1)S(1)}, bf16[160,1024]{1,0:T(8,128)(2,1)S(1)}, u32[]{:S(2)}, u32[]{:S(2)}) collective-permute-start(bf16[160,1024]{1,0:T(8,128)(2,1)S(1)} %get-tuple-element.166), channel_id=1, source_target_pairs={{0,8},{8,0},{16,24},{24,16},{1,9},{9,1},{17,25},{25,17},{2,10},{10... | collective-permute-start | bytes 983048 | tf_op jit(solution)/shard_map/ppermute | solution.py:1205
  465.7 15.5 %expert_backward.6 = (bf16[160,1024]{1,0:T(8,128)(2,1)}, bf16[160,1024]{1,0:T(8,128)(2,1)}, bf16[3,320,2816]{2,1,0:T(8,128)(2,1)}) custom-call(bf16[160,1024]{1,0:T(8,128)(2,1)} %copy-done.40, bf16[160,1024]{1,0:T(8,128)(2,1)} %copy-done.42, bf16[2,320,2816]{2,1,0:T(8,128)(2,1)} %get-tuple-element.167.refs_2_, bf16[2,1,1024,5632]{3,2,1,0:T(8,128)(2,1)} %refs_5_.7, ...), custom_call_target="tpu_custom_call" | custom-call | flops 5536481280 | bytes 17301504 | tf_op jit(solution)/shard_map/expert_backward/pallas_call | solution.py:955
  487.0 16.0 %expert_backward.7 = (bf16[160,1024]{1,0:T(8,128)(2,1)}, bf16[160,1024]{1,0:T(8,128)(2,1)}, bf16[3,320,2816]{2,1,0:T(8,128)(2,1)}) custom-call(bf16[160,1024]{1,0:T(8,128)(2,1)} %copy-done.60, bf16[160,1024]{1,0:T(8,128)(2,1)} %copy-done.62, bf16[2,160,2816]{2,1,0:T(8,128)(2,1)} %get-tuple-element.172.refs_2_, ...), custom_call_target="tpu_custom_call" | custom-call | flops 5536481280 | bytes 17301504 | tf_op jit(solution)/shard_map/expert_backward/pallas_call | solution.py:955
  502.9 7.6 %collective-permute-start.34 = (bf16[160,1024]{1,0:T(8,128)(2,1)}, bf16[160,1024]{1,0:T(8,128)(2,1)S(1)}, u32[]{:S(2)}, u32[]{:S(2)}) collective-permute-start(bf16[160,1024]{1,0:T(8,128)(2,1)} %get-tuple-element.174), channel_id=1, source_target_pairs={{0,16},{8,24},{16,0},{24,8},{1,17},{9,25},{17,1},{25,9},{2,18},{10... | collective-permute-start | bytes 983048 | tf_op jit(solution)/shard_map/ppermute | solution.py:1205
  514.8 20.4 %expert_grads.3.refs_0_ = bf16[8,3,128,2816]{3,2,1,0:T(8,128)(2,1)} custom-call(bf16[160,1024]{1,0:T(8,128)(2,1)S(1)} %copy-done.29, bf16[160,1024]{1,0:T(8,128)(2,1)S(1)} %copy-done.31, bf16[160,1024]{1,0:T(8,128)(2,1)S(1)} %copy-done.33, bf16[160,1024]{1,0:T(8,128)(2,1)S(1)} %copy-done.35, bf16[160,1024]{1,0:T(8,128)(2,1)S(1)} %copy-done.41, ...), custom_call_target="tpu_custom_call" | custom-call | flops 5536481280 | bytes 17301504 | tf_op jit(solution)/shard_map/expert_grads/pallas_call | solution.py:955
  556.1 11.9 %collective-permute-done.38.refs_3_.refs_4_ = bf16[256,1024]{1,0:T(8,128)(2,1)S(1)} collective-permute-done((bf16[256,1024]{1,0:T(8,128)(2,1)S(1)}, bf16[256,1024]{1,0:T(8,128)(2,1)S(1)}, u32[]{:S(2)}, u32[]{:S(2)}) %collective-permute-start.38) | collective-permute-done | bytes 524320 | tf_op jit(solution)/shard_map/ppermute | solution.py:1151
  576.1 15.2 %attention_backward.3 = (bf16[1024,768]{1,0:T(8,128)(2,1)S(1)}, f32[512,1024]{1,0:T(8,128)S(1)}, bf16[512,1024]{1,0:T(8,128)(2,1)}, f32[8,512]{1,0:T(8,128)S(1)}, f32[8,1024]{1,0:T(8,128)S(1)}) custom-call(s32[3]{0:T(128)S(1)} %pad_add_fusion.refs_0_, bf16[256,1024]{1,0:T(8,128)(2,1)S(1)} %copy-done.72, ...), custom_call_target="tpu_custom_call" | custom-call | flops 4831838208 | bytes 13225996 | tf_op jit(solution)/shard_map/attention_backward/pallas_call | solution.py:96
  617.4 17.3 %collective-permute-done.41.refs_4_ = bf16[256,1024]{1,0:T(8,128)(2,1)} collective-permute-done((bf16[256,1024]{1,0:T(8,128)(2,1)}, bf16[256,1024]{1,0:T(8,128)(2,1)}, u32[]{:S(2)}, u32[]{:S(2)}) %collective-permute-start.41) | collective-permute-done | bytes 524320 | tf_op jit(solution)/shard_map/ppermute | solution.py:1160
  663.4 8.1 %all-to-all-done.6.refs_0_ = bf16[4,2,32,896]{3,2,1,0:T(8,128)(2,1)S(1)} async-done(((bf16[4,2,32,896]{3,2,1,0:T(8,128)(2,1)}), bf16[4,2,32,896]{3,2,1,0:T(8,128)(2,1)S(1)}, u32[]{:S(2)}, u32[]{:S(2)}) %all-to-all-start.6) | async-done | bytes 458784 | tf_op jit(solution)/shard_map/all_to_all | solution.py:1238
  (412 shorter events, 228.9 us)
Async XLA Ops:
  7.2 69.2 %all-gather.5.cloned.1.call-start = ((), (), s32[]{:S(2)}) async-start(), calls=%async_computation.11 | async-start | bytes 2654208 | tf_op jit(solution)/shard_map/all_gather | solution.py:1251
  24.1 112.3 %all-gather.7.cloned.1.call-start = ((), (), s32[]{:S(2)}) async-start(), calls=%async_computation.12 | async-start | bytes 2359296 | tf_op jit(solution)/shard_map/all_gather | solution.py:1251
  25.3 53.9 %collective-permute-start = (bf16[256,1024]{1,0:T(8,128)(2,1)S(1)}, bf16[256,1024]{1,0:T(8,128)(2,1)S(1)}, u32[]{:S(2)}, u32[]{:S(2)}) collective-permute-start(bf16[256,1024]{1,0:T(8,128)(2,1)S(1)} %bitcast.46), channel_id=1, source_target_pairs={{0,2},{2,0},{4,6},{6,4},{1,3},{3,1},{5,7},{7,5},{8,10},{10,8},{12,... | collective-permute-start | bytes 1572872 | tf_op jit(solution)/shard_map/ppermute | solution.py:1152
  38.7 40.5 %collective-permute-start.2 = (bf16[256,1024]{1,0:T(8,128)(2,1)S(1)}, bf16[256,1024]{1,0:T(8,128)(2,1)S(1)}, u32[]{:S(2)}, u32[]{:S(2)}) collective-permute-start(bf16[256,1024]{1,0:T(8,128)(2,1)S(1)} %collective-permute-done.1.refs_3_), channel_id=1, source_target_pairs={{0,2},{2,0},{4,6},{6,4},{1,3},{3,1},{5,7},{7,5},{8,10},{10,8},{12,... | collective-permute-start | bytes 1572872 | tf_op jit(solution)/shard_map/ppermute | solution.py:1153
  118.3 21.6 %collective-permute-start.5 = (bf16[160,1024]{1,0:T(8,128)(2,1)}, bf16[160,1024]{1,0:T(8,128)(2,1)S(1)}, u32[]{:S(2)}, u32[]{:S(2)}) collective-permute-start(bf16[160,1024]{1,0:T(8,128)(2,1)} %get-tuple-element.120), channel_id=1, source_target_pairs={{0,8},{8,0},{16,24},{24,16},{1,9},{9,1},{17,25},{25,17},{2,10},{10... | collective-permute-start | bytes 983048 | tf_op jit(solution)/shard_map/ppermute | solution.py:1205
  119.8 33.7 %collective-permute-start.7 = (bf16[160,1024]{1,0:T(8,128)(2,1)}, bf16[160,1024]{1,0:T(8,128)(2,1)S(1)}, u32[]{:S(2)}, u32[]{:S(2)}) collective-permute-start(bf16[160,1024]{1,0:T(8,128)(2,1)} %get-tuple-element.124), channel_id=1, source_target_pairs={{0,16},{8,24},{16,0},{24,8},{1,17},{9,25},{17,1},{25,9},{2,18},{10... | collective-permute-start | bytes 983048 | tf_op jit(solution)/shard_map/ppermute | solution.py:1205
  120.7 46.0 %collective-permute-start.9 = (bf16[160,1024]{1,0:T(8,128)(2,1)}, bf16[160,1024]{1,0:T(8,128)(2,1)S(1)}, u32[]{:S(2)}, u32[]{:S(2)}) collective-permute-start(bf16[160,1024]{1,0:T(8,128)(2,1)} %get-tuple-element.126), channel_id=1, source_target_pairs={{0,24},{8,16},{16,8},{24,0},{1,25},{9,17},{17,9},{25,1},{2,26},{10... | collective-permute-start | bytes 983048 | tf_op jit(solution)/shard_map/ppermute | solution.py:1205
  153.5 25.8 %collective-permute-start.6 = (bf16[160,1024]{1,0:T(8,128)(2,1)}, bf16[160,1024]{1,0:T(8,128)(2,1)S(1)}, u32[]{:S(2)}, u32[]{:S(2)}) collective-permute-start(bf16[160,1024]{1,0:T(8,128)(2,1)} %get-tuple-element.123), channel_id=1, source_target_pairs={{0,8},{8,0},{16,24},{24,16},{1,9},{9,1},{17,25},{25,17},{2,10},{10... | collective-permute-start | bytes 983048 | tf_op jit(solution)/shard_map/ppermute | solution.py:1205
  164.2 25.8 %collective-permute-start.8 = (bf16[160,1024]{1,0:T(8,128)(2,1)}, bf16[160,1024]{1,0:T(8,128)(2,1)S(1)}, u32[]{:S(2)}, u32[]{:S(2)}) collective-permute-start(bf16[160,1024]{1,0:T(8,128)(2,1)} %get-tuple-element.125.refs_4_), channel_id=1, source_target_pairs={{0,16},{8,24},{16,0},{24,8},{1,17},{9,25},{17,1},{25,9},{2,18},{10... | collective-permute-start | bytes 983048 | tf_op jit(solution)/shard_map/ppermute | solution.py:1205
  193.9 39.6 %all-to-all-start.1 = ((bf16[4,160,1024]{2,1,0:T(8,128)(2,1)}), bf16[4,160,1024]{2,1,0:T(8,128)(2,1)}, u32[]{:S(2)}, u32[]{:S(2)}) async-start(bf16[4,160,1024]{2,1,0:T(8,128)(2,1)} %bitcast.11), calls=%async_computation.1 | async-start | bytes 2621440 | tf_op jit(solution)/shard_map/all_to_all | solution.py:1199
  260.7 28.3 %all-to-all-start.2 = ((f32[4,160,128]{2,1,0:T(8,128)}), f32[4,160,128]{2,1,0:T(8,128)S(1)}, u32[]{:S(2)}, u32[]{:S(2)}) async-start(f32[4,160,128]{2,1,0:T(8,128)} %bitcast.13), calls=%async_computation.2 | async-start | bytes 655360 | tf_op jit(solution)/shard_map/all_to_all | solution.py:1199
  264.2 349.6 %reduce-scatter.3.cloned.1.call-start = ((), (), s32[]{:S(2)}) async-start(), calls=%async_computation.9 | async-start | bytes 19464192 | tf_op jit(solution)/shard_map/reduce_scatter | solution.py:1360
  264.7 44.4 %collective-permute-start.18 = (bf16[160,1024]{1,0:T(8,128)(2,1)}, bf16[160,1024]{1,0:T(8,128)(2,1)S(1)}, u32[]{:S(2)}, u32[]{:S(2)}) collective-permute-start(bf16[160,1024]{1,0:T(8,128)(2,1)} %get-tuple-element.140), channel_id=1, source_target_pairs={{0,16},{8,24},{16,0},{24,8},{1,17},{9,25},{17,1},{25,9},{2,18},{10... | collective-permute-start | bytes 983048 | tf_op jit(solution)/shard_map/ppermute | solution.py:1205
  267.6 41.6 %collective-permute-start.19 = (bf16[160,1024]{1,0:T(8,128)(2,1)}, bf16[160,1024]{1,0:T(8,128)(2,1)S(1)}, u32[]{:S(2)}, u32[]{:S(2)}) collective-permute-start(bf16[160,1024]{1,0:T(8,128)(2,1)} %get-tuple-element.141), channel_id=1, source_target_pairs={{0,24},{8,16},{16,8},{24,0},{1,25},{9,17},{17,9},{25,1},{2,26},{10... | collective-permute-start | bytes 983048 | tf_op jit(solution)/shard_map/ppermute | solution.py:1205
  285.2 57.0 %collective-permute-start.17 = (bf16[160,1024]{1,0:T(8,128)(2,1)}, bf16[160,1024]{1,0:T(8,128)(2,1)S(1)}, u32[]{:S(2)}, u32[]{:S(2)}) collective-permute-start(bf16[160,1024]{1,0:T(8,128)(2,1)} %get-tuple-element.139), channel_id=1, source_target_pairs={{0,8},{8,0},{16,24},{24,16},{1,9},{9,1},{17,25},{25,17},{2,10},{10... | collective-permute-start | bytes 983048 | tf_op jit(solution)/shard_map/ppermute | solution.py:1205
  309.1 67.8 %collective-permute-start.22 = (bf16[160,1024]{1,0:T(8,128)(2,1)}, bf16[160,1024]{1,0:T(8,128)(2,1)S(1)}, u32[]{:S(2)}, u32[]{:S(2)}) collective-permute-start(bf16[160,1024]{1,0:T(8,128)(2,1)} %get-tuple-element.149), channel_id=1, source_target_pairs={{0,8},{8,0},{16,24},{24,16},{1,9},{9,1},{17,25},{25,17},{2,10},{10... | collective-permute-start | bytes 983048 | tf_op jit(solution)/shard_map/ppermute | solution.py:1205
  322.8 32.8 %collective-permute-start.20 = (bf16[160,1024]{1,0:T(8,128)(2,1)}, bf16[160,1024]{1,0:T(8,128)(2,1)S(1)}, u32[]{:S(2)}, u32[]{:S(2)}) collective-permute-start(bf16[160,1024]{1,0:T(8,128)(2,1)} %get-tuple-element.147), channel_id=1, source_target_pairs={{0,16},{8,24},{16,0},{24,8},{1,17},{9,25},{17,1},{25,9},{2,18},{10... | collective-permute-start | bytes 983048 | tf_op jit(solution)/shard_map/ppermute | solution.py:1205
  322.8 32.8 %collective-permute-start.21 = (bf16[160,1024]{1,0:T(8,128)(2,1)}, bf16[160,1024]{1,0:T(8,128)(2,1)S(1)}, u32[]{:S(2)}, u32[]{:S(2)}) collective-permute-start(bf16[160,1024]{1,0:T(8,128)(2,1)} %get-tuple-element.148), channel_id=1, source_target_pairs={{0,24},{8,16},{16,8},{24,0},{1,25},{9,17},{17,9},{25,1},{2,26},{10... | collective-permute-start | bytes 983048 | tf_op jit(solution)/shard_map/ppermute | solution.py:1205
  342.2 34.8 %collective-permute-start.23 = (bf16[160,1024]{1,0:T(8,128)(2,1)}, bf16[160,1024]{1,0:T(8,128)(2,1)S(1)}, u32[]{:S(2)}, u32[]{:S(2)}) collective-permute-start(bf16[160,1024]{1,0:T(8,128)(2,1)} %get-tuple-element.153), channel_id=1, source_target_pairs={{0,16},{8,24},{16,0},{24,8},{1,17},{9,25},{17,1},{25,9},{2,18},{10... | collective-permute-start | bytes 983048 | tf_op jit(solution)/shard_map/ppermute | solution.py:1205
  342.2 34.8 %collective-permute-start.24 = (bf16[160,1024]{1,0:T(8,128)(2,1)}, bf16[160,1024]{1,0:T(8,128)(2,1)S(1)}, u32[]{:S(2)}, u32[]{:S(2)}) collective-permute-start(bf16[160,1024]{1,0:T(8,128)(2,1)} %get-tuple-element.154), channel_id=1, source_target_pairs={{0,24},{8,16},{16,8},{24,0},{1,25},{9,17},{17,9},{25,1},{2,26},{10... | collective-permute-start | bytes 983048 | tf_op jit(solution)/shard_map/ppermute | solution.py:1205
  378.6 296.1 %reduce-scatter.5.cloned.1.call-start = ((), (), s32[]{:S(2)}) async-start(), calls=%async_computation.10 | async-start | bytes 19464192 | tf_op jit(solution)/shard_map/reduce_scatter | solution.py:1360
  417.4 24.4 %collective-permute-start.29 = (bf16[256,1024]{1,0:T(8,128)(2,1)S(1)}, bf16[256,1024]{1,0:T(8,128)(2,1)S(1)}, u32[]{:S(2)}, u32[]{:S(2)}) collective-permute-start(bf16[256,1024]{1,0:T(8,128)(2,1)S(1)} %add_convert_fusion.3), channel_id=1, source_target_pairs={{0,4},{2,6},{4,0},{6,2},{1,5},{3,7},{5,1},{7,3},{8,12},{10,14},{12... | collective-permute-start | bytes 1572872 | tf_op jit(solution)/shard_map/ppermute | solution.py:1160
  461.8 50.0 %collective-permute-start.36 = (bf16[4,128,1152]{2,1,0:T(8,128)(2,1)S(1)}, bf16[4,128,1152]{2,1,0:T(8,128)(2,1)S(1)}, u32[]{:S(2)}, u32[]{:S(2)}) collective-permute-start(bf16[4,128,1152]{2,1,0:T(8,128)(2,1)S(1)} %get-tuple-element.185), channel_id=1, source_target_pairs={{0,1},{1,0},{2,3},{3,2},{4,5},{5,4},{6,7},{7,6},{8,9},{9,8},{10,11... | collective-permute-start | bytes 3538952 | tf_op jit(solution)/shard_map/ppermute | solution.py:1393
  462.3 23.7 %collective-permute-start.32 = (bf16[160,1024]{1,0:T(8,128)(2,1)S(1)}, bf16[160,1024]{1,0:T(8,128)(2,1)S(1)}, u32[]{:S(2)}, u32[]{:S(2)}) collective-permute-start(bf16[160,1024]{1,0:T(8,128)(2,1)S(1)} %get-tuple-element.170), channel_id=1, source_target_pairs={{0,16},{8,24},{16,0},{24,8},{1,17},{9,25},{17,1},{25,9},{2,18},{10... | collective-permute-start | bytes 983048 | tf_op jit(solution)/shard_map/ppermute | solution.py:1205
  463.4 22.7 %collective-permute-start.33 = (bf16[160,1024]{1,0:T(8,128)(2,1)S(1)}, bf16[160,1024]{1,0:T(8,128)(2,1)S(1)}, u32[]{:S(2)}, u32[]{:S(2)}) collective-permute-start(bf16[160,1024]{1,0:T(8,128)(2,1)S(1)} %get-tuple-element.171), channel_id=1, source_target_pairs={{0,24},{8,16},{16,8},{24,0},{1,25},{9,17},{17,9},{25,1},{2,26},{10... | collective-permute-start | bytes 983048 | tf_op jit(solution)/shard_map/ppermute | solution.py:1205
  481.2 54.0 %collective-permute-start.31 = (bf16[160,1024]{1,0:T(8,128)(2,1)}, bf16[160,1024]{1,0:T(8,128)(2,1)}, u32[]{:S(2)}, u32[]{:S(2)}) collective-permute-start(bf16[160,1024]{1,0:T(8,128)(2,1)} %get-tuple-element.169.refs_7_), channel_id=1, source_target_pairs={{0,8},{8,0},{16,24},{24,16},{1,9},{9,1},{17,25},{25,17},{2,10},{10... | collective-permute-start | bytes 983048 | tf_op jit(solution)/shard_map/ppermute | solution.py:1205
  502.9 32.3 %collective-permute-start.34 = (bf16[160,1024]{1,0:T(8,128)(2,1)}, bf16[160,1024]{1,0:T(8,128)(2,1)S(1)}, u32[]{:S(2)}, u32[]{:S(2)}) collective-permute-start(bf16[160,1024]{1,0:T(8,128)(2,1)} %get-tuple-element.174), channel_id=1, source_target_pairs={{0,16},{8,24},{16,0},{24,8},{1,17},{9,25},{17,1},{25,9},{2,18},{10... | collective-permute-start | bytes 983048 | tf_op jit(solution)/shard_map/ppermute | solution.py:1205
  510.5 24.7 %collective-permute-start.35 = (bf16[160,1024]{1,0:T(8,128)(2,1)}, bf16[160,1024]{1,0:T(8,128)(2,1)S(1)}, u32[]{:S(2)}, u32[]{:S(2)}) collective-permute-start(bf16[160,1024]{1,0:T(8,128)(2,1)} %get-tuple-element.175), channel_id=1, source_target_pairs={{0,24},{8,16},{16,8},{24,0},{1,25},{9,17},{17,9},{25,1},{2,26},{10... | collective-permute-start | bytes 983048 | tf_op jit(solution)/shard_map/ppermute | solution.py:1205
  548.2 45.4 %all-to-all-start.3 = ((bf16[4,128,1152]{2,1,0:T(8,128)(2,1)}), bf16[4,128,1152]{2,1,0:T(8,128)(2,1)}, u32[]{:S(2)}, u32[]{:S(2)}) async-start(bf16[4,128,1152]{2,1,0:T(8,128)(2,1)} %add_convert_fusion), calls=%async_computation.4 | async-start | bytes 2359296 | tf_op jit(solution)/shard_map/all_to_all | solution.py:1199
  602.3 37.7 %all-to-all-start.5 = ((bf16[4,2,128,640]{3,2,1,0:T(8,128)(2,1)}), bf16[4,2,128,640]{3,2,1,0:T(8,128)(2,1)}, u32[]{:S(2)}, u32[]{:S(2)}) async-start(bf16[4,2,128,640]{3,2,1,0:T(8,128)(2,1)} %copy-done.52), calls=%async_computation.6 | async-start | bytes 2621440 | tf_op jit(solution)/shard_map/all_to_all | solution.py:1199
  609.5 25.2 %collective-permute-start.41 = (bf16[256,1024]{1,0:T(8,128)(2,1)}, bf16[256,1024]{1,0:T(8,128)(2,1)}, u32[]{:S(2)}, u32[]{:S(2)}) collective-permute-start(bf16[256,1024]{1,0:T(8,128)(2,1)} %add_convert_fusion.2), channel_id=1, source_target_pairs={{0,4},{2,6},{4,0},{6,2},{1,5},{3,7},{5,1},{7,3},{8,12},{10,14},{12... | collective-permute-start | bytes 1572872 | tf_op jit(solution)/shard_map/ppermute | solution.py:1160
  610.8 26.8 %collective-permute-start.42 = (bf16[4,128,512]{2,1,0:T(8,128)(2,1)}, bf16[4,128,512]{2,1,0:T(8,128)(2,1)}, u32[]{:S(2)}, u32[]{:S(2)}) collective-permute-start(bf16[4,128,512]{2,1,0:T(8,128)(2,1)} %copy-done.99), channel_id=1, source_target_pairs={{0,1},{1,0},{2,3},{3,2},{4,5},{5,4},{6,7},{7,6},{8,9},{9,8},{10,11... | collective-permute-start | bytes 1572872 | tf_op jit(solution)/shard_map/ppermute | solution.py:1393
  (153 other events, 1926.9 us)
Sparse Core Ops, SparseCore 0:
  24.2 52.2 all-gather.4
  79.1 57.2 all-gather.6
  378.7 142.0 reduce-scatter.2
  536.2 134.3 reduce-scatter.4

commit v6 on v5

--- a/solution.py
+++ b/solution.py
@@ -170,8 +170,8 @@
     row = lax.broadcasted_iota(jnp.int32, (share, LANES), 0)
     for layer in range(LAYERS):
         top = 32 * layer
-        small = small + dot(router_ref[layer], placed(router_ref.shape[2], top), 1, 0)
-        small = small + dot(gains_ref[layer], placed(2, top + 16), 1, 0)
+        small = small + dot(router_ref[layer], placed(router_ref.shape[1], top), 0, 0)
+        small = small + dot(gains_ref[layer], placed(2, top + 16), 0, 0)
         bucket = dot(table_ref[layer : layer + 1, :], placed(table_ref.shape[1], top + 64), 1, 0)
         small = small + jnp.where(row == 0, bucket, 0.0)
     for c in range(GROUP):
@@ -1232,7 +1232,9 @@
     grad_in = out_grad[0]
     hits = jnp.asarray(bucket_hits())
 
-    packets = prepare(direct, attn_in, attn_out, router, gains, rel_table)
+    packets = prepare(
+        direct, attn_in, attn_out, router.transpose(0, 2, 1), gains.transpose(0, 2, 1), rel_table
+    )
 
     def spread(packet):
         return lax.all_to_all(packet, "context", split_axis=0, concat_axis=0)
@@ -1304,14 +1306,14 @@
         if last:
             gates = exchange(sent[blocks])
         produced, acts, drows, parts = [], [], [], []
-        order = second if layer == 0 else []
+        order = []
         for chunk in coarse if last else fine:
             done, kept_acts = expert_forward(
                 layer, [arrived[k] for k in chunk], expert_in, expert_out, after=order
             )
             produced += done
             acts.append(kept_acts)
-            order = done[:1]
+            order = done[:1] + (second if layer == 0 and len(acts) == 1 else [])
             if last:
                 if not drows:
                     arrived_grad = apply_gates(experts, blocks, place, arrived_grad, gates)

time: 696 us -> 693 us (level)
    all_gather x2, waiting for transfers between devices: 51.2 us -> 38.5 us  [together(): return lax.all_gather(part, ('experts', 'dp'), axis=0, tiled=False)]
    ppermute x21, waiting for transfers between devices: 32.6 us -> 44.3 us  [swap(): lax.ppermute(part, 'experts', [(i, i ^ k) for i in range(experts)])]
where the time goes in v6:
time: 693 us; the launch traced here: 682 us
  Pallas kernels  263 us (38%)
  waiting for transfers between devices  231 us (33%)
  starting transfers between devices  90.6 us (13%)
  local copies, waits for them, and re-layouts  56.9 us (8%)
  between operations  15.1 us (2%)
  other arithmetic  13.9 us (2%)
  blocking collectives  11.8 us (2%)
    pallas_call x11, Pallas kernels, expert_call(): pl.pallas_call(ordered, grid=(steps,), out_shape=tuple(outs), in_specs=li...  160 us
    pallas_call x14, Pallas kernels, whole_call(): pl.pallas_call(ordered, out_shape=outs, in_specs=specs, out_specs=tuple((...  68.4 us
    ppermute x4, waiting for transfers between devices, sum_pieces(): return (keep, recv, lax.ppermute(other, 'context', ACROSS))  65.3 us
    unnamed x267, local copies, waits for them, and re-layouts  56 us
    ppermute x4, waiting for transfers between devices, share_pieces(): across = lax.ppermute(piece, 'context', ACROSS)  49 us
    ppermute x21, waiting for transfers between devices, swap(): lax.ppermute(part, 'experts', [(i, i ^ k) for i in range(experts)])  44.3 us
    ppermute x21, starting transfers between devices, swap(): lax.ppermute(part, 'experts', [(i, i ^ k) for i in range(experts)])  42.5 us
    all_gather x2, waiting for transfers between devices, together(): return lax.all_gather(part, ('experts', 'dp'), axis=0, tiled=False)  38.5 us
  transfers between devices with their start and end apart: 54, of which 25 were waited for; matrix products, arithmetic and copies ran while one was open for 2% of the time, Pallas kernels for 37%

profile of v6, /device:TPU:0, one launch (start us, length us, event | category | flops | bytes accessed | tf_op | source)
XLA Modules:
  0.0 682.2 jit_solution(17340427269416203853)
XLA Ops:
  8.7 11.8 %all_to_all.47 = bf16[4,32,1664]{2,1,0:T(8,128)(2,1)S(1)} all-to-all(bf16[4,32,1664]{2,1,0:T(8,128)(2,1)S(1)} %get-tuple-element.109), channel_id=1, replica_groups=mesh['experts'=4,'context'=4,'dp'=2] {'context'}, dimensions={0} | all-to-all | bytes 851968 | tf_op jit(solution)/shard_map/all_to_all | solution.py:1240
  22.6 12.6 %collective-permute-done.1.refs_3_ = bf16[256,1024]{1,0:T(8,128)(2,1)S(1)} collective-permute-done((bf16[256,1024]{1,0:T(8,128)(2,1)S(1)}, bf16[256,1024]{1,0:T(8,128)(2,1)S(1)}, u32[]{:S(2)}, u32[]{:S(2)}) %collective-permute-start.1) | collective-permute-done | bytes 524320 | tf_op jit(solution)/shard_map/ppermute | solution.py:1151
  35.4 38.5 %all-gather.5.cloned.1.call-done = bf16[32,32,1152]{2,1,0:T(8,128)(2,1)} async-done(((bf16[4,32,1152]{2,1,0:T(8,128)(2,1)}), bf16[32,32,1152]{2,1,0:T(8,128)(2,1)}) %all-gather.5.cloned.1.call-update) | async-done | bytes 2359312 | tf_op jit(solution)/shard_map/all_gather | solution.py:1253
  76.7 9.9 %attention_forward.2 = (bf16[1024,768]{1,0:T(8,128)(2,1)S(1)}, f32[8,1024]{1,0:T(8,128)S(1)}, bf16[1024,256]{1,0:T(8,128)(2,1)S(1)}, f32[512,1024]{1,0:T(8,128)S...) custom-call(s32[3]{0:T(128)S(1)} %pad_add_fusion.refs_0_, bf16[256,1024]{1,0:T(8,128)(2,1)S(1)} %bitcast.49, ...), custom_call_target="tpu_custom_call" | custom-call | flops 3221225472 | bytes 12128268 | tf_op jit(solution)/shard_map/attention_forward/pallas_call | solution.py:96
  95.2 12.3 %collective-permute-done.4.refs_4_ = bf16[256,1024]{1,0:T(8,128)(2,1)S(1)} collective-permute-done((bf16[256,1024]{1,0:T(8,128)(2,1)S(1)}, bf16[256,1024]{1,0:T(8,128)(2,1)S(1)}, u32[]{:S(2)}, u32[]{:S(2)}) %collective-permute-start.4) | collective-permute-done | bytes 524320 | tf_op jit(solution)/shard_map/ppermute | solution.py:1160
  119.9 17.2 %collective-permute-done.5.refs_1_ = bf16[160,1024]{1,0:T(8,128)(2,1)S(1)} collective-permute-done((bf16[160,1024]{1,0:T(8,128)(2,1)S(1)}, bf16[160,1024]{1,0:T(8,128)(2,1)S(1)}, u32[]{:S(2)}, u32[]{:S(2)}) %collective-permute-start.5) | collective-permute-done | bytes 327712 | tf_op jit(solution)/shard_map/ppermute | solution.py:1205
  137.8 12.8 %expert_forward.5 = (bf16[160,1024]{1,0:T(8,128)(2,1)}, bf16[160,1024]{1,0:T(8,128)(2,1)}, bf16[2,320,2816]{2,1,0:T(8,128)(2,1)}) custom-call(bf16[160,1024]{1,0:T(8,128)(2,1)} %copy-done.28, bf16[160,1024]{1,0:T(8,128)(2,1)} %copy-done.30, bf16[2,1,1024,5632]{3,2,1,0:T(8,128)(2,1)} %refs_5_.7, bf16[2,1,1024,5632]{3,2,1,0:T(8,128)(2,1)} %refs_5_.7, ...), custom_call_target="tpu_custom_call" | custom-call | flops 5536481280 | bytes 17301504 | tf_op jit(solution)/shard_map/expert_forward/pallas_call | solution.py:955
  151.4 9.9 %expert_forward.6 = (bf16[160,1024]{1,0:T(8,128)(2,1)}, bf16[2,160,2816]{2,1,0:T(8,128)(2,1)}) custom-call(bf16[160,1024]{1,0:T(8,128)(2,1)} %copy-done.32, bf16[2,1,1024,5632]{3,2,1,0:T(8,128)(2,1)} %refs_5_.7, bf16[2,1,1024,5632]{3,2,1,0:T(8,128)(2,1)} %refs_5_.7, bf16[2,1,1024,2816]{3,2,1,0:T(8,128)(2,1)} %refs_6_.1, ...), custom_call_target="tpu_custom_call" | custom-call | flops 5536481280 | bytes 17301504 | tf_op jit(solution)/shard_map/expert_forward/pallas_call | solution.py:955
  164.3 9.9 %expert_forward.7 = (bf16[160,1024]{1,0:T(8,128)(2,1)}, bf16[2,160,2816]{2,1,0:T(8,128)(2,1)}) custom-call(bf16[160,1024]{1,0:T(8,128)(2,1)} %copy-done.34, bf16[2,1,1024,5632]{3,2,1,0:T(8,128)(2,1)} %refs_5_.7, bf16[2,1,1024,5632]{3,2,1,0:T(8,128)(2,1)} %refs_5_.7, bf16[2,1,1024,2816]{3,2,1,0:T(8,128)(2,1)} %refs_6_.1, ...), custom_call_target="tpu_custom_call" | custom-call | flops 5536481280 | bytes 17301504 | tf_op jit(solution)/shard_map/expert_forward/pallas_call | solution.py:955
  177.8 7.1 %collective-permute-done.10.refs_5_.refs_3_ = bf16[160,1024]{1,0:T(8,128)(2,1)S(1)} collective-permute-done((bf16[160,1024]{1,0:T(8,128)(2,1)}, bf16[160,1024]{1,0:T(8,128)(2,1)S(1)}, u32[]{:S(2)}, u32[]{:S(2)}) %collective-permute-start.10) | collective-permute-done | bytes 327712 | tf_op jit(solution)/shard_map/ppermute | solution.py:1205
  188.8 9.7 %all-to-all-start.1 = ((bf16[4,160,1024]{2,1,0:T(8,128)(2,1)}), bf16[4,160,1024]{2,1,0:T(8,128)(2,1)}, u32[]{:S(2)}, u32[]{:S(2)}) async-start(bf16[4,160,1024]{2,1,0:T(8,128)(2,1)} %bitcast.13), calls=%async_computation.1 | async-start | bytes 2621440 | tf_op jit(solution)/shard_map/all_to_all | solution.py:1199
  200.1 12.3 %collective-permute-done.12.refs_3_.refs_14_ = bf16[256,1024]{1,0:T(8,128)(2,1)S(1)} collective-permute-done((bf16[256,1024]{1,0:T(8,128)(2,1)}, bf16[256,1024]{1,0:T(8,128)(2,1)S(1)}, u32[]{:S(2)}, u32[]{:S(2)}) %collective-permute-start.12) | collective-permute-done | bytes 524320 | tf_op jit(solution)/shard_map/ppermute | solution.py:1151
  214.3 9.8 %attention_forward.3 = (bf16[1024,768]{1,0:T(8,128)(2,1)S(1)}, f32[8,1024]{1,0:T(8,128)S(1)}, bf16[1024,256]{1,0:T(8,128)(2,1)S(1)}, f32[512,1024]{1,0:T(8,128)S(1)}, bf16[512,1024]{1,0:T(8,128)(2,1)S(1)}) custom-call(s32[3]{0:T(128)S(1)} %pad_add_fusion.refs_0_, bf16[256,1024]{1,0:T(8,128)(2,1)S(1)} %copy-done.76, ...), custom_call_target="tpu_custom_call" | custom-call | flops 3221225472 | bytes 10031116 | tf_op jit(solution)/shard_map/attention_forward/pallas_call | solution.py:96
  235.8 12.5 %collective-permute-done.15.refs_4_ = bf16[256,1024]{1,0:T(8,128)(2,1)S(1)} collective-permute-done((bf16[256,1024]{1,0:T(8,128)(2,1)S(1)}, bf16[256,1024]{1,0:T(8,128)(2,1)S(1)}, u32[]{:S(2)}, u32[]{:S(2)}) %collective-permute-start.15) | collective-permute-done | bytes 524320 | tf_op jit(solution)/shard_map/ppermute | solution.py:1160
  269.8 12.8 %expert_forward.8 = (bf16[160,1024]{1,0:T(8,128)(2,1)}, bf16[160,1024]{1,0:T(8,128)(2,1)}, bf16[2,320,2816]{2,1,0:T(8,128)(2,1)}) custom-call(bf16[160,1024]{1,0:T(8,128)(2,1)} %copy-done.36, bf16[160,1024]{1,0:T(8,128)(2,1)} %copy-done.38, bf16[2,1,1024,5632]{3,2,1,0:T(8,128)(2,1)} %refs_5_.7, bf16[2,1,1024,5632]{3,2,1,0:T(8,128)(2,1)} %refs_5_.7, ...), custom_call_target="tpu_custom_call" | custom-call | flops 5536481280 | bytes 17301504 | tf_op jit(solution)/shard_map/expert_forward/pallas_call | solution.py:955
  291.0 14.8 %expert_backward.4 = (bf16[160,1024]{1,0:T(8,128)(2,1)}, bf16[160,1024]{1,0:T(8,128)(2,1)}, bf16[3,320,2816]{2,1,0:T(8,128)(2,1)}) custom-call(bf16[160,1024]{1,0:T(8,128)(2,1)} %copy-done.44, bf16[160,1024]{1,0:T(8,128)(2,1)} %copy-done.46, bf16[2,320,2816]{2,1,0:T(8,128)(2,1)} %get-tuple-element.145.refs_2_, bf16[2,1,1024,5632]{3,2,1,0:T(8,128)(2,1)} %refs_5_.7, ...), custom_call_target="tpu_custom_call" | custom-call | flops 5536481280 | bytes 17301504 | tf_op jit(solution)/shard_map/expert_backward/pallas_call | solution.py:955
  306.6 12.7 %expert_forward.9 = (bf16[160,1024]{1,0:T(8,128)(2,1)}, bf16[160,1024]{1,0:T(8,128)(2,1)}, bf16[2,320,2816]{2,1,0:T(8,128)(2,1)}) custom-call(bf16[160,1024]{1,0:T(8,128)(2,1)} %copy-done.56, bf16[160,1024]{1,0:T(8,128)(2,1)} %copy-done.58, bf16[2,1,1024,5632]{3,2,1,0:T(8,128)(2,1)} %refs_5_.7, bf16[2,1,1024,5632]{3,2,1,0:T(8,128)(2,1)} %refs_5_.7, ...), custom_call_target="tpu_custom_call" | custom-call | flops 5536481280 | bytes 17301504 | tf_op jit(solution)/shard_map/expert_forward/pallas_call | solution.py:955
  323.8 15.0 %expert_backward.5 = (bf16[160,1024]{1,0:T(8,128)(2,1)}, bf16[160,1024]{1,0:T(8,128)(2,1)}, bf16[3,320,2816]{2,1,0:T(8,128)(2,1)}) custom-call(bf16[160,1024]{1,0:T(8,128)(2,1)} %copy-done.48, bf16[160,1024]{1,0:T(8,128)(2,1)} %copy-done.50, bf16[2,320,2816]{2,1,0:T(8,128)(2,1)} %get-tuple-element.152.refs_2_, bf16[2,1,1024,5632]{3,2,1,0:T(8,128)(2,1)} %refs_5_.7, ...), custom_call_target="tpu_custom_call" | custom-call | flops 5536481280 | bytes 17301504 | tf_op jit(solution)/shard_map/expert_backward/pallas_call | solution.py:955
  340.2 11.9 %collective-permute-done.20.refs_4_.refs_12_.refs_2_ = bf16[160,1024]{1,0:T(8,128)(2,1)S(1)} collective-permute-done((bf16[160,1024]{1,0:T(8,128)(2,1)}, bf16[160,1024]{1,0:T(8,128)(2,1)S(1)}, u32[]{:S(2)}, u32[]{:S(2)}) %collective-permute-start.20) | collective-permute-done | bytes 327712 | tf_op jit(solution)/shard_map/ppermute | solution.py:1205
  353.0 20.4 %expert_grads.2.refs_0_ = bf16[8,3,128,2816]{3,2,1,0:T(8,128)(2,1)} custom-call(bf16[160,1024]{1,0:T(8,128)(2,1)S(1)} %copy-done.37, bf16[160,1024]{1,0:T(8,128)(2,1)S(1)} %copy-done.39, bf16[160,1024]{1,0:T(8,128)(2,1)S(1)} %copy-done.57, bf16[160,1024]{1,0:T(8,128)(2,1)S(1)} %copy-done.59, bf16[160,1024]{1,0:T(8,128)(2,1)S(1)} %copy-done.45, ...), custom_call_target="tpu_custom_call" | custom-call | flops 5536481280 | bytes 17301504 | tf_op jit(solution)/shard_map/expert_grads/pallas_call | solution.py:955
  383.1 11.8 %collective-permute-done.26.refs_3_.refs_7_ = bf16[256,1024]{1,0:T(8,128)(2,1)S(1)} collective-permute-done((bf16[256,1024]{1,0:T(8,128)(2,1)S(1)}, bf16[256,1024]{1,0:T(8,128)(2,1)S(1)}, u32[]{:S(2)}, u32[]{:S(2)}) %collective-permute-start.26) | collective-permute-done | bytes 524320 | tf_op jit(solution)/shard_map/ppermute | solution.py:1151
  396.9 14.3 %attention_backward.2 = (bf16[1024,768]{1,0:T(8,128)(2,1)S(1)}, f32[512,1024]{1,0:T(8,128)S(1)}, bf16[512,1024]{1,0:T(8,128)(2,1)S(1)}, f32[8,512]{1,0:T(8,128)S(1)}, f32[8,1024]{1,0:T(8,128)S(1)}) custom-call(s32[3]{0:T(128)S(1)} %pad_add_fusion.refs_0_, bf16[256,1024]{1,0:T(8,128)(2,1)S(1)} %get-tuple-element.159.refs_1_.refs_5_, ...), custom_call_target="tpu_custom_call" | custom-call | flops 4831838208 | bytes 13225996 | tf_op jit(solution)/shard_map/attention_backward/pallas_call | solution.py:96
  416.1 22.9 %collective-permute-done.29.refs_4_ = bf16[256,1024]{1,0:T(8,128)(2,1)S(1)} collective-permute-done((bf16[256,1024]{1,0:T(8,128)(2,1)S(1)}, bf16[256,1024]{1,0:T(8,128)(2,1)S(1)}, u32[]{:S(2)}, u32[]{:S(2)}) %collective-permute-start.29) | collective-permute-done | bytes 524320 | tf_op jit(solution)/shard_map/ppermute | solution.py:1160
  442.8 8.6 %collective-permute-start.30 = (bf16[160,1024]{1,0:T(8,128)(2,1)S(1)}, bf16[160,1024]{1,0:T(8,128)(2,1)S(1)}, u32[]{:S(2)}, u32[]{:S(2)}) collective-permute-start(bf16[160,1024]{1,0:T(8,128)(2,1)S(1)} %get-tuple-element.166), channel_id=1, source_target_pairs={{0,8},{8,0},{16,24},{24,16},{1,9},{9,1},{17,25},{25,17},{2,10},{10... | collective-permute-start | bytes 983048 | tf_op jit(solution)/shard_map/ppermute | solution.py:1205
  463.1 15.5 %expert_backward.6 = (bf16[160,1024]{1,0:T(8,128)(2,1)}, bf16[160,1024]{1,0:T(8,128)(2,1)}, bf16[3,320,2816]{2,1,0:T(8,128)(2,1)}) custom-call(bf16[160,1024]{1,0:T(8,128)(2,1)} %copy-done.40, bf16[160,1024]{1,0:T(8,128)(2,1)} %copy-done.42, bf16[2,320,2816]{2,1,0:T(8,128)(2,1)} %get-tuple-element.167.refs_2_, bf16[2,1,1024,5632]{3,2,1,0:T(8,128)(2,1)} %refs_5_.7, ...), custom_call_target="tpu_custom_call" | custom-call | flops 5536481280 | bytes 17301504 | tf_op jit(solution)/shard_map/expert_backward/pallas_call | solution.py:955
  484.2 15.9 %expert_backward.7 = (bf16[160,1024]{1,0:T(8,128)(2,1)}, bf16[160,1024]{1,0:T(8,128)(2,1)}, bf16[3,320,2816]{2,1,0:T(8,128)(2,1)}) custom-call(bf16[160,1024]{1,0:T(8,128)(2,1)} %copy-done.60, bf16[160,1024]{1,0:T(8,128)(2,1)} %copy-done.62, bf16[2,160,2816]{2,1,0:T(8,128)(2,1)} %get-tuple-element.172.refs_2_, ...), custom_call_target="tpu_custom_call" | custom-call | flops 5536481280 | bytes 17301504 | tf_op jit(solution)/shard_map/expert_backward/pallas_call | solution.py:955
  500.2 7.3 %collective-permute-start.34 = (bf16[160,1024]{1,0:T(8,128)(2,1)}, bf16[160,1024]{1,0:T(8,128)(2,1)S(1)}, u32[]{:S(2)}, u32[]{:S(2)}) collective-permute-start(bf16[160,1024]{1,0:T(8,128)(2,1)} %get-tuple-element.174), channel_id=1, source_target_pairs={{0,16},{8,24},{16,0},{24,8},{1,17},{9,25},{17,1},{25,9},{2,18},{10... | collective-permute-start | bytes 983048 | tf_op jit(solution)/shard_map/ppermute | solution.py:1205
  511.5 20.5 %expert_grads.3.refs_0_ = bf16[8,3,128,2816]{3,2,1,0:T(8,128)(2,1)} custom-call(bf16[160,1024]{1,0:T(8,128)(2,1)S(1)} %copy-done.29, bf16[160,1024]{1,0:T(8,128)(2,1)S(1)} %copy-done.31, bf16[160,1024]{1,0:T(8,128)(2,1)S(1)} %copy-done.33, bf16[160,1024]{1,0:T(8,128)(2,1)S(1)} %copy-done.35, bf16[160,1024]{1,0:T(8,128)(2,1)S(1)} %copy-done.41, ...), custom_call_target="tpu_custom_call" | custom-call | flops 5536481280 | bytes 17301504 | tf_op jit(solution)/shard_map/expert_grads/pallas_call | solution.py:955
  552.9 12.3 %collective-permute-done.38.refs_3_.refs_4_ = bf16[256,1024]{1,0:T(8,128)(2,1)S(1)} collective-permute-done((bf16[256,1024]{1,0:T(8,128)(2,1)S(1)}, bf16[256,1024]{1,0:T(8,128)(2,1)S(1)}, u32[]{:S(2)}, u32[]{:S(2)}) %collective-permute-start.38) | collective-permute-done | bytes 524320 | tf_op jit(solution)/shard_map/ppermute | solution.py:1151
  573.3 15.1 %attention_backward.3 = (bf16[1024,768]{1,0:T(8,128)(2,1)S(1)}, f32[512,1024]{1,0:T(8,128)S(1)}, bf16[512,1024]{1,0:T(8,128)(2,1)}, f32[8,512]{1,0:T(8,128)S(1)}, f32[8,1024]{1,0:T(8,128)S(1)}) custom-call(s32[3]{0:T(128)S(1)} %pad_add_fusion.refs_0_, bf16[256,1024]{1,0:T(8,128)(2,1)S(1)} %copy-done.72, ...), custom_call_target="tpu_custom_call" | custom-call | flops 4831838208 | bytes 13225996 | tf_op jit(solution)/shard_map/attention_backward/pallas_call | solution.py:96
  614.4 17.6 %collective-permute-done.41.refs_4_ = bf16[256,1024]{1,0:T(8,128)(2,1)} collective-permute-done((bf16[256,1024]{1,0:T(8,128)(2,1)}, bf16[256,1024]{1,0:T(8,128)(2,1)}, u32[]{:S(2)}, u32[]{:S(2)}) %collective-permute-start.41) | collective-permute-done | bytes 524320 | tf_op jit(solution)/shard_map/ppermute | solution.py:1160
  660.6 8.2 %all-to-all-done.6.refs_0_ = bf16[4,2,32,896]{3,2,1,0:T(8,128)(2,1)S(1)} async-done(((bf16[4,2,32,896]{3,2,1,0:T(8,128)(2,1)}), bf16[4,2,32,896]{3,2,1,0:T(8,128)(2,1)S(1)}, u32[]{:S(2)}, u32[]{:S(2)}) %all-to-all-start.6) | async-done | bytes 458784 | tf_op jit(solution)/shard_map/all_to_all | solution.py:1240
  (412 shorter events, 223.4 us)
Async XLA Ops:
  7.2 66.6 %all-gather.5.cloned.1.call-start = ((), (), s32[]{:S(2)}) async-start(), calls=%async_computation.11 | async-start | bytes 2654208 | tf_op jit(solution)/shard_map/all_gather | solution.py:1253
  21.3 129.3 %all-gather.7.cloned.1.call-start = ((), (), s32[]{:S(2)}) async-start(), calls=%async_computation.12 | async-start | bytes 2359296 | tf_op jit(solution)/shard_map/all_gather | solution.py:1253
  22.6 54.1 %collective-permute-start = (bf16[256,1024]{1,0:T(8,128)(2,1)S(1)}, bf16[256,1024]{1,0:T(8,128)(2,1)S(1)}, u32[]{:S(2)}, u32[]{:S(2)}) collective-permute-start(bf16[256,1024]{1,0:T(8,128)(2,1)S(1)} %bitcast.48), channel_id=1, source_target_pairs={{0,2},{2,0},{4,6},{6,4},{1,3},{3,1},{5,7},{7,5},{8,10},{10,8},{12,... | collective-permute-start | bytes 1572872 | tf_op jit(solution)/shard_map/ppermute | solution.py:1152
  35.2 41.5 %collective-permute-start.2 = (bf16[256,1024]{1,0:T(8,128)(2,1)S(1)}, bf16[256,1024]{1,0:T(8,128)(2,1)S(1)}, u32[]{:S(2)}, u32[]{:S(2)}) collective-permute-start(bf16[256,1024]{1,0:T(8,128)(2,1)S(1)} %collective-permute-done.1.refs_3_), channel_id=1, source_target_pairs={{0,2},{2,0},{4,6},{6,4},{1,3},{3,1},{5,7},{7,5},{8,10},{10,8},{12,... | collective-permute-start | bytes 1572872 | tf_op jit(solution)/shard_map/ppermute | solution.py:1153
  115.5 21.6 %collective-permute-start.5 = (bf16[160,1024]{1,0:T(8,128)(2,1)S(1)}, bf16[160,1024]{1,0:T(8,128)(2,1)S(1)}, u32[]{:S(2)}, u32[]{:S(2)}) collective-permute-start(bf16[160,1024]{1,0:T(8,128)(2,1)S(1)} %get-tuple-element.120), channel_id=1, source_target_pairs={{0,8},{8,0},{16,24},{24,16},{1,9},{9,1},{17,25},{25,17},{2,10},{10... | collective-permute-start | bytes 983048 | tf_op jit(solution)/shard_map/ppermute | solution.py:1205
  117.0 33.6 %collective-permute-start.7 = (bf16[160,1024]{1,0:T(8,128)(2,1)}, bf16[160,1024]{1,0:T(8,128)(2,1)S(1)}, u32[]{:S(2)}, u32[]{:S(2)}) collective-permute-start(bf16[160,1024]{1,0:T(8,128)(2,1)} %get-tuple-element.123), channel_id=1, source_target_pairs={{0,16},{8,24},{16,0},{24,8},{1,17},{9,25},{17,1},{25,9},{2,18},{10... | collective-permute-start | bytes 983048 | tf_op jit(solution)/shard_map/ppermute | solution.py:1205
  118.0 45.6 %collective-permute-start.9 = (bf16[160,1024]{1,0:T(8,128)(2,1)}, bf16[160,1024]{1,0:T(8,128)(2,1)S(1)}, u32[]{:S(2)}, u32[]{:S(2)}) collective-permute-start(bf16[160,1024]{1,0:T(8,128)(2,1)} %get-tuple-element.126), channel_id=1, source_target_pairs={{0,24},{8,16},{16,8},{24,0},{1,25},{9,17},{17,9},{25,1},{2,26},{10... | collective-permute-start | bytes 983048 | tf_op jit(solution)/shard_map/ppermute | solution.py:1205
  188.8 42.3 %all-to-all-start.1 = ((bf16[4,160,1024]{2,1,0:T(8,128)(2,1)}), bf16[4,160,1024]{2,1,0:T(8,128)(2,1)}, u32[]{:S(2)}, u32[]{:S(2)}) async-start(bf16[4,160,1024]{2,1,0:T(8,128)(2,1)} %bitcast.13), calls=%async_computation.1 | async-start | bytes 2621440 | tf_op jit(solution)/shard_map/all_to_all | solution.py:1199
  257.8 27.9 %all-to-all-start.2 = ((f32[4,160,128]{2,1,0:T(8,128)}), f32[4,160,128]{2,1,0:T(8,128)S(1)}, u32[]{:S(2)}, u32[]{:S(2)}) async-start(f32[4,160,128]{2,1,0:T(8,128)} %bitcast.15), calls=%async_computation.2 | async-start | bytes 655360 | tf_op jit(solution)/shard_map/all_to_all | solution.py:1199
  261.3 349.5 %reduce-scatter.3.cloned.1.call-start = ((), (), s32[]{:S(2)}) async-start(), calls=%async_computation.9 | async-start | bytes 19464192 | tf_op jit(solution)/shard_map/reduce_scatter | solution.py:1362
  261.8 44.0 %collective-permute-start.18 = (bf16[160,1024]{1,0:T(8,128)(2,1)}, bf16[160,1024]{1,0:T(8,128)(2,1)S(1)}, u32[]{:S(2)}, u32[]{:S(2)}) collective-permute-start(bf16[160,1024]{1,0:T(8,128)(2,1)} %get-tuple-element.140), channel_id=1, source_target_pairs={{0,16},{8,24},{16,0},{24,8},{1,17},{9,25},{17,1},{25,9},{2,18},{10... | collective-permute-start | bytes 983048 | tf_op jit(solution)/shard_map/ppermute | solution.py:1205
  264.8 41.0 %collective-permute-start.19 = (bf16[160,1024]{1,0:T(8,128)(2,1)}, bf16[160,1024]{1,0:T(8,128)(2,1)S(1)}, u32[]{:S(2)}, u32[]{:S(2)}) collective-permute-start(bf16[160,1024]{1,0:T(8,128)(2,1)} %get-tuple-element.141), channel_id=1, source_target_pairs={{0,24},{8,16},{16,8},{24,0},{1,25},{9,17},{17,9},{25,1},{2,26},{10... | collective-permute-start | bytes 983048 | tf_op jit(solution)/shard_map/ppermute | solution.py:1205
  282.5 56.4 %collective-permute-start.17 = (bf16[160,1024]{1,0:T(8,128)(2,1)}, bf16[160,1024]{1,0:T(8,128)(2,1)S(1)}, u32[]{:S(2)}, u32[]{:S(2)}) collective-permute-start(bf16[160,1024]{1,0:T(8,128)(2,1)} %get-tuple-element.139), channel_id=1, source_target_pairs={{0,8},{8,0},{16,24},{24,16},{1,9},{9,1},{17,25},{25,17},{2,10},{10... | collective-permute-start | bytes 983048 | tf_op jit(solution)/shard_map/ppermute | solution.py:1205
  305.8 67.7 %collective-permute-start.22 = (bf16[160,1024]{1,0:T(8,128)(2,1)}, bf16[160,1024]{1,0:T(8,128)(2,1)S(1)}, u32[]{:S(2)}, u32[]{:S(2)}) collective-permute-start(bf16[160,1024]{1,0:T(8,128)(2,1)} %get-tuple-element.149), channel_id=1, source_target_pairs={{0,8},{8,0},{16,24},{24,16},{1,9},{9,1},{17,25},{25,17},{2,10},{10... | collective-permute-start | bytes 983048 | tf_op jit(solution)/shard_map/ppermute | solution.py:1205
  319.4 32.8 %collective-permute-start.20 = (bf16[160,1024]{1,0:T(8,128)(2,1)}, bf16[160,1024]{1,0:T(8,128)(2,1)S(1)}, u32[]{:S(2)}, u32[]{:S(2)}) collective-permute-start(bf16[160,1024]{1,0:T(8,128)(2,1)} %get-tuple-element.147), channel_id=1, source_target_pairs={{0,16},{8,24},{16,0},{24,8},{1,17},{9,25},{17,1},{25,9},{2,18},{10... | collective-permute-start | bytes 983048 | tf_op jit(solution)/shard_map/ppermute | solution.py:1205
  320.6 31.5 %collective-permute-start.21 = (bf16[160,1024]{1,0:T(8,128)(2,1)}, bf16[160,1024]{1,0:T(8,128)(2,1)S(1)}, u32[]{:S(2)}, u32[]{:S(2)}) collective-permute-start(bf16[160,1024]{1,0:T(8,128)(2,1)} %get-tuple-element.148), channel_id=1, source_target_pairs={{0,24},{8,16},{16,8},{24,0},{1,25},{9,17},{17,9},{25,1},{2,26},{10... | collective-permute-start | bytes 983048 | tf_op jit(solution)/shard_map/ppermute | solution.py:1205
  338.7 34.7 %collective-permute-start.23 = (bf16[160,1024]{1,0:T(8,128)(2,1)}, bf16[160,1024]{1,0:T(8,128)(2,1)S(1)}, u32[]{:S(2)}, u32[]{:S(2)}) collective-permute-start(bf16[160,1024]{1,0:T(8,128)(2,1)} %get-tuple-element.153), channel_id=1, source_target_pairs={{0,16},{8,24},{16,0},{24,8},{1,17},{9,25},{17,1},{25,9},{2,18},{10... | collective-permute-start | bytes 983048 | tf_op jit(solution)/shard_map/ppermute | solution.py:1205
  339.0 34.5 %collective-permute-start.24 = (bf16[160,1024]{1,0:T(8,128)(2,1)}, bf16[160,1024]{1,0:T(8,128)(2,1)S(1)}, u32[]{:S(2)}, u32[]{:S(2)}) collective-permute-start(bf16[160,1024]{1,0:T(8,128)(2,1)} %get-tuple-element.154), channel_id=1, source_target_pairs={{0,24},{8,16},{16,8},{24,0},{1,25},{9,17},{17,9},{25,1},{2,26},{10... | collective-permute-start | bytes 983048 | tf_op jit(solution)/shard_map/ppermute | solution.py:1205
  375.0 297.0 %reduce-scatter.5.cloned.1.call-start = ((), (), s32[]{:S(2)}) async-start(), calls=%async_computation.10 | async-start | bytes 19464192 | tf_op jit(solution)/shard_map/reduce_scatter | solution.py:1362
  414.2 24.8 %collective-permute-start.29 = (bf16[256,1024]{1,0:T(8,128)(2,1)S(1)}, bf16[256,1024]{1,0:T(8,128)(2,1)S(1)}, u32[]{:S(2)}, u32[]{:S(2)}) collective-permute-start(bf16[256,1024]{1,0:T(8,128)(2,1)S(1)} %add_convert_fusion.3), channel_id=1, source_target_pairs={{0,4},{2,6},{4,0},{6,2},{1,5},{3,7},{5,1},{7,3},{8,12},{10,14},{12... | collective-permute-start | bytes 1572872 | tf_op jit(solution)/shard_map/ppermute | solution.py:1160
  442.8 19.6 %collective-permute-start.30 = (bf16[160,1024]{1,0:T(8,128)(2,1)S(1)}, bf16[160,1024]{1,0:T(8,128)(2,1)S(1)}, u32[]{:S(2)}, u32[]{:S(2)}) collective-permute-start(bf16[160,1024]{1,0:T(8,128)(2,1)S(1)} %get-tuple-element.166), channel_id=1, source_target_pairs={{0,8},{8,0},{16,24},{24,16},{1,9},{9,1},{17,25},{25,17},{2,10},{10... | collective-permute-start | bytes 983048 | tf_op jit(solution)/shard_map/ppermute | solution.py:1205
  458.7 49.8 %collective-permute-start.36 = (bf16[4,128,1152]{2,1,0:T(8,128)(2,1)S(1)}, bf16[4,128,1152]{2,1,0:T(8,128)(2,1)S(1)}, u32[]{:S(2)}, u32[]{:S(2)}) collective-permute-start(bf16[4,128,1152]{2,1,0:T(8,128)(2,1)S(1)} %get-tuple-element.185), channel_id=1, source_target_pairs={{0,1},{1,0},{2,3},{3,2},{4,5},{5,4},{6,7},{7,6},{8,9},{9,8},{10,11... | collective-permute-start | bytes 3538952 | tf_op jit(solution)/shard_map/ppermute | solution.py:1395
  459.1 24.2 %collective-permute-start.32 = (bf16[160,1024]{1,0:T(8,128)(2,1)S(1)}, bf16[160,1024]{1,0:T(8,128)(2,1)S(1)}, u32[]{:S(2)}, u32[]{:S(2)}) collective-permute-start(bf16[160,1024]{1,0:T(8,128)(2,1)S(1)} %get-tuple-element.170), channel_id=1, source_target_pairs={{0,16},{8,24},{16,0},{24,8},{1,17},{9,25},{17,1},{25,9},{2,18},{10... | collective-permute-start | bytes 983048 | tf_op jit(solution)/shard_map/ppermute | solution.py:1205
  460.7 22.6 %collective-permute-start.33 = (bf16[160,1024]{1,0:T(8,128)(2,1)S(1)}, bf16[160,1024]{1,0:T(8,128)(2,1)S(1)}, u32[]{:S(2)}, u32[]{:S(2)}) collective-permute-start(bf16[160,1024]{1,0:T(8,128)(2,1)S(1)} %get-tuple-element.171), channel_id=1, source_target_pairs={{0,24},{8,16},{16,8},{24,0},{1,25},{9,17},{17,9},{25,1},{2,26},{10... | collective-permute-start | bytes 983048 | tf_op jit(solution)/shard_map/ppermute | solution.py:1205
  478.6 53.3 %collective-permute-start.31 = (bf16[160,1024]{1,0:T(8,128)(2,1)}, bf16[160,1024]{1,0:T(8,128)(2,1)}, u32[]{:S(2)}, u32[]{:S(2)}) collective-permute-start(bf16[160,1024]{1,0:T(8,128)(2,1)} %get-tuple-element.169.refs_7_), channel_id=1, source_target_pairs={{0,8},{8,0},{16,24},{24,16},{1,9},{9,1},{17,25},{25,17},{2,10},{10... | collective-permute-start | bytes 983048 | tf_op jit(solution)/shard_map/ppermute | solution.py:1205
  500.2 31.8 %collective-permute-start.34 = (bf16[160,1024]{1,0:T(8,128)(2,1)}, bf16[160,1024]{1,0:T(8,128)(2,1)S(1)}, u32[]{:S(2)}, u32[]{:S(2)}) collective-permute-start(bf16[160,1024]{1,0:T(8,128)(2,1)} %get-tuple-element.174), channel_id=1, source_target_pairs={{0,16},{8,24},{16,0},{24,8},{1,17},{9,25},{17,1},{25,9},{2,18},{10... | collective-permute-start | bytes 983048 | tf_op jit(solution)/shard_map/ppermute | solution.py:1205
  507.4 24.6 %collective-permute-start.35 = (bf16[160,1024]{1,0:T(8,128)(2,1)}, bf16[160,1024]{1,0:T(8,128)(2,1)S(1)}, u32[]{:S(2)}, u32[]{:S(2)}) collective-permute-start(bf16[160,1024]{1,0:T(8,128)(2,1)} %get-tuple-element.175), channel_id=1, source_target_pairs={{0,24},{8,16},{16,8},{24,0},{1,25},{9,17},{17,9},{25,1},{2,26},{10... | collective-permute-start | bytes 983048 | tf_op jit(solution)/shard_map/ppermute | solution.py:1205
  545.0 45.8 %all-to-all-start.3 = ((bf16[4,128,1152]{2,1,0:T(8,128)(2,1)}), bf16[4,128,1152]{2,1,0:T(8,128)(2,1)}, u32[]{:S(2)}, u32[]{:S(2)}) async-start(bf16[4,128,1152]{2,1,0:T(8,128)(2,1)} %add_convert_fusion), calls=%async_computation.4 | async-start | bytes 2359296 | tf_op jit(solution)/shard_map/all_to_all | solution.py:1199
  599.4 37.9 %all-to-all-start.5 = ((bf16[4,2,128,640]{3,2,1,0:T(8,128)(2,1)}), bf16[4,2,128,640]{3,2,1,0:T(8,128)(2,1)}, u32[]{:S(2)}, u32[]{:S(2)}) async-start(bf16[4,2,128,640]{3,2,1,0:T(8,128)(2,1)} %copy-done.52), calls=%async_computation.6 | async-start | bytes 2621440 | tf_op jit(solution)/shard_map/all_to_all | solution.py:1199
  606.7 25.3 %collective-permute-start.41 = (bf16[256,1024]{1,0:T(8,128)(2,1)}, bf16[256,1024]{1,0:T(8,128)(2,1)}, u32[]{:S(2)}, u32[]{:S(2)}) collective-permute-start(bf16[256,1024]{1,0:T(8,128)(2,1)} %add_convert_fusion.2), channel_id=1, source_target_pairs={{0,4},{2,6},{4,0},{6,2},{1,5},{3,7},{5,1},{7,3},{8,12},{10,14},{12... | collective-permute-start | bytes 1572872 | tf_op jit(solution)/shard_map/ppermute | solution.py:1160
  607.1 27.8 %collective-permute-start.42 = (bf16[4,128,512]{2,1,0:T(8,128)(2,1)}, bf16[4,128,512]{2,1,0:T(8,128)(2,1)}, u32[]{:S(2)}, u32[]{:S(2)}) collective-permute-start(bf16[4,128,512]{2,1,0:T(8,128)(2,1)} %copy-done.99), channel_id=1, source_target_pairs={{0,1},{1,0},{2,3},{3,2},{4,5},{5,4},{6,7},{7,6},{8,9},{9,8},{10,11... | collective-permute-start | bytes 1572872 | tf_op jit(solution)/shard_map/ppermute | solution.py:1395
  637.2 19.0 %all-to-all-start.4 = ((bf16[4,128,512]{2,1,0:T(8,128)(2,1)}), bf16[4,128,512]{2,1,0:T(8,128)(2,1)S(1)}, u32[]{:S(2)}, u32[]{:S(2)}) async-start(bf16[4,128,512]{2,1,0:T(8,128)(2,1)} %add_convert_fusion.1), calls=%async_computation.5 | async-start | bytes 1048576 | tf_op jit(solution)/shard_map/all_to_all | solution.py:1199
  (154 other events, 1923.8 us)
Sparse Core Ops, SparseCore 0:
  21.4 52.3 all-gather.4
  76.5 57.1 all-gather.6
  375.1 143.6 reduce-scatter.2
  533.0 135.8 reduce-scatter.4

commit v7 on v6

--- a/solution.py
+++ b/solution.py
@@ -1153,10 +1153,12 @@
     return [piece, twin, across, lax.ppermute(across, "context", TWIN)]
 
 
-def sum_pieces(keep, send):
+def sum_pieces(keep, send, after=()):
     rows = keep.shape[0] // 2
     recv = lax.ppermute(send, "context", TWIN)
     other = (keep[rows:] + recv[rows:].astype(f32)).astype(bf16)
+    if after:
+        other = hold(other, after)
     return keep, recv, lax.ppermute(other, "context", ACROSS)
 
 
@@ -1296,9 +1298,7 @@
         )
         normed_rows = normed_all if layer == 0 else pieces
         last = layer == LAYERS - 1
-        if last:
-            send = hold(send, [arrived_grad])
-        keep, recv, far = sum_pieces(keep, send)
+        keep, recv, far = sum_pieces(keep, send, [arrived_grad] if last else [])
         middle, soft, meta, dest, *sent = route(
             layer, experts, capacity, blocks, place, x, keep, recv, far, feature, ids, idst, last,
         )

time: 693 us -> 703 us (1.014)
  starting transfers between devices: 90.6 us -> 100 us
    all_to_all x5, waiting for transfers between devices: 5.76 us -> 16.4 us  [exchange(): lax.all_to_all(rows, 'experts', split_axis=0, concat_axis=0, tiled=True)]
    unnamed x267 -> x273, local copies, waits for them, and re-layouts: 56 us -> 56.6 us
  transfers between devices with their start and end apart: 54 -> 54, of which waited for: 25 -> 25; matrix products, arithmetic and copies ran while one was open for 2% -> 2% of each run, Pallas kernels for 37% -> 36%
where the time goes in v7:
time: 703 us; the launch traced here: 692 us
  Pallas kernels  261 us (37%)
  waiting for transfers between devices  232 us (33%)
  starting transfers between devices  100 us (14%)
  local copies, waits for them, and re-layouts  57.5 us (8%)
  between operations  15.1 us (2%)
  other arithmetic  14.6 us (2%)
  blocking collectives  11.8 us (2%)
    pallas_call x11, Pallas kernels, expert_call(): pl.pallas_call(ordered, grid=(steps,), out_shape=tuple(outs), in_specs=li...  160 us
    pallas_call x14, Pallas kernels, whole_call(): pl.pallas_call(ordered, out_shape=outs, in_specs=specs, out_specs=tuple((...  66.6 us
    ppermute x4, waiting for transfers between devices, sum_pieces(): return (keep, recv, lax.ppermute(other, 'context', ACROSS))  60.4 us
    unnamed x273, local copies, waits for them, and re-layouts  56.6 us
    ppermute x21, starting transfers between devices, swap(): lax.ppermute(part, 'experts', [(i, i ^ k) for i in range(experts)])  48.3 us
    ppermute x21, waiting for transfers between devices, swap(): lax.ppermute(part, 'experts', [(i, i ^ k) for i in range(experts)])  46.8 us
    ppermute x4, waiting for transfers between devices, share_pieces(): across = lax.ppermute(piece, 'context', ACROSS)  42.4 us
    all_gather x2, waiting for transfers between devices, together(): return lax.all_gather(part, ('experts', 'dp'), axis=0, tiled=False)  38.5 us
  transfers between devices with their start and end apart: 54, of which 25 were waited for; matrix products, arithmetic and copies ran while one was open for 2% of the time, Pallas kernels for 36%

profile of v7, /device:TPU:0, one launch (start us, length us, event | category | flops | bytes accessed | tf_op | source)
XLA Modules:
  0.0 692.1 jit_solution(16463764989563651017)
XLA Ops:
  8.7 11.8 %all_to_all.47 = bf16[4,32,1664]{2,1,0:T(8,128)(2,1)S(1)} all-to-all(bf16[4,32,1664]{2,1,0:T(8,128)(2,1)S(1)} %get-tuple-element.109), channel_id=1, replica_groups=mesh['experts'=4,'context'=4,'dp'=2] {'context'}, dimensions={0} | all-to-all | bytes 851968 | tf_op jit(solution)/shard_map/all_to_all | solution.py:1242
  22.6 12.6 %collective-permute-done.1.refs_3_ = bf16[256,1024]{1,0:T(8,128)(2,1)S(1)} collective-permute-done((bf16[256,1024]{1,0:T(8,128)(2,1)S(1)}, bf16[256,1024]{1,0:T(8,128)(2,1)S(1)}, u32[]{:S(2)}, u32[]{:S(2)}) %collective-permute-start.1) | collective-permute-done | bytes 524320 | tf_op jit(solution)/shard_map/ppermute | solution.py:1151
  35.4 38.5 %all-gather.5.cloned.1.call-done = bf16[32,32,1152]{2,1,0:T(8,128)(2,1)} async-done(((bf16[4,32,1152]{2,1,0:T(8,128)(2,1)}), bf16[32,32,1152]{2,1,0:T(8,128)(2,1)}) %all-gather.5.cloned.1.call-update) | async-done | bytes 2359312 | tf_op jit(solution)/shard_map/all_gather | solution.py:1255
  76.7 9.9 %attention_forward.2 = (bf16[1024,768]{1,0:T(8,128)(2,1)S(1)}, f32[8,1024]{1,0:T(8,128)S(1)}, bf16[1024,256]{1,0:T(8,128)(2,1)S(1)}, f32[512,1024]{1,0:T(8,128)S...) custom-call(s32[3]{0:T(128)S(1)} %pad_add_fusion.refs_0_, bf16[256,1024]{1,0:T(8,128)(2,1)S(1)} %bitcast.50, ...), custom_call_target="tpu_custom_call" | custom-call | flops 3221225472 | bytes 12128268 | tf_op jit(solution)/shard_map/attention_forward/pallas_call | solution.py:96
  95.2 12.3 %collective-permute-done.4.refs_4_ = bf16[256,1024]{1,0:T(8,128)(2,1)S(1)} collective-permute-done((bf16[256,1024]{1,0:T(8,128)(2,1)S(1)}, bf16[256,1024]{1,0:T(8,128)(2,1)S(1)}, u32[]{:S(2)}, u32[]{:S(2)}) %collective-permute-start.4) | collective-permute-done | bytes 524320 | tf_op jit(solution)/shard_map/ppermute | solution.py:1162
  119.9 17.2 %collective-permute-done.5.refs_1_ = bf16[160,1024]{1,0:T(8,128)(2,1)S(1)} collective-permute-done((bf16[160,1024]{1,0:T(8,128)(2,1)S(1)}, bf16[160,1024]{1,0:T(8,128)(2,1)S(1)}, u32[]{:S(2)}, u32[]{:S(2)}) %collective-permute-start.5) | collective-permute-done | bytes 327712 | tf_op jit(solution)/shard_map/ppermute | solution.py:1207
  137.8 12.7 %expert_forward.5 = (bf16[160,1024]{1,0:T(8,128)(2,1)}, bf16[160,1024]{1,0:T(8,128)(2,1)}, bf16[2,320,2816]{2,1,0:T(8,128)(2,1)}) custom-call(bf16[160,1024]{1,0:T(8,128)(2,1)} %copy-done.29, bf16[160,1024]{1,0:T(8,128)(2,1)} %copy-done.31, bf16[2,1,1024,5632]{3,2,1,0:T(8,128)(2,1)} %refs_5_.7, bf16[2,1,1024,5632]{3,2,1,0:T(8,128)(2,1)} %refs_5_.7, ...), custom_call_target="tpu_custom_call" | custom-call | flops 5536481280 | bytes 17301504 | tf_op jit(solution)/shard_map/expert_forward/pallas_call | solution.py:955
  151.3 10.0 %expert_forward.6 = (bf16[160,1024]{1,0:T(8,128)(2,1)}, bf16[2,160,2816]{2,1,0:T(8,128)(2,1)}) custom-call(bf16[160,1024]{1,0:T(8,128)(2,1)} %copy-done.33, bf16[2,1,1024,5632]{3,2,1,0:T(8,128)(2,1)} %refs_5_.7, bf16[2,1,1024,5632]{3,2,1,0:T(8,128)(2,1)} %refs_5_.7, bf16[2,1,1024,2816]{3,2,1,0:T(8,128)(2,1)} %refs_6_.1, ...), custom_call_target="tpu_custom_call" | custom-call | flops 5536481280 | bytes 17301504 | tf_op jit(solution)/shard_map/expert_forward/pallas_call | solution.py:955
  164.3 9.9 %expert_forward.7 = (bf16[160,1024]{1,0:T(8,128)(2,1)}, bf16[2,160,2816]{2,1,0:T(8,128)(2,1)}) custom-call(bf16[160,1024]{1,0:T(8,128)(2,1)} %copy-done.35, bf16[2,1,1024,5632]{3,2,1,0:T(8,128)(2,1)} %refs_5_.7, bf16[2,1,1024,5632]{3,2,1,0:T(8,128)(2,1)} %refs_5_.7, bf16[2,1,1024,2816]{3,2,1,0:T(8,128)(2,1)} %refs_6_.1, ...), custom_call_target="tpu_custom_call" | custom-call | flops 5536481280 | bytes 17301504 | tf_op jit(solution)/shard_map/expert_forward/pallas_call | solution.py:955
  190.3 10.4 %collective-permute-done.12.refs_3_.refs_14_ = bf16[256,1024]{1,0:T(8,128)(2,1)S(1)} collective-permute-done((bf16[256,1024]{1,0:T(8,128)(2,1)}, bf16[256,1024]{1,0:T(8,128)(2,1)S(1)}, u32[]{:S(2)}, u32[]{:S(2)}) %collective-permute-start.12) | collective-permute-done | bytes 524320 | tf_op jit(solution)/shard_map/ppermute | solution.py:1151
  200.7 12.0 %all-to-all-start.1 = ((bf16[4,160,1024]{2,1,0:T(8,128)(2,1)}), bf16[4,160,1024]{2,1,0:T(8,128)(2,1)}, u32[]{:S(2)}, u32[]{:S(2)}) async-start(bf16[4,160,1024]{2,1,0:T(8,128)(2,1)} %bitcast.37), calls=%async_computation.1 | async-start | bytes 2621440 | tf_op jit(solution)/shard_map/all_to_all | solution.py:1201
  215.1 9.8 %attention_forward.3 = (bf16[1024,768]{1,0:T(8,128)(2,1)S(1)}, f32[8,1024]{1,0:T(8,128)S(1)}, bf16[1024,256]{1,0:T(8,128)(2,1)S(1)}, f32[512,1024]{1,0:T(8,128)S(1)}, bf16[512,1024]{1,0:T(8,128)(2,1)S(1)}) custom-call(s32[3]{0:T(128)S(1)} %pad_add_fusion.refs_0_, bf16[256,1024]{1,0:T(8,128)(2,1)S(1)} %copy-done.76, ...), custom_call_target="tpu_custom_call" | custom-call | flops 3221225472 | bytes 10031116 | tf_op jit(solution)/shard_map/attention_forward/pallas_call | solution.py:96
  231.8 13.7 %all-to-all-done.1 = bf16[4,160,1024]{2,1,0:T(8,128)(2,1)} async-done(((bf16[4,160,1024]{2,1,0:T(8,128)(2,1)}), bf16[4,160,1024]{2,1,0:T(8,128)(2,1)}, u32[]{:S(2)}, u32[]{:S(2)}) %all-to-all-start.1) | async-done | bytes 1310752 | tf_op jit(solution)/shard_map/all_to_all | solution.py:1201
  246.9 12.5 %collective-permute-done.15.refs_4_ = bf16[256,1024]{1,0:T(8,128)(2,1)S(1)} collective-permute-done((bf16[256,1024]{1,0:T(8,128)(2,1)}, bf16[256,1024]{1,0:T(8,128)(2,1)S(1)}, u32[]{:S(2)}, u32[]{:S(2)}) %collective-permute-start.15) | collective-permute-done | bytes 524320 | tf_op jit(solution)/shard_map/ppermute | solution.py:1162
  282.7 12.7 %expert_forward.8 = (bf16[160,1024]{1,0:T(8,128)(2,1)}, bf16[160,1024]{1,0:T(8,128)(2,1)}, bf16[2,320,2816]{2,1,0:T(8,128)(2,1)}) custom-call(bf16[160,1024]{1,0:T(8,128)(2,1)} %copy-done.37, bf16[160,1024]{1,0:T(8,128)(2,1)} %copy-done.39, bf16[2,1,1024,5632]{3,2,1,0:T(8,128)(2,1)} %refs_5_.7, bf16[2,1,1024,5632]{3,2,1,0:T(8,128)(2,1)} %refs_5_.7, ...), custom_call_target="tpu_custom_call" | custom-call | flops 5536481280 | bytes 17301504 | tf_op jit(solution)/shard_map/expert_forward/pallas_call | solution.py:955
  301.3 14.9 %expert_backward.4 = (bf16[160,1024]{1,0:T(8,128)(2,1)}, bf16[160,1024]{1,0:T(8,128)(2,1)}, bf16[3,320,2816]{2,1,0:T(8,128)(2,1)}) custom-call(bf16[160,1024]{1,0:T(8,128)(2,1)} %copy-done.45, bf16[160,1024]{1,0:T(8,128)(2,1)} %copy-done.47, bf16[2,320,2816]{2,1,0:T(8,128)(2,1)} %get-tuple-element.145.refs_2_, bf16[2,1,1024,5632]{3,2,1,0:T(8,128)(2,1)} %refs_5_.7, ...), custom_call_target="tpu_custom_call" | custom-call | flops 5536481280 | bytes 17301504 | tf_op jit(solution)/shard_map/expert_backward/pallas_call | solution.py:955
  318.4 12.7 %expert_forward.9 = (bf16[160,1024]{1,0:T(8,128)(2,1)}, bf16[160,1024]{1,0:T(8,128)(2,1)}, bf16[2,320,2816]{2,1,0:T(8,128)(2,1)}) custom-call(bf16[160,1024]{1,0:T(8,128)(2,1)} %copy-done.57, bf16[160,1024]{1,0:T(8,128)(2,1)} %copy-done.59, bf16[2,1,1024,5632]{3,2,1,0:T(8,128)(2,1)} %refs_5_.7, bf16[2,1,1024,5632]{3,2,1,0:T(8,128)(2,1)} %refs_5_.7, ...), custom_call_target="tpu_custom_call" | custom-call | flops 5536481280 | bytes 17301504 | tf_op jit(solution)/shard_map/expert_forward/pallas_call | solution.py:955
  334.2 15.0 %expert_backward.5 = (bf16[160,1024]{1,0:T(8,128)(2,1)}, bf16[160,1024]{1,0:T(8,128)(2,1)}, bf16[3,320,2816]{2,1,0:T(8,128)(2,1)}) custom-call(bf16[160,1024]{1,0:T(8,128)(2,1)} %copy-done.49, bf16[160,1024]{1,0:T(8,128)(2,1)} %copy-done.51, bf16[2,320,2816]{2,1,0:T(8,128)(2,1)} %get-tuple-element.152.refs_2_, bf16[2,1,1024,5632]{3,2,1,0:T(8,128)(2,1)} %refs_5_.7, ...), custom_call_target="tpu_custom_call" | custom-call | flops 5536481280 | bytes 17301504 | tf_op jit(solution)/shard_map/expert_backward/pallas_call | solution.py:955
  352.0 11.9 %collective-permute-done.20.refs_4_.refs_12_.refs_2_ = bf16[160,1024]{1,0:T(8,128)(2,1)S(1)} collective-permute-done((bf16[160,1024]{1,0:T(8,128)(2,1)}, bf16[160,1024]{1,0:T(8,128)(2,1)S(1)}, u32[]{:S(2)}, u32[]{:S(2)}) %collective-permute-start.20) | collective-permute-done | bytes 327712 | tf_op jit(solution)/shard_map/ppermute | solution.py:1207
  364.8 20.4 %expert_grads.2.refs_0_ = bf16[8,3,128,2816]{3,2,1,0:T(8,128)(2,1)} custom-call(bf16[160,1024]{1,0:T(8,128)(2,1)S(1)} %copy-done.38, bf16[160,1024]{1,0:T(8,128)(2,1)S(1)} %copy-done.40, bf16[160,1024]{1,0:T(8,128)(2,1)S(1)} %copy-done.58, bf16[160,1024]{1,0:T(8,128)(2,1)S(1)} %copy-done.60, bf16[160,1024]{1,0:T(8,128)(2,1)S(1)} %copy-done.46, ...), custom_call_target="tpu_custom_call" | custom-call | flops 5536481280 | bytes 17301504 | tf_op jit(solution)/shard_map/expert_grads/pallas_call | solution.py:955
  395.0 7.7 %collective-permute-done.26.refs_3_.refs_7_ = bf16[256,1024]{1,0:T(8,128)(2,1)S(1)} collective-permute-done((bf16[256,1024]{1,0:T(8,128)(2,1)S(1)}, bf16[256,1024]{1,0:T(8,128)(2,1)S(1)}, u32[]{:S(2)}, u32[]{:S(2)}) %collective-permute-start.26) | collective-permute-done | bytes 524320 | tf_op jit(solution)/shard_map/ppermute | solution.py:1151
  405.0 14.3 %attention_backward.2 = (bf16[1024,768]{1,0:T(8,128)(2,1)S(1)}, f32[512,1024]{1,0:T(8,128)S(1)}, bf16[512,1024]{1,0:T(8,128)(2,1)S(1)}, f32[8,512]{1,0:T(8,128)S(1)}, f32[8,1024]{1,0:T(8,128)S(1)}) custom-call(s32[3]{0:T(128)S(1)} %pad_add_fusion.refs_0_, bf16[256,1024]{1,0:T(8,128)(2,1)S(1)} %get-tuple-element.159.refs_1_.refs_5_, ...), custom_call_target="tpu_custom_call" | custom-call | flops 4831838208 | bytes 13225996 | tf_op jit(solution)/shard_map/attention_backward/pallas_call | solution.py:96
  424.2 18.8 %collective-permute-done.29.refs_4_ = bf16[256,1024]{1,0:T(8,128)(2,1)S(1)} collective-permute-done((bf16[256,1024]{1,0:T(8,128)(2,1)S(1)}, bf16[256,1024]{1,0:T(8,128)(2,1)S(1)}, u32[]{:S(2)}, u32[]{:S(2)}) %collective-permute-start.29) | collective-permute-done | bytes 524320 | tf_op jit(solution)/shard_map/ppermute | solution.py:1162
  446.8 13.7 %collective-permute-start.30 = (bf16[160,1024]{1,0:T(8,128)(2,1)S(1)}, bf16[160,1024]{1,0:T(8,128)(2,1)S(1)}, u32[]{:S(2)}, u32[]{:S(2)}) collective-permute-start(bf16[160,1024]{1,0:T(8,128)(2,1)S(1)} %get-tuple-element.166), channel_id=1, source_target_pairs={{0,8},{8,0},{16,24},{24,16},{1,9},{9,1},{17,25},{25,17},{2,10},{10... | collective-permute-start | bytes 983048 | tf_op jit(solution)/shard_map/ppermute | solution.py:1207
  471.5 15.5 %expert_backward.6 = (bf16[160,1024]{1,0:T(8,128)(2,1)}, bf16[160,1024]{1,0:T(8,128)(2,1)}, bf16[3,320,2816]{2,1,0:T(8,128)(2,1)}) custom-call(bf16[160,1024]{1,0:T(8,128)(2,1)} %copy-done.41, bf16[160,1024]{1,0:T(8,128)(2,1)} %copy-done.43, bf16[2,320,2816]{2,1,0:T(8,128)(2,1)} %get-tuple-element.167.refs_2_, bf16[2,1,1024,5632]{3,2,1,0:T(8,128)(2,1)} %refs_5_.7, ...), custom_call_target="tpu_custom_call" | custom-call | flops 5536481280 | bytes 17301504 | tf_op jit(solution)/shard_map/expert_backward/pallas_call | solution.py:955
  492.7 15.2 %expert_backward.7 = (bf16[160,1024]{1,0:T(8,128)(2,1)}, bf16[160,1024]{1,0:T(8,128)(2,1)}, bf16[3,320,2816]{2,1,0:T(8,128)(2,1)}) custom-call(bf16[160,1024]{1,0:T(8,128)(2,1)} %copy-done.61, bf16[160,1024]{1,0:T(8,128)(2,1)} %copy-done.63, bf16[2,160,2816]{2,1,0:T(8,128)(2,1)} %get-tuple-element.172.refs_2_, ...), custom_call_target="tpu_custom_call" | custom-call | flops 5536481280 | bytes 17301504 | tf_op jit(solution)/shard_map/expert_backward/pallas_call | solution.py:955
  507.9 8.9 %collective-permute-start.34 = (bf16[160,1024]{1,0:T(8,128)(2,1)}, bf16[160,1024]{1,0:T(8,128)(2,1)S(1)}, u32[]{:S(2)}, u32[]{:S(2)}) collective-permute-start(bf16[160,1024]{1,0:T(8,128)(2,1)} %get-tuple-element.174), channel_id=1, source_target_pairs={{0,16},{8,24},{16,0},{24,8},{1,17},{9,25},{17,1},{25,9},{2,18},{10... | collective-permute-start | bytes 983048 | tf_op jit(solution)/shard_map/ppermute | solution.py:1207
  521.4 20.4 %expert_grads.3.refs_0_ = bf16[8,3,128,2816]{3,2,1,0:T(8,128)(2,1)} custom-call(bf16[160,1024]{1,0:T(8,128)(2,1)S(1)} %copy-done.30, bf16[160,1024]{1,0:T(8,128)(2,1)S(1)} %copy-done.32, bf16[160,1024]{1,0:T(8,128)(2,1)S(1)} %copy-done.34, bf16[160,1024]{1,0:T(8,128)(2,1)S(1)} %copy-done.36, bf16[160,1024]{1,0:T(8,128)(2,1)S(1)} %copy-done.42, ...), custom_call_target="tpu_custom_call" | custom-call | flops 5536481280 | bytes 17301504 | tf_op jit(solution)/shard_map/expert_grads/pallas_call | solution.py:955
  562.4 11.7 %collective-permute-done.38.refs_3_.refs_4_ = bf16[256,1024]{1,0:T(8,128)(2,1)S(1)} collective-permute-done((bf16[256,1024]{1,0:T(8,128)(2,1)S(1)}, bf16[256,1024]{1,0:T(8,128)(2,1)S(1)}, u32[]{:S(2)}, u32[]{:S(2)}) %collective-permute-start.38) | collective-permute-done | bytes 524320 | tf_op jit(solution)/shard_map/ppermute | solution.py:1151
  581.6 15.1 %attention_backward.3 = (bf16[1024,768]{1,0:T(8,128)(2,1)S(1)}, f32[512,1024]{1,0:T(8,128)S(1)}, bf16[512,1024]{1,0:T(8,128)(2,1)}, f32[8,512]{1,0:T(8,128)S(1)}, f32[8,1024]{1,0:T(8,128)S(1)}) custom-call(s32[3]{0:T(128)S(1)} %pad_add_fusion.refs_0_, bf16[256,1024]{1,0:T(8,128)(2,1)S(1)} %copy-done.72, ...), custom_call_target="tpu_custom_call" | custom-call | flops 4831838208 | bytes 13225996 | tf_op jit(solution)/shard_map/attention_backward/pallas_call | solution.py:96
  624.3 16.9 %collective-permute-done.41.refs_4_ = bf16[256,1024]{1,0:T(8,128)(2,1)} collective-permute-done((bf16[256,1024]{1,0:T(8,128)(2,1)}, bf16[256,1024]{1,0:T(8,128)(2,1)}, u32[]{:S(2)}, u32[]{:S(2)}) %collective-permute-start.41) | collective-permute-done | bytes 524320 | tf_op jit(solution)/shard_map/ppermute | solution.py:1162
  669.5 9.2 %all-to-all-done.6.refs_0_ = bf16[4,2,32,896]{3,2,1,0:T(8,128)(2,1)S(1)} async-done(((bf16[4,2,32,896]{3,2,1,0:T(8,128)(2,1)}), bf16[4,2,32,896]{3,2,1,0:T(8,128)(2,1)S(1)}, u32[]{:S(2)}, u32[]{:S(2)}) %all-to-all-start.6) | async-done | bytes 458784 | tf_op jit(solution)/shard_map/all_to_all | solution.py:1242
  (418 shorter events, 228.6 us)
Async XLA Ops:
  7.2 66.6 %all-gather.5.cloned.1.call-start = ((), (), s32[]{:S(2)}) async-start(), calls=%async_computation.11 | async-start | bytes 2654208 | tf_op jit(solution)/shard_map/all_gather | solution.py:1255
  21.3 129.2 %all-gather.7.cloned.1.call-start = ((), (), s32[]{:S(2)}) async-start(), calls=%async_computation.12 | async-start | bytes 2359296 | tf_op jit(solution)/shard_map/all_gather | solution.py:1255
  22.6 54.1 %collective-permute-start = (bf16[256,1024]{1,0:T(8,128)(2,1)S(1)}, bf16[256,1024]{1,0:T(8,128)(2,1)S(1)}, u32[]{:S(2)}, u32[]{:S(2)}) collective-permute-start(bf16[256,1024]{1,0:T(8,128)(2,1)S(1)} %bitcast.49), channel_id=1, source_target_pairs={{0,2},{2,0},{4,6},{6,4},{1,3},{3,1},{5,7},{7,5},{8,10},{10,8},{12,... | collective-permute-start | bytes 1572872 | tf_op jit(solution)/shard_map/ppermute | solution.py:1152
  35.2 41.5 %collective-permute-start.2 = (bf16[256,1024]{1,0:T(8,128)(2,1)S(1)}, bf16[256,1024]{1,0:T(8,128)(2,1)S(1)}, u32[]{:S(2)}, u32[]{:S(2)}) collective-permute-start(bf16[256,1024]{1,0:T(8,128)(2,1)S(1)} %collective-permute-done.1.refs_3_), channel_id=1, source_target_pairs={{0,2},{2,0},{4,6},{6,4},{1,3},{3,1},{5,7},{7,5},{8,10},{10,8},{12,... | collective-permute-start | bytes 1572872 | tf_op jit(solution)/shard_map/ppermute | solution.py:1153
  115.5 21.5 %collective-permute-start.5 = (bf16[160,1024]{1,0:T(8,128)(2,1)S(1)}, bf16[160,1024]{1,0:T(8,128)(2,1)S(1)}, u32[]{:S(2)}, u32[]{:S(2)}) collective-permute-start(bf16[160,1024]{1,0:T(8,128)(2,1)S(1)} %get-tuple-element.120), channel_id=1, source_target_pairs={{0,8},{8,0},{16,24},{24,16},{1,9},{9,1},{17,25},{25,17},{2,10},{10... | collective-permute-start | bytes 983048 | tf_op jit(solution)/shard_map/ppermute | solution.py:1207
  117.0 33.6 %collective-permute-start.7 = (bf16[160,1024]{1,0:T(8,128)(2,1)}, bf16[160,1024]{1,0:T(8,128)(2,1)S(1)}, u32[]{:S(2)}, u32[]{:S(2)}) collective-permute-start(bf16[160,1024]{1,0:T(8,128)(2,1)} %get-tuple-element.123), channel_id=1, source_target_pairs={{0,16},{8,24},{16,0},{24,8},{1,17},{9,25},{17,1},{25,9},{2,18},{10... | collective-permute-start | bytes 983048 | tf_op jit(solution)/shard_map/ppermute | solution.py:1207
  117.9 45.7 %collective-permute-start.9 = (bf16[160,1024]{1,0:T(8,128)(2,1)}, bf16[160,1024]{1,0:T(8,128)(2,1)S(1)}, u32[]{:S(2)}, u32[]{:S(2)}) collective-permute-start(bf16[160,1024]{1,0:T(8,128)(2,1)} %get-tuple-element.126), channel_id=1, source_target_pairs={{0,24},{8,16},{16,8},{24,0},{1,25},{9,17},{17,9},{25,1},{2,26},{10... | collective-permute-start | bytes 983048 | tf_op jit(solution)/shard_map/ppermute | solution.py:1207
  190.3 24.7 %collective-permute-start.11 = (bf16[256,1024]{1,0:T(8,128)(2,1)}, bf16[256,1024]{1,0:T(8,128)(2,1)S(1)}, u32[]{:S(2)}, u32[]{:S(2)}) collective-permute-start(bf16[256,1024]{1,0:T(8,128)(2,1)} %hold.6.refs_1_.refs_12_), channel_id=1, source_target_pairs={{0,2},{2,0},{4,6},{6,4},{1,3},{3,1},{5,7},{7,5},{8,10},{10,8},{12,... | collective-permute-start | bytes 1572872 | tf_op jit(solution)/shard_map/ppermute | solution.py:1152
  200.7 44.7 %all-to-all-start.1 = ((bf16[4,160,1024]{2,1,0:T(8,128)(2,1)}), bf16[4,160,1024]{2,1,0:T(8,128)(2,1)}, u32[]{:S(2)}, u32[]{:S(2)}) async-start(bf16[4,160,1024]{2,1,0:T(8,128)(2,1)} %bitcast.37), calls=%async_computation.1 | async-start | bytes 2621440 | tf_op jit(solution)/shard_map/all_to_all | solution.py:1201
  267.9 28.1 %all-to-all-start.2 = ((f32[4,160,128]{2,1,0:T(8,128)}), f32[4,160,128]{2,1,0:T(8,128)S(1)}, u32[]{:S(2)}, u32[]{:S(2)}) async-start(f32[4,160,128]{2,1,0:T(8,128)} %bitcast.53), calls=%async_computation.2 | async-start | bytes 655360 | tf_op jit(solution)/shard_map/all_to_all | solution.py:1201
  271.4 349.2 %reduce-scatter.3.cloned.1.call-start = ((), (), s32[]{:S(2)}) async-start(), calls=%async_computation.9 | async-start | bytes 19464192 | tf_op jit(solution)/shard_map/reduce_scatter | solution.py:1362
  271.9 45.7 %collective-permute-start.18 = (bf16[160,1024]{1,0:T(8,128)(2,1)}, bf16[160,1024]{1,0:T(8,128)(2,1)S(1)}, u32[]{:S(2)}, u32[]{:S(2)}) collective-permute-start(bf16[160,1024]{1,0:T(8,128)(2,1)} %copy-done.105), channel_id=1, source_target_pairs={{0,16},{8,24},{16,0},{24,8},{1,17},{9,25},{17,1},{25,9},{2,18},{10... | collective-permute-start | bytes 983048 | tf_op jit(solution)/shard_map/ppermute | solution.py:1207
  274.8 42.8 %collective-permute-start.19 = (bf16[160,1024]{1,0:T(8,128)(2,1)}, bf16[160,1024]{1,0:T(8,128)(2,1)S(1)}, u32[]{:S(2)}, u32[]{:S(2)}) collective-permute-start(bf16[160,1024]{1,0:T(8,128)(2,1)} %copy-done.104), channel_id=1, source_target_pairs={{0,24},{8,16},{16,8},{24,0},{1,25},{9,17},{17,9},{25,1},{2,26},{10... | collective-permute-start | bytes 983048 | tf_op jit(solution)/shard_map/ppermute | solution.py:1207
  295.4 55.1 %collective-permute-start.17 = (bf16[160,1024]{1,0:T(8,128)(2,1)}, bf16[160,1024]{1,0:T(8,128)(2,1)S(1)}, u32[]{:S(2)}, u32[]{:S(2)}) collective-permute-start(bf16[160,1024]{1,0:T(8,128)(2,1)} %get-tuple-element.139), channel_id=1, source_target_pairs={{0,8},{8,0},{16,24},{24,16},{1,9},{9,1},{17,25},{25,17},{2,10},{10... | collective-permute-start | bytes 983048 | tf_op jit(solution)/shard_map/ppermute | solution.py:1207
  316.2 69.1 %collective-permute-start.22 = (bf16[160,1024]{1,0:T(8,128)(2,1)}, bf16[160,1024]{1,0:T(8,128)(2,1)S(1)}, u32[]{:S(2)}, u32[]{:S(2)}) collective-permute-start(bf16[160,1024]{1,0:T(8,128)(2,1)} %get-tuple-element.149), channel_id=1, source_target_pairs={{0,8},{8,0},{16,24},{24,16},{1,9},{9,1},{17,25},{25,17},{2,10},{10... | collective-permute-start | bytes 983048 | tf_op jit(solution)/shard_map/ppermute | solution.py:1207
  331.1 32.8 %collective-permute-start.20 = (bf16[160,1024]{1,0:T(8,128)(2,1)}, bf16[160,1024]{1,0:T(8,128)(2,1)S(1)}, u32[]{:S(2)}, u32[]{:S(2)}) collective-permute-start(bf16[160,1024]{1,0:T(8,128)(2,1)} %get-tuple-element.147), channel_id=1, source_target_pairs={{0,16},{8,24},{16,0},{24,8},{1,17},{9,25},{17,1},{25,9},{2,18},{10... | collective-permute-start | bytes 983048 | tf_op jit(solution)/shard_map/ppermute | solution.py:1207
  332.0 32.0 %collective-permute-start.21 = (bf16[160,1024]{1,0:T(8,128)(2,1)}, bf16[160,1024]{1,0:T(8,128)(2,1)S(1)}, u32[]{:S(2)}, u32[]{:S(2)}) collective-permute-start(bf16[160,1024]{1,0:T(8,128)(2,1)} %get-tuple-element.148), channel_id=1, source_target_pairs={{0,24},{8,16},{16,8},{24,0},{1,25},{9,17},{17,9},{25,1},{2,26},{10... | collective-permute-start | bytes 983048 | tf_op jit(solution)/shard_map/ppermute | solution.py:1207
  349.2 36.1 %collective-permute-start.23 = (bf16[160,1024]{1,0:T(8,128)(2,1)}, bf16[160,1024]{1,0:T(8,128)(2,1)S(1)}, u32[]{:S(2)}, u32[]{:S(2)}) collective-permute-start(bf16[160,1024]{1,0:T(8,128)(2,1)} %get-tuple-element.153), channel_id=1, source_target_pairs={{0,16},{8,24},{16,0},{24,8},{1,17},{9,25},{17,1},{25,9},{2,18},{10... | collective-permute-start | bytes 983048 | tf_op jit(solution)/shard_map/ppermute | solution.py:1207
  350.5 34.8 %collective-permute-start.24 = (bf16[160,1024]{1,0:T(8,128)(2,1)}, bf16[160,1024]{1,0:T(8,128)(2,1)S(1)}, u32[]{:S(2)}, u32[]{:S(2)}) collective-permute-start(bf16[160,1024]{1,0:T(8,128)(2,1)} %get-tuple-element.154), channel_id=1, source_target_pairs={{0,24},{8,16},{16,8},{24,0},{1,25},{9,17},{17,9},{25,1},{2,26},{10... | collective-permute-start | bytes 983048 | tf_op jit(solution)/shard_map/ppermute | solution.py:1207
  386.9 295.0 %reduce-scatter.5.cloned.1.call-start = ((), (), s32[]{:S(2)}) async-start(), calls=%async_computation.10 | async-start | bytes 19464192 | tf_op jit(solution)/shard_map/reduce_scatter | solution.py:1362
  422.3 20.7 %collective-permute-start.29 = (bf16[256,1024]{1,0:T(8,128)(2,1)S(1)}, bf16[256,1024]{1,0:T(8,128)(2,1)S(1)}, u32[]{:S(2)}, u32[]{:S(2)}) collective-permute-start(bf16[256,1024]{1,0:T(8,128)(2,1)S(1)} %add_convert_fusion.3), channel_id=1, source_target_pairs={{0,4},{2,6},{4,0},{6,2},{1,5},{3,7},{5,1},{7,3},{8,12},{10,14},{12... | collective-permute-start | bytes 1572872 | tf_op jit(solution)/shard_map/ppermute | solution.py:1162
  446.8 24.0 %collective-permute-start.30 = (bf16[160,1024]{1,0:T(8,128)(2,1)S(1)}, bf16[160,1024]{1,0:T(8,128)(2,1)S(1)}, u32[]{:S(2)}, u32[]{:S(2)}) collective-permute-start(bf16[160,1024]{1,0:T(8,128)(2,1)S(1)} %get-tuple-element.166), channel_id=1, source_target_pairs={{0,8},{8,0},{16,24},{24,16},{1,9},{9,1},{17,25},{25,17},{2,10},{10... | collective-permute-start | bytes 983048 | tf_op jit(solution)/shard_map/ppermute | solution.py:1207
  467.8 50.5 %collective-permute-start.36 = (bf16[4,128,1152]{2,1,0:T(8,128)(2,1)S(1)}, bf16[4,128,1152]{2,1,0:T(8,128)(2,1)S(1)}, u32[]{:S(2)}, u32[]{:S(2)}) collective-permute-start(bf16[4,128,1152]{2,1,0:T(8,128)(2,1)S(1)} %get-tuple-element.185), channel_id=1, source_target_pairs={{0,1},{1,0},{2,3},{3,2},{4,5},{5,4},{6,7},{7,6},{8,9},{9,8},{10,11... | collective-permute-start | bytes 3538952 | tf_op jit(solution)/shard_map/ppermute | solution.py:1395
  468.3 23.5 %collective-permute-start.32 = (bf16[160,1024]{1,0:T(8,128)(2,1)S(1)}, bf16[160,1024]{1,0:T(8,128)(2,1)S(1)}, u32[]{:S(2)}, u32[]{:S(2)}) collective-permute-start(bf16[160,1024]{1,0:T(8,128)(2,1)S(1)} %get-tuple-element.170), channel_id=1, source_target_pairs={{0,16},{8,24},{16,0},{24,8},{1,17},{9,25},{17,1},{25,9},{2,18},{10... | collective-permute-start | bytes 983048 | tf_op jit(solution)/shard_map/ppermute | solution.py:1207
  469.0 22.8 %collective-permute-start.33 = (bf16[160,1024]{1,0:T(8,128)(2,1)S(1)}, bf16[160,1024]{1,0:T(8,128)(2,1)S(1)}, u32[]{:S(2)}, u32[]{:S(2)}) collective-permute-start(bf16[160,1024]{1,0:T(8,128)(2,1)S(1)} %get-tuple-element.171), channel_id=1, source_target_pairs={{0,24},{8,16},{16,8},{24,0},{1,25},{9,17},{17,9},{25,1},{2,26},{10... | collective-permute-start | bytes 983048 | tf_op jit(solution)/shard_map/ppermute | solution.py:1207
  487.0 54.8 %collective-permute-start.31 = (bf16[160,1024]{1,0:T(8,128)(2,1)}, bf16[160,1024]{1,0:T(8,128)(2,1)}, u32[]{:S(2)}, u32[]{:S(2)}) collective-permute-start(bf16[160,1024]{1,0:T(8,128)(2,1)} %get-tuple-element.169.refs_7_), channel_id=1, source_target_pairs={{0,8},{8,0},{16,24},{24,16},{1,9},{9,1},{17,25},{25,17},{2,10},{10... | collective-permute-start | bytes 983048 | tf_op jit(solution)/shard_map/ppermute | solution.py:1207
  507.9 33.9 %collective-permute-start.34 = (bf16[160,1024]{1,0:T(8,128)(2,1)}, bf16[160,1024]{1,0:T(8,128)(2,1)S(1)}, u32[]{:S(2)}, u32[]{:S(2)}) collective-permute-start(bf16[160,1024]{1,0:T(8,128)(2,1)} %get-tuple-element.174), channel_id=1, source_target_pairs={{0,16},{8,24},{16,0},{24,8},{1,17},{9,25},{17,1},{25,9},{2,18},{10... | collective-permute-start | bytes 983048 | tf_op jit(solution)/shard_map/ppermute | solution.py:1207
  516.8 25.0 %collective-permute-start.35 = (bf16[160,1024]{1,0:T(8,128)(2,1)}, bf16[160,1024]{1,0:T(8,128)(2,1)S(1)}, u32[]{:S(2)}, u32[]{:S(2)}) collective-permute-start(bf16[160,1024]{1,0:T(8,128)(2,1)} %get-tuple-element.175), channel_id=1, source_target_pairs={{0,24},{8,16},{16,8},{24,0},{1,25},{9,17},{17,9},{25,1},{2,26},{10... | collective-permute-start | bytes 983048 | tf_op jit(solution)/shard_map/ppermute | solution.py:1207
  554.7 44.6 %all-to-all-start.3 = ((bf16[4,128,1152]{2,1,0:T(8,128)(2,1)}), bf16[4,128,1152]{2,1,0:T(8,128)(2,1)}, u32[]{:S(2)}, u32[]{:S(2)}) async-start(bf16[4,128,1152]{2,1,0:T(8,128)(2,1)} %add_convert_fusion), calls=%async_computation.4 | async-start | bytes 2359296 | tf_op jit(solution)/shard_map/all_to_all | solution.py:1201
  608.0 38.4 %all-to-all-start.5 = ((bf16[4,2,128,640]{3,2,1,0:T(8,128)(2,1)}), bf16[4,2,128,640]{3,2,1,0:T(8,128)(2,1)}, u32[]{:S(2)}, u32[]{:S(2)}) async-start(bf16[4,2,128,640]{3,2,1,0:T(8,128)(2,1)} %copy-done.53), calls=%async_computation.6 | async-start | bytes 2621440 | tf_op jit(solution)/shard_map/all_to_all | solution.py:1201
  615.2 26.0 %collective-permute-start.41 = (bf16[256,1024]{1,0:T(8,128)(2,1)}, bf16[256,1024]{1,0:T(8,128)(2,1)}, u32[]{:S(2)}, u32[]{:S(2)}) collective-permute-start(bf16[256,1024]{1,0:T(8,128)(2,1)} %add_convert_fusion.2), channel_id=1, source_target_pairs={{0,4},{2,6},{4,0},{6,2},{1,5},{3,7},{5,1},{7,3},{8,12},{10,14},{12... | collective-permute-start | bytes 1572872 | tf_op jit(solution)/shard_map/ppermute | solution.py:1162
  616.2 27.9 %collective-permute-start.42 = (bf16[4,128,512]{2,1,0:T(8,128)(2,1)}, bf16[4,128,512]{2,1,0:T(8,128)(2,1)}, u32[]{:S(2)}, u32[]{:S(2)}) collective-permute-start(bf16[4,128,512]{2,1,0:T(8,128)(2,1)} %copy-done.100), channel_id=1, source_target_pairs={{0,1},{1,0},{2,3},{3,2},{4,5},{5,4},{6,7},{7,6},{8,9},{9,8},{10,11... | collective-permute-start | bytes 1572872 | tf_op jit(solution)/shard_map/ppermute | solution.py:1395
  (157 other events, 1971.2 us)
Sparse Core Ops, SparseCore 0:
  21.4 52.3 all-gather.4
  76.5 57.1 all-gather.6
  387.0 142.8 reduce-scatter.2
  542.8 135.8 reduce-scatter.4

commit v8 on v6

--- a/solution.py
+++ b/solution.py
@@ -1356,7 +1356,7 @@
         came = swap(drows, experts)
         early = [] if other is None else [other]
         weight_grads = expert_grads(
-            GROUP * pairs, arrived, arrived_grad, parts, after=(back if layer else []) + early
+            GROUP * pairs, arrived, arrived_grad, parts, after=early
         )
         weight_grads = hold(weight_grads, came)
         total = lax.psum_scatter(

time: 693 us -> 717 us (1.035)
  waiting for transfers between devices: 231 us -> 245 us
    unnamed x267 -> x275, local copies, waits for them, and re-layouts: 56 us -> 62.3 us
  transfers between devices with their start and end apart: 54 -> 54, of which waited for: 25 -> 27; matrix products, arithmetic and copies ran while one was open for 2% -> 2% of each run, Pallas kernels for 37% -> 36%
where the time goes in v8:
time: 717 us; the launch traced here: 706 us
  Pallas kernels  263 us (37%)
  waiting for transfers between devices  245 us (34%)
  starting transfers between devices  93.8 us (13%)
  local copies, waits for them, and re-layouts  63.2 us (9%)
  between operations  15 us (2%)
  other arithmetic  14.2 us (2%)
  blocking collectives  11.8 us (2%)
    pallas_call x11, Pallas kernels, expert_call(): pl.pallas_call(ordered, grid=(steps,), out_shape=tuple(outs), in_specs=li...  160 us
    pallas_call x14, Pallas kernels, whole_call(): pl.pallas_call(ordered, out_shape=outs, in_specs=specs, out_specs=tuple((...  68.4 us
    ppermute x4, waiting for transfers between devices, sum_pieces(): return (keep, recv, lax.ppermute(other, 'context', ACROSS))  63.9 us
    unnamed x275, local copies, waits for them, and re-layouts  62.3 us
    ppermute x4, waiting for transfers between devices, share_pieces(): across = lax.ppermute(piece, 'context', ACROSS)  54.8 us
    ppermute x21, waiting for transfers between devices, swap(): lax.ppermute(part, 'experts', [(i, i ^ k) for i in range(experts)])  50.7 us
    ppermute x21, starting transfers between devices, swap(): lax.ppermute(part, 'experts', [(i, i ^ k) for i in range(experts)])  45.1 us
    all_gather x2, waiting for transfers between devices, together(): return lax.all_gather(part, ('experts', 'dp'), axis=0, tiled=False)  38.5 us
  transfers between devices with their start and end apart: 54, of which 27 were waited for; matrix products, arithmetic and copies ran while one was open for 2% of the time, Pallas kernels for 36%

profile of v8, /device:TPU:0, one launch (start us, length us, event | category | flops | bytes accessed | tf_op | source)
XLA Modules:
  0.0 706.0 jit_solution(13441303999145386630)
XLA Ops:
  8.7 11.8 %all_to_all.47 = bf16[4,32,1664]{2,1,0:T(8,128)(2,1)S(1)} all-to-all(bf16[4,32,1664]{2,1,0:T(8,128)(2,1)S(1)} %get-tuple-element.109), channel_id=1, replica_groups=mesh['experts'=4,'context'=4,'dp'=2] {'context'}, dimensions={0} | all-to-all | bytes 851968 | tf_op jit(solution)/shard_map/all_to_all | solution.py:1240
  22.6 12.6 %collective-permute-done.1.refs_3_ = bf16[256,1024]{1,0:T(8,128)(2,1)S(1)} collective-permute-done((bf16[256,1024]{1,0:T(8,128)(2,1)S(1)}, bf16[256,1024]{1,0:T(8,128)(2,1)S(1)}, u32[]{:S(2)}, u32[]{:S(2)}) %collective-permute-start.1) | collective-permute-done | bytes 524320 | tf_op jit(solution)/shard_map/ppermute | solution.py:1151
  35.4 38.5 %all-gather.5.cloned.1.call-done = bf16[32,32,1152]{2,1,0:T(8,128)(2,1)} async-done(((bf16[4,32,1152]{2,1,0:T(8,128)(2,1)}), bf16[32,32,1152]{2,1,0:T(8,128)(2,1)}) %all-gather.5.cloned.1.call-update) | async-done | bytes 2359312 | tf_op jit(solution)/shard_map/all_gather | solution.py:1253
  76.7 9.9 %attention_forward.2 = (bf16[1024,768]{1,0:T(8,128)(2,1)S(1)}, f32[8,1024]{1,0:T(8,128)S(1)}, bf16[1024,256]{1,0:T(8,128)(2,1)S(1)}, f32[512,1024]{1,0:T(8,128)S...) custom-call(s32[3]{0:T(128)S(1)} %pad_add_fusion.refs_0_, bf16[256,1024]{1,0:T(8,128)(2,1)S(1)} %bitcast.49, ...), custom_call_target="tpu_custom_call" | custom-call | flops 3221225472 | bytes 12128268 | tf_op jit(solution)/shard_map/attention_forward/pallas_call | solution.py:96
  94.6 12.3 %collective-permute-done.4.refs_4_ = bf16[256,1024]{1,0:T(8,128)(2,1)S(1)} collective-permute-done((bf16[256,1024]{1,0:T(8,128)(2,1)S(1)}, bf16[256,1024]{1,0:T(8,128)(2,1)S(1)}, u32[]{:S(2)}, u32[]{:S(2)}) %collective-permute-start.4) | collective-permute-done | bytes 524320 | tf_op jit(solution)/shard_map/ppermute | solution.py:1160
  119.4 17.3 %collective-permute-done.5.refs_1_ = bf16[160,1024]{1,0:T(8,128)(2,1)S(1)} collective-permute-done((bf16[160,1024]{1,0:T(8,128)(2,1)S(1)}, bf16[160,1024]{1,0:T(8,128)(2,1)S(1)}, u32[]{:S(2)}, u32[]{:S(2)}) %collective-permute-start.5) | collective-permute-done | bytes 327712 | tf_op jit(solution)/shard_map/ppermute | solution.py:1205
  137.4 12.8 %expert_forward.5 = (bf16[160,1024]{1,0:T(8,128)(2,1)}, bf16[160,1024]{1,0:T(8,128)(2,1)}, bf16[2,320,2816]{2,1,0:T(8,128)(2,1)}) custom-call(bf16[160,1024]{1,0:T(8,128)(2,1)} %copy-done.20, bf16[160,1024]{1,0:T(8,128)(2,1)} %copy-done.22, bf16[2,1,1024,5632]{3,2,1,0:T(8,128)(2,1)} %refs_5_.7, bf16[2,1,1024,5632]{3,2,1,0:T(8,128)(2,1)} %refs_5_.7, ...), custom_call_target="tpu_custom_call" | custom-call | flops 5536481280 | bytes 17301504 | tf_op jit(solution)/shard_map/expert_forward/pallas_call | solution.py:955
  150.9 10.0 %expert_forward.6 = (bf16[160,1024]{1,0:T(8,128)(2,1)}, bf16[2,160,2816]{2,1,0:T(8,128)(2,1)}) custom-call(bf16[160,1024]{1,0:T(8,128)(2,1)} %copy-done.24, bf16[2,1,1024,5632]{3,2,1,0:T(8,128)(2,1)} %refs_5_.7, bf16[2,1,1024,5632]{3,2,1,0:T(8,128)(2,1)} %refs_5_.7, bf16[2,1,1024,2816]{3,2,1,0:T(8,128)(2,1)} %refs_6_.1, ...), custom_call_target="tpu_custom_call" | custom-call | flops 5536481280 | bytes 17301504 | tf_op jit(solution)/shard_map/expert_forward/pallas_call | solution.py:955
  163.9 10.0 %expert_forward.7 = (bf16[160,1024]{1,0:T(8,128)(2,1)}, bf16[2,160,2816]{2,1,0:T(8,128)(2,1)}) custom-call(bf16[160,1024]{1,0:T(8,128)(2,1)} %copy-done.26, bf16[2,1,1024,5632]{3,2,1,0:T(8,128)(2,1)} %refs_5_.7, bf16[2,1,1024,5632]{3,2,1,0:T(8,128)(2,1)} %refs_5_.7, bf16[2,1,1024,2816]{3,2,1,0:T(8,128)(2,1)} %refs_6_.1, ...), custom_call_target="tpu_custom_call" | custom-call | flops 5536481280 | bytes 17301504 | tf_op jit(solution)/shard_map/expert_forward/pallas_call | solution.py:955
  189.0 9.6 %all-to-all-start.1 = ((bf16[4,160,1024]{2,1,0:T(8,128)(2,1)}), bf16[4,160,1024]{2,1,0:T(8,128)(2,1)}, u32[]{:S(2)}, u32[]{:S(2)}) async-start(bf16[4,160,1024]{2,1,0:T(8,128)(2,1)} %bitcast.13), calls=%async_computation.1 | async-start | bytes 2621440 | tf_op jit(solution)/shard_map/all_to_all | solution.py:1199
  200.2 12.2 %collective-permute-done.12.refs_3_.refs_14_ = bf16[256,1024]{1,0:T(8,128)(2,1)S(1)} collective-permute-done((bf16[256,1024]{1,0:T(8,128)(2,1)}, bf16[256,1024]{1,0:T(8,128)(2,1)S(1)}, u32[]{:S(2)}, u32[]{:S(2)}) %collective-permute-start.12) | collective-permute-done | bytes 524320 | tf_op jit(solution)/shard_map/ppermute | solution.py:1151
  214.4 9.8 %attention_forward.3 = (bf16[1024,768]{1,0:T(8,128)(2,1)S(1)}, f32[8,1024]{1,0:T(8,128)S(1)}, bf16[1024,256]{1,0:T(8,128)(2,1)S(1)}, f32[512,1024]{1,0:T(8,128)S(1)}, bf16[512,1024]{1,0:T(8,128)(2,1)S(1)}) custom-call(s32[3]{0:T(128)S(1)} %pad_add_fusion.refs_0_, bf16[256,1024]{1,0:T(8,128)(2,1)S(1)} %copy-done.76, ...), custom_call_target="tpu_custom_call" | custom-call | flops 3221225472 | bytes 10031116 | tf_op jit(solution)/shard_map/attention_forward/pallas_call | solution.py:96
  236.6 12.5 %collective-permute-done.15.refs_4_ = bf16[256,1024]{1,0:T(8,128)(2,1)S(1)} collective-permute-done((bf16[256,1024]{1,0:T(8,128)(2,1)S(1)}, bf16[256,1024]{1,0:T(8,128)(2,1)S(1)}, u32[]{:S(2)}, u32[]{:S(2)}) %collective-permute-start.15) | collective-permute-done | bytes 524320 | tf_op jit(solution)/shard_map/ppermute | solution.py:1160
  271.3 12.8 %expert_forward.8 = (bf16[160,1024]{1,0:T(8,128)(2,1)}, bf16[160,1024]{1,0:T(8,128)(2,1)}, bf16[2,320,2816]{2,1,0:T(8,128)(2,1)}) custom-call(bf16[160,1024]{1,0:T(8,128)(2,1)} %copy-done.30, bf16[160,1024]{1,0:T(8,128)(2,1)} %copy-done.34, bf16[2,1,1024,5632]{3,2,1,0:T(8,128)(2,1)} %refs_5_.7, bf16[2,1,1024,5632]{3,2,1,0:T(8,128)(2,1)} %refs_5_.7, ...), custom_call_target="tpu_custom_call" | custom-call | flops 5536481280 | bytes 17301504 | tf_op jit(solution)/shard_map/expert_forward/pallas_call | solution.py:955
  294.3 14.8 %expert_backward.4 = (bf16[160,1024]{1,0:T(8,128)(2,1)}, bf16[160,1024]{1,0:T(8,128)(2,1)}, bf16[3,320,2816]{2,1,0:T(8,128)(2,1)}) custom-call(bf16[160,1024]{1,0:T(8,128)(2,1)} %copy-done.36, bf16[160,1024]{1,0:T(8,128)(2,1)} %copy-done.38, bf16[2,320,2816]{2,1,0:T(8,128)(2,1)} %get-tuple-element.145.refs_2_, bf16[2,1,1024,5632]{3,2,1,0:T(8,128)(2,1)} %refs_5_.7, ...), custom_call_target="tpu_custom_call" | custom-call | flops 5536481280 | bytes 17301504 | tf_op jit(solution)/shard_map/expert_backward/pallas_call | solution.py:955
  310.1 12.7 %expert_forward.9 = (bf16[160,1024]{1,0:T(8,128)(2,1)}, bf16[160,1024]{1,0:T(8,128)(2,1)}, bf16[2,320,2816]{2,1,0:T(8,128)(2,1)}) custom-call(bf16[160,1024]{1,0:T(8,128)(2,1)} %copy-done.55, bf16[160,1024]{1,0:T(8,128)(2,1)} %copy-done.57, bf16[2,1,1024,5632]{3,2,1,0:T(8,128)(2,1)} %refs_5_.7, bf16[2,1,1024,5632]{3,2,1,0:T(8,128)(2,1)} %refs_5_.7, ...), custom_call_target="tpu_custom_call" | custom-call | flops 5536481280 | bytes 17301504 | tf_op jit(solution)/shard_map/expert_forward/pallas_call | solution.py:955
  322.8 15.0 %expert_backward.5 = (bf16[160,1024]{1,0:T(8,128)(2,1)}, bf16[160,1024]{1,0:T(8,128)(2,1)}, bf16[3,320,2816]{2,1,0:T(8,128)(2,1)}) custom-call(bf16[160,1024]{1,0:T(8,128)(2,1)} %copy-done.40, bf16[160,1024]{1,0:T(8,128)(2,1)} %copy-done.42, bf16[2,320,2816]{2,1,0:T(8,128)(2,1)} %get-tuple-element.152.refs_2_, bf16[2,1,1024,5632]{3,2,1,0:T(8,128)(2,1)} %refs_5_.7, ...), custom_call_target="tpu_custom_call" | custom-call | flops 5536481280 | bytes 17301504 | tf_op jit(solution)/shard_map/expert_backward/pallas_call | solution.py:955
  342.2 20.4 %expert_grads.2.refs_0_ = bf16[8,3,128,2816]{3,2,1,0:T(8,128)(2,1)} custom-call(bf16[160,1024]{1,0:T(8,128)(2,1)S(1)} %copy-done.31, bf16[160,1024]{1,0:T(8,128)(2,1)S(1)} %copy-done.35, bf16[160,1024]{1,0:T(8,128)(2,1)S(1)} %copy-done.56, bf16[160,1024]{1,0:T(8,128)(2,1)S(1)} %copy-done.58, bf16[160,1024]{1,0:T(8,128)(2,1)S(1)} %copy-done.37, ...), custom_call_target="tpu_custom_call" | custom-call | flops 5536481280 | bytes 17301504 | tf_op jit(solution)/shard_map/expert_grads/pallas_call | solution.py:955
  373.4 15.2 %collective-permute-done.20.refs_4_.refs_2_ = bf16[160,1024]{1,0:T(8,128)(2,1)S(1)} collective-permute-done((bf16[160,1024]{1,0:T(8,128)(2,1)S(1)}, bf16[160,1024]{1,0:T(8,128)(2,1)S(1)}, u32[]{:S(2)}, u32[]{:S(2)}) %collective-permute-start.20) | collective-permute-done | bytes 327712 | tf_op jit(solution)/shard_map/ppermute | solution.py:1205
  398.2 17.6 %collective-permute-done.26.refs_3_.refs_7_ = bf16[256,1024]{1,0:T(8,128)(2,1)S(1)} collective-permute-done((bf16[256,1024]{1,0:T(8,128)(2,1)S(1)}, bf16[256,1024]{1,0:T(8,128)(2,1)S(1)}, u32[]{:S(2)}, u32[]{:S(2)}) %collective-permute-start.26) | collective-permute-done | bytes 524320 | tf_op jit(solution)/shard_map/ppermute | solution.py:1151
  417.8 14.3 %attention_backward.2 = (bf16[1024,768]{1,0:T(8,128)(2,1)S(1)}, f32[512,1024]{1,0:T(8,128)S(1)}, bf16[512,1024]{1,0:T(8,128)(2,1)S(1)}, f32[8,512]{1,0:T(8,128)S(1)}, f32[8,1024]{1,0:T(8,128)S(1)}) custom-call(s32[3]{0:T(128)S(1)} %pad_add_fusion.refs_0_, bf16[256,1024]{1,0:T(8,128)(2,1)S(1)} %get-tuple-element.159.refs_1_.refs_5_, ...), custom_call_target="tpu_custom_call" | custom-call | flops 4831838208 | bytes 13225996 | tf_op jit(solution)/shard_map/attention_backward/pallas_call | solution.py:96
  438.5 23.8 %collective-permute-done.29.refs_4_ = bf16[256,1024]{1,0:T(8,128)(2,1)S(1)} collective-permute-done((bf16[256,1024]{1,0:T(8,128)(2,1)S(1)}, bf16[256,1024]{1,0:T(8,128)(2,1)S(1)}, u32[]{:S(2)}, u32[]{:S(2)}) %collective-permute-start.29) | collective-permute-done | bytes 524320 | tf_op jit(solution)/shard_map/ppermute | solution.py:1160
  466.1 8.0 %collective-permute-start.30 = (bf16[160,1024]{1,0:T(8,128)(2,1)S(1)}, bf16[160,1024]{1,0:T(8,128)(2,1)S(1)}, u32[]{:S(2)}, u32[]{:S(2)}) collective-permute-start(bf16[160,1024]{1,0:T(8,128)(2,1)S(1)} %get-tuple-element.166), channel_id=1, source_target_pairs={{0,8},{8,0},{16,24},{24,16},{1,9},{9,1},{17,25},{25,17},{2,10},{10... | collective-permute-start | bytes 983048 | tf_op jit(solution)/shard_map/ppermute | solution.py:1205
  486.6 15.4 %expert_backward.6 = (bf16[160,1024]{1,0:T(8,128)(2,1)}, bf16[160,1024]{1,0:T(8,128)(2,1)}, bf16[3,320,2816]{2,1,0:T(8,128)(2,1)}) custom-call(bf16[160,1024]{1,0:T(8,128)(2,1)} %copy-done.28, bf16[160,1024]{1,0:T(8,128)(2,1)} %copy-done.32, bf16[2,320,2816]{2,1,0:T(8,128)(2,1)} %get-tuple-element.167.refs_2_, bf16[2,1,1024,5632]{3,2,1,0:T(8,128)(2,1)} %refs_5_.7, ...), custom_call_target="tpu_custom_call" | custom-call | flops 5536481280 | bytes 17301504 | tf_op jit(solution)/shard_map/expert_backward/pallas_call | solution.py:955
  508.1 15.3 %expert_backward.7 = (bf16[160,1024]{1,0:T(8,128)(2,1)}, bf16[160,1024]{1,0:T(8,128)(2,1)}, bf16[3,320,2816]{2,1,0:T(8,128)(2,1)}) custom-call(bf16[160,1024]{1,0:T(8,128)(2,1)} %copy-done.59, bf16[160,1024]{1,0:T(8,128)(2,1)} %copy-done.61, bf16[2,160,2816]{2,1,0:T(8,128)(2,1)} %get-tuple-element.172.refs_2_, ...), custom_call_target="tpu_custom_call" | custom-call | flops 5536481280 | bytes 17301504 | tf_op jit(solution)/shard_map/expert_backward/pallas_call | solution.py:955
  523.4 8.0 %collective-permute-start.34 = (bf16[160,1024]{1,0:T(8,128)(2,1)}, bf16[160,1024]{1,0:T(8,128)(2,1)S(1)}, u32[]{:S(2)}, u32[]{:S(2)}) collective-permute-start(bf16[160,1024]{1,0:T(8,128)(2,1)} %get-tuple-element.174), channel_id=1, source_target_pairs={{0,16},{8,24},{16,0},{24,8},{1,17},{9,25},{17,1},{25,9},{2,18},{10... | collective-permute-start | bytes 983048 | tf_op jit(solution)/shard_map/ppermute | solution.py:1205
  535.3 20.5 %expert_grads.3.refs_0_ = bf16[8,3,128,2816]{3,2,1,0:T(8,128)(2,1)} custom-call(bf16[160,1024]{1,0:T(8,128)(2,1)S(1)} %copy-done.21, bf16[160,1024]{1,0:T(8,128)(2,1)S(1)} %copy-done.23, bf16[160,1024]{1,0:T(8,128)(2,1)S(1)} %copy-done.25, bf16[160,1024]{1,0:T(8,128)(2,1)S(1)} %copy-done.27, bf16[160,1024]{1,0:T(8,128)(2,1)S(1)} %copy-done.29, ...), custom_call_target="tpu_custom_call" | custom-call | flops 5536481280 | bytes 17301504 | tf_op jit(solution)/shard_map/expert_grads/pallas_call | solution.py:955
  569.0 7.1 %all-to-all-start.3 = ((bf16[4,128,1152]{2,1,0:T(8,128)(2,1)}), bf16[4,128,1152]{2,1,0:T(8,128)(2,1)}, u32[]{:S(2)}, u32[]{:S(2)}) async-start(bf16[4,128,1152]{2,1,0:T(8,128)(2,1)} %add_convert_fusion), calls=%async_computation.4 | async-start | bytes 2359296 | tf_op jit(solution)/shard_map/all_to_all | solution.py:1199
  577.2 12.3 %collective-permute-done.38.refs_3_.refs_4_ = bf16[256,1024]{1,0:T(8,128)(2,1)S(1)} collective-permute-done((bf16[256,1024]{1,0:T(8,128)(2,1)S(1)}, bf16[256,1024]{1,0:T(8,128)(2,1)S(1)}, u32[]{:S(2)}, u32[]{:S(2)}) %collective-permute-start.38) | collective-permute-done | bytes 524320 | tf_op jit(solution)/shard_map/ppermute | solution.py:1151
  598.6 15.1 %attention_backward.3 = (bf16[1024,768]{1,0:T(8,128)(2,1)S(1)}, f32[512,1024]{1,0:T(8,128)S(1)}, bf16[512,1024]{1,0:T(8,128)(2,1)}, f32[8,512]{1,0:T(8,128)S(1)}, f32[8,1024]{1,0:T(8,128)S(1)}) custom-call(s32[3]{0:T(128)S(1)} %pad_add_fusion.refs_0_, bf16[256,1024]{1,0:T(8,128)(2,1)S(1)} %copy-done.72, ...), custom_call_target="tpu_custom_call" | custom-call | flops 4831838208 | bytes 13225996 | tf_op jit(solution)/shard_map/attention_backward/pallas_call | solution.py:96
  640.1 15.3 %collective-permute-done.41.refs_4_ = bf16[256,1024]{1,0:T(8,128)(2,1)} collective-permute-done((bf16[256,1024]{1,0:T(8,128)(2,1)}, bf16[256,1024]{1,0:T(8,128)(2,1)}, u32[]{:S(2)}, u32[]{:S(2)}) %collective-permute-start.41) | collective-permute-done | bytes 524320 | tf_op jit(solution)/shard_map/ppermute | solution.py:1160
  684.6 8.1 %all-to-all-done.6.refs_0_ = bf16[4,2,32,896]{3,2,1,0:T(8,128)(2,1)S(1)} async-done(((bf16[4,2,32,896]{3,2,1,0:T(8,128)(2,1)}), bf16[4,2,32,896]{3,2,1,0:T(8,128)(2,1)S(1)}, u32[]{:S(2)}, u32[]{:S(2)}) %all-to-all-start.6) | async-done | bytes 458784 | tf_op jit(solution)/shard_map/all_to_all | solution.py:1240
  (420 shorter events, 239.9 us)
Async XLA Ops:
  7.2 66.6 %all-gather.5.cloned.1.call-start = ((), (), s32[]{:S(2)}) async-start(), calls=%async_computation.11 | async-start | bytes 2654208 | tf_op jit(solution)/shard_map/all_gather | solution.py:1253
  21.3 128.9 %all-gather.7.cloned.1.call-start = ((), (), s32[]{:S(2)}) async-start(), calls=%async_computation.12 | async-start | bytes 2359296 | tf_op jit(solution)/shard_map/all_gather | solution.py:1253
  22.5 54.1 %collective-permute-start = (bf16[256,1024]{1,0:T(8,128)(2,1)S(1)}, bf16[256,1024]{1,0:T(8,128)(2,1)S(1)}, u32[]{:S(2)}, u32[]{:S(2)}) collective-permute-start(bf16[256,1024]{1,0:T(8,128)(2,1)S(1)} %bitcast.48), channel_id=1, source_target_pairs={{0,2},{2,0},{4,6},{6,4},{1,3},{3,1},{5,7},{7,5},{8,10},{10,8},{12,... | collective-permute-start | bytes 1572872 | tf_op jit(solution)/shard_map/ppermute | solution.py:1152
  35.2 41.5 %collective-permute-start.2 = (bf16[256,1024]{1,0:T(8,128)(2,1)S(1)}, bf16[256,1024]{1,0:T(8,128)(2,1)S(1)}, u32[]{:S(2)}, u32[]{:S(2)}) collective-permute-start(bf16[256,1024]{1,0:T(8,128)(2,1)S(1)} %collective-permute-done.1.refs_3_), channel_id=1, source_target_pairs={{0,2},{2,0},{4,6},{6,4},{1,3},{3,1},{5,7},{7,5},{8,10},{10,8},{12,... | collective-permute-start | bytes 1572872 | tf_op jit(solution)/shard_map/ppermute | solution.py:1153
  115.0 21.7 %collective-permute-start.5 = (bf16[160,1024]{1,0:T(8,128)(2,1)S(1)}, bf16[160,1024]{1,0:T(8,128)(2,1)S(1)}, u32[]{:S(2)}, u32[]{:S(2)}) collective-permute-start(bf16[160,1024]{1,0:T(8,128)(2,1)S(1)} %get-tuple-element.120), channel_id=1, source_target_pairs={{0,8},{8,0},{16,24},{24,16},{1,9},{9,1},{17,25},{25,17},{2,10},{10... | collective-permute-start | bytes 983048 | tf_op jit(solution)/shard_map/ppermute | solution.py:1205
  116.5 33.7 %collective-permute-start.7 = (bf16[160,1024]{1,0:T(8,128)(2,1)}, bf16[160,1024]{1,0:T(8,128)(2,1)S(1)}, u32[]{:S(2)}, u32[]{:S(2)}) collective-permute-start(bf16[160,1024]{1,0:T(8,128)(2,1)} %get-tuple-element.123), channel_id=1, source_target_pairs={{0,16},{8,24},{16,0},{24,8},{1,17},{9,25},{17,1},{25,9},{2,18},{10... | collective-permute-start | bytes 983048 | tf_op jit(solution)/shard_map/ppermute | solution.py:1205
  117.4 45.8 %collective-permute-start.9 = (bf16[160,1024]{1,0:T(8,128)(2,1)}, bf16[160,1024]{1,0:T(8,128)(2,1)S(1)}, u32[]{:S(2)}, u32[]{:S(2)}) collective-permute-start(bf16[160,1024]{1,0:T(8,128)(2,1)} %get-tuple-element.126), channel_id=1, source_target_pairs={{0,24},{8,16},{16,8},{24,0},{1,25},{9,17},{17,9},{25,1},{2,26},{10... | collective-permute-start | bytes 983048 | tf_op jit(solution)/shard_map/ppermute | solution.py:1205
  189.0 42.9 %all-to-all-start.1 = ((bf16[4,160,1024]{2,1,0:T(8,128)(2,1)}), bf16[4,160,1024]{2,1,0:T(8,128)(2,1)}, u32[]{:S(2)}, u32[]{:S(2)}) async-start(bf16[4,160,1024]{2,1,0:T(8,128)(2,1)} %bitcast.13), calls=%async_computation.1 | async-start | bytes 2621440 | tf_op jit(solution)/shard_map/all_to_all | solution.py:1199
  260.2 29.5 %all-to-all-start.2 = ((f32[4,160,128]{2,1,0:T(8,128)}), f32[4,160,128]{2,1,0:T(8,128)}, u32[]{:S(2)}, u32[]{:S(2)}) async-start(f32[4,160,128]{2,1,0:T(8,128)} %bitcast.15), calls=%async_computation.2 | async-start | bytes 655360 | tf_op jit(solution)/shard_map/all_to_all | solution.py:1199
  264.3 372.2 %reduce-scatter.3.cloned.1.call-start = ((), (), s32[]{:S(2)}) async-start(), calls=%async_computation.9 | async-start | bytes 19464192 | tf_op jit(solution)/shard_map/reduce_scatter | solution.py:1362
  264.8 44.4 %collective-permute-start.18 = (bf16[160,1024]{1,0:T(8,128)(2,1)}, bf16[160,1024]{1,0:T(8,128)(2,1)S(1)}, u32[]{:S(2)}, u32[]{:S(2)}) collective-permute-start(bf16[160,1024]{1,0:T(8,128)(2,1)} %copy-done.103), channel_id=1, source_target_pairs={{0,16},{8,24},{16,0},{24,8},{1,17},{9,25},{17,1},{25,9},{2,18},{10... | collective-permute-start | bytes 983048 | tf_op jit(solution)/shard_map/ppermute | solution.py:1205
  267.7 41.5 %collective-permute-start.19 = (bf16[160,1024]{1,0:T(8,128)(2,1)}, bf16[160,1024]{1,0:T(8,128)(2,1)S(1)}, u32[]{:S(2)}, u32[]{:S(2)}) collective-permute-start(bf16[160,1024]{1,0:T(8,128)(2,1)} %copy-done.102), channel_id=1, source_target_pairs={{0,24},{8,16},{16,8},{24,0},{1,25},{9,17},{17,9},{25,1},{2,26},{10... | collective-permute-start | bytes 983048 | tf_op jit(solution)/shard_map/ppermute | solution.py:1205
  309.2 53.5 %collective-permute-start.22 = (bf16[160,1024]{1,0:T(8,128)(2,1)}, bf16[160,1024]{1,0:T(8,128)(2,1)S(1)}, u32[]{:S(2)}, u32[]{:S(2)}) collective-permute-start(bf16[160,1024]{1,0:T(8,128)(2,1)} %get-tuple-element.149), channel_id=1, source_target_pairs={{0,8},{8,0},{16,24},{24,16},{1,9},{9,1},{17,25},{25,17},{2,10},{10... | collective-permute-start | bytes 983048 | tf_op jit(solution)/shard_map/ppermute | solution.py:1205
  337.8 24.9 %collective-permute-start.23 = (bf16[160,1024]{1,0:T(8,128)(2,1)}, bf16[160,1024]{1,0:T(8,128)(2,1)S(1)}, u32[]{:S(2)}, u32[]{:S(2)}) collective-permute-start(bf16[160,1024]{1,0:T(8,128)(2,1)} %get-tuple-element.153), channel_id=1, source_target_pairs={{0,16},{8,24},{16,0},{24,8},{1,17},{9,25},{17,1},{25,9},{2,18},{10... | collective-permute-start | bytes 983048 | tf_op jit(solution)/shard_map/ppermute | solution.py:1205
  339.5 23.1 %collective-permute-start.24 = (bf16[160,1024]{1,0:T(8,128)(2,1)}, bf16[160,1024]{1,0:T(8,128)(2,1)S(1)}, u32[]{:S(2)}, u32[]{:S(2)}) collective-permute-start(bf16[160,1024]{1,0:T(8,128)(2,1)} %get-tuple-element.154), channel_id=1, source_target_pairs={{0,24},{8,16},{16,8},{24,0},{1,25},{9,17},{17,9},{25,1},{2,26},{10... | collective-permute-start | bytes 983048 | tf_op jit(solution)/shard_map/ppermute | solution.py:1205
  364.3 331.5 %reduce-scatter.5.cloned.1.call-start = ((), (), s32[]{:S(2)}) async-start(), calls=%async_computation.10 | async-start | bytes 19464192 | tf_op jit(solution)/shard_map/reduce_scatter | solution.py:1362
  365.3 23.3 %collective-permute-start.20 = (bf16[160,1024]{1,0:T(8,128)(2,1)S(1)}, bf16[160,1024]{1,0:T(8,128)(2,1)S(1)}, u32[]{:S(2)}, u32[]{:S(2)}) collective-permute-start(bf16[160,1024]{1,0:T(8,128)(2,1)S(1)} %copy-done.134), channel_id=1, source_target_pairs={{0,16},{8,24},{16,0},{24,8},{1,17},{9,25},{17,1},{25,9},{2,18},{10... | collective-permute-start | bytes 983048 | tf_op jit(solution)/shard_map/ppermute | solution.py:1205
  367.0 21.7 %collective-permute-start.21 = (bf16[160,1024]{1,0:T(8,128)(2,1)S(1)}, bf16[160,1024]{1,0:T(8,128)(2,1)S(1)}, u32[]{:S(2)}, u32[]{:S(2)}) collective-permute-start(bf16[160,1024]{1,0:T(8,128)(2,1)S(1)} %copy-done.133), channel_id=1, source_target_pairs={{0,24},{8,16},{16,8},{24,0},{1,25},{9,17},{17,9},{25,1},{2,26},{10... | collective-permute-start | bytes 983048 | tf_op jit(solution)/shard_map/ppermute | solution.py:1205
  396.7 19.2 %collective-permute-start.26 = (bf16[256,1024]{1,0:T(8,128)(2,1)S(1)}, bf16[256,1024]{1,0:T(8,128)(2,1)S(1)}, u32[]{:S(2)}, u32[]{:S(2)}) collective-permute-start(bf16[256,1024]{1,0:T(8,128)(2,1)S(1)} %get-tuple-element.159.refs_1_.refs_5_), channel_id=1, source_target_pairs={{0,4},{2,6},{4,0},{6,2},{1,5},{3,7},{5,1},{7,3},{8,12},{10,14},{12... | collective-permute-start | bytes 1572872 | tf_op jit(solution)/shard_map/ppermute | solution.py:1151
  436.1 26.2 %collective-permute-start.29 = (bf16[256,1024]{1,0:T(8,128)(2,1)S(1)}, bf16[256,1024]{1,0:T(8,128)(2,1)S(1)}, u32[]{:S(2)}, u32[]{:S(2)}) collective-permute-start(bf16[256,1024]{1,0:T(8,128)(2,1)S(1)} %add_convert_fusion.3), channel_id=1, source_target_pairs={{0,4},{2,6},{4,0},{6,2},{1,5},{3,7},{5,1},{7,3},{8,12},{10,14},{12... | collective-permute-start | bytes 1572872 | tf_op jit(solution)/shard_map/ppermute | solution.py:1160
  466.1 19.7 %collective-permute-start.30 = (bf16[160,1024]{1,0:T(8,128)(2,1)S(1)}, bf16[160,1024]{1,0:T(8,128)(2,1)S(1)}, u32[]{:S(2)}, u32[]{:S(2)}) collective-permute-start(bf16[160,1024]{1,0:T(8,128)(2,1)S(1)} %get-tuple-element.166), channel_id=1, source_target_pairs={{0,8},{8,0},{16,24},{24,16},{1,9},{9,1},{17,25},{25,17},{2,10},{10... | collective-permute-start | bytes 983048 | tf_op jit(solution)/shard_map/ppermute | solution.py:1205
  481.6 50.8 %collective-permute-start.36 = (bf16[4,128,1152]{2,1,0:T(8,128)(2,1)S(1)}, bf16[4,128,1152]{2,1,0:T(8,128)(2,1)S(1)}, u32[]{:S(2)}, u32[]{:S(2)}) collective-permute-start(bf16[4,128,1152]{2,1,0:T(8,128)(2,1)S(1)} %get-tuple-element.185), channel_id=1, source_target_pairs={{0,1},{1,0},{2,3},{3,2},{4,5},{5,4},{6,7},{7,6},{8,9},{9,8},{10,11... | collective-permute-start | bytes 3538952 | tf_op jit(solution)/shard_map/ppermute | solution.py:1395
  482.6 24.6 %collective-permute-start.32 = (bf16[160,1024]{1,0:T(8,128)(2,1)S(1)}, bf16[160,1024]{1,0:T(8,128)(2,1)S(1)}, u32[]{:S(2)}, u32[]{:S(2)}) collective-permute-start(bf16[160,1024]{1,0:T(8,128)(2,1)S(1)} %get-tuple-element.170), channel_id=1, source_target_pairs={{0,16},{8,24},{16,0},{24,8},{1,17},{9,25},{17,1},{25,9},{2,18},{10... | collective-permute-start | bytes 983048 | tf_op jit(solution)/shard_map/ppermute | solution.py:1205
  484.3 22.9 %collective-permute-start.33 = (bf16[160,1024]{1,0:T(8,128)(2,1)S(1)}, bf16[160,1024]{1,0:T(8,128)(2,1)S(1)}, u32[]{:S(2)}, u32[]{:S(2)}) collective-permute-start(bf16[160,1024]{1,0:T(8,128)(2,1)S(1)} %get-tuple-element.171), channel_id=1, source_target_pairs={{0,24},{8,16},{16,8},{24,0},{1,25},{9,17},{17,9},{25,1},{2,26},{10... | collective-permute-start | bytes 983048 | tf_op jit(solution)/shard_map/ppermute | solution.py:1205
  502.0 53.8 %collective-permute-start.31 = (bf16[160,1024]{1,0:T(8,128)(2,1)}, bf16[160,1024]{1,0:T(8,128)(2,1)S(1)}, u32[]{:S(2)}, u32[]{:S(2)}) collective-permute-start(bf16[160,1024]{1,0:T(8,128)(2,1)} %get-tuple-element.169.refs_7_), channel_id=1, source_target_pairs={{0,8},{8,0},{16,24},{24,16},{1,9},{9,1},{17,25},{25,17},{2,10},{10... | collective-permute-start | bytes 983048 | tf_op jit(solution)/shard_map/ppermute | solution.py:1205
  523.4 32.4 %collective-permute-start.34 = (bf16[160,1024]{1,0:T(8,128)(2,1)}, bf16[160,1024]{1,0:T(8,128)(2,1)S(1)}, u32[]{:S(2)}, u32[]{:S(2)}) collective-permute-start(bf16[160,1024]{1,0:T(8,128)(2,1)} %get-tuple-element.174), channel_id=1, source_target_pairs={{0,16},{8,24},{16,0},{24,8},{1,17},{9,25},{17,1},{25,9},{2,18},{10... | collective-permute-start | bytes 983048 | tf_op jit(solution)/shard_map/ppermute | solution.py:1205
  531.4 24.4 %collective-permute-start.35 = (bf16[160,1024]{1,0:T(8,128)(2,1)}, bf16[160,1024]{1,0:T(8,128)(2,1)S(1)}, u32[]{:S(2)}, u32[]{:S(2)}) collective-permute-start(bf16[160,1024]{1,0:T(8,128)(2,1)} %get-tuple-element.175), channel_id=1, source_target_pairs={{0,24},{8,16},{16,8},{24,0},{1,25},{9,17},{17,9},{25,1},{2,26},{10... | collective-permute-start | bytes 983048 | tf_op jit(solution)/shard_map/ppermute | solution.py:1205
  569.0 47.4 %all-to-all-start.3 = ((bf16[4,128,1152]{2,1,0:T(8,128)(2,1)}), bf16[4,128,1152]{2,1,0:T(8,128)(2,1)}, u32[]{:S(2)}, u32[]{:S(2)}) async-start(bf16[4,128,1152]{2,1,0:T(8,128)(2,1)} %add_convert_fusion), calls=%async_computation.4 | async-start | bytes 2359296 | tf_op jit(solution)/shard_map/all_to_all | solution.py:1199
  625.0 36.9 %all-to-all-start.5 = ((bf16[4,2,128,640]{3,2,1,0:T(8,128)(2,1)}), bf16[4,2,128,640]{3,2,1,0:T(8,128)(2,1)}, u32[]{:S(2)}, u32[]{:S(2)}) async-start(bf16[4,2,128,640]{3,2,1,0:T(8,128)(2,1)} %copy-done.44), calls=%async_computation.6 | async-start | bytes 2621440 | tf_op jit(solution)/shard_map/all_to_all | solution.py:1199
  632.0 23.4 %collective-permute-start.41 = (bf16[256,1024]{1,0:T(8,128)(2,1)}, bf16[256,1024]{1,0:T(8,128)(2,1)}, u32[]{:S(2)}, u32[]{:S(2)}) collective-permute-start(bf16[256,1024]{1,0:T(8,128)(2,1)} %add_convert_fusion.2), channel_id=1, source_target_pairs={{0,4},{2,6},{4,0},{6,2},{1,5},{3,7},{5,1},{7,3},{8,12},{10,14},{12... | collective-permute-start | bytes 1572872 | tf_op jit(solution)/shard_map/ppermute | solution.py:1160
  632.6 25.7 %collective-permute-start.42 = (bf16[4,128,512]{2,1,0:T(8,128)(2,1)}, bf16[4,128,512]{2,1,0:T(8,128)(2,1)}, u32[]{:S(2)}, u32[]{:S(2)}) collective-permute-start(bf16[4,128,512]{2,1,0:T(8,128)(2,1)} %copy-done.98), channel_id=1, source_target_pairs={{0,1},{1,0},{2,3},{3,2},{4,5},{5,4},{6,7},{7,6},{8,9},{9,8},{10,11... | collective-permute-start | bytes 1572872 | tf_op jit(solution)/shard_map/ppermute | solution.py:1395
  661.9 18.2 %all-to-all-start.4 = ((bf16[4,128,512]{2,1,0:T(8,128)(2,1)}), bf16[4,128,512]{2,1,0:T(8,128)(2,1)S(1)}, u32[]{:S(2)}, u32[]{:S(2)}) async-start(bf16[4,128,512]{2,1,0:T(8,128)(2,1)} %add_convert_fusion.1), calls=%async_computation.5 | async-start | bytes 1048576 | tf_op jit(solution)/shard_map/all_to_all | solution.py:1199
  (158 other events, 1801.4 us)
Sparse Core Ops, SparseCore 0:
  21.4 52.3 all-gather.4
  76.5 56.9 all-gather.6
  364.4 152.2 reduce-scatter.2
  556.9 133.0 reduce-scatter.4
